TPU v7x, 32 devices: a whole 2x2x4 slice. The times are simulated.
32 devices in a mesh: expert: 8 (over z, x), tensor: 4 (over y, core).
Axes of the slice: x: 2, y: 2, z: 4, core: 2. Of those that a mesh axis runs over, the one named last changes fastest.
Arguments:
- tokens: bfloat16 [8192, 768], P('expert'), may hold values from -6 to 6
- gain_attn: float32 [768], replicated, may hold values from 0.5 to 1.5
- w_qkv: bfloat16 [3, 768, 768], P(None, None, 'tensor'), may hold values from -0.21875 to 0.21875
- w_proj: bfloat16 [768, 768], P('tensor'), may hold values from -3.5 to 3.5
- rel_bias: float32 [12, 32], P('tensor'), may hold values from -1 to 1
- gain_ffn: float32 [768], replicated, may hold values from 0.5 to 1.5
- w_router: bfloat16 [768, 8], replicated, may hold values from -0.109375 to 0.109375
- w_in: bfloat16 [8, 768, 3072], P('expert', None, 'tensor'), may hold values from -0.21875 to 0.21875
- w_out: bfloat16 [8, 3072, 768], P('expert', 'tensor'), may hold values from -1.5 to 1.5
- routes: int32 [8192, 1], P('expert'), may hold values from 0 to 7; in each aligned block of 1024 rows (0 to 1023, 1024 to 2047, ...) at most 192 rows name the same one
- segment_ids: int32 [8, 1024], P('expert'), may hold values from 0 to 3, never falling along the last dimension, each value on 1 to 512 neighbouring positions
- cotangent: bfloat16 [8192, 768], P('expert'), may hold values from -6 to 6
Outputs:
- output: bfloat16 [8192, 768], P('expert')
- grad_input: float32 [8192, 768], P('expert')
- grad_gain_attn: float32 [768], replicated
- grad_qkv: float32 [3, 768, 768], P(None, None, 'tensor')
- grad_proj: float32 [768, 768], P('tensor')
- grad_rel: float32 [12, 32], P('tensor')
- grad_gain_ffn: float32 [768], replicated
- grad_router: float32 [768, 8], replicated
- grad_w_in: float32 [8, 768, 3072], P('expert', None, 'tensor')
- grad_w_out: float32 [8, 3072, 768], P('expert', 'tensor')
Inputs may be any that keep to these rules, and one draw needn't show every extreme that they name: `routes`: among the 1024 tokens of one sequence no expert is named more than 192 times, a bound that some block reaches. `segment_ids`: within each sequence the document numbers never fall, each document has at most 512 positions.
All inputs are finite; a program needn't handle non-finite values.
Results may differ from a plain program's by a relative error of at most 0.017.
Values may be sent and summed in bfloat16 or wider, within the bound.
No kernel may reach another device: no remote copies, remote signals or barrier semaphores. Data moves between devices by JAX's collectives and lax.ppermute only.
A program may use at most 192 MiB of HBM per device.

v0:
```python
import functools

import jax
import jax.numpy as jnp
from jax import lax
from jax.experimental import pallas as pl
from jax.experimental.pallas import tpu as pltpu
from jax.sharding import PartitionSpec as P

FAR_LIMITS = (12, 16, 23, 32, 46, 64, 91)
HIGH = lax.Precision.HIGHEST
F32 = jnp.float32
BF16 = jnp.bfloat16
MASKED = -1e30
QB = 256
PAD = 256
FAR = FAR_LIMITS[-1]
SMALL = pl.CostEstimate(flops=1 << 20, bytes_accessed=1 << 16, transcendentals=0)

STEPS = (
    [(1 - limit, 14 - i) for i, limit in enumerate(reversed(FAR_LIMITS))]
    + [(-n, n) for n in range(7, -1, -1)]
    + [(n, 16 + n) for n in range(1, 8)]
    + [(8, 24)]
    + [(limit, 25 + i) for i, limit in enumerate(FAR_LIMITS)]
)


def norm_rows(values, gain):
    return values * lax.rsqrt(jnp.mean(values * values, -1, keepdims=True) + 1e-06) * gain


def nt_dot(left, right):
    return lax.dot_general(left, right, (((1,), (1,)), ((), ())), preferred_element_type=F32)


def nn_dot(left, right):
    return jnp.dot(left, right, preferred_element_type=F32)


def strip_shape(length):
    return 2 * length - QB


def near_rows(length):
    base = length - QB
    first = (base - FAR) // 32 * 32
    last = -(-(base + 127 + FAR) // 32) * 32
    return base, first, last


def build_strip(strip_ref, bias_ref, length, heads):
    total = strip_shape(length)
    base, first, last = near_rows(length)
    for h in range(heads):
        low = jnp.full((8, 128), bias_ref[h, 15], F32)
        high = jnp.full((8, 128), bias_ref[h, 31], F32)
        for half in range(QB // 128):
            cols = slice(half * 128, half * 128 + 128)
            lo_end, hi_start = first + half * 128, last + half * 128
            strip_ref[h, 0:lo_end, cols] = jnp.broadcast_to(low[:1], (lo_end, 128))
            strip_ref[h, hi_start:total, cols] = jnp.broadcast_to(high[:1], (total - hi_start, 128))
    for start in range(first, last, 32):
        offset = (
            lax.broadcasted_iota(jnp.int32, (32, 128), 0)
            - lax.broadcasted_iota(jnp.int32, (32, 128), 1)
            + (start - base)
        )
        tiles = [jnp.full((32, 128), bias_ref[h, 15], F32) for h in range(heads)]
        for begin, bucket in STEPS:
            reached = offset >= begin
            tiles = [jnp.where(reached, bias_ref[h, bucket], tiles[h]) for h in range(heads)]
        for h in range(heads):
            for half in range(QB // 128):
                at = start + half * 128
                strip_ref[h, at : at + 32, half * 128 : half * 128 + 128] = tiles[h]


def head_lanes(rows, h, dim, keep_tail, heads):
    lane = lax.broadcasted_iota(jnp.int32, (rows, PAD), 1)
    inside = (lane >= h * dim) & (lane < (h + 1) * dim)
    if keep_tail:
        inside = inside | (lane >= heads * dim)
    return inside


def attend_kernel(
    length, heads, dim,
    x_ref, gain_ref, w_ref, doc_ref, bias_ref,
    att_ref, lse_ref, proj_ref, kt_ref, normed_ref,
    kh_ref, strip_ref, vt_ref, pad_ref,
):
    inner = heads * dim
    build_strip(strip_ref, bias_ref, length, heads)
    lane = lax.broadcasted_iota(jnp.int32, (QB, PAD), 1) - inner
    pad_ref[...] = jnp.zeros_like(pad_ref)
    for t in range(3):
        pad_ref[t * PAD : t * PAD + inner, :] = w_ref[t]

    def project(b, carry):
        at = pl.multiple_of(b * QB, QB)
        here = x_ref[pl.ds(at, QB), :].astype(F32)
        normed = norm_rows(here, gain_ref[...]).astype(BF16)
        normed_ref[pl.ds(at, QB), :] = normed
        every = nt_dot(normed, pad_ref[...])
        same = doc_ref[pl.ds(at, QB), :] == lane
        queries = (every[:, 0:PAD].astype(BF16) * jnp.bfloat16(dim ** (-0.5))).astype(F32)
        queries = queries + jnp.where((lane < 0) | same, 0.0, MASKED)
        keys = every[:, PAD : 2 * PAD]
        values = every[:, 2 * PAD : 3 * PAD]
        proj_ref[pl.ds(at, QB), 0:PAD] = queries.astype(BF16)
        proj_ref[pl.ds(at, QB), PAD : 2 * PAD] = (keys + jnp.where(same, 1.0, 0.0)).astype(BF16)
        proj_ref[pl.ds(at, QB), 2 * PAD : 3 * PAD] = values.astype(BF16)
        kt_ref[:, pl.ds(at, QB)] = keys.T[:inner].astype(BF16)
        vt_ref[:, pl.ds(at, QB)] = values.T[:inner].astype(BF16)
        return carry

    lax.fori_loop(0, length // QB, project, 0)
    keys = proj_ref[:, PAD : 2 * PAD]
    for h in range(heads):
        kh_ref[h] = jnp.where(head_lanes(length, h, dim, True, heads), keys, jnp.zeros_like(keys))

    def block(b, carry):
        at = pl.multiple_of(b * QB, QB)
        from_row = pl.multiple_of(length - QB - b * QB, QB)
        queries = proj_ref[pl.ds(at, QB), 0:PAD]
        for h in range(heads):
            scores = nt_dot(kh_ref[h], queries) + strip_ref[h, pl.ds(from_row, length), :]
            top = jnp.max(scores, 0, keepdims=True)
            probs = jnp.exp(scores - top)
            total = jnp.sum(probs, 0, keepdims=True)
            out = nn_dot(vt_ref[h * dim : (h + 1) * dim, :], probs.astype(BF16))
            att_ref[h * dim : (h + 1) * dim, pl.ds(at, QB)] = (out / total).astype(BF16)
            lse_ref[h : h + 1, pl.ds(at, QB)] = top + jnp.log(total)
        return carry

    lax.fori_loop(0, length // QB, block, 0)


def attend_back_kernel(
    length, heads, dim,
    proj_ref, kt_ref, lse_ref, da_ref, normed_ref, w_ref, gproj_ref, bias_ref, low_ref,
    grad_ref, kept_ref, sent_ref, drel_ref,
    kh_ref, vh_ref, strip_ref, dstrip_ref, pcat_ref, dcat_ref, dacat_ref, qcat_ref, dk_ref, dv_ref, dqt_ref,
    dq_ref, pad_ref,
):
    inner = heads * dim
    scale = dim ** (-0.5)
    total = strip_shape(length)
    base, first, last = near_rows(length)
    build_strip(strip_ref, bias_ref, length, heads)
    dstrip_ref[...] = jnp.zeros_like(dstrip_ref)
    dk_ref[...] = jnp.zeros_like(dk_ref)
    dv_ref[...] = jnp.zeros_like(dv_ref)
    dqt_ref[...] = jnp.zeros_like(dqt_ref)
    keys = proj_ref[:, PAD : 2 * PAD]
    values = proj_ref[:, 2 * PAD : 3 * PAD]
    for h in range(heads):
        kh_ref[h] = jnp.where(head_lanes(length, h, dim, True, heads), keys, jnp.zeros_like(keys))
        vh_ref[h] = jnp.where(head_lanes(length, h, dim, False, heads), values, jnp.zeros_like(values))

    def block(b, carry):
        at = pl.multiple_of(b * QB, QB)
        from_row = pl.multiple_of(length - QB - b * QB, QB)
        queries = proj_ref[pl.ds(at, QB), 0:PAD]
        grads = da_ref[pl.ds(at, QB), :]
        for h in range(heads):
            mine = head_lanes(QB, h, dim, False, heads)
            cols = slice(h * QB, (h + 1) * QB)
            qcat_ref[cols, :] = jnp.where(mine, queries, jnp.zeros_like(queries))
            dacat_ref[cols, :] = jnp.where(mine, grads, jnp.zeros_like(grads))
            scores = nt_dot(kh_ref[h], queries) + strip_ref[h, pl.ds(from_row, length), :]
            probs = jnp.exp(scores - lse_ref[h : h + 1, pl.ds(at, QB)])
            weighted = probs * nt_dot(vh_ref[h], grads)
            delta = jnp.sum(weighted, 0, keepdims=True)
            dscore = weighted - probs * delta
            dstrip_ref[h, pl.ds(from_row, length), :] += dscore
            dlow = dscore.astype(BF16)
            pcat_ref[:, cols] = probs.astype(BF16)
            dcat_ref[:, cols] = dlow
            dqt_ref[h * dim : (h + 1) * dim, :] = nn_dot(kt_ref[h * dim : (h + 1) * dim, :], dlow) * scale
        dk_ref[...] += nn_dot(dcat_ref[...], qcat_ref[...])
        dv_ref[...] += nn_dot(pcat_ref[...], dacat_ref[...])
        dq_ref[pl.ds(at, QB), :] = dqt_ref[...].T
        return carry

    lax.fori_loop(0, length // QB, block, 0)

    for t, ref in enumerate((dq_ref, dk_ref, dv_ref)):
        turned = ref[...].T[:inner].astype(BF16)
        grad_ref[t * inner : (t + 1) * inner, :] = nn_dot(turned, normed_ref[...]).astype(BF16)

    grad_ref[3 * inner :, :] = gproj_ref[...]

    pad_ref[...] = jnp.zeros_like(pad_ref)
    for t in range(3):
        pad_ref[t, 0:inner, :] = w_ref[t]
    half = length // 2

    def part(start):
        total = jnp.zeros((QB, w_ref.shape[2]), F32)
        for t, ref in enumerate((dq_ref, dk_ref, dv_ref)):
            total = total + nn_dot(ref[pl.ds(start, QB), :].astype(BF16), pad_ref[t])
        return total

    for i in range(half // QB):
        rows = slice(i * QB, (i + 1) * QB)
        kept_ref[rows, :] = part(pl.multiple_of(low_ref[0] * half + i * QB, QB))
        sent_ref[rows, :] = part(pl.multiple_of((1 - low_ref[0]) * half + i * QB, QB)).astype(BF16)

    offset = (
        lax.broadcasted_iota(jnp.int32, (last - first, 128), 0)
        - lax.broadcasted_iota(jnp.int32, (last - first, 128), 1)
        + (first - base)
    )
    begins = [-(1 << 20)] + [begin for begin, bucket in STEPS] + [1 << 20]
    buckets = [15] + [bucket for begin, bucket in STEPS]
    for h in range(heads):
        near = jnp.zeros((last - first, 128), F32)
        low = jnp.zeros((1, 128), F32)
        high = jnp.zeros((1, 128), F32)
        for half in range(QB // 128):
            cols = slice(half * 128, half * 128 + 128)
            lo_end, hi_start = first + half * 128, last + half * 128
            near = near + dstrip_ref[h, lo_end:hi_start, cols]
            low = low + jnp.sum(dstrip_ref[h, 0:lo_end, cols], 0, keepdims=True)
            high = high + jnp.sum(dstrip_ref[h, hi_start:total, cols], 0, keepdims=True)
        drel_ref[h, 16:17, :] = jnp.zeros((1, 128), F32)
        for i, bucket in enumerate(buckets):
            inside = (offset >= begins[i]) & (offset < begins[i + 1])
            row = jnp.sum(jnp.where(inside, near, 0.0), 0, keepdims=True)
            if bucket == 15:
                row = row + low
            if bucket == 31:
                row = row + high
            drel_ref[h, bucket : bucket + 1, :] = row


def whole_vmem(count):
    return [pl.BlockSpec(memory_space=pltpu.VMEM)] * count


def attend(tokens, gain, w_qkv, segments, rel_bias):
    length, width = tokens.shape
    heads = rel_bias.shape[0]
    inner = w_qkv.shape[1]
    return pl.pallas_call(
        functools.partial(attend_kernel, length, heads, inner // heads),
        out_shape=(
            jax.ShapeDtypeStruct((inner, length), BF16),
            jax.ShapeDtypeStruct((8, length), F32),
            jax.ShapeDtypeStruct((length, 3 * PAD), BF16),
            jax.ShapeDtypeStruct((inner, length), BF16),
            jax.ShapeDtypeStruct((length, width), BF16),
        ),
        in_specs=whole_vmem(4) + [pl.BlockSpec(memory_space=pltpu.SMEM)],
        out_specs=tuple(whole_vmem(5)),
        scratch_shapes=[
            pltpu.VMEM((heads, length, PAD), BF16),
            pltpu.VMEM((heads, strip_shape(length), QB), F32),
            pltpu.VMEM((inner, length), BF16),
            pltpu.VMEM((3 * PAD, width), BF16),
        ],
        compiler_params=pltpu.CompilerParams(vmem_limit_bytes=20 << 20),
        cost_estimate=SMALL,
    )(tokens, gain[None, :], w_qkv, segments[:, None], rel_bias)


def attend_back(proj, kt, lse, da, normed, w_qkv, grad_proj, rel_bias, low_bit):
    length, width = normed.shape
    heads, buckets = rel_bias.shape
    inner = w_qkv.shape[1]
    return pl.pallas_call(
        functools.partial(attend_back_kernel, length, heads, inner // heads),
        out_shape=(
            jax.ShapeDtypeStruct((4 * inner, width), BF16),
            jax.ShapeDtypeStruct((length // 2, width), F32),
            jax.ShapeDtypeStruct((length // 2, width), BF16),
            jax.ShapeDtypeStruct((heads, buckets, 128), F32),
        ),
        in_specs=whole_vmem(7) + [pl.BlockSpec(memory_space=pltpu.SMEM)] * 2,
        out_specs=tuple(whole_vmem(4)),
        scratch_shapes=[
            pltpu.VMEM((heads, length, PAD), BF16),
            pltpu.VMEM((heads, length, PAD), BF16),
            pltpu.VMEM((heads, strip_shape(length), QB), F32),
            pltpu.VMEM((heads, strip_shape(length), QB), F32),
            pltpu.VMEM((length, heads * QB), BF16),
            pltpu.VMEM((length, heads * QB), BF16),
            pltpu.VMEM((heads * QB, PAD), BF16),
            pltpu.VMEM((heads * QB, PAD), BF16),
            pltpu.VMEM((length, PAD), F32),
            pltpu.VMEM((length, PAD), F32),
            pltpu.VMEM((PAD, QB), F32),
            pltpu.VMEM((length, PAD), F32),
            pltpu.VMEM((3, PAD, width), BF16),
        ],
        compiler_params=pltpu.CompilerParams(vmem_limit_bytes=36 << 20),
        cost_estimate=SMALL,
    )(proj, kt, lse, da, normed, w_qkv, grad_proj, rel_bias, low_bit)


def gelu_pair(v):
    inner = 0.7978845608028654 * (v + 0.044715 * (v * v * v))
    bend = jnp.tanh(inner)
    half = 0.5 * (1.0 + bend)
    slope = half + 0.5 * v * (1.0 - bend * bend) * (0.7978845608028654 * (1.0 + 0.134145 * (v * v)))
    return v * half, slope


def expert_kernel(
    members, experts,
    rows_ref, cot_ref, router_ref, group_ref, *refs,
):
    first, second = refs[:members], refs[members : 2 * members]
    reply_ref, share_ref, act_ref, gpre_ref, grad_ref, grouter_ref = refs[2 * members :]
    rows = rows_ref[...]
    count = rows.shape[0]
    lane = lax.broadcasted_iota(jnp.int32, (count, 128), 1)
    logits = jnp.where(lane < experts, nn_dot(rows, router_ref[...]), MASKED)
    raised = jnp.exp(logits - jnp.max(logits, -1, keepdims=True))
    probs = raised / jnp.sum(raised, -1, keepdims=True)
    own = jnp.where(lane == group_ref[0], 1.0, 0.0)
    gate = jnp.sum(probs * own, -1, keepdims=True)
    cot = cot_ref[...].astype(F32)
    grads = (gate * cot).astype(BF16)
    grad_ref[...] = grads
    reply = jnp.zeros(rows.shape, F32)
    share = jnp.zeros(rows.shape, F32)
    for k in range(members):
        act, slope = gelu_pair(nn_dot(rows, first[k][...]))
        act = act.astype(BF16)
        act_ref[k] = act
        reply = reply + nn_dot(act, second[k][...])
        gpre = (nt_dot(grads, second[k][...]) * slope).astype(BF16)
        gpre_ref[k] = gpre
        share = share + nt_dot(gpre, first[k][...])
    reply = reply.astype(BF16)
    reply_ref[...] = reply
    gate_grad = jnp.sum(cot * reply.astype(F32), -1, keepdims=True)
    logit_grad = probs * (own - gate) * gate_grad
    share_ref[...] = (share + nt_dot(logit_grad.astype(BF16), router_ref[...])).astype(BF16)
    grouter_ref[...] = nn_dot(logit_grad.T.astype(BF16), rows)


def expert_step(rows, cot, experts, router, group, first, second):
    members = len(first)
    count, width = rows.shape
    hidden = first[0].shape[1]
    return pl.pallas_call(
        functools.partial(expert_kernel, members, experts),
        out_shape=(
            jax.ShapeDtypeStruct((count, width), BF16),
            jax.ShapeDtypeStruct((count, width), BF16),
            jax.ShapeDtypeStruct((members, count, hidden), BF16),
            jax.ShapeDtypeStruct((members, count, hidden), BF16),
            jax.ShapeDtypeStruct((count, width), BF16),
            jax.ShapeDtypeStruct((128, width), F32),
        ),
        in_specs=whole_vmem(3) + [pl.BlockSpec(memory_space=pltpu.SMEM)] + whole_vmem(2 * members),
        out_specs=tuple(whole_vmem(6)),
        compiler_params=pltpu.CompilerParams(vmem_limit_bytes=24 << 20),
        cost_estimate=SMALL,
    )(rows, cot, router, group, *first, *second)


def rows_of(count, columns):
    return pl.BlockSpec((count, columns), lambda i: (i, 0))


def whole_of(*shape):
    return pl.BlockSpec(shape, lambda i: (0,) * len(shape))


def enter_kernel(
    members, experts,
    x_ref, gain_ref, router_ref, route_ref, flat_ref, ids_ref, *refs,
):
    att, proj = refs[:members], refs[members : 2 * members]
    hidden_ref, gate_ref, leave_ref, total_ref = refs[2 * members :]
    step = pl.program_id(0)
    hidden = x_ref[...].astype(F32)
    for k in range(members):
        hidden = hidden + lax.dot_general(
            att[k][...], proj[k][...], (((0,), (0,)), ((), ())), preferred_element_type=F32
        )
    hidden_ref[...] = hidden
    normed = norm_rows(hidden, gain_ref[...]).astype(BF16)
    lane = lax.broadcasted_iota(jnp.int32, (QB, 128), 1)
    logits = jnp.where(lane < experts, nn_dot(normed, router_ref[...]), MASKED)
    raised = jnp.exp(logits - jnp.max(logits, -1, keepdims=True))
    chosen = jnp.sum(jnp.where(lane == route_ref[...], raised, 0.0), -1, keepdims=True)
    gate_ref[...] = chosen / jnp.sum(raised, -1, keepdims=True)
    table = jnp.where(ids_ref[...] == flat_ref[...], 1.0, 0.0).astype(BF16)

    @pl.when(step == 0)
    def _():
        total_ref[...] = jnp.zeros_like(total_ref)

    total_ref[...] += nn_dot(table, normed)

    @pl.when(step == pl.num_programs(0) - 1)
    def _():
        leave_ref[...] = total_ref[...].astype(BF16)


def enter_experts(tokens, experts, gain, router, route, flat_id, ids, att, proj):
    length, width = tokens.shape
    members = len(att)
    inner = att[0].shape[0]
    count = ids.shape[0]
    return pl.pallas_call(
        functools.partial(enter_kernel, members, experts),
        grid=(length // QB,),
        out_shape=(
            jax.ShapeDtypeStruct((length, width), F32),
            jax.ShapeDtypeStruct((length, 1), F32),
            jax.ShapeDtypeStruct((count, width), BF16),
        ),
        in_specs=[
            rows_of(QB, width),
            whole_of(1, width),
            whole_of(width, 128),
            rows_of(QB, 1),
            pl.BlockSpec((1, QB), lambda i: (0, i)),
            whole_of(count, 1),
        ]
        + [pl.BlockSpec((inner, QB), lambda i: (0, i))] * members
        + [whole_of(inner, width)] * members,
        out_specs=(rows_of(QB, width), rows_of(QB, 1), whole_of(count, width)),
        scratch_shapes=[pltpu.VMEM((count, width), F32)],
        compiler_params=pltpu.CompilerParams(vmem_limit_bytes=20 << 20),
        cost_estimate=SMALL,
    )(
        tokens, gain, router, route, flat_id, ids, *att, *proj,
    )


def weight_kernel(half, rows_ref, grads_ref, act_ref, gpre_ref, kept_ref, sent_ref):
    step = pl.program_id(0)

    def product(left, right):
        return lax.dot_general(
            left, right, (((0,), (0,)), ((), ())), preferred_element_type=F32
        ).astype(BF16)

    @pl.when(step < half)
    def _():
        k = 2 * step
        kept_ref[0] = product(act_ref[k], grads_ref[...])
        sent_ref[0] = product(act_ref[k + 1], grads_ref[...])

    @pl.when(step >= half)
    def _():
        k = 2 * (step - half)
        kept_ref[0] = product(rows_ref[...], gpre_ref[k])
        sent_ref[0] = product(rows_ref[...], gpre_ref[k + 1])


def weight_grads(rows, grads, act, gpre):
    members, count, hidden = act.shape
    width = rows.shape[1]
    assert hidden == width
    one = pl.BlockSpec((1, width, width), lambda i: (i, 0, 0))
    return pl.pallas_call(
        functools.partial(weight_kernel, members // 2),
        grid=(members,),
        out_shape=(
            jax.ShapeDtypeStruct((members, width, width), BF16),
            jax.ShapeDtypeStruct((members, width, width), BF16),
        ),
        in_specs=[whole_of(count, width)] * 2 + [whole_of(members, count, hidden)] * 2,
        out_specs=(one, one),
        compiler_params=pltpu.CompilerParams(vmem_limit_bytes=24 << 20),
        cost_estimate=SMALL,
    )(rows, grads, act, gpre)


def leave_kernel(
    members,
    hidden_ref, cot_ref, gain_ref, flat_ref, ids_ref, wproj_ref, att_ref, *refs,
):
    blocks = refs[:members]
    gh_ref, da_ref, ggain_ref, gproj_ref, total_ref = refs[members:]
    step = pl.program_id(0)
    share = blocks[0].shape[0]
    grad = jnp.zeros(hidden_ref.shape, F32)
    for k in range(members):
        hit = flat_ref[...] == ids_ref[:, k * share : (k + 1) * share]
        grad = grad + nn_dot(jnp.where(hit, 1.0, 0.0).astype(BF16), blocks[k][...])
    hidden = hidden_ref[...]
    inverse = lax.rsqrt(jnp.mean(hidden * hidden, -1, keepdims=True) + 1e-06)
    unit = hidden * inverse
    scaled = gain_ref[...] * grad
    back = inverse * (scaled - unit * jnp.mean(unit * scaled, -1, keepdims=True))
    total = cot_ref[...].astype(F32) + back
    gh_ref[...] = total
    low = total.astype(BF16)
    da_ref[...] = nt_dot(low, wproj_ref[...]).astype(BF16)

    @pl.when(step == 0)
    def _():
        ggain_ref[...] = jnp.zeros_like(ggain_ref)
        total_ref[...] = jnp.zeros_like(total_ref)

    ggain_ref[...] += jnp.sum(grad * unit, 0, keepdims=True)
    total_ref[...] += nn_dot(att_ref[...], low)

    @pl.when(step == pl.num_programs(0) - 1)
    def _():
        gproj_ref[...] = total_ref[...].astype(BF16)


def leave_experts(hidden1, cotangent, gain, flat_id, ids, w_proj, attended_t, blocks):
    length, width = hidden1.shape
    inner = attended_t.shape[0]
    members = len(blocks)
    share = blocks[0].shape[0]
    return pl.pallas_call(
        functools.partial(leave_kernel, members),
        grid=(length // QB,),
        out_shape=(
            jax.ShapeDtypeStruct((length, width), F32),
            jax.ShapeDtypeStruct((length, PAD), BF16),
            jax.ShapeDtypeStruct((1, width), F32),
            jax.ShapeDtypeStruct((inner, width), BF16),
        ),
        in_specs=[
            rows_of(QB, width),
            rows_of(QB, width),
            whole_of(1, width),
            rows_of(QB, 1),
            whole_of(1, members * share),
            whole_of(PAD, width),
            pl.BlockSpec((inner, QB), lambda i: (0, i)),
        ]
        + [whole_of(share, width)] * members,
        out_specs=(
            rows_of(QB, width),
            rows_of(QB, PAD),
            whole_of(1, width),
            whole_of(inner, width),
        ),
        scratch_shapes=[pltpu.VMEM((inner, width), F32)],
        compiler_params=pltpu.CompilerParams(vmem_limit_bytes=24 << 20),
        cost_estimate=SMALL,
    )(
        hidden1, cotangent, gain, flat_id, ids, w_proj, attended_t, *blocks,
    )


def output_kernel(members, hidden_ref, gate_ref, flat_ref, ids_ref, *refs):
    blocks, out_ref = refs[:members], refs[members]
    share = blocks[0].shape[0]
    reply = jnp.zeros(hidden_ref.shape, F32)
    for k in range(members):
        hit = flat_ref[...] == ids_ref[:, k * share : (k + 1) * share]
        reply = reply + nn_dot(jnp.where(hit, 1.0, 0.0).astype(BF16), blocks[k][...])
    out_ref[...] = (hidden_ref[...] + gate_ref[...] * reply).astype(BF16)


def output_rows(hidden1, gate, flat_id, ids, blocks):
    length, width = hidden1.shape
    members = len(blocks)
    share = blocks[0].shape[0]
    return pl.pallas_call(
        functools.partial(output_kernel, members),
        grid=(length // QB,),
        out_shape=jax.ShapeDtypeStruct((length, width), BF16),
        in_specs=[rows_of(QB, width), rows_of(QB, 1), rows_of(QB, 1), whole_of(1, members * share)]
        + [whole_of(share, width)] * members,
        out_specs=rows_of(QB, width),
        compiler_params=pltpu.CompilerParams(vmem_limit_bytes=20 << 20),
        cost_estimate=SMALL,
    )(hidden1, gate, flat_id, ids, *blocks)


def input_kernel(halves, kept_ref, other_ref, x_ref, gain_ref, gh_ref, low_ref, out_ref, ggain_ref):
    step = pl.program_id(0)
    part = jnp.where(step // halves == low_ref[0], kept_ref[...].astype(F32), other_ref[...].astype(F32))
    x = x_ref[...].astype(F32)
    inverse = lax.rsqrt(jnp.mean(x * x, -1, keepdims=True) + 1e-06)
    unit = x * inverse
    scaled = gain_ref[...] * part
    out_ref[...] = gh_ref[...] + inverse * (scaled - unit * jnp.mean(unit * scaled, -1, keepdims=True))

    @pl.when(step == 0)
    def _():
        ggain_ref[...] = jnp.zeros_like(ggain_ref)

    ggain_ref[...] += jnp.sum(part * unit, 0, keepdims=True)


def input_grads(kept, other, tokens, gain, grad_hidden1, low_bit):
    length, width = tokens.shape
    halves = kept.shape[0] // QB
    half = pl.BlockSpec((QB, width), lambda i: (i % halves, 0))
    return pl.pallas_call(
        functools.partial(input_kernel, halves),
        grid=(length // QB,),
        out_shape=(
            jax.ShapeDtypeStruct((length, width), F32),
            jax.ShapeDtypeStruct((1, width), F32),
        ),
        in_specs=[
            half,
            half,
            rows_of(QB, width),
            whole_of(1, width),
            rows_of(QB, width),
            pl.BlockSpec(memory_space=pltpu.SMEM),
        ],
        out_specs=(rows_of(QB, width), whole_of(1, width)),
        compiler_params=pltpu.CompilerParams(vmem_limit_bytes=16 << 20),
        cost_estimate=SMALL,
    )(kept, other, tokens, gain[None, :], grad_hidden1, low_bit)


def copies_kernel(came_ref, small_ref, out_ref, mine_ref):
    groups, large = came_ref.shape[:2]

    @pl.when(pl.program_id(0) == 0)
    def _():
        total = came_ref[0].astype(F32)
        for g in range(1, groups):
            total = total + came_ref[g].astype(F32)
        mine_ref[:large, :] = total.astype(BF16)
        mine_ref[large:, :] = small_ref[...].astype(BF16)

    out_ref[0] = mine_ref[...]


def sum_copies(came, small):
    groups, large, width = came.shape
    count = large + small.shape[0]
    return pl.pallas_call(
        copies_kernel,
        grid=(groups,),
        out_shape=jax.ShapeDtypeStruct((groups, count, width), BF16),
        in_specs=[whole_of(groups, large, width), whole_of(*small.shape)],
        out_specs=pl.BlockSpec((1, count, width), lambda i: (i, 0, 0)),
        scratch_shapes=[pltpu.VMEM((count, width), BF16)],
        compiler_params=pltpu.CompilerParams(vmem_limit_bytes=12 << 20),
        cost_estimate=SMALL,
    )(came, small)


def final_kernel(large, inner, totals_ref, qkv_ref, proj_ref, small_ref):
    groups = totals_ref.shape[0]
    split = 3 * inner
    small = totals_ref[0, large:, :].astype(F32)
    for g in range(groups):
        start, stop = g * large, (g + 1) * large
        if start < split:
            count = min(stop, split) - start
            qkv_ref[start : start + count, :] = totals_ref[g, :count, :].astype(F32)
        if stop > split:
            skip = max(start, split) - start
            proj_ref[start + skip - split : stop - split, :] = totals_ref[g, skip:large, :].astype(F32)
        if g:
            small = small + totals_ref[g, large:, :].astype(F32)
    small_ref[...] = small


def final_weights(totals, large, inner):
    groups, count, width = totals.shape
    return pl.pallas_call(
        functools.partial(final_kernel, large, inner),
        out_shape=(
            jax.ShapeDtypeStruct((3 * inner, width), F32),
            jax.ShapeDtypeStruct((inner, width), F32),
            jax.ShapeDtypeStruct((count - large, width), F32),
        ),
        in_specs=whole_vmem(1),
        out_specs=tuple(whole_vmem(3)),
        compiler_params=pltpu.CompilerParams(vmem_limit_bytes=8 << 20),
        cost_estimate=SMALL,
    )(totals)


def shards(
    tokens,
    gain_attn,
    w_qkv,
    w_proj,
    rel_bias,
    gain_ffn,
    w_router,
    w_in,
    w_out,
    routes,
    segment_ids,
    cotangent,
):
    length, width = tokens.shape
    experts = w_router.shape[1]
    capacity = max(2, 3 * length // (2 * experts))
    inner_here = w_proj.shape[0]
    members = lax.axis_size("tensor")
    groups = lax.axis_size("expert")
    member = lax.axis_index("tensor")
    group = lax.axis_index("expert")
    share = capacity // members
    segments = segment_ids[0]
    route = routes[:, 0]

    def swap(value, bit):
        return lax.ppermute(value, "tensor", [(i, i ^ bit) for i in range(members)])

    bits = [1 << i for i in range(members.bit_length() - 1)]

    def gather_far(value):
        blocks = {0: value}
        for bit in reversed(bits[1:]):
            blocks.update({k ^ bit: swap(block, bit) for k, block in blocks.items()})
        return blocks

    def gather_near(blocks):
        blocks = dict(blocks)
        for bit in bits[:1]:
            blocks.update({k ^ bit: swap(block, bit) for k, block in blocks.items()})
        return [blocks[k] for k in range(members)]

    def gather_members(value):
        return gather_near(gather_far(value))

    def gather_groups(value):
        copies = jnp.broadcast_to(value[None], (groups,) + value.shape)
        return exchange(copies)

    def exchange(value):
        return lax.all_to_all(value, "expert", split_axis=0, concat_axis=0, tiled=True)

    tie = lax.optimization_barrier

    expert_ids = jnp.arange(experts, dtype=jnp.int32)
    onehot_low = (route[:, None] == expert_ids[None, :]).astype(BF16)
    onehot = onehot_low.astype(F32)
    positions = jnp.arange(length, dtype=jnp.int32)
    lower_ones = (positions[:, None] >= positions[None, :]).astype(BF16)
    running = nn_dot(lower_ones, onehot_low)
    slot = (jnp.sum(running * onehot, 1) - 1.0).astype(jnp.int32)
    flat_id = route * capacity + slot

    def ids_of(owner):
        slots = owner * share + jnp.arange(share, dtype=jnp.int32)
        return (expert_ids[:, None] * capacity + slots[None, :]).reshape(-1)

    send_table = (ids_of(member)[:, None] == flat_id[None, :]).astype(BF16)
    all_ids = jnp.concatenate([ids_of(member ^ k) for k in range(members)])

    def dispatch(rows):
        out = nn_dot(send_table, rows).astype(BF16).reshape(groups, -1, width)
        return exchange(out).reshape(-1, width)

    cot_share = dispatch(cotangent)
    w_proj_far = gather_far(w_proj)
    w_in_far = gather_far(w_in[0])
    w_qkv_t = jnp.swapaxes(w_qkv, 1, 2)
    attended_t, lse, proj, keys_t, normed1 = attend(tokens, gain_attn, w_qkv_t, segments, rel_bias)
    attended_t, w_in_far, cot_share = tie((attended_t, w_in_far, cot_share))

    attended_far = gather_far(attended_t)
    gain_row = gain_ffn[None, :]
    router = jnp.pad(w_router, ((0, 0), (0, 128 - experts)))
    w_proj_pad = jnp.pad(w_proj, ((0, PAD - inner_here), (0, 0)))
    flat_row, flat_column = flat_id[None, :], flat_id[:, None]
    send_ids, back_ids = ids_of(member)[:, None], all_ids[None, :]
    (
        attended_far, w_proj_far, w_out_here, gain_row, router, w_proj_pad,
        flat_row, flat_column, send_ids, back_ids,
    ) = tie((
        attended_far, w_proj_far, w_out[0], gain_row, router, w_proj_pad,
        flat_row, flat_column, send_ids, back_ids,
    ))
    attended_blocks = gather_near(attended_far)
    w_proj_blocks = gather_near(w_proj_far)
    w_in_all = gather_near(w_in_far)
    w_out_far = gather_far(w_out_here)
    hidden1, gate, leaving = enter_experts(
        tokens, experts, gain_row, router, routes, flat_row, send_ids, attended_blocks, w_proj_blocks
    )
    rows = exchange(leaving.reshape(groups, -1, width)).reshape(-1, width)
    rows, w_out_far, w_in_all = tie((rows, w_out_far, w_in_all))
    w_out_all = gather_near(w_out_far)

    reply, grad_share, act, grad_pre, grad_rows, grad_router = expert_step(
        rows, cot_share, experts, router, group[None], w_in_all, w_out_all
    )
    grad_back = exchange(grad_share.reshape(groups, -1, width)).reshape(-1, width)
    grad_router = grad_router[:experts]
    grad_router = grad_router + swap(grad_router, 1)
    grad_router, rows, grad_rows, act, grad_pre = tie((grad_router, rows, grad_rows, act, grad_pre))
    kept_weights, sent_weights = weight_grads(rows, grad_rows, act, grad_pre)
    near_weights = swap(sent_weights, 1)
    for bit in bits[1:]:
        grad_router = grad_router + swap(grad_router, bit)
    grad_back, reply, near_weights, grad_router = tie((grad_back, reply, near_weights, grad_router))
    grad_far = gather_far(grad_back)
    out_sent = (kept_weights[1].astype(F32) + near_weights[1].astype(F32)).astype(BF16)
    in_sent = (kept_weights[3].astype(F32) + near_weights[3].astype(F32)).astype(BF16)
    grad_far, out_sent, in_sent = tie((grad_far, out_sent, in_sent))
    out_came, in_came = swap(out_sent, 2), swap(in_sent, 2)
    grad_blocks = gather_near(grad_far)
    reply_back = exchange(reply.reshape(groups, -1, width)).reshape(-1, width)
    grad_hidden1, attended_grad, grad_gain_ffn, grad_proj = leave_experts(
        hidden1, cotangent, gain_row, flat_column, back_ids, w_proj_pad, attended_t, grad_blocks
    )

    low_bit = (member & 1)[None]
    grads, kept, sent, rel_parts = attend_back(
        proj, keys_t, lse, attended_grad, normed1, w_qkv_t, grad_proj, rel_bias, low_bit
    )
    grads, kept, sent, reply_back, out_came, in_came = tie(
        (grads, kept, sent, reply_back, out_came, in_came)
    )
    kept = kept + swap(sent, 1).astype(F32)
    kept_low, grads = tie((kept.astype(BF16), grads))
    far = swap(kept_low, 2)
    came = exchange(grads.reshape(groups, -1, width))
    reply_far = gather_far(reply_back)
    grad_w_out = kept_weights[0].astype(F32) + near_weights[0].astype(F32) + out_came.astype(F32)
    grad_w_in = kept_weights[2].astype(F32) + near_weights[2].astype(F32) + in_came.astype(F32)

    rel_row = jnp.sum(rel_parts, -1).reshape(1, -1)
    rel_row = jnp.pad(rel_row, ((0, 0), (0, width - rel_row.shape[1])))
    small = jnp.concatenate([grad_gain_ffn, rel_row, grad_router], 0)
    small = jnp.pad(small, ((0, -small.shape[0] % 16), (0, 0)))
    large = came.shape[1]
    if large % 16 == 0:
        copies = sum_copies(came, small)
    else:
        copies = jnp.concatenate([jnp.sum(came.astype(F32), 0), small], 0).astype(BF16)
        copies = jnp.broadcast_to(copies[None], (groups,) + copies.shape)
    far, copies, grad_w_out, grad_w_in, reply_far = tie((far, copies, grad_w_out, grad_w_in, reply_far))
    totals = exchange(copies)
    kept = (kept + far.astype(F32)).astype(BF16)
    other = swap(kept, 1)
    grad_input, gain_part = input_grads(kept, other, tokens, gain_attn, grad_hidden1, low_bit)
    grad_gain_attn = jnp.sum(gather_groups(gain_part), (0, 1))
    output = output_rows(hidden1, gate, flat_column, back_ids, gather_near(reply_far))
    if large % 16 == 0:
        grad_qkv_t, grad_proj, small = final_weights(totals, large, inner_here)
    else:
        shared = totals[:, :large].reshape(-1, width).astype(F32)
        grad_qkv_t, grad_proj = shared[: 3 * inner_here], shared[3 * inner_here :]
        small = jnp.sum(totals[:, large:].astype(F32), 0)
    grad_qkv = jnp.swapaxes(grad_qkv_t.reshape(3, inner_here, width), 1, 2)
    grad_gain_ffn = small[0]
    grad_rel = small[1, : rel_bias.size].reshape(rel_bias.shape)
    grad_router = small[2 : 2 + experts].T
    return (
        output,
        grad_input,
        grad_gain_attn,
        grad_qkv,
        grad_proj,
        grad_rel,
        grad_gain_ffn,
        grad_router,
        grad_w_in[None],
        grad_w_out[None],
    )


def solution(mesh):
    placed = (
        P("expert", None),
        P(),
        P(None, None, "tensor"),
        P("tensor", None),
        P("tensor", None),
        P(),
        P(),
        P("expert", None, "tensor"),
        P("expert", "tensor", None),
        P("expert", None),
        P("expert", None),
        P("expert", None),
    )
    return jax.shard_map(
        shards,
        mesh=mesh,
        in_specs=placed,
        out_specs=(
            P("expert", None),
            P("expert", None),
            P(),
            P(None, None, "tensor"),
            P("tensor", None),
            P("tensor", None),
            P(),
            P(),
            P("expert", None, "tensor"),
            P("expert", "tensor", None),
        ),
        check_vma=False,
    )
```

profile of v0, /device:TPU:0, one launch (start us, length us, event | category | flops | bytes accessed | tf_op | source)
XLA Modules:
  0.0 303.3 jit_solution(18364751732710516814)
XLA Ops:
  0.6 3.0 collective-permute-start
  3.7 1.2 fusion.9
  5.8 3.1 %fusion.3 = bf16[384,768]{1,0:T(8,128)(2,1)} fusion(bf16[1024,768]{1,0:T(8,128)(2,1)} %cot_ref.1, s32[1024]{0:T(1024)S(1)} %multiply_add_fusion.1, s32[384]{0:T(512)S(1)} %add.222), kind=kOutput, calls=%fused_computation.10 | convolution fusion | flops 604667904 | bytes 2168320 | tf_op jit(solution)/shard_map/dot_general | solution.py:38
  8.9 5.9 %all-to-all-start = ((bf16[8,48,768]{2,1,0:T(8,128)(2,1)}), bf16[8,48,768]{2,1,0:T(8,128)(2,1)S(1)}, u32[]{:S(2)}, u32[]{:S(2)}) async-start(bf16[8,48,768]{2,1,0:T(8,128)(2,1)} %bitcast.49), calls=%async_computation | async-start | bytes 1179648 | tf_op jit(solution)/shard_map/all_to_all | solution.py:732
  15.4 1.0 copy.37.doc_ref
  16.4 1.0 copy-done.11
  17.5 11.4 %shard_map.195 = (bf16[192,1024]{1,0:T(8,128)(2,1)S(1)}, f32[8,1024]{1,0:T(8,128)S(1)}, bf16[1024,768]{1,0:T(8,128)(2,1)S(1)}, bf16[192,1024]{1,0:T(8,128)(2,1)S(1)}, bf16[1024,768]{1,0:T(8,128)(2,1)S(1)}) custom-call(bf16[1024,768]{1,0:T(8,128)(2,1)S(1)} %copy-done, f32[1,768]{1,0:T(1,128)S(1)} %broadcast_in_dim.18.gain_ref, ...), custom_call_target="tpu_custom_call" | custom-call | flops 1048576 | bytes 65536 | tf_op jit(solution)/shard_map/pallas_call | solution.py:247
  29.7 1.1 copy-done.17
  30.8 1.1 copy-done.19
  32.7 1.5 collective-permute-start.1
  35.0 1.8 pad.17.wproj_ref
  36.8 1.0 copy.40
  37.9 1.2 multiply_add_fusion
  39.1 5.6 %collective-permute-done.1.refs_2_ = bf16[192,1024]{1,0:T(8,128)(2,1)} collective-permute-done((bf16[192,1024]{1,0:T(8,128)(2,1)}, bf16[192,1024]{1,0:T(8,128)(2,1)}, u32[]{:S(2)}, u32[]{:S(2)}) %collective-permute-start.1) | collective-permute-done | bytes 393248 | tf_op jit(solution)/shard_map/ppermute | solution.py:708
  48.1 1.8 collective-permute-start.7
  50.7 1.0 copy-done.13
  51.7 1.0 copy-done.21
  53.5 1.0 copy-done.34
  54.5 1.0 copy-done.36
  55.5 7.9 %shard_map.196 = (f32[1024,768]{1,0:T(8,128)S(1)}, f32[1024,1]{1,0:T(8,128)S(1)}, bf16[384,768]{1,0:T(8,128)(2,1)S(1)}) custom-call(bf16[1024,768]{1,0:T(8,128)(2,1)S(1)} %copy-done, f32[1,768]{1,0:T(1,128)S(1)} %broadcast_in_dim.19.gain_ref, bf16[768,128]{1,0:T(8,128)(2,1)S(1)} %pad.16.router_ref, s32[1024,1]{1,0:T(8,128)S(1)} %copy.39.route_ref, ...), custom_call_target="tpu_custom_call" | custom-call | flops 1048576 | bytes 65536 | tf_op jit(solution)/shard_map/pallas_call | solution.py:412
  63.4 1.6 copy-done.1
  66.6 5.8 %all-to-all-start.1 = ((bf16[8,48,768]{2,1,0:T(8,128)(2,1)}), bf16[8,48,768]{2,1,0:T(8,128)(2,1)S(1)}, u32[]{:S(2)}, u32[]{:S(2)}) async-start(bf16[8,48,768]{2,1,0:T(8,128)(2,1)} %bitcast.46), calls=%async_computation.1 | async-start | bytes 1179648 | tf_op jit(solution)/shard_map/all_to_all | solution.py:732
  72.5 4.2 %collective-permute-done.7.refs_6_ = bf16[768,768]{1,0:T(8,128)(2,1)} collective-permute-done((bf16[768,768]{1,0:T(8,128)(2,1)}, bf16[768,768]{1,0:T(8,128)(2,1)}, u32[]{:S(2)}, u32[]{:S(2)}) %collective-permute-start.7) | collective-permute-done | bytes 1179680 | tf_op jit(solution)/shard_map/ppermute | solution.py:708
  76.6 11.9 %all-to-all-done.1 = bf16[8,48,768]{2,1,0:T(8,128)(2,1)S(1)} async-done(((bf16[8,48,768]{2,1,0:T(8,128)(2,1)}), bf16[8,48,768]{2,1,0:T(8,128)(2,1)S(1)}, u32[]{:S(2)}, u32[]{:S(2)}) %all-to-all-start.1) | async-done | bytes 589856 | tf_op jit(solution)/shard_map/all_to_all | solution.py:732
  89.1 2.7 collective-permute-done.10.refs_5_
  91.8 1.7 collective-permute-done.11.refs_7_
  93.5 12.6 %shard_map.197 = (bf16[384,768]{1,0:T(8,128)(2,1)S(1)}, bf16[384,768]{1,0:T(8,128)(2,1)S(1)}, bf16[4,384,768]{2,1,0:T(8,128)(2,1)S(1)}, bf16[4,384,768]{2,1,0:T(...) custom-call(bf16[384,768]{1,0:T(8,128)(2,1)S(1)} %bitcast.35, bf16[384,768]{1,0:T(8,128)(2,1)S(1)} %bitcast.42, ...), custom_call_target="tpu_custom_call" | custom-call | flops 1048576 | bytes 65536 | tf_op jit(solution)/shard_map/pallas_call | solution.py:350
  106.3 1.1 collective-permute-done.12
  107.4 6.8 %shard_map.198 = (bf16[4,768,768]{2,1,0:T(8,128)(2,1)S(1)}, bf16[4,768,768]{2,1,0:T(8,128)(2,1)}) custom-call(bf16[384,768]{1,0:T(8,128)(2,1)S(1)} %bitcast.36, bf16[384,768]{1,0:T(8,128)(2,1)S(1)} %get-tuple-element.126.grads_ref, bf16[4,384,768]{2,1,0:T(8,128)(2,1)S(1)} %get-tuple-element.127.act_ref, bf16[4,384,768]{2,1,0:T(8,128)(2,1)S(1)} %get-tuple-element.128.gpre_ref), custom_call_target="tpu_custom_call" | custom-call | flops 1048576 | bytes 65536 | tf_op jit(solution)/shard_map/pallas_call | solution.py:465
  114.1 2.1 copy-done.6
  116.4 3.6 %all-to-all-start.2 = ((bf16[8,48,768]{2,1,0:T(8,128)(2,1)}), bf16[8,48,768]{2,1,0:T(8,128)(2,1)S(1)}, u32[]{:S(2)}, u32[]{:S(2)}) async-start(bf16[8,48,768]{2,1,0:T(8,128)(2,1)} %bitcast.45), calls=%async_computation.2 | async-start | bytes 1179648 | tf_op jit(solution)/shard_map/all_to_all | solution.py:732
  120.6 3.3 %collective-permute-done.14 = f32[8,768]{1,0:T(8,128)S(1)} collective-permute-done((f32[8,768]{1,0:T(8,128)S(1)}, f32[8,768]{1,0:T(8,128)S(1)}, u32[]{:S(2)}, u32[]{:S(2)}) %collective-permute-start.14) | collective-permute-done | bytes 24608 | tf_op jit(solution)/shard_map/ppermute | solution.py:708
  123.9 12.7 %all-to-all-done.2 = bf16[8,48,768]{2,1,0:T(8,128)(2,1)S(1)} async-done(((bf16[8,48,768]{2,1,0:T(8,128)(2,1)}), bf16[8,48,768]{2,1,0:T(8,128)(2,1)S(1)}, u32[]{:S(2)}, u32[]{:S(2)}) %all-to-all-start.2) | async-done | bytes 589856 | tf_op jit(solution)/shard_map/all_to_all | solution.py:732
  137.1 4.4 %fusion.7 = (bf16[768,768]{1,0:T(8,128)(2,1)}, bf16[768,768]{1,0:T(8,128)(2,1)}) fusion(bf16[4,768,768]{2,1,0:T(8,128)(2,1)} %collective-permute-done.13, bf16[4,768,768]{2,1,0:T(8,128)(2,1)} %copy-done.6), kind=kLoop, calls=%fused_computation.12 | loop fusion | flops 4718592 | bytes 7077888 | tf_op jit(solution)/shard_map/convert_element_type | solution.py:801
  141.4 9.7 %collective-permute-done.15.refs_2_ = bf16[384,768]{1,0:T(8,128)(2,1)S(1)} collective-permute-done((bf16[384,768]{1,0:T(8,128)(2,1)S(1)}, bf16[384,768]{1,0:T(8,128)(2,1)S(1)}, u32[]{:S(2)}, u32[]{:S(2)}) %collective-permute-start.15) | collective-permute-done | bytes 589856 | tf_op jit(solution)/shard_map/ppermute | solution.py:708
  152.4 1.5 collective-permute-start.19
  154.0 4.4 %all-to-all-start.3 = ((bf16[8,48,768]{2,1,0:T(8,128)(2,1)}), bf16[8,48,768]{2,1,0:T(8,128)(2,1)}, u32[]{:S(2)}, u32[]{:S(2)}) async-start(bf16[8,48,768]{2,1,0:T(8,128)(2,1)} %bitcast.44), calls=%async_computation.3 | async-start | bytes 1179648 | tf_op jit(solution)/shard_map/all_to_all | solution.py:732
  159.0 1.7 collective-permute-done.16.refs_1_
  160.6 1.0 collective-permute-done.17.refs_3_
  161.7 1.9 copy-done.2
  163.6 1.4 copy-done.16
  165.0 1.1 copy-done.25
  166.0 9.6 %shard_map.199 = (f32[1024,768]{1,0:T(8,128)S(1)}, bf16[1024,256]{1,0:T(8,128)(2,1)S(1)}, f32[1,768]{1,0:T(1,128)S(1)}, bf16[192,768]{1,0:T(8,128)(2,1)S(1)}) custom-call(f32[1024,768]{1,0:T(8,128)S(1)} %copy-done.2, bf16[1024,768]{1,0:T(8,128)(2,1)S(1)} %copy-done.16, f32[1,768]{1,0:T(1,128)S(1)} %broadcast_in_dim.19.gain_ref, ...), custom_call_target="tpu_custom_call" | custom-call | flops 1048576 | bytes 65536 | tf_op jit(solution)/shard_map/pallas_call | solution.py:519
  175.7 1.7 copy-done.9
  177.3 19.7 %shard_map.200 = (bf16[768,768]{1,0:T(8,128)(2,1)S(1)}, f32[512,768]{1,0:T(8,128)S(1)}, bf16[512,768]{1,0:T(8,128)(2,1)S(1)}, f32[3,32,128]{2,1,0:T(8,128)S(1)}) custom-call(bf16[1024,768]{1,0:T(8,128)(2,1)S(1)} %copy-done.18, bf16[192,1024]{1,0:T(8,128)(2,1)S(1)} %copy-done.32, f32[8,1024]{1,0:T(8,128)S(1)} %get-tuple-element.105.lse_ref, ...), custom_call_target="tpu_custom_call" | custom-call | flops 1048576 | bytes 65536 | tf_op jit(solution)/shard_map/pallas_call | solution.py:273
  197.1 1.0 copy-done.22
  199.0 4.9 %collective-permute-done.19 = bf16[768,768]{1,0:T(8,128)(2,1)} collective-permute-done((bf16[768,768]{1,0:T(8,128)(2,1)}, bf16[768,768]{1,0:T(8,128)(2,1)}, u32[]{:S(2)}, u32[]{:S(2)}) %collective-permute-start.19) | collective-permute-done | bytes 1179680 | tf_op jit(solution)/shard_map/ppermute | solution.py:708
  203.8 2.5 collective-permute-done.20
  206.3 1.2 fusion.10
  207.5 5.1 %all-to-all-start.4 = ((bf16[8,96,768]{2,1,0:T(8,128)(2,1)}), bf16[8,96,768]{2,1,0:T(8,128)(2,1)}, u32[]{:S(2)}, u32[]{:S(2)}) async-start(bf16[8,96,768]{2,1,0:T(8,128)(2,1)} %bitcast.43), calls=%async_computation.4 | async-start | bytes 2359296 | tf_op jit(solution)/shard_map/all_to_all | solution.py:732
  213.1 1.5 collective-permute-start.22
  214.8 6.0 %bitcast_add_fusion = (f32[768,768]{1,0:T(8,128)}, f32[768,768]{1,0:T(8,128)}) fusion(bf16[768,768]{1,0:T(8,128)(2,1)} %collective-permute-done.19, bf16[4,768,768]{2,1,0:T(8,128)(2,1)} %collective-permute-done.13, bf16[4,768,768]{2,1,0:T(8,128)(2,1)} %copy-done.6, bf16[768,768]{1,0:T(8,128)(2,1)} %collective-permute-done.18), kind=kLoop, calls=%fused_computation.2 | loop fusion | flops 5898240 | bytes 11796480 | tf_op jit(solution)/shard_map/add | solution.py:823
  220.8 20.7 %all-to-all-done.4.came_ref = bf16[8,96,768]{2,1,0:T(8,128)(2,1)} async-done(((bf16[8,96,768]{2,1,0:T(8,128)(2,1)}), bf16[8,96,768]{2,1,0:T(8,128)(2,1)}, u32[]{:S(2)}, u32[]{:S(2)}) %all-to-all-start.4) | async-done | bytes 1179680 | tf_op jit(solution)/shard_map/all_to_all | solution.py:732
  241.6 4.3 %shard_map.201 = bf16[8,112,768]{2,1,0:T(8,128)(2,1)} custom-call(bf16[8,96,768]{2,1,0:T(8,128)(2,1)} %all-to-all-done.4.came_ref, f32[16,768]{1,0:T(8,128)S(1)} %pad.19.small_ref), custom_call_target="tpu_custom_call" | custom-call | flops 1048576 | bytes 65536 | tf_op jit(solution)/shard_map/pallas_call | solution.py:636
  245.9 1.6 add_convert_fusion.2.kept_ref
  247.5 2.3 collective-permute-done.25.other_ref
  249.8 3.2 %shard_map.203 = (f32[1024,768]{1,0:T(8,128)}, f32[1,768]{1,0:T(1,128)S(1)}) custom-call(bf16[512,768]{1,0:T(8,128)(2,1)S(1)} %add_convert_fusion.2.kept_ref, bf16[512,768]{1,0:T(8,128)(2,1)S(1)} %collective-permute-done.25.other_ref, bf16[1024,768]{1,0:T(8,128)(2,1)S(1)} %copy-done, f32[1,768]{1,0:T(1,128)S(1)} %broadcast_in_dim.18.gain_ref, ...), custom_call_target="tpu_custom_call" | custom-call | flops 1048576 | bytes 65536 | tf_op jit(solution)/shard_map/pallas_call | solution.py:598
  253.0 11.3 %all_to_all.35 = f32[8,1,768]{2,1,0:T(1,128)S(1)} all-to-all(f32[8,1,768]{2,1,0:T(1,128)S(1)} %broadcast_in_dim.24), channel_id=1, replica_groups=mesh['expert'=8,'tensor'=4] {'expert'}, dimensions={0} | all-to-all | bytes 49152 | tf_op jit(solution)/shard_map/all_to_all | solution.py:732
  264.3 3.6 %all-to-all-start.6 = ((bf16[8,112,768]{2,1,0:T(8,128)(2,1)}), bf16[8,112,768]{2,1,0:T(8,128)(2,1)S(1)}, u32[]{:S(2)}, u32[]{:S(2)}) async-start(bf16[8,112,768]{2,1,0:T(8,128)(2,1)} %shard_map.201), calls=%async_computation.6 | async-start | bytes 2752512 | tf_op jit(solution)/shard_map/all_to_all | solution.py:732
  268.4 1.7 collective-permute-done.23.refs_1_
  271.0 1.9 copy-done.3
  272.9 6.2 %shard_map.202 = bf16[1024,768]{1,0:T(8,128)(2,1)} custom-call(f32[1024,768]{1,0:T(8,128)S(1)} %copy-done.3, f32[1024,1]{1,0:T(8,128)S(1)} %copy-done.30, s32[1024,1]{1,0:T(8,128)S(1)} %copy-done.5, s32[1,1536]{1,0:T(1,128)S(1)} %broadcast_in_dim.20.ids_ref, bf16[384,768]{1,0:T(8,128)(2,1)} %bitcast.18.refs_0_, ...), custom_call_target="tpu_custom_call" | custom-call | flops 1048576 | bytes 65536 | tf_op jit(solution)/shard_map/pallas_call | solution.py:566
  279.7 20.2 %all-to-all-done.6.totals_ref = bf16[8,112,768]{2,1,0:T(8,128)(2,1)S(1)} async-done(((bf16[8,112,768]{2,1,0:T(8,128)(2,1)}), bf16[8,112,768]{2,1,0:T(8,128)(2,1)S(1)}, u32[]{:S(2)}, u32[]{:S(2)}) %all-to-all-start.6) | async-done | bytes 1376288 | tf_op jit(solution)/shard_map/all_to_all | solution.py:732
  299.9 1.5 shard_map.204
  (147 shorter events, 19.9 us)
Async XLA Ops:
  0.6 32.1 %collective-permute-start = (bf16[768,768]{1,0:T(8,128)(2,1)}, bf16[768,768]{1,0:T(8,128)(2,1)}, u32[]{:S(2)}, u32[]{:S(2)}) collective-permute-start(bf16[768,768]{1,0:T(8,128)(2,1)} %bitcast.2.refs_0_), channel_id=1, source_target_pairs={{0,2},{1,3},{2,0},{3,1},{4,6},{5,7},{6,4},{7,5},{8,10},{9,11},{10,... | collective-permute-start | bytes 3538952 | tf_op jit(solution)/shard_map/ppermute | solution.py:708
  5.8 9.6 %copy-start.44 = (f32[768]{0:T(1024)S(1)}, f32[768]{0:T(1024)}, u32[]{:S(2)}) copy-start(f32[768]{0:T(1024)} %param.13) | copy-start | bytes 9220
  5.8 9.6 %copy-start.43 = (s32[1,1024]{1,0:T(1,128)S(1)}, s32[1,1024]{1,0:T(1,128)}, u32[]{:S(2)}) copy-start(s32[1,1024]{1,0:T(1,128)} %param.22) | copy-start | bytes 12292
  5.8 10.6 %copy-start.7 = (bf16[3,768,192]{1,2,0:T(8,128)(2,1)S(1)}, bf16[3,768,192]{1,2,0:T(8,128)(2,1)}, u32[]{:S(2)}) copy-start(bf16[3,768,192]{1,2,0:T(8,128)(2,1)} %param.14) | copy-start | bytes 2654212
  8.9 7.5 %copy-start = (bf16[1024,768]{1,0:T(8,128)(2,1)S(1)}, bf16[1024,768]{1,0:T(8,128)(2,1)}, u32[]{:S(2)}) copy-start(bf16[1024,768]{1,0:T(8,128)(2,1)} %x_ref.5) | copy-start | bytes 4718596
  8.9 7.5 %copy-start.37 = (f32[3,32]{1,0:T(4,128)S(1)}, f32[3,32]{1,0:T(4,128)}, u32[]{:S(2)}) copy-start(f32[3,32]{1,0:T(4,128)} %bias_ref.3) | copy-start | bytes 1156
  8.9 23.8 %all-to-all-start = ((bf16[8,48,768]{2,1,0:T(8,128)(2,1)}), bf16[8,48,768]{2,1,0:T(8,128)(2,1)S(1)}, u32[]{:S(2)}, u32[]{:S(2)}) async-start(bf16[8,48,768]{2,1,0:T(8,128)(2,1)} %bitcast.49), calls=%async_computation | async-start | bytes 1179648 | tf_op jit(solution)/shard_map/all_to_all | solution.py:732
  14.9 24.3 %collective-permute-start.2 = (bf16[192,768]{1,0:T(8,128)(2,1)}, bf16[192,768]{1,0:T(8,128)(2,1)}, u32[]{:S(2)}, u32[]{:S(2)}) collective-permute-start(bf16[192,768]{1,0:T(8,128)(2,1)} %refs_4_), channel_id=1, source_target_pairs={{0,2},{1,3},{2,0},{3,1},{4,6},{5,7},{6,4},{7,5},{8,10},{9,11},{10,... | collective-permute-start | bytes 884744 | tf_op jit(solution)/shard_map/ppermute | solution.py:708
  16.4 1.0 copy-start.11
  17.5 17.1 %copy-start.41 = (s32[1024,1]{0,1:T(1,128)S(1)}, s32[1024,1]{0,1:T(1,128)}, u32[]{:S(2)}) copy-start(s32[1024,1]{0,1:T(1,128)} %param.21) | copy-start | bytes 12292
  17.5 17.3 %copy-start.45 = (f32[768]{0:T(1024)S(1)}, f32[768]{0:T(1024)}, u32[]{:S(2)}) copy-start(f32[768]{0:T(1024)} %param.17) | copy-start | bytes 9220
  17.5 17.4 %copy-start.42 = (bf16[768,8]{0,1:T(8,128)(2,1)S(1)}, bf16[768,8]{0,1:T(8,128)(2,1)}, u32[]{:S(2)}) copy-start(bf16[768,8]{0,1:T(8,128)(2,1)} %param.18) | copy-start | bytes 36868
  29.7 1.1 copy-start.17
  30.8 1.1 copy-start.19
  32.7 12.0 %collective-permute-start.1 = (bf16[192,1024]{1,0:T(8,128)(2,1)}, bf16[192,1024]{1,0:T(8,128)(2,1)}, u32[]{:S(2)}, u32[]{:S(2)}) collective-permute-start(bf16[192,1024]{1,0:T(8,128)(2,1)} %copy-done.12), channel_id=1, source_target_pairs={{0,2},{1,3},{2,0},{3,1},{4,6},{5,7},{6,4},{7,5},{8,10},{9,11},{10,... | collective-permute-start | bytes 1179656 | tf_op jit(solution)/shard_map/ppermute | solution.py:708
  39.1 122.5 %copy-start.4 = (s32[1024,1]{1,0:T(8,128)}, s32[1024,1]{1,0:T(8,128)S(1)}, u32[]{:S(2)}) copy-start(s32[1024,1]{1,0:T(8,128)S(1)} %get-tuple-element.101.flat_ref) | copy-start | bytes 12292
  44.7 1.8 collective-permute-start.5
  44.7 2.6 collective-permute-start.6
  45.2 5.4 %collective-permute-start.3 = (bf16[192,1024]{1,0:T(8,128)(2,1)}, bf16[192,1024]{1,0:T(8,128)(2,1)}, u32[]{:S(2)}, u32[]{:S(2)}) collective-permute-start(bf16[192,1024]{1,0:T(8,128)(2,1)} %copy-done.12), channel_id=1, source_target_pairs={{0,1},{1,0},{2,3},{3,2},{4,5},{5,4},{6,7},{7,6},{8,9},{9,8},{10,11... | collective-permute-start | bytes 1179656 | tf_op jit(solution)/shard_map/ppermute | solution.py:708
  45.2 5.4 %collective-permute-start.4 = (bf16[192,1024]{1,0:T(8,128)(2,1)}, bf16[192,1024]{1,0:T(8,128)(2,1)}, u32[]{:S(2)}, u32[]{:S(2)}) collective-permute-start(bf16[192,1024]{1,0:T(8,128)(2,1)} %collective-permute-done.1.refs_2_), channel_id=1, source_target_pairs={{0,1},{1,0},{2,3},{3,2},{4,5},{5,4},{6,7},{7,6},{8,9},{9,8},{10,11... | collective-permute-start | bytes 1179656 | tf_op jit(solution)/shard_map/ppermute | solution.py:708
  45.7 26.7 %collective-permute-start.8 = (bf16[768,768]{1,0:T(8,128)(2,1)}, bf16[768,768]{1,0:T(8,128)(2,1)}, u32[]{:S(2)}, u32[]{:S(2)}) collective-permute-start(bf16[768,768]{1,0:T(8,128)(2,1)} %bitcast.2.refs_0_), channel_id=1, source_target_pairs={{0,1},{1,0},{2,3},{3,2},{4,5},{5,4},{6,7},{7,6},{8,9},{9,8},{10,11... | collective-permute-start | bytes 3538952 | tf_op jit(solution)/shard_map/ppermute | solution.py:708
  47.2 25.2 %collective-permute-start.9 = (bf16[768,768]{1,0:T(8,128)(2,1)}, bf16[768,768]{1,0:T(8,128)(2,1)}, u32[]{:S(2)}, u32[]{:S(2)}) collective-permute-start(bf16[768,768]{1,0:T(8,128)(2,1)} %collective-permute-done.refs_2_), channel_id=1, source_target_pairs={{0,1},{1,0},{2,3},{3,2},{4,5},{5,4},{6,7},{7,6},{8,9},{9,8},{10,11... | collective-permute-start | bytes 3538952 | tf_op jit(solution)/shard_map/ppermute | solution.py:708
  48.1 28.6 %collective-permute-start.7 = (bf16[768,768]{1,0:T(8,128)(2,1)}, bf16[768,768]{1,0:T(8,128)(2,1)}, u32[]{:S(2)}, u32[]{:S(2)}) collective-permute-start(bf16[768,768]{1,0:T(8,128)(2,1)} %bitcast.6.refs_4_), channel_id=1, source_target_pairs={{0,2},{1,3},{2,0},{3,1},{4,6},{5,7},{6,4},{7,5},{8,10},{9,11},{10,... | collective-permute-start | bytes 3538952 | tf_op jit(solution)/shard_map/ppermute | solution.py:708
  63.4 1.6 copy-start.1
  66.6 21.9 %all-to-all-start.1 = ((bf16[8,48,768]{2,1,0:T(8,128)(2,1)}), bf16[8,48,768]{2,1,0:T(8,128)(2,1)S(1)}, u32[]{:S(2)}, u32[]{:S(2)}) async-start(bf16[8,48,768]{2,1,0:T(8,128)(2,1)} %bitcast.46), calls=%async_computation.1 | async-start | bytes 1179648 | tf_op jit(solution)/shard_map/all_to_all | solution.py:732
  88.6 3.2 %collective-permute-start.10 = (bf16[768,768]{1,0:T(8,128)(2,1)}, bf16[768,768]{1,0:T(8,128)(2,1)}, u32[]{:S(2)}, u32[]{:S(2)}) collective-permute-start(bf16[768,768]{1,0:T(8,128)(2,1)} %bitcast.6.refs_4_), channel_id=1, source_target_pairs={{0,1},{1,0},{2,3},{3,2},{4,5},{5,4},{6,7},{7,6},{8,9},{9,8},{10,11... | collective-permute-start | bytes 3538952 | tf_op jit(solution)/shard_map/ppermute | solution.py:708
  88.6 4.9 %collective-permute-start.11 = (bf16[768,768]{1,0:T(8,128)(2,1)}, bf16[768,768]{1,0:T(8,128)(2,1)}, u32[]{:S(2)}, u32[]{:S(2)}) collective-permute-start(bf16[768,768]{1,0:T(8,128)(2,1)} %collective-permute-done.7.refs_6_), channel_id=1, source_target_pairs={{0,1},{1,0},{2,3},{3,2},{4,5},{5,4},{6,7},{7,6},{8,9},{9,8},{10,11... | collective-permute-start | bytes 3538952 | tf_op jit(solution)/shard_map/ppermute | solution.py:708
  106.0 8.1 %copy-start.26 = (bf16[384,768]{1,0:T(8,128)(2,1)}, bf16[384,768]{1,0:T(8,128)(2,1)S(1)}, u32[]{:S(2)}) copy-start(bf16[384,768]{1,0:T(8,128)(2,1)S(1)} %get-tuple-element.142) | copy-start | bytes 1769476
  106.1 8.1 %copy-start.27 = (bf16[384,768]{1,0:T(8,128)(2,1)}, bf16[384,768]{1,0:T(8,128)(2,1)S(1)}, u32[]{:S(2)}) copy-start(bf16[384,768]{1,0:T(8,128)(2,1)S(1)} %get-tuple-element.119) | copy-start | bytes 1769476
  106.1 1.3 collective-permute-start.12
  114.1 2.1 copy-start.6
  116.2 20.3 %collective-permute-start.13 = (bf16[4,768,768]{2,1,0:T(8,128)(2,1)}, bf16[4,768,768]{2,1,0:T(8,128)(2,1)}, u32[]{:S(2)}, u32[]{:S(2)}) collective-permute-start(bf16[4,768,768]{2,1,0:T(8,128)(2,1)} %get-tuple-element.129), channel_id=1, source_target_pairs={{0,1},{1,0},{2,3},{3,2},{4,5},{5,4},{6,7},{7,6},{8,9},{9,8},{10,11... | collective-permute-start | bytes 14155784 | tf_op jit(solution)/shard_map/ppermute | solution.py:708
  116.4 20.1 %all-to-all-start.2 = ((bf16[8,48,768]{2,1,0:T(8,128)(2,1)}), bf16[8,48,768]{2,1,0:T(8,128)(2,1)S(1)}, u32[]{:S(2)}, u32[]{:S(2)}) async-start(bf16[8,48,768]{2,1,0:T(8,128)(2,1)} %bitcast.45), calls=%async_computation.2 | async-start | bytes 1179648 | tf_op jit(solution)/shard_map/all_to_all | solution.py:732
  120.1 3.8 %collective-permute-start.14 = (f32[8,768]{1,0:T(8,128)S(1)}, f32[8,768]{1,0:T(8,128)S(1)}, u32[]{:S(2)}, u32[]{:S(2)}) collective-permute-start(f32[8,768]{1,0:T(8,128)S(1)} %slice_add_fusion), channel_id=1, source_target_pairs={{0,2},{1,3},{2,0},{3,1},{4,6},{5,7},{6,4},{7,5},{8,10},{9,11},{10,... | collective-permute-start | bytes 73736 | tf_op jit(solution)/shard_map/ppermute | solution.py:708
  136.6 14.6 %collective-permute-start.15 = (bf16[384,768]{1,0:T(8,128)(2,1)S(1)}, bf16[384,768]{1,0:T(8,128)(2,1)S(1)}, u32[]{:S(2)}, u32[]{:S(2)}) collective-permute-start(bf16[384,768]{1,0:T(8,128)(2,1)S(1)} %bitcast.39), channel_id=1, source_target_pairs={{0,2},{1,3},{2,0},{3,1},{4,6},{5,7},{6,4},{7,5},{8,10},{9,11},{10,... | collective-permute-start | bytes 1769480 | tf_op jit(solution)/shard_map/ppermute | solution.py:708
  137.1 24.6 %copy-start.14 = (bf16[192,1024]{1,0:T(8,128)(2,1)S(1)}, bf16[192,1024]{1,0:T(8,128)(2,1)}, u32[]{:S(2)}) copy-start(bf16[192,1024]{1,0:T(8,128)(2,1)} %copy-done.12) | copy-start | bytes 1179652
  137.1 24.6 %copy-start.15 = (bf16[256,768]{1,0:T(8,128)(2,1)S(1)}, bf16[256,768]{1,0:T(8,128)(2,1)}, u32[]{:S(2)}) copy-start(bf16[256,768]{1,0:T(8,128)(2,1)} %pad.17.wproj_ref) | copy-start | bytes 1179652
  151.9 47.0 %collective-permute-start.18 = (bf16[768,768]{1,0:T(8,128)(2,1)}, bf16[768,768]{1,0:T(8,128)(2,1)}, u32[]{:S(2)}, u32[]{:S(2)}) collective-permute-start(bf16[768,768]{1,0:T(8,128)(2,1)} %get-tuple-element.143), channel_id=1, source_target_pairs={{0,2},{1,3},{2,0},{3,1},{4,6},{5,7},{6,4},{7,5},{8,10},{9,11},{10,... | collective-permute-start | bytes 3538952 | tf_op jit(solution)/shard_map/ppermute | solution.py:708
  152.4 51.4 %collective-permute-start.19 = (bf16[768,768]{1,0:T(8,128)(2,1)}, bf16[768,768]{1,0:T(8,128)(2,1)}, u32[]{:S(2)}, u32[]{:S(2)}) collective-permute-start(bf16[768,768]{1,0:T(8,128)(2,1)} %get-tuple-element.144), channel_id=1, source_target_pairs={{0,2},{1,3},{2,0},{3,1},{4,6},{5,7},{6,4},{7,5},{8,10},{9,11},{10,... | collective-permute-start | bytes 3538952 | tf_op jit(solution)/shard_map/ppermute | solution.py:708
  154.0 45.0 %all-to-all-start.3 = ((bf16[8,48,768]{2,1,0:T(8,128)(2,1)}), bf16[8,48,768]{2,1,0:T(8,128)(2,1)}, u32[]{:S(2)}, u32[]{:S(2)}) async-start(bf16[8,48,768]{2,1,0:T(8,128)(2,1)} %bitcast.44), calls=%async_computation.3 | async-start | bytes 1179648 | tf_op jit(solution)/shard_map/all_to_all | solution.py:732
  158.4 2.2 collective-permute-start.16
  158.5 3.2 %collective-permute-start.17 = (bf16[384,768]{1,0:T(8,128)(2,1)}, bf16[384,768]{1,0:T(8,128)(2,1)}, u32[]{:S(2)}, u32[]{:S(2)}) collective-permute-start(bf16[384,768]{1,0:T(8,128)(2,1)} %copy-done.24), channel_id=1, source_target_pairs={{0,1},{1,0},{2,3},{3,2},{4,5},{5,4},{6,7},{7,6},{8,9},{9,8},{10,11... | collective-permute-start | bytes 1769480 | tf_op jit(solution)/shard_map/ppermute | solution.py:708
  161.7 1.9 copy-start.2
  163.6 1.4 copy-start.16
  165.0 1.1 copy-start.25
  166.0 11.3 %copy-start.8 = (bf16[3,768,192]{1,2,0:T(8,128)(2,1)S(1)}, bf16[3,768,192]{1,2,0:T(8,128)(2,1)}, u32[]{:S(2)}) copy-start(bf16[3,768,192]{1,2,0:T(8,128)(2,1)} %param.14) | copy-start | bytes 2654212
  166.0 11.3 %copy-start.18 = (bf16[1024,768]{1,0:T(8,128)(2,1)S(1)}, bf16[1024,768]{1,0:T(8,128)(2,1)}, u32[]{:S(2)}) copy-start(bf16[1024,768]{1,0:T(8,128)(2,1)} %copy-done.17) | copy-start | bytes 4718596
  166.0 11.3 %copy-start.20 = (bf16[1024,768]{1,0:T(8,128)(2,1)S(1)}, bf16[1024,768]{1,0:T(8,128)(2,1)}, u32[]{:S(2)}) copy-start(bf16[1024,768]{1,0:T(8,128)(2,1)} %copy-done.19) | copy-start | bytes 4718596
  166.0 11.3 %copy-start.32 = (bf16[192,1024]{1,0:T(8,128)(2,1)S(1)}, bf16[192,1024]{1,0:T(8,128)(2,1)}, u32[]{:S(2)}) copy-start(bf16[192,1024]{1,0:T(8,128)(2,1)} %copy-done.31) | copy-start | bytes 1179652
  175.7 1.7 copy-start.9
  203.8 2.5 collective-permute-start.20
  206.3 1.2 copy-start.39
  207.5 34.1 %all-to-all-start.4 = ((bf16[8,96,768]{2,1,0:T(8,128)(2,1)}), bf16[8,96,768]{2,1,0:T(8,128)(2,1)}, u32[]{:S(2)}, u32[]{:S(2)}) async-start(bf16[8,96,768]{2,1,0:T(8,128)(2,1)} %bitcast.43), calls=%async_computation.4 | async-start | bytes 2359296 | tf_op jit(solution)/shard_map/all_to_all | solution.py:732
  212.6 33.3 %collective-permute-start.21 = (bf16[512,768]{1,0:T(8,128)(2,1)}, bf16[512,768]{1,0:T(8,128)(2,1)}, u32[]{:S(2)}, u32[]{:S(2)}) collective-permute-start(bf16[512,768]{1,0:T(8,128)(2,1)} %fusion.10), channel_id=1, source_target_pairs={{0,2},{1,3},{2,0},{3,1},{4,6},{5,7},{6,4},{7,5},{8,10},{9,11},{10,... | collective-permute-start | bytes 2359304 | tf_op jit(solution)/shard_map/ppermute | solution.py:708
  213.1 32.8 %collective-permute-start.22 = (bf16[384,768]{1,0:T(8,128)(2,1)}, bf16[384,768]{1,0:T(8,128)(2,1)}, u32[]{:S(2)}, u32[]{:S(2)}) collective-permute-start(bf16[384,768]{1,0:T(8,128)(2,1)} %bitcast.18.refs_0_), channel_id=1, source_target_pairs={{0,2},{1,3},{2,0},{3,1},{4,6},{5,7},{6,4},{7,5},{8,10},{9,11},{10,... | collective-permute-start | bytes 1769480 | tf_op jit(solution)/shard_map/ppermute | solution.py:708
  241.6 4.3 %copy-start.40 = (bf16[512,768]{1,0:T(8,128)(2,1)S(1)}, bf16[512,768]{1,0:T(8,128)(2,1)}, u32[]{:S(2)}) copy-start(bf16[512,768]{1,0:T(8,128)(2,1)} %copy-done.39) | copy-start | bytes 2359300
  245.9 3.9 %copy-start.10 = (f32[1024,768]{1,0:T(8,128)S(1)}, f32[1024,768]{1,0:T(8,128)}, u32[]{:S(2)}) copy-start(f32[1024,768]{1,0:T(8,128)} %copy-done.9) | copy-start | bytes 9437188
  247.4 2.4 collective-permute-start.25
  253.0 18.0 %copy-start.5 = (s32[1024,1]{1,0:T(8,128)S(1)}, s32[1024,1]{1,0:T(8,128)}, u32[]{:S(2)}) copy-start(s32[1024,1]{1,0:T(8,128)} %copy-done.4) | copy-start | bytes 12292
  253.0 18.0 %copy-start.30 = (f32[1024,1]{1,0:T(8,128)S(1)}, f32[1024,1]{1,0:T(8,128)}, u32[]{:S(2)}) copy-start(f32[1024,1]{1,0:T(8,128)} %copy-done.29) | copy-start | bytes 12292
  264.3 35.6 %all-to-all-start.6 = ((bf16[8,112,768]{2,1,0:T(8,128)(2,1)}), bf16[8,112,768]{2,1,0:T(8,128)(2,1)S(1)}, u32[]{:S(2)}, u32[]{:S(2)}) async-start(bf16[8,112,768]{2,1,0:T(8,128)(2,1)} %shard_map.201), calls=%async_computation.6 | async-start | bytes 2752512 | tf_op jit(solution)/shard_map/all_to_all | solution.py:732
  267.9 2.3 collective-permute-start.23
  267.9 3.0 %collective-permute-start.24 = (bf16[384,768]{1,0:T(8,128)(2,1)}, bf16[384,768]{1,0:T(8,128)(2,1)S(1)}, u32[]{:S(2)}, u32[]{:S(2)}) collective-permute-start(bf16[384,768]{1,0:T(8,128)(2,1)} %collective-permute-done.22.refs_2_), channel_id=1, source_target_pairs={{0,1},{1,0},{2,3},{3,2},{4,5},{5,4},{6,7},{7,6},{8,9},{9,8},{10,11... | collective-permute-start | bytes 1769480 | tf_op jit(solution)/shard_map/ppermute | solution.py:708
  271.0 1.9 copy-start.3
  (14 other events, 12.1 us)
where the time goes:
time: 305 us; the launch traced here: 303 us
  waiting for transfers between devices  109 us (36%)
  Pallas kernels  83.1 us (27%)
  starting transfers between devices  43.6 us (14%)
  local copies, waits for them, and re-layouts  34.6 us (11%)
  other arithmetic  15.9 us (5%)
  blocking collectives  11.3 us (4%)
  matrix products  4.37 us (1%)
    all_to_all x6, waiting for transfers between devices, exchange(): lax.all_to_all(value, 'expert', split_axis=0, concat_axis=0, tiled=True)  65.6 us
    ppermute x26, waiting for transfers between devices, swap(): return lax.ppermute(value, 'tensor', [(i, i ^ bit) for i in range(members)])  43.9 us
    all_to_all x6, starting transfers between devices, exchange(): lax.all_to_all(value, 'expert', split_axis=0, concat_axis=0, tiled=True)  28.5 us
    unnamed x94, local copies, waits for them, and re-layouts  27.5 us
    pallas_call x1, Pallas kernels, attend_back(): pl.pallas_call(functools.partial(attend_back_kernel, length, heads, inner...  19.7 us
    ppermute x26, starting transfers between devices, swap(): return lax.ppermute(value, 'tensor', [(i, i ^ bit) for i in range(members)])  15.1 us
    pallas_call x1, Pallas kernels, expert_step(): pl.pallas_call(functools.partial(expert_kernel, members, experts), out_sh...  12.6 us
    pallas_call x1, Pallas kernels, attend(): pl.pallas_call(functools.partial(attend_kernel, length, heads, inner // h...  11.4 us
  transfers between devices with their start and end apart: 32, of which 19 were waited for; matrix products, arithmetic and copies ran while one was open for 8% of the time, Pallas kernels for 19%

commit v1 on v0

--- a/solution.py
+++ b/solution.py
@@ -236,50 +236,64 @@
             drel_ref[h, bucket : bucket + 1, :] = row
 
 
-def whole_vmem(count):
-    return [pl.BlockSpec(memory_space=pltpu.VMEM)] * count
+def rows_of(count, columns):
+    return pl.BlockSpec((count, columns), lambda i: (i, 0))
+
+
+def whole_of(*shape):
+    return pl.BlockSpec(shape, lambda i: (0,) * len(shape))
+
+
+def whole_like(*arrays):
+    return [whole_of(*array.shape) for array in arrays]
 
 
 def attend(tokens, gain, w_qkv, segments, rel_bias):
     length, width = tokens.shape
     heads = rel_bias.shape[0]
     inner = w_qkv.shape[1]
+    operands = (tokens, gain[None, :], w_qkv, segments[:, None])
+    results = (
+        jax.ShapeDtypeStruct((inner, length), BF16),
+        jax.ShapeDtypeStruct((8, length), F32),
+        jax.ShapeDtypeStruct((length, 3 * PAD), BF16),
+        jax.ShapeDtypeStruct((inner, length), BF16),
+        jax.ShapeDtypeStruct((length, width), BF16),
+    )
     return pl.pallas_call(
         functools.partial(attend_kernel, length, heads, inner // heads),
-        out_shape=(
-            jax.ShapeDtypeStruct((inner, length), BF16),
-            jax.ShapeDtypeStruct((8, length), F32),
-            jax.ShapeDtypeStruct((length, 3 * PAD), BF16),
-            jax.ShapeDtypeStruct((inner, length), BF16),
-            jax.ShapeDtypeStruct((length, width), BF16),
-        ),
-        in_specs=whole_vmem(4) + [pl.BlockSpec(memory_space=pltpu.SMEM)],
-        out_specs=tuple(whole_vmem(5)),
+        grid=(1,),
+        out_shape=results,
+        in_specs=whole_like(*operands) + [pl.BlockSpec(memory_space=pltpu.SMEM)],
+        out_specs=tuple(whole_like(*results)),
         scratch_shapes=[
             pltpu.VMEM((heads, length, PAD), BF16),
             pltpu.VMEM((heads, strip_shape(length), QB), F32),
             pltpu.VMEM((inner, length), BF16),
             pltpu.VMEM((3 * PAD, width), BF16),
         ],
-        compiler_params=pltpu.CompilerParams(vmem_limit_bytes=20 << 20),
+        compiler_params=pltpu.CompilerParams(vmem_limit_bytes=60 << 20),
         cost_estimate=SMALL,
-    )(tokens, gain[None, :], w_qkv, segments[:, None], rel_bias)
+    )(*operands, rel_bias)
 
 
 def attend_back(proj, kt, lse, da, normed, w_qkv, grad_proj, rel_bias, low_bit):
     length, width = normed.shape
     heads, buckets = rel_bias.shape
     inner = w_qkv.shape[1]
+    operands = (proj, kt, lse, da, normed, w_qkv, grad_proj)
+    results = (
+        jax.ShapeDtypeStruct((4 * inner, width), BF16),
+        jax.ShapeDtypeStruct((length // 2, width), F32),
+        jax.ShapeDtypeStruct((length // 2, width), BF16),
+        jax.ShapeDtypeStruct((heads, buckets, 128), F32),
+    )
     return pl.pallas_call(
         functools.partial(attend_back_kernel, length, heads, inner // heads),
-        out_shape=(
-            jax.ShapeDtypeStruct((4 * inner, width), BF16),
-            jax.ShapeDtypeStruct((length // 2, width), F32),
-            jax.ShapeDtypeStruct((length // 2, width), BF16),
-            jax.ShapeDtypeStruct((heads, buckets, 128), F32),
-        ),
-        in_specs=whole_vmem(7) + [pl.BlockSpec(memory_space=pltpu.SMEM)] * 2,
-        out_specs=tuple(whole_vmem(4)),
+        grid=(1,),
+        out_shape=results,
+        in_specs=whole_like(*operands) + [pl.BlockSpec(memory_space=pltpu.SMEM)] * 2,
+        out_specs=tuple(whole_like(*results)),
         scratch_shapes=[
             pltpu.VMEM((heads, length, PAD), BF16),
             pltpu.VMEM((heads, length, PAD), BF16),
@@ -295,9 +309,9 @@
             pltpu.VMEM((length, PAD), F32),
             pltpu.VMEM((3, PAD, width), BF16),
         ],
-        compiler_params=pltpu.CompilerParams(vmem_limit_bytes=36 << 20),
+        compiler_params=pltpu.CompilerParams(vmem_limit_bytes=60 << 20),
         cost_estimate=SMALL,
-    )(proj, kt, lse, da, normed, w_qkv, grad_proj, rel_bias, low_bit)
+    )(*operands, rel_bias, low_bit)
 
 
 def gelu_pair(v):
@@ -347,29 +361,26 @@
     members = len(first)
     count, width = rows.shape
     hidden = first[0].shape[1]
+    weights = (*first, *second)
+    results = (
+        jax.ShapeDtypeStruct((count, width), BF16),
+        jax.ShapeDtypeStruct((count, width), BF16),
+        jax.ShapeDtypeStruct((members, count, hidden), BF16),
+        jax.ShapeDtypeStruct((members, count, hidden), BF16),
+        jax.ShapeDtypeStruct((count, width), BF16),
+        jax.ShapeDtypeStruct((128, width), F32),
+    )
     return pl.pallas_call(
         functools.partial(expert_kernel, members, experts),
-        out_shape=(
-            jax.ShapeDtypeStruct((count, width), BF16),
-            jax.ShapeDtypeStruct((count, width), BF16),
-            jax.ShapeDtypeStruct((members, count, hidden), BF16),
-            jax.ShapeDtypeStruct((members, count, hidden), BF16),
-            jax.ShapeDtypeStruct((count, width), BF16),
-            jax.ShapeDtypeStruct((128, width), F32),
-        ),
-        in_specs=whole_vmem(3) + [pl.BlockSpec(memory_space=pltpu.SMEM)] + whole_vmem(2 * members),
-        out_specs=tuple(whole_vmem(6)),
-        compiler_params=pltpu.CompilerParams(vmem_limit_bytes=24 << 20),
+        grid=(1,),
+        out_shape=results,
+        in_specs=whole_like(rows, cot, router)
+        + [pl.BlockSpec(memory_space=pltpu.SMEM)]
+        + whole_like(*weights),
+        out_specs=tuple(whole_like(*results)),
+        compiler_params=pltpu.CompilerParams(vmem_limit_bytes=60 << 20),
         cost_estimate=SMALL,
-    )(rows, cot, router, group, *first, *second)
-
-
-def rows_of(count, columns):
-    return pl.BlockSpec((count, columns), lambda i: (i, 0))
-
-
-def whole_of(*shape):
-    return pl.BlockSpec(shape, lambda i: (0,) * len(shape))
+    )(rows, cot, router, group, *weights)
 
 
 def enter_kernel(
@@ -429,7 +440,7 @@
         + [whole_of(inner, width)] * members,
         out_specs=(rows_of(QB, width), rows_of(QB, 1), whole_of(count, width)),
         scratch_shapes=[pltpu.VMEM((count, width), F32)],
-        compiler_params=pltpu.CompilerParams(vmem_limit_bytes=20 << 20),
+        compiler_params=pltpu.CompilerParams(vmem_limit_bytes=60 << 20),
         cost_estimate=SMALL,
     )(
         tokens, gain, router, route, flat_id, ids, *att, *proj,
@@ -471,7 +482,7 @@
         ),
         in_specs=[whole_of(count, width)] * 2 + [whole_of(members, count, hidden)] * 2,
         out_specs=(one, one),
-        compiler_params=pltpu.CompilerParams(vmem_limit_bytes=24 << 20),
+        compiler_params=pltpu.CompilerParams(vmem_limit_bytes=60 << 20),
         cost_estimate=SMALL,
     )(rows, grads, act, gpre)
 
@@ -542,7 +553,7 @@
             whole_of(inner, width),
         ),
         scratch_shapes=[pltpu.VMEM((inner, width), F32)],
-        compiler_params=pltpu.CompilerParams(vmem_limit_bytes=24 << 20),
+        compiler_params=pltpu.CompilerParams(vmem_limit_bytes=60 << 20),
         cost_estimate=SMALL,
     )(
         hidden1, cotangent, gain, flat_id, ids, w_proj, attended_t, *blocks,
@@ -570,7 +581,7 @@
         in_specs=[rows_of(QB, width), rows_of(QB, 1), rows_of(QB, 1), whole_of(1, members * share)]
         + [whole_of(share, width)] * members,
         out_specs=rows_of(QB, width),
-        compiler_params=pltpu.CompilerParams(vmem_limit_bytes=20 << 20),
+        compiler_params=pltpu.CompilerParams(vmem_limit_bytes=60 << 20),
         cost_estimate=SMALL,
     )(hidden1, gate, flat_id, ids, *blocks)
 
@@ -611,12 +622,12 @@
             pl.BlockSpec(memory_space=pltpu.SMEM),
         ],
         out_specs=(rows_of(QB, width), whole_of(1, width)),
-        compiler_params=pltpu.CompilerParams(vmem_limit_bytes=16 << 20),
+        compiler_params=pltpu.CompilerParams(vmem_limit_bytes=60 << 20),
         cost_estimate=SMALL,
     )(kept, other, tokens, gain[None, :], grad_hidden1, low_bit)
 
 
-def copies_kernel(came_ref, small_ref, out_ref, mine_ref):
+def copies_kernel(came_ref, small_ref, ggain_ref, out_ref, mine_ref):
     groups, large = came_ref.shape[:2]
 
     @pl.when(pl.program_id(0) == 0)
@@ -625,24 +636,25 @@
         for g in range(1, groups):
             total = total + came_ref[g].astype(F32)
         mine_ref[:large, :] = total.astype(BF16)
-        mine_ref[large:, :] = small_ref[...].astype(BF16)
+        row = lax.broadcasted_iota(jnp.int32, small_ref.shape, 0)
+        mine_ref[large:, :] = (small_ref[...] + jnp.where(row == 2, ggain_ref[...], 0.0)).astype(BF16)
 
     out_ref[0] = mine_ref[...]
 
 
-def sum_copies(came, small):
+def sum_copies(came, small, ggain):
     groups, large, width = came.shape
     count = large + small.shape[0]
     return pl.pallas_call(
         copies_kernel,
         grid=(groups,),
         out_shape=jax.ShapeDtypeStruct((groups, count, width), BF16),
-        in_specs=[whole_of(groups, large, width), whole_of(*small.shape)],
+        in_specs=whole_like(came, small, ggain),
         out_specs=pl.BlockSpec((1, count, width), lambda i: (i, 0, 0)),
         scratch_shapes=[pltpu.VMEM((count, width), BF16)],
-        compiler_params=pltpu.CompilerParams(vmem_limit_bytes=12 << 20),
+        compiler_params=pltpu.CompilerParams(vmem_limit_bytes=60 << 20),
         cost_estimate=SMALL,
-    )(came, small)
+    )(came, small, ggain)
 
 
 def final_kernel(large, inner, totals_ref, qkv_ref, proj_ref, small_ref):
@@ -664,16 +676,18 @@
 
 def final_weights(totals, large, inner):
     groups, count, width = totals.shape
+    results = (
+        jax.ShapeDtypeStruct((3 * inner, width), F32),
+        jax.ShapeDtypeStruct((inner, width), F32),
+        jax.ShapeDtypeStruct((count - large, width), F32),
+    )
     return pl.pallas_call(
         functools.partial(final_kernel, large, inner),
-        out_shape=(
-            jax.ShapeDtypeStruct((3 * inner, width), F32),
-            jax.ShapeDtypeStruct((inner, width), F32),
-            jax.ShapeDtypeStruct((count - large, width), F32),
-        ),
-        in_specs=whole_vmem(1),
-        out_specs=tuple(whole_vmem(3)),
-        compiler_params=pltpu.CompilerParams(vmem_limit_bytes=8 << 20),
+        grid=(1,),
+        out_shape=results,
+        in_specs=whole_like(totals),
+        out_specs=tuple(whole_like(*results)),
+        compiler_params=pltpu.CompilerParams(vmem_limit_bytes=60 << 20),
         cost_estimate=SMALL,
     )(totals)
 
@@ -789,13 +803,13 @@
     )
     grad_back = exchange(grad_share.reshape(groups, -1, width)).reshape(-1, width)
     grad_router = grad_router[:experts]
-    grad_router = grad_router + swap(grad_router, 1)
-    grad_router, rows, grad_rows, act, grad_pre = tie((grad_router, rows, grad_rows, act, grad_pre))
+    for bit in bits:
+        grad_router = grad_router + swap(grad_router, bit)
     kept_weights, sent_weights = weight_grads(rows, grad_rows, act, grad_pre)
+    grad_back, reply, kept_weights, sent_weights, grad_router = tie(
+        (grad_back, reply, kept_weights, sent_weights, grad_router)
+    )
     near_weights = swap(sent_weights, 1)
-    for bit in bits[1:]:
-        grad_router = grad_router + swap(grad_router, bit)
-    grad_back, reply, near_weights, grad_router = tie((grad_back, reply, near_weights, grad_router))
     grad_far = gather_far(grad_back)
     out_sent = (kept_weights[1].astype(F32) + near_weights[1].astype(F32)).astype(BF16)
     in_sent = (kept_weights[3].astype(F32) + near_weights[3].astype(F32)).astype(BF16)
@@ -811,9 +825,7 @@
     grads, kept, sent, rel_parts = attend_back(
         proj, keys_t, lse, attended_grad, normed1, w_qkv_t, grad_proj, rel_bias, low_bit
     )
-    grads, kept, sent, reply_back, out_came, in_came = tie(
-        (grads, kept, sent, reply_back, out_came, in_came)
-    )
+    grads, kept, sent, reply_back = tie((grads, kept, sent, reply_back))
     kept = kept + swap(sent, 1).astype(F32)
     kept_low, grads = tie((kept.astype(BF16), grads))
     far = swap(kept_low, 2)
@@ -821,23 +833,23 @@
     reply_far = gather_far(reply_back)
     grad_w_out = kept_weights[0].astype(F32) + near_weights[0].astype(F32) + out_came.astype(F32)
     grad_w_in = kept_weights[2].astype(F32) + near_weights[2].astype(F32) + in_came.astype(F32)
+    far, grad_w_out, grad_w_in, reply_far = tie((far, grad_w_out, grad_w_in, reply_far))
+    kept = (kept + far.astype(F32)).astype(BF16)
+    other = swap(kept, 1)
+    grad_input, gain_part = input_grads(kept, other, tokens, gain_attn, grad_hidden1, low_bit)
 
     rel_row = jnp.sum(rel_parts, -1).reshape(1, -1)
     rel_row = jnp.pad(rel_row, ((0, 0), (0, width - rel_row.shape[1])))
-    small = jnp.concatenate([grad_gain_ffn, rel_row, grad_router], 0)
+    small = jnp.concatenate([grad_gain_ffn, rel_row, jnp.zeros((1, width), F32), grad_router], 0)
     small = jnp.pad(small, ((0, -small.shape[0] % 16), (0, 0)))
     large = came.shape[1]
     if large % 16 == 0:
-        copies = sum_copies(came, small)
+        copies = sum_copies(came, small, gain_part)
     else:
+        small = small.at[2].add(gain_part[0])
         copies = jnp.concatenate([jnp.sum(came.astype(F32), 0), small], 0).astype(BF16)
         copies = jnp.broadcast_to(copies[None], (groups,) + copies.shape)
-    far, copies, grad_w_out, grad_w_in, reply_far = tie((far, copies, grad_w_out, grad_w_in, reply_far))
     totals = exchange(copies)
-    kept = (kept + far.astype(F32)).astype(BF16)
-    other = swap(kept, 1)
-    grad_input, gain_part = input_grads(kept, other, tokens, gain_attn, grad_hidden1, low_bit)
-    grad_gain_attn = jnp.sum(gather_groups(gain_part), (0, 1))
     output = output_rows(hidden1, gate, flat_column, back_ids, gather_near(reply_far))
     if large % 16 == 0:
         grad_qkv_t, grad_proj, small = final_weights(totals, large, inner_here)
@@ -848,7 +860,8 @@
     grad_qkv = jnp.swapaxes(grad_qkv_t.reshape(3, inner_here, width), 1, 2)
     grad_gain_ffn = small[0]
     grad_rel = small[1, : rel_bias.size].reshape(rel_bias.shape)
-    grad_router = small[2 : 2 + experts].T
+    grad_gain_attn = small[2]
+    grad_router = small[3 : 3 + experts].T
     return (
         output,
         grad_input,

time: 305 us -> 322 us (1.056)
  waiting for transfers between devices: 109 us -> 134 us
  Pallas kernels: 83.1 us -> 103 us
  local copies, waits for them, and re-layouts: 34.6 us -> 21.2 us
  blocking collectives: 11.3 us -> 0 us
    ppermute x26, waiting for transfers between devices: 43.9 us -> 101 us  [swap(): return lax.ppermute(value, 'tensor', [(i, i ^ bit) for i in range(members)])]
    all_to_all x6, waiting for transfers between devices: 65.6 us -> 32.7 us  [exchange(): lax.all_to_all(value, 'expert', split_axis=0, concat_axis=0, tiled=True)]
    unnamed x94 -> x68, local copies, waits for them, and re-layouts: 27.5 us -> 8.78 us
    all_to_all x1 -> x0, blocking collectives: 11.3 us -> none  [exchange(): lax.all_to_all(value, 'expert', split_axis=0, concat_axis=0, tiled=True)]
    pallas_call x2, Pallas kernels: 14.1 us -> 17.7 us  [the longest x1 14.9 us: expert_step(): pl.pallas_call(functools.partial(expert_kernel, members, experts), grid=(...]
  transfers between devices with their start and end apart: 32 -> 32, of which waited for: 19 -> 21; matrix products, arithmetic and copies ran while one was open for 8% -> 9% of each run, Pallas kernels for 19% -> 25%
where the time goes in v1:
time: 322 us; the launch traced here: 320 us
  waiting for transfers between devices  134 us (42%)
  Pallas kernels  103 us (32%)
  starting transfers between devices  42 us (13%)
  local copies, waits for them, and re-layouts  21.2 us (7%)
  other arithmetic  15.3 us (5%)
  matrix products  4.34 us (1%)
    ppermute x26, waiting for transfers between devices, swap(): return lax.ppermute(value, 'tensor', [(i, i ^ bit) for i in range(members)])  101 us
    all_to_all x6, waiting for transfers between devices, exchange(): lax.all_to_all(value, 'expert', split_axis=0, concat_axis=0, tiled=True)  32.7 us
    all_to_all x6, starting transfers between devices, exchange(): lax.all_to_all(value, 'expert', split_axis=0, concat_axis=0, tiled=True)  26.8 us
    pallas_call x1, Pallas kernels, attend_back(): pl.pallas_call(functools.partial(attend_back_kernel, length, heads, inner...  22.2 us
    ppermute x26, starting transfers between devices, swap(): return lax.ppermute(value, 'tensor', [(i, i ^ bit) for i in range(members)])  15.1 us
    pallas_call x1, Pallas kernels, expert_step(): pl.pallas_call(functools.partial(expert_kernel, members, experts), grid=(...  14.9 us
    pallas_call x1, Pallas kernels, attend(): pl.pallas_call(functools.partial(attend_kernel, length, heads, inner // h...  14.4 us
    pallas_call x1, Pallas kernels, leave_experts(): pl.pallas_call(functools.partial(leave_kernel, members), grid=(length //...  11.6 us
  transfers between devices with their start and end apart: 32, of which 21 were waited for; matrix products, arithmetic and copies ran while one was open for 9% of the time, Pallas kernels for 25%

profile of v1, /device:TPU:0, one launch (start us, length us, event | category | flops | bytes accessed | tf_op | source)
XLA Modules:
  0.0 320.5 jit_solution(8617152185500406968)
XLA Ops:
  0.6 3.0 collective-permute-start
  3.8 1.2 fusion.9
  5.8 3.1 fusion.3
  8.9 5.8 %all-to-all-start = ((bf16[8,48,768]{2,1,0:T(8,128)(2,1)}), bf16[8,48,768]{2,1,0:T(8,128)(2,1)S(1)}, u32[]{:S(2)}, u32[]{:S(2)}) async-start(bf16[8,48,768]{2,1,0:T(8,128)(2,1)} %bitcast.4), calls=%async_computation | async-start | bytes 1179648 | tf_op jit(solution)/shard_map/all_to_all | solution.py:746
  15.9 1.0 copy.25.doc_ref
  16.9 14.4 %shard_map.195 = (bf16[192,1024]{1,0:T(8,128)(2,1)}, f32[8,1024]{1,0:T(8,128)}, bf16[1024,768]{1,0:T(8,128)(2,1)}, bf16[192,1024]{1,0:T(8,128)(2,1)}, bf16[1024,768]{1,0:T(8,128)(2,1)}) custom-call(bf16[1024,768]{1,0:T(8,128)(2,1)} %x_ref.5, f32[1,768]{1,0:T(1,128)} %broadcast_in_dim.16.gain_ref, bf16[3,192,768]{2,1,0:T(8,128)(2,1)} %bitcast.38, ...), custom_call_target="tpu_custom_call" | custom-call | flops 1048576 | bytes 65536 | tf_op jit(solution)/shard_map/pallas_call | solution.py:263
  31.3 1.6 collective-permute-start.1
  34.4 0.8 copy.26
  35.2 0.8 pad.17.wproj_ref
  36.0 1.7 pad.16.router_ref
  38.2 0.9 multiply_add_fusion
  39.7 5.0 %collective-permute-done.1.refs_2_ = bf16[192,1024]{1,0:T(8,128)(2,1)} collective-permute-done((bf16[192,1024]{1,0:T(8,128)(2,1)}, bf16[192,1024]{1,0:T(8,128)(2,1)}, u32[]{:S(2)}, u32[]{:S(2)}) %collective-permute-start.1) | collective-permute-done | bytes 393248 | tf_op jit(solution)/shard_map/ppermute | solution.py:722
  45.7 0.9 collective-permute-done.5.refs_5_
  47.0 1.8 collective-permute-start.7
  48.7 0.8 copy.30.ids_ref
  49.6 0.7 copy-done.22
  50.3 0.7 copy-done.23
  51.1 9.8 %shard_map.196 = (f32[1024,768]{1,0:T(8,128)}, f32[1024,1]{1,0:T(8,128)}, bf16[384,768]{1,0:T(8,128)(2,1)}) custom-call(bf16[1024,768]{1,0:T(8,128)(2,1)} %x_ref.5, f32[1,768]{1,0:T(1,128)} %broadcast_in_dim.17.gain_ref, bf16[768,128]{1,0:T(8,128)(2,1)} %pad.16.router_ref, s32[1024,1]{1,0:T(8,128)} %copy-done.3, s32[1,1024]{1,0:T(1,128)} %add.224.flat_ref, ...), custom_call_target="tpu_custom_call" | custom-call | flops 1048576 | bytes 65536 | tf_op jit(solution)/shard_map/pallas_call | solution.py:423
  60.9 5.8 %all-to-all-start.1 = ((bf16[8,48,768]{2,1,0:T(8,128)(2,1)}), bf16[8,48,768]{2,1,0:T(8,128)(2,1)S(1)}, u32[]{:S(2)}, u32[]{:S(2)}) async-start(bf16[8,48,768]{2,1,0:T(8,128)(2,1)} %bitcast.54), calls=%async_computation.1 | async-start | bytes 1179648 | tf_op jit(solution)/shard_map/all_to_all | solution.py:746
  66.7 8.8 %collective-permute-done.7.refs_6_ = bf16[768,768]{1,0:T(8,128)(2,1)} collective-permute-done((bf16[768,768]{1,0:T(8,128)(2,1)}, bf16[768,768]{1,0:T(8,128)(2,1)}, u32[]{:S(2)}, u32[]{:S(2)}) %collective-permute-start.7) | collective-permute-done | bytes 1179680 | tf_op jit(solution)/shard_map/ppermute | solution.py:722
  75.6 7.3 %all-to-all-done.1 = bf16[8,48,768]{2,1,0:T(8,128)(2,1)S(1)} async-done(((bf16[8,48,768]{2,1,0:T(8,128)(2,1)}), bf16[8,48,768]{2,1,0:T(8,128)(2,1)S(1)}, u32[]{:S(2)}, u32[]{:S(2)}) %all-to-all-start.1) | async-done | bytes 589856 | tf_op jit(solution)/shard_map/all_to_all | solution.py:746
  83.4 2.5 collective-permute-done.10.refs_5_
  85.9 1.7 collective-permute-done.11.refs_7_
  87.6 1.0 copy-done.13
  88.6 14.9 %shard_map.197 = (bf16[384,768]{1,0:T(8,128)(2,1)}, bf16[384,768]{1,0:T(8,128)(2,1)}, bf16[4,384,768]{2,1,0:T(8,128)(2,1)}, bf16[4,384,768]{2,1,0:T(8,128)(2,1)}...) custom-call(bf16[384,768]{1,0:T(8,128)(2,1)} %bitcast.36, bf16[384,768]{1,0:T(8,128)(2,1)} %bitcast.48, ...), custom_call_target="tpu_custom_call" | custom-call | flops 1048576 | bytes 65536 | tf_op jit(solution)/shard_map/pallas_call | solution.py:373
  103.6 3.6 %all-to-all-start.2 = ((bf16[8,48,768]{2,1,0:T(8,128)(2,1)}), bf16[8,48,768]{2,1,0:T(8,128)(2,1)S(1)}, u32[]{:S(2)}, u32[]{:S(2)}) async-start(bf16[8,48,768]{2,1,0:T(8,128)(2,1)} %bitcast.53), calls=%async_computation.2 | async-start | bytes 1179648 | tf_op jit(solution)/shard_map/all_to_all | solution.py:746
  107.2 0.7 slice.39
  108.0 1.2 collective-permute-done.12
  109.1 0.7 slice_add_fusion
  110.4 9.9 %shard_map.198 = (bf16[4,768,768]{2,1,0:T(8,128)(2,1)}, bf16[4,768,768]{2,1,0:T(8,128)(2,1)}) custom-call(bf16[384,768]{1,0:T(8,128)(2,1)} %bitcast.37, bf16[384,768]{1,0:T(8,128)(2,1)} %get-tuple-element.114.grads_ref, bf16[4,384,768]{2,1,0:T(8,128)(2,1)} %get-tuple-element.115.act_ref, bf16[4,384,768]{2,1,0:T(8,128)(2,1)} %get-tuple-element.116.gpre_ref), custom_call_target="tpu_custom_call" | custom-call | flops 1048576 | bytes 65536 | tf_op jit(solution)/shard_map/pallas_call | solution.py:476
  120.3 3.2 all-to-all-done.2
  124.0 4.0 %all-to-all-start.3 = ((bf16[8,48,768]{2,1,0:T(8,128)(2,1)}), bf16[8,48,768]{2,1,0:T(8,128)(2,1)S(1)}, u32[]{:S(2)}, u32[]{:S(2)}) async-start(bf16[8,48,768]{2,1,0:T(8,128)(2,1)} %bitcast.17), calls=%async_computation.3 | async-start | bytes 1179648 | tf_op jit(solution)/shard_map/all_to_all | solution.py:746
  128.0 3.8 %collective-permute-done.15 = bf16[4,768,768]{2,1,0:T(8,128)(2,1)} collective-permute-done((bf16[4,768,768]{2,1,0:T(8,128)(2,1)}, bf16[4,768,768]{2,1,0:T(8,128)(2,1)}, u32[]{:S(2)}, u32[]{:S(2)}) %collective-permute-start.15) | collective-permute-done | bytes 4718624 | tf_op jit(solution)/shard_map/ppermute | solution.py:722
  131.8 4.3 %fusion.7 = (bf16[768,768]{1,0:T(8,128)(2,1)}, bf16[768,768]{1,0:T(8,128)(2,1)}) fusion(bf16[4,768,768]{2,1,0:T(8,128)(2,1)} %collective-permute-done.15, bf16[4,768,768]{2,1,0:T(8,128)(2,1)} %get-tuple-element.121), kind=kLoop, calls=%fused_computation.12 | loop fusion | flops 4718592 | bytes 7077888 | tf_op jit(solution)/shard_map/convert_element_type | solution.py:815
  136.0 3.2 collective-permute-done.14.refs_2_
  139.8 1.5 collective-permute-done.16.refs_1_
  141.3 0.8 collective-permute-done.17.refs_3_
  142.1 0.8 copy-done.19
  142.9 11.6 %shard_map.199 = (f32[1024,768]{1,0:T(8,128)}, bf16[1024,256]{1,0:T(8,128)(2,1)}, f32[1,768]{1,0:T(1,128)}, bf16[192,768]{1,0:T(8,128)(2,1)}) custom-call(f32[1024,768]{1,0:T(8,128)} %get-tuple-element.92.hidden_ref, bf16[1024,768]{1,0:T(8,128)(2,1)} %cot_ref.1, f32[1,768]{1,0:T(1,128)} %broadcast_in_dim.17.gain_ref, s32[1024,1]{1,0:T(8,128)} %get-tuple-element.94.flat_ref, ...), custom_call_target="tpu_custom_call" | custom-call | flops 1048576 | bytes 65536 | tf_op jit(solution)/shard_map/pallas_call | solution.py:530
  154.5 22.2 %shard_map.200 = (bf16[768,768]{1,0:T(8,128)(2,1)}, f32[512,768]{1,0:T(8,128)}, bf16[512,768]{1,0:T(8,128)(2,1)}, f32[3,32,128]{2,1,0:T(8,128)}) custom-call(bf16[1024,768]{1,0:T(8,128)(2,1)} %get-tuple-element.96.proj_ref, bf16[192,1024]{1,0:T(8,128)(2,1)} %get-tuple-element.97.kt_ref, f32[8,1024]{1,0:T(8,128)} %get-tuple-element.98.lse_ref, ...), custom_call_target="tpu_custom_call" | custom-call | flops 1048576 | bytes 65536 | tf_op jit(solution)/shard_map/pallas_call | solution.py:291
  177.5 1.5 collective-permute-start.21
  179.3 1.6 fusion.10
  180.9 3.8 %all-to-all-start.4 = ((bf16[8,96,768]{2,1,0:T(8,128)(2,1)}), bf16[8,96,768]{2,1,0:T(8,128)(2,1)S(1)}, u32[]{:S(2)}, u32[]{:S(2)}) async-start(bf16[8,96,768]{2,1,0:T(8,128)(2,1)} %bitcast.49), calls=%async_computation.4 | async-start | bytes 2359296 | tf_op jit(solution)/shard_map/all_to_all | solution.py:746
  185.4 1.4 collective-permute-start.22
  186.8 19.2 %collective-permute-done.20 = bf16[768,768]{1,0:T(8,128)(2,1)} collective-permute-done((bf16[768,768]{1,0:T(8,128)(2,1)}, bf16[768,768]{1,0:T(8,128)(2,1)}, u32[]{:S(2)}, u32[]{:S(2)}) %collective-permute-start.20) | collective-permute-done | bytes 1179680 | tf_op jit(solution)/shard_map/ppermute | solution.py:722
  206.1 25.3 %collective-permute-done.21 = bf16[768,768]{1,0:T(8,128)(2,1)} collective-permute-done((bf16[768,768]{1,0:T(8,128)(2,1)}, bf16[768,768]{1,0:T(8,128)(2,1)}, u32[]{:S(2)}, u32[]{:S(2)}) %collective-permute-start.21) | collective-permute-done | bytes 1179680 | tf_op jit(solution)/shard_map/ppermute | solution.py:722
  231.3 6.0 %bitcast_add_fusion = (f32[768,768]{1,0:T(8,128)}, f32[768,768]{1,0:T(8,128)}) fusion(bf16[768,768]{1,0:T(8,128)(2,1)} %collective-permute-done.21, bf16[4,768,768]{2,1,0:T(8,128)(2,1)} %collective-permute-done.15, bf16[4,768,768]{2,1,0:T(8,128)(2,1)} %get-tuple-element.121, bf16[768,768]{1,0:T(8,128)(2,1)} %collective-permute-done.20), kind=kLoop, calls=%fused_computation.2 | loop fusion | flops 5898240 | bytes 11796480 | tf_op jit(solution)/shard_map/add | solution.py:835
  237.3 22.9 %collective-permute-done.22.refs_2_ = bf16[384,768]{1,0:T(8,128)(2,1)S(1)} collective-permute-done((bf16[384,768]{1,0:T(8,128)(2,1)S(1)}, bf16[384,768]{1,0:T(8,128)(2,1)S(1)}, u32[]{:S(2)}, u32[]{:S(2)}) %collective-permute-start.22) | collective-permute-done | bytes 589856 | tf_op jit(solution)/shard_map/ppermute | solution.py:722
  262.0 1.3 collective-permute-done.25.other_ref
  263.3 0.9 copy-done.14
  264.2 5.9 %shard_map.202 = (f32[1024,768]{1,0:T(8,128)}, f32[1,768]{1,0:T(1,128)}) custom-call(bf16[512,768]{1,0:T(8,128)(2,1)} %copy-done.5, bf16[512,768]{1,0:T(8,128)(2,1)} %copy-done.14, bf16[1024,768]{1,0:T(8,128)(2,1)} %x_ref.5, f32[1,768]{1,0:T(1,128)} %broadcast_in_dim.16.gain_ref, f32[1024,768]{1,0:T(8,128)} %get-tuple-element.142.gh_ref, s32[1]{0:T(128)} %bitcast.16.low_ref), custom_call_target="tpu_custom_call" | custom-call | flops 1048576 | bytes 65536 | tf_op jit(solution)/shard_map/pallas_call | solution.py:609
  270.1 1.0 copy-done.4
  271.1 4.2 %shard_map.203 = bf16[8,112,768]{2,1,0:T(8,128)(2,1)} custom-call(bf16[8,96,768]{2,1,0:T(8,128)(2,1)} %copy-done.4, f32[16,768]{1,0:T(8,128)} %pad.19.small_ref, f32[1,768]{1,0:T(1,128)} %get-tuple-element.148.ggain_ref), custom_call_target="tpu_custom_call" | custom-call | flops 1048576 | bytes 65536 | tf_op jit(solution)/shard_map/pallas_call | solution.py:648
  275.4 3.8 %all-to-all-start.5 = ((bf16[8,112,768]{2,1,0:T(8,128)(2,1)}), bf16[8,112,768]{2,1,0:T(8,128)(2,1)S(1)}, u32[]{:S(2)}, u32[]{:S(2)}) async-start(bf16[8,112,768]{2,1,0:T(8,128)(2,1)} %shard_map.203), calls=%async_computation.5 | async-start | bytes 2752512 | tf_op jit(solution)/shard_map/all_to_all | solution.py:746
  279.7 1.5 collective-permute-done.23.refs_1_
  281.2 0.8 collective-permute-done.24.refs_3_
  282.0 0.8 copy-done.21
  282.9 7.3 %shard_map.201 = bf16[1024,768]{1,0:T(8,128)(2,1)} custom-call(f32[1024,768]{1,0:T(8,128)} %get-tuple-element.92.hidden_ref, f32[1024,1]{1,0:T(8,128)} %get-tuple-element.93.gate_ref, s32[1024,1]{1,0:T(8,128)} %get-tuple-element.94.flat_ref, s32[1,1536]{1,0:T(1,128)} %broadcast_in_dim.18.ids_ref, bf16[384,768]{1,0:T(8,128)(2,1)} %bitcast.42, ...), custom_call_target="tpu_custom_call" | custom-call | flops 1048576 | bytes 65536 | tf_op jit(solution)/shard_map/pallas_call | solution.py:577
  290.2 22.2 %all-to-all-done.5.totals_ref = bf16[8,112,768]{2,1,0:T(8,128)(2,1)S(1)} async-done(((bf16[8,112,768]{2,1,0:T(8,128)(2,1)}), bf16[8,112,768]{2,1,0:T(8,128)(2,1)S(1)}, u32[]{:S(2)}, u32[]{:S(2)}) %all-to-all-start.5) | async-done | bytes 1376288 | tf_op jit(solution)/shard_map/all_to_all | solution.py:746
  312.4 1.1 copy-done.1
  313.5 2.8 shard_map.204
  316.2 1.4 slice_bitcast_fusion
  317.7 1.4 slice_reduce_fusion
  319.1 0.7 slice_reduce_fusion.2
  (118 shorter events, 12.9 us)
Async XLA Ops:
  0.6 30.7 %collective-permute-start = (bf16[768,768]{1,0:T(8,128)(2,1)}, bf16[768,768]{1,0:T(8,128)(2,1)}, u32[]{:S(2)}, u32[]{:S(2)}) collective-permute-start(bf16[768,768]{1,0:T(8,128)(2,1)} %bitcast.50), channel_id=1, source_target_pairs={{0,2},{1,3},{2,0},{3,1},{4,6},{5,7},{6,4},{7,5},{8,10},{9,11},{10,... | collective-permute-start | bytes 3538952 | tf_op jit(solution)/shard_map/ppermute | solution.py:722
  5.8 8.9 %copy-start.10 = (bf16[192,768]{1,0:T(8,128)(2,1)S(1)}, bf16[192,768]{1,0:T(8,128)(2,1)}, u32[]{:S(2)}) copy-start(bf16[192,768]{1,0:T(8,128)(2,1)} %refs_4_) | copy-start | bytes 884740
  5.8 9.5 %copy-start.30 = (f32[768]{0:T(1024)S(1)}, f32[768]{0:T(1024)}, u32[]{:S(2)}) copy-start(f32[768]{0:T(1024)} %param.13) | copy-start | bytes 9220
  5.8 10.1 %copy-start.29 = (s32[1,1024]{1,0:T(1,128)S(1)}, s32[1,1024]{1,0:T(1,128)}, u32[]{:S(2)}) copy-start(s32[1,1024]{1,0:T(1,128)} %param.22) | copy-start | bytes 12292
  8.9 22.4 %all-to-all-start = ((bf16[8,48,768]{2,1,0:T(8,128)(2,1)}), bf16[8,48,768]{2,1,0:T(8,128)(2,1)S(1)}, u32[]{:S(2)}, u32[]{:S(2)}) async-start(bf16[8,48,768]{2,1,0:T(8,128)(2,1)} %bitcast.4), calls=%async_computation | async-start | bytes 1179648 | tf_op jit(solution)/shard_map/all_to_all | solution.py:746
  14.7 25.0 %collective-permute-start.2 = (bf16[192,768]{1,0:T(8,128)(2,1)S(1)}, bf16[192,768]{1,0:T(8,128)(2,1)}, u32[]{:S(2)}, u32[]{:S(2)}) collective-permute-start(bf16[192,768]{1,0:T(8,128)(2,1)S(1)} %copy-done.10), channel_id=1, source_target_pairs={{0,2},{1,3},{2,0},{3,1},{4,6},{5,7},{6,4},{7,5},{8,10},{9,11},{10,... | collective-permute-start | bytes 884744 | tf_op jit(solution)/shard_map/ppermute | solution.py:722
  16.9 16.3 %copy-start.27 = (s32[1024,1]{0,1:T(1,128)S(1)}, s32[1024,1]{0,1:T(1,128)}, u32[]{:S(2)}) copy-start(s32[1024,1]{0,1:T(1,128)} %param.21) | copy-start | bytes 12292
  16.9 17.5 %copy-start.28 = (bf16[768,8]{0,1:T(8,128)(2,1)S(1)}, bf16[768,8]{0,1:T(8,128)(2,1)}, u32[]{:S(2)}) copy-start(bf16[768,8]{0,1:T(8,128)(2,1)} %param.18) | copy-start | bytes 36868
  31.3 6.4 %copy-start.31 = (f32[768]{0:T(1024)S(1)}, f32[768]{0:T(1024)}, u32[]{:S(2)}) copy-start(f32[768]{0:T(1024)} %param.17) | copy-start | bytes 9220
  31.3 7.8 %copy-start.8 = (bf16[8,48,768]{2,1,0:T(8,128)(2,1)}, bf16[8,48,768]{2,1,0:T(8,128)(2,1)S(1)}, u32[]{:S(2)}) copy-start(bf16[8,48,768]{2,1,0:T(8,128)(2,1)S(1)} %all-to-all-done) | copy-start | bytes 1769476
  31.3 13.4 %collective-permute-start.1 = (bf16[192,1024]{1,0:T(8,128)(2,1)}, bf16[192,1024]{1,0:T(8,128)(2,1)}, u32[]{:S(2)}, u32[]{:S(2)}) collective-permute-start(bf16[192,1024]{1,0:T(8,128)(2,1)} %get-tuple-element.88.refs_0_.att_ref), channel_id=1, source_target_pairs={{0,2},{1,3},{2,0},{3,1},{4,6},{5,7},{6,4},{7,5},{8,10},{9,11},{10,... | collective-permute-start | bytes 1179656 | tf_op jit(solution)/shard_map/ppermute | solution.py:722
  33.5 5.6 %copy-start.3 = (s32[1024,1]{1,0:T(8,128)}, s32[1024,1]{1,0:T(8,128)S(1)}, u32[]{:S(2)}) copy-start(s32[1024,1]{1,0:T(8,128)S(1)} %copy.27.route_ref) | copy-start | bytes 12292
  34.4 10.8 %copy-start.9 = (bf16[192,1024]{1,0:T(8,128)(2,1)S(1)}, bf16[192,1024]{1,0:T(8,128)(2,1)}, u32[]{:S(2)}) copy-start(bf16[192,1024]{1,0:T(8,128)(2,1)} %get-tuple-element.88.refs_0_.att_ref) | copy-start | bytes 1179652
  34.4 11.3 %copy-start.11 = (bf16[1,768,768]{2,1,0:T(8,128)(2,1)S(1)}, bf16[1,768,768]{2,1,0:T(8,128)(2,1)}, u32[]{:S(2)}) copy-start(bf16[1,768,768]{2,1,0:T(8,128)(2,1)} %param.19) | copy-start | bytes 3538948
  44.7 2.0 collective-permute-start.5
  44.7 2.3 collective-permute-start.6
  45.2 4.4 %collective-permute-start.3 = (bf16[192,1024]{1,0:T(8,128)(2,1)S(1)}, bf16[192,1024]{1,0:T(8,128)(2,1)S(1)}, u32[]{:S(2)}, u32[]{:S(2)}) collective-permute-start(bf16[192,1024]{1,0:T(8,128)(2,1)S(1)} %copy-done.9), channel_id=1, source_target_pairs={{0,1},{1,0},{2,3},{3,2},{4,5},{5,4},{6,7},{7,6},{8,9},{9,8},{10,11... | collective-permute-start | bytes 1179656 | tf_op jit(solution)/shard_map/ppermute | solution.py:722
  45.2 4.4 %collective-permute-start.4 = (bf16[192,1024]{1,0:T(8,128)(2,1)}, bf16[192,1024]{1,0:T(8,128)(2,1)S(1)}, u32[]{:S(2)}, u32[]{:S(2)}) collective-permute-start(bf16[192,1024]{1,0:T(8,128)(2,1)} %collective-permute-done.1.refs_2_), channel_id=1, source_target_pairs={{0,1},{1,0},{2,3},{3,2},{4,5},{5,4},{6,7},{7,6},{8,9},{9,8},{10,11... | collective-permute-start | bytes 1179656 | tf_op jit(solution)/shard_map/ppermute | solution.py:722
  45.7 21.0 %collective-permute-start.8 = (bf16[768,768]{1,0:T(8,128)(2,1)S(1)}, bf16[768,768]{1,0:T(8,128)(2,1)}, u32[]{:S(2)}, u32[]{:S(2)}) collective-permute-start(bf16[768,768]{1,0:T(8,128)(2,1)S(1)} %bitcast.52), channel_id=1, source_target_pairs={{0,1},{1,0},{2,3},{3,2},{4,5},{5,4},{6,7},{7,6},{8,9},{9,8},{10,11... | collective-permute-start | bytes 3538952 | tf_op jit(solution)/shard_map/ppermute | solution.py:722
  46.7 2.9 copy-start.24
  46.7 20.1 %collective-permute-start.9 = (bf16[768,768]{1,0:T(8,128)(2,1)}, bf16[768,768]{1,0:T(8,128)(2,1)}, u32[]{:S(2)}, u32[]{:S(2)}) collective-permute-start(bf16[768,768]{1,0:T(8,128)(2,1)} %collective-permute-done.refs_2_), channel_id=1, source_target_pairs={{0,1},{1,0},{2,3},{3,2},{4,5},{5,4},{6,7},{7,6},{8,9},{9,8},{10,11... | collective-permute-start | bytes 3538952 | tf_op jit(solution)/shard_map/ppermute | solution.py:722
  47.0 2.6 copy-start.25
  47.0 28.6 %collective-permute-start.7 = (bf16[768,768]{1,0:T(8,128)(2,1)}, bf16[768,768]{1,0:T(8,128)(2,1)}, u32[]{:S(2)}, u32[]{:S(2)}) collective-permute-start(bf16[768,768]{1,0:T(8,128)(2,1)} %bitcast.6.refs_4_), channel_id=1, source_target_pairs={{0,2},{1,3},{2,0},{3,1},{4,6},{5,7},{6,4},{7,5},{8,10},{9,11},{10,... | collective-permute-start | bytes 3538952 | tf_op jit(solution)/shard_map/ppermute | solution.py:722
  49.6 0.7 copy-start.22
  60.9 21.9 %all-to-all-start.1 = ((bf16[8,48,768]{2,1,0:T(8,128)(2,1)}), bf16[8,48,768]{2,1,0:T(8,128)(2,1)S(1)}, u32[]{:S(2)}, u32[]{:S(2)}) async-start(bf16[8,48,768]{2,1,0:T(8,128)(2,1)} %bitcast.54), calls=%async_computation.1 | async-start | bytes 1179648 | tf_op jit(solution)/shard_map/all_to_all | solution.py:746
  82.9 4.8 %copy-start.2 = (bf16[8,48,768]{2,1,0:T(8,128)(2,1)}, bf16[8,48,768]{2,1,0:T(8,128)(2,1)S(1)}, u32[]{:S(2)}) copy-start(bf16[8,48,768]{2,1,0:T(8,128)(2,1)S(1)} %all-to-all-done.1) | copy-start | bytes 1769476
  82.9 3.1 collective-permute-start.10
  82.9 4.7 %collective-permute-start.11 = (bf16[768,768]{1,0:T(8,128)(2,1)}, bf16[768,768]{1,0:T(8,128)(2,1)S(1)}, u32[]{:S(2)}, u32[]{:S(2)}) collective-permute-start(bf16[768,768]{1,0:T(8,128)(2,1)} %collective-permute-done.7.refs_6_), channel_id=1, source_target_pairs={{0,1},{1,0},{2,3},{3,2},{4,5},{5,4},{6,7},{7,6},{8,9},{9,8},{10,11... | collective-permute-start | bytes 3538952 | tf_op jit(solution)/shard_map/ppermute | solution.py:722
  85.9 1.7 copy-start.12
  87.6 1.0 copy-start.13
  103.6 19.9 %all-to-all-start.2 = ((bf16[8,48,768]{2,1,0:T(8,128)(2,1)}), bf16[8,48,768]{2,1,0:T(8,128)(2,1)S(1)}, u32[]{:S(2)}, u32[]{:S(2)}) async-start(bf16[8,48,768]{2,1,0:T(8,128)(2,1)} %bitcast.53), calls=%async_computation.2 | async-start | bytes 1179648 | tf_op jit(solution)/shard_map/all_to_all | solution.py:746
  107.9 1.2 collective-permute-start.12
  109.9 10.4 %collective-permute-start.13 = (f32[8,768]{1,0:T(8,128)S(1)}, f32[8,768]{1,0:T(8,128)S(1)}, u32[]{:S(2)}, u32[]{:S(2)}) collective-permute-start(f32[8,768]{1,0:T(8,128)S(1)} %slice_add_fusion), channel_id=1, source_target_pairs={{0,2},{1,3},{2,0},{3,1},{4,6},{5,7},{6,4},{7,5},{8,10},{9,11},{10,... | collective-permute-start | bytes 73736 | tf_op jit(solution)/shard_map/ppermute | solution.py:722
  123.5 15.8 %copy-start.7 = (bf16[8,48,768]{2,1,0:T(8,128)(2,1)}, bf16[8,48,768]{2,1,0:T(8,128)(2,1)S(1)}, u32[]{:S(2)}) copy-start(bf16[8,48,768]{2,1,0:T(8,128)(2,1)S(1)} %all-to-all-done.2) | copy-start | bytes 1769476
  123.5 8.3 %collective-permute-start.15 = (bf16[4,768,768]{2,1,0:T(8,128)(2,1)}, bf16[4,768,768]{2,1,0:T(8,128)(2,1)}, u32[]{:S(2)}, u32[]{:S(2)}) collective-permute-start(bf16[4,768,768]{2,1,0:T(8,128)(2,1)} %get-tuple-element.122), channel_id=1, source_target_pairs={{0,1},{1,0},{2,3},{3,2},{4,5},{5,4},{6,7},{7,6},{8,9},{9,8},{10,11... | collective-permute-start | bytes 14155784 | tf_op jit(solution)/shard_map/ppermute | solution.py:722
  123.5 15.7 %collective-permute-start.14 = (bf16[384,768]{1,0:T(8,128)(2,1)S(1)}, bf16[384,768]{1,0:T(8,128)(2,1)S(1)}, u32[]{:S(2)}, u32[]{:S(2)}) collective-permute-start(bf16[384,768]{1,0:T(8,128)(2,1)S(1)} %bitcast.43), channel_id=1, source_target_pairs={{0,2},{1,3},{2,0},{3,1},{4,6},{5,7},{6,4},{7,5},{8,10},{9,11},{10,... | collective-permute-start | bytes 1769480 | tf_op jit(solution)/shard_map/ppermute | solution.py:722
  124.0 52.7 %all-to-all-start.3 = ((bf16[8,48,768]{2,1,0:T(8,128)(2,1)}), bf16[8,48,768]{2,1,0:T(8,128)(2,1)S(1)}, u32[]{:S(2)}, u32[]{:S(2)}) async-start(bf16[8,48,768]{2,1,0:T(8,128)(2,1)} %bitcast.17), calls=%async_computation.3 | async-start | bytes 1179648 | tf_op jit(solution)/shard_map/all_to_all | solution.py:746
  139.2 2.9 copy-start.17
  139.2 2.0 collective-permute-start.16
  139.3 2.8 collective-permute-start.17
  141.3 0.9 copy-start.18
  142.1 0.8 copy-start.19
  176.7 102.4 %copy-start.6 = (bf16[8,48,768]{2,1,0:T(8,128)(2,1)}, bf16[8,48,768]{2,1,0:T(8,128)(2,1)S(1)}, u32[]{:S(2)}) copy-start(bf16[8,48,768]{2,1,0:T(8,128)(2,1)S(1)} %all-to-all-done.3) | copy-start | bytes 1769476
  176.7 2.6 collective-permute-start.18
  177.0 29.1 %collective-permute-start.20 = (bf16[768,768]{1,0:T(8,128)(2,1)}, bf16[768,768]{1,0:T(8,128)(2,1)}, u32[]{:S(2)}, u32[]{:S(2)}) collective-permute-start(bf16[768,768]{1,0:T(8,128)(2,1)} %get-tuple-element.136), channel_id=1, source_target_pairs={{0,2},{1,3},{2,0},{3,1},{4,6},{5,7},{6,4},{7,5},{8,10},{9,11},{10,... | collective-permute-start | bytes 3538952 | tf_op jit(solution)/shard_map/ppermute | solution.py:722
  177.5 53.9 %collective-permute-start.21 = (bf16[768,768]{1,0:T(8,128)(2,1)}, bf16[768,768]{1,0:T(8,128)(2,1)}, u32[]{:S(2)}, u32[]{:S(2)}) collective-permute-start(bf16[768,768]{1,0:T(8,128)(2,1)} %get-tuple-element.137), channel_id=1, source_target_pairs={{0,2},{1,3},{2,0},{3,1},{4,6},{5,7},{6,4},{7,5},{8,10},{9,11},{10,... | collective-permute-start | bytes 3538952 | tf_op jit(solution)/shard_map/ppermute | solution.py:722
  180.9 89.2 %all-to-all-start.4 = ((bf16[8,96,768]{2,1,0:T(8,128)(2,1)}), bf16[8,96,768]{2,1,0:T(8,128)(2,1)S(1)}, u32[]{:S(2)}, u32[]{:S(2)}) async-start(bf16[8,96,768]{2,1,0:T(8,128)(2,1)} %bitcast.49), calls=%async_computation.4 | async-start | bytes 2359296 | tf_op jit(solution)/shard_map/all_to_all | solution.py:746
  184.7 75.5 %copy-start = (f32[512,768]{1,0:T(8,128)S(1)}, f32[512,768]{1,0:T(8,128)}, u32[]{:S(2)}) copy-start(f32[512,768]{1,0:T(8,128)} %get-tuple-element.132) | copy-start | bytes 4718596
  184.7 75.5 %collective-permute-start.19 = (bf16[512,768]{1,0:T(8,128)(2,1)S(1)}, bf16[512,768]{1,0:T(8,128)(2,1)S(1)}, u32[]{:S(2)}, u32[]{:S(2)}) collective-permute-start(bf16[512,768]{1,0:T(8,128)(2,1)S(1)} %fusion.10), channel_id=1, source_target_pairs={{0,2},{1,3},{2,0},{3,1},{4,6},{5,7},{6,4},{7,5},{8,10},{9,11},{10,... | collective-permute-start | bytes 2359304 | tf_op jit(solution)/shard_map/ppermute | solution.py:722
  185.4 74.8 %collective-permute-start.22 = (bf16[384,768]{1,0:T(8,128)(2,1)S(1)}, bf16[384,768]{1,0:T(8,128)(2,1)S(1)}, u32[]{:S(2)}, u32[]{:S(2)}) collective-permute-start(bf16[384,768]{1,0:T(8,128)(2,1)S(1)} %bitcast.40), channel_id=1, source_target_pairs={{0,2},{1,3},{2,0},{3,1},{4,6},{5,7},{6,4},{7,5},{8,10},{9,11},{10,... | collective-permute-start | bytes 1769480 | tf_op jit(solution)/shard_map/ppermute | solution.py:722
  260.2 0.8 copy-start.15
  260.2 0.9 copy-start.26
  260.2 1.1 copy-start.32
  261.0 2.3 copy-start.5
  261.0 2.3 collective-permute-start.25
  263.3 0.9 copy-start.14
  270.1 1.0 copy-start.4
  275.3 3.9 %copy-start.16 = (bf16[384,768]{1,0:T(8,128)(2,1)S(1)}, bf16[384,768]{1,0:T(8,128)(2,1)}, u32[]{:S(2)}) copy-start(bf16[384,768]{1,0:T(8,128)(2,1)} %copy-done.15) | copy-start | bytes 1769476
  275.4 37.0 %all-to-all-start.5 = ((bf16[8,112,768]{2,1,0:T(8,128)(2,1)}), bf16[8,112,768]{2,1,0:T(8,128)(2,1)S(1)}, u32[]{:S(2)}, u32[]{:S(2)}) async-start(bf16[8,112,768]{2,1,0:T(8,128)(2,1)} %shard_map.203), calls=%async_computation.5 | async-start | bytes 2752512 | tf_op jit(solution)/shard_map/all_to_all | solution.py:746
  279.1 2.1 collective-permute-start.23
  279.3 2.7 collective-permute-start.24
  281.2 1.7 copy-start.20
  282.0 0.8 copy-start.21
  312.4 1.1 copy-start.1
  (1 other events, 0.7 us)

commit v2 on v1

--- a/solution.py
+++ b/solution.py
@@ -657,7 +657,7 @@
     )(came, small, ggain)
 
 
-def final_kernel(large, inner, totals_ref, qkv_ref, proj_ref, small_ref):
+def final_kernel(large, inner, totals_ref, qkv_ref, proj_ref, gffn_ref, rel_ref, gattn_ref, router_ref):
     groups = totals_ref.shape[0]
     split = 3 * inner
     small = totals_ref[0, large:, :].astype(F32)
@@ -671,15 +671,21 @@
             proj_ref[start + skip - split : stop - split, :] = totals_ref[g, skip:large, :].astype(F32)
         if g:
             small = small + totals_ref[g, large:, :].astype(F32)
-    small_ref[...] = small
-
-
-def final_weights(totals, large, inner):
+    gffn_ref[...] = small[0:1]
+    rel_ref[...] = small[1:2]
+    gattn_ref[...] = small[2:3]
+    router_ref[...] = small[3 : 3 + router_ref.shape[0]]
+
+
+def final_weights(totals, large, inner, experts):
     groups, count, width = totals.shape
     results = (
         jax.ShapeDtypeStruct((3 * inner, width), F32),
         jax.ShapeDtypeStruct((inner, width), F32),
-        jax.ShapeDtypeStruct((count - large, width), F32),
+        jax.ShapeDtypeStruct((1, width), F32),
+        jax.ShapeDtypeStruct((1, width), F32),
+        jax.ShapeDtypeStruct((1, width), F32),
+        jax.ShapeDtypeStruct((experts, width), F32),
     )
     return pl.pallas_call(
         functools.partial(final_kernel, large, inner),
@@ -687,7 +693,7 @@
         out_shape=results,
         in_specs=whole_like(totals),
         out_specs=tuple(whole_like(*results)),
-        compiler_params=pltpu.CompilerParams(vmem_limit_bytes=60 << 20),
+        compiler_params=pltpu.CompilerParams(vmem_limit_bytes=16 << 20),
         cost_estimate=SMALL,
     )(totals)
 
@@ -811,10 +817,15 @@
     )
     near_weights = swap(sent_weights, 1)
     grad_far = gather_far(grad_back)
-    out_sent = (kept_weights[1].astype(F32) + near_weights[1].astype(F32)).astype(BF16)
-    in_sent = (kept_weights[3].astype(F32) + near_weights[3].astype(F32)).astype(BF16)
-    grad_far, out_sent, in_sent = tie((grad_far, out_sent, in_sent))
-    out_came, in_came = swap(out_sent, 2), swap(in_sent, 2)
+    cut = width // 2
+
+    def pair(k, rows_cut):
+        return kept_weights[k, rows_cut].astype(F32) + near_weights[k, rows_cut].astype(F32)
+
+    out_sent = pair(1, slice(0, width)).astype(BF16)
+    fore_sent, rest_sent = pair(3, slice(0, cut)).astype(BF16), pair(3, slice(cut, width)).astype(BF16)
+    grad_far, out_sent, fore_sent, rest_sent = tie((grad_far, out_sent, fore_sent, rest_sent))
+    out_came, fore_came = swap(out_sent, 2), swap(fore_sent, 2)
     grad_blocks = gather_near(grad_far)
     reply_back = exchange(reply.reshape(groups, -1, width)).reshape(-1, width)
     grad_hidden1, attended_grad, grad_gain_ffn, grad_proj = leave_experts(
@@ -825,15 +836,18 @@
     grads, kept, sent, rel_parts = attend_back(
         proj, keys_t, lse, attended_grad, normed1, w_qkv_t, grad_proj, rel_bias, low_bit
     )
-    grads, kept, sent, reply_back = tie((grads, kept, sent, reply_back))
+    grads, kept, sent, reply_back, out_came, fore_came, rest_sent = tie(
+        (grads, kept, sent, reply_back, out_came, fore_came, rest_sent)
+    )
     kept = kept + swap(sent, 1).astype(F32)
     kept_low, grads = tie((kept.astype(BF16), grads))
     far = swap(kept_low, 2)
     came = exchange(grads.reshape(groups, -1, width))
+    rest_came = swap(rest_sent, 2)
+    grad_w_out = pair(0, slice(0, width)) + out_came.astype(F32)
+    far, grad_w_out, reply_back = tie((far, grad_w_out, reply_back))
     reply_far = gather_far(reply_back)
-    grad_w_out = kept_weights[0].astype(F32) + near_weights[0].astype(F32) + out_came.astype(F32)
-    grad_w_in = kept_weights[2].astype(F32) + near_weights[2].astype(F32) + in_came.astype(F32)
-    far, grad_w_out, grad_w_in, reply_far = tie((far, grad_w_out, grad_w_in, reply_far))
+    grad_w_in = pair(2, slice(0, width)) + jnp.concatenate([fore_came, rest_came], 0).astype(F32)
     kept = (kept + far.astype(F32)).astype(BF16)
     other = swap(kept, 1)
     grad_input, gain_part = input_grads(kept, other, tokens, gain_attn, grad_hidden1, low_bit)
@@ -852,16 +866,19 @@
     totals = exchange(copies)
     output = output_rows(hidden1, gate, flat_column, back_ids, gather_near(reply_far))
     if large % 16 == 0:
-        grad_qkv_t, grad_proj, small = final_weights(totals, large, inner_here)
+        grad_qkv_t, grad_proj, grad_gain_ffn, rel_row, grad_gain_attn, grad_router = final_weights(
+            totals, large, inner_here, experts
+        )
     else:
         shared = totals[:, :large].reshape(-1, width).astype(F32)
         grad_qkv_t, grad_proj = shared[: 3 * inner_here], shared[3 * inner_here :]
         small = jnp.sum(totals[:, large:].astype(F32), 0)
+        grad_gain_ffn, rel_row, grad_gain_attn = small[0], small[1], small[2]
+        grad_router = small[3 : 3 + experts]
     grad_qkv = jnp.swapaxes(grad_qkv_t.reshape(3, inner_here, width), 1, 2)
-    grad_gain_ffn = small[0]
-    grad_rel = small[1, : rel_bias.size].reshape(rel_bias.shape)
-    grad_gain_attn = small[2]
-    grad_router = small[3 : 3 + experts].T
+    grad_gain_ffn, grad_gain_attn = grad_gain_ffn.reshape(-1), grad_gain_attn.reshape(-1)
+    grad_rel = rel_row.reshape(-1)[: rel_bias.size].reshape(rel_bias.shape)
+    grad_router = grad_router.T
     return (
         output,
         grad_input,

time: 322 us -> 276 us (0.86)
  waiting for transfers between devices: 134 us -> 86.4 us
  local copies, waits for them, and re-layouts: 21.2 us -> 16.9 us
  other arithmetic: 15.3 us -> 19.3 us
  starting transfers between devices: 42 us -> 45.7 us
    ppermute x26 -> x27, waiting for transfers between devices: 101 us -> 76.4 us  [swap(): return lax.ppermute(value, 'tensor', [(i, i ^ bit) for i in range(members)])]
    all_to_all x6, waiting for transfers between devices: 32.7 us -> 9.94 us  [exchange(): lax.all_to_all(value, 'expert', split_axis=0, concat_axis=0, tiled=True)]
    all_to_all x6, starting transfers between devices: 26.8 us -> 31 us  [exchange(): lax.all_to_all(value, 'expert', split_axis=0, concat_axis=0, tiled=True)]
    add x1 -> x2, other arithmetic: 5.98 us -> 7.44 us  [the longest x1 3.77 us: shards(): grad_w_out = pair(0, slice(0, width)) + out_came.astype(F32)]
    unnamed x68 -> x66, local copies, waits for them, and re-layouts: 8.78 us -> 7.9 us
    ppermute x26 -> x27, starting transfers between devices: 15.1 us -> 14.7 us  [swap(): return lax.ppermute(value, 'tensor', [(i, i ^ bit) for i in range(members)])]
  transfers between devices with their start and end apart: 32 -> 33, of which waited for: 21 -> 18; matrix products, arithmetic and copies ran while one was open for 9% -> 11% of each run, Pallas kernels for 25% -> 29%
where the time goes in v2:
time: 276 us; the launch traced here: 275 us
  Pallas kernels  102 us (37%)
  waiting for transfers between devices  86.4 us (31%)
  starting transfers between devices  45.7 us (17%)
  other arithmetic  19.3 us (7%)
  local copies, waits for them, and re-layouts  16.9 us (6%)
  matrix products  4.33 us (2%)
    ppermute x27, waiting for transfers between devices, swap(): return lax.ppermute(value, 'tensor', [(i, i ^ bit) for i in range(members)])  76.4 us
    all_to_all x6, starting transfers between devices, exchange(): lax.all_to_all(value, 'expert', split_axis=0, concat_axis=0, tiled=True)  31 us
    pallas_call x1, Pallas kernels, attend_back(): pl.pallas_call(functools.partial(attend_back_kernel, length, heads, inner...  22.2 us
    pallas_call x1, Pallas kernels, expert_step(): pl.pallas_call(functools.partial(expert_kernel, members, experts), grid=(...  14.9 us
    ppermute x27, starting transfers between devices, swap(): return lax.ppermute(value, 'tensor', [(i, i ^ bit) for i in range(members)])  14.7 us
    pallas_call x1, Pallas kernels, attend(): pl.pallas_call(functools.partial(attend_kernel, length, heads, inner // h...  14.4 us
    pallas_call x1, Pallas kernels, leave_experts(): pl.pallas_call(functools.partial(leave_kernel, members), grid=(length //...  11.6 us
    all_to_all x6, waiting for transfers between devices, exchange(): lax.all_to_all(value, 'expert', split_axis=0, concat_axis=0, tiled=True)  9.94 us
  transfers between devices with their start and end apart: 33, of which 18 were waited for; matrix products, arithmetic and copies ran while one was open for 11% of the time, Pallas kernels for 29%

profile of v2, /device:TPU:0, one launch (start us, length us, event | category | flops | bytes accessed | tf_op | source)
XLA Modules:
  0.0 275.3 jit_solution(17998190040299842985)
XLA Ops:
  0.6 3.0 %collective-permute-start = (bf16[768,768]{1,0:T(8,128)(2,1)}, bf16[768,768]{1,0:T(8,128)(2,1)}, u32[]{:S(2)}, u32[]{:S(2)}) collective-permute-start(bf16[768,768]{1,0:T(8,128)(2,1)} %bitcast.49), channel_id=1, source_target_pairs={{0,2},{1,3},{2,0},{3,1},{4,6},{5,7},{6,4},{7,5},{8,10},{9,11},{10,... | collective-permute-start | bytes 3538952 | tf_op jit(solution)/shard_map/ppermute | solution.py:728
  3.8 1.2 fusion.8
  5.1 0.7 multiply_add_fusion.1
  5.8 3.1 %fusion.3 = bf16[384,768]{1,0:T(8,128)(2,1)} fusion(bf16[1024,768]{1,0:T(8,128)(2,1)} %cot_ref.1, s32[1024]{0:T(1024)S(1)} %multiply_add_fusion.1, s32[384]{0:T(512)S(1)} %add.225), kind=kOutput, calls=%fused_computation.9 | convolution fusion | flops 604667904 | bytes 2168320 | tf_op jit(solution)/shard_map/dot_general | solution.py:38
  8.9 5.8 %all-to-all-start = ((bf16[8,48,768]{2,1,0:T(8,128)(2,1)}), bf16[8,48,768]{2,1,0:T(8,128)(2,1)S(1)}, u32[]{:S(2)}, u32[]{:S(2)}) async-start(bf16[8,48,768]{2,1,0:T(8,128)(2,1)} %bitcast.4), calls=%async_computation | async-start | bytes 1179648 | tf_op jit(solution)/shard_map/all_to_all | solution.py:752
  15.9 1.0 copy.25.doc_ref
  16.9 14.4 %shard_map.195 = (bf16[192,1024]{1,0:T(8,128)(2,1)}, f32[8,1024]{1,0:T(8,128)}, bf16[1024,768]{1,0:T(8,128)(2,1)}, bf16[192,1024]{1,0:T(8,128)(2,1)}, bf16[1024,768]{1,0:T(8,128)(2,1)}) custom-call(bf16[1024,768]{1,0:T(8,128)(2,1)} %x_ref.5, f32[1,768]{1,0:T(1,128)} %broadcast_in_dim.14.gain_ref, bf16[3,192,768]{2,1,0:T(8,128)(2,1)} %bitcast.38, ...), custom_call_target="tpu_custom_call" | custom-call | flops 1048576 | bytes 65536 | tf_op jit(solution)/shard_map/pallas_call | solution.py:263
  31.3 1.6 collective-permute-start.1
  34.4 0.8 copy.26
  35.2 0.8 pad.17.wproj_ref
  36.0 1.6 pad.16.router_ref
  38.2 0.9 multiply_add_fusion
  39.7 5.0 %collective-permute-done.1.refs_2_ = bf16[192,1024]{1,0:T(8,128)(2,1)} collective-permute-done((bf16[192,1024]{1,0:T(8,128)(2,1)}, bf16[192,1024]{1,0:T(8,128)(2,1)}, u32[]{:S(2)}, u32[]{:S(2)}) %collective-permute-start.1) | collective-permute-done | bytes 393248 | tf_op jit(solution)/shard_map/ppermute | solution.py:728
  45.7 0.9 collective-permute-done.5.refs_5_
  47.0 1.8 collective-permute-start.7
  48.7 0.8 copy.30.ids_ref
  49.6 0.7 copy-done.20
  50.3 0.7 copy-done.21
  51.1 9.8 %shard_map.196 = (f32[1024,768]{1,0:T(8,128)}, f32[1024,1]{1,0:T(8,128)}, bf16[384,768]{1,0:T(8,128)(2,1)}) custom-call(bf16[1024,768]{1,0:T(8,128)(2,1)} %x_ref.5, f32[1,768]{1,0:T(1,128)} %broadcast_in_dim.15.gain_ref, bf16[768,128]{1,0:T(8,128)(2,1)} %pad.16.router_ref, s32[1024,1]{1,0:T(8,128)} %copy-done.2, s32[1,1024]{1,0:T(1,128)} %add.227.flat_ref, ...), custom_call_target="tpu_custom_call" | custom-call | flops 1048576 | bytes 65536 | tf_op jit(solution)/shard_map/pallas_call | solution.py:423
  60.9 5.8 %all-to-all-start.1 = ((bf16[8,48,768]{2,1,0:T(8,128)(2,1)}), bf16[8,48,768]{2,1,0:T(8,128)(2,1)S(1)}, u32[]{:S(2)}, u32[]{:S(2)}) async-start(bf16[8,48,768]{2,1,0:T(8,128)(2,1)} %bitcast.55), calls=%async_computation.1 | async-start | bytes 1179648 | tf_op jit(solution)/shard_map/all_to_all | solution.py:752
  66.8 8.8 %collective-permute-done.7.refs_6_ = bf16[768,768]{1,0:T(8,128)(2,1)} collective-permute-done((bf16[768,768]{1,0:T(8,128)(2,1)}, bf16[768,768]{1,0:T(8,128)(2,1)}, u32[]{:S(2)}, u32[]{:S(2)}) %collective-permute-start.7) | collective-permute-done | bytes 1179680 | tf_op jit(solution)/shard_map/ppermute | solution.py:728
  75.6 7.3 %all-to-all-done.1 = bf16[8,48,768]{2,1,0:T(8,128)(2,1)S(1)} async-done(((bf16[8,48,768]{2,1,0:T(8,128)(2,1)}), bf16[8,48,768]{2,1,0:T(8,128)(2,1)S(1)}, u32[]{:S(2)}, u32[]{:S(2)}) %all-to-all-start.1) | async-done | bytes 589856 | tf_op jit(solution)/shard_map/all_to_all | solution.py:752
  83.4 2.5 collective-permute-done.10.refs_5_
  85.9 1.7 collective-permute-done.11.refs_7_
  87.6 1.0 copy-done.14
  88.7 14.9 %shard_map.197 = (bf16[384,768]{1,0:T(8,128)(2,1)}, bf16[384,768]{1,0:T(8,128)(2,1)}, bf16[4,384,768]{2,1,0:T(8,128)(2,1)}, bf16[4,384,768]{2,1,0:T(8,128)(2,1)}...) custom-call(bf16[384,768]{1,0:T(8,128)(2,1)} %bitcast.36, bf16[384,768]{1,0:T(8,128)(2,1)} %bitcast.47, ...), custom_call_target="tpu_custom_call" | custom-call | flops 1048576 | bytes 65536 | tf_op jit(solution)/shard_map/pallas_call | solution.py:373
  103.6 3.6 %all-to-all-start.2 = ((bf16[8,48,768]{2,1,0:T(8,128)(2,1)}), bf16[8,48,768]{2,1,0:T(8,128)(2,1)S(1)}, u32[]{:S(2)}, u32[]{:S(2)}) async-start(bf16[8,48,768]{2,1,0:T(8,128)(2,1)} %bitcast.54), calls=%async_computation.2 | async-start | bytes 1179648 | tf_op jit(solution)/shard_map/all_to_all | solution.py:752
  107.2 0.7 slice.37
  108.0 1.2 collective-permute-done.12
  109.2 0.7 slice_add_fusion
  110.4 9.9 %shard_map.198 = (bf16[4,768,768]{2,1,0:T(8,128)(2,1)}, bf16[4,768,768]{2,1,0:T(8,128)(2,1)}) custom-call(bf16[384,768]{1,0:T(8,128)(2,1)} %bitcast.37, bf16[384,768]{1,0:T(8,128)(2,1)} %get-tuple-element.119.grads_ref, bf16[4,384,768]{2,1,0:T(8,128)(2,1)} %get-tuple-element.120.act_ref, bf16[4,384,768]{2,1,0:T(8,128)(2,1)} %get-tuple-element.121.gpre_ref), custom_call_target="tpu_custom_call" | custom-call | flops 1048576 | bytes 65536 | tf_op jit(solution)/shard_map/pallas_call | solution.py:476
  120.9 2.6 all-to-all-done.2
  124.0 7.6 %collective-permute-done.15 = bf16[4,768,768]{2,1,0:T(8,128)(2,1)S(1)} collective-permute-done((bf16[4,768,768]{2,1,0:T(8,128)(2,1)}, bf16[4,768,768]{2,1,0:T(8,128)(2,1)S(1)}, u32[]{:S(2)}, u32[]{:S(2)}) %collective-permute-start.15) | collective-permute-done | bytes 4718624 | tf_op jit(solution)/shard_map/ppermute | solution.py:728
  131.6 3.4 %fusion.13 = (bf16[384,768]{1,0:T(8,128)(2,1)}, bf16[384,768]{1,0:T(8,128)(2,1)}) fusion(bf16[4,768,768]{2,1,0:T(8,128)(2,1)S(1)} %collective-permute-done.15, bf16[4,768,768]{2,1,0:T(8,128)(2,1)} %get-tuple-element.126), kind=kLoop, calls=%fused_computation.19 | loop fusion | flops 2359296 | bytes 3538944 | tf_op jit(solution)/shard_map/convert_element_type | solution.py:826
  135.0 1.6 fusion.6
  136.7 2.6 collective-permute-done.14.refs_2_
  140.1 4.1 %all-to-all-start.3 = ((bf16[8,48,768]{2,1,0:T(8,128)(2,1)}), bf16[8,48,768]{2,1,0:T(8,128)(2,1)S(1)}, u32[]{:S(2)}, u32[]{:S(2)}) async-start(bf16[8,48,768]{2,1,0:T(8,128)(2,1)} %bitcast.53), calls=%async_computation.3 | async-start | bytes 1179648 | tf_op jit(solution)/shard_map/all_to_all | solution.py:752
  144.8 0.9 collective-permute-start.19
  145.6 0.8 collective-permute-done.16.refs_1_
  146.5 1.0 collective-permute-done.17.refs_3_
  147.5 11.6 %shard_map.199 = (f32[1024,768]{1,0:T(8,128)}, bf16[1024,256]{1,0:T(8,128)(2,1)}, f32[1,768]{1,0:T(1,128)}, bf16[192,768]{1,0:T(8,128)(2,1)}) custom-call(f32[1024,768]{1,0:T(8,128)} %get-tuple-element.97.hidden_ref, bf16[1024,768]{1,0:T(8,128)(2,1)} %cot_ref.1, f32[1,768]{1,0:T(1,128)} %broadcast_in_dim.15.gain_ref, s32[1024,1]{1,0:T(8,128)} %get-tuple-element.99.flat_ref, ...), custom_call_target="tpu_custom_call" | custom-call | flops 1048576 | bytes 65536 | tf_op jit(solution)/shard_map/pallas_call | solution.py:530
  159.1 22.2 %shard_map.200 = (bf16[768,768]{1,0:T(8,128)(2,1)}, f32[512,768]{1,0:T(8,128)}, bf16[512,768]{1,0:T(8,128)(2,1)}, f32[3,32,128]{2,1,0:T(8,128)}) custom-call(bf16[1024,768]{1,0:T(8,128)(2,1)} %get-tuple-element.101.proj_ref, bf16[192,1024]{1,0:T(8,128)(2,1)} %get-tuple-element.102.kt_ref, f32[8,1024]{1,0:T(8,128)} %get-tuple-element.103.lse_ref, ...), custom_call_target="tpu_custom_call" | custom-call | flops 1048576 | bytes 65536 | tf_op jit(solution)/shard_map/pallas_call | solution.py:291
  181.3 1.0 copy-done.12
  182.5 2.4 collective-permute-done.20
  184.9 1.6 fusion.9
  186.4 5.9 %all-to-all-start.4 = ((bf16[8,96,768]{2,1,0:T(8,128)(2,1)}), bf16[8,96,768]{2,1,0:T(8,128)(2,1)S(1)}, u32[]{:S(2)}, u32[]{:S(2)}) async-start(bf16[8,96,768]{2,1,0:T(8,128)(2,1)} %bitcast.48), calls=%async_computation.4 | async-start | bytes 2359296 | tf_op jit(solution)/shard_map/all_to_all | solution.py:752
  192.4 0.9 collective-permute-start.21
  193.3 3.8 %bitcast_add_fusion = f32[768,768]{1,0:T(8,128)} fusion(bf16[768,768]{1,0:T(8,128)(2,1)} %copy-done.12, bf16[4,768,768]{2,1,0:T(8,128)(2,1)} %copy-done.3, bf16[4,768,768]{2,1,0:T(8,128)(2,1)} %get-tuple-element.126), kind=kLoop, calls=%fused_computation.2 | loop fusion | flops 2949120 | bytes 5898240 | tf_op jit(solution)/shard_map/add | solution.py:847
  197.0 14.7 %collective-permute-done.21 = bf16[512,768]{1,0:T(8,128)(2,1)S(1)} collective-permute-done((bf16[512,768]{1,0:T(8,128)(2,1)S(1)}, bf16[512,768]{1,0:T(8,128)(2,1)S(1)}, u32[]{:S(2)}, u32[]{:S(2)}) %collective-permute-start.21) | collective-permute-done | bytes 786464 | tf_op jit(solution)/shard_map/ppermute | solution.py:728
  213.1 1.3 collective-permute-done.25.other_ref
  214.4 0.9 copy-done.15
  215.3 5.9 %shard_map.202 = (f32[1024,768]{1,0:T(8,128)}, f32[1,768]{1,0:T(1,128)}) custom-call(bf16[512,768]{1,0:T(8,128)(2,1)} %copy-done.5, bf16[512,768]{1,0:T(8,128)(2,1)} %copy-done.15, bf16[1024,768]{1,0:T(8,128)(2,1)} %x_ref.5, f32[1,768]{1,0:T(1,128)} %broadcast_in_dim.14.gain_ref, f32[1024,768]{1,0:T(8,128)} %get-tuple-element.148.gh_ref, s32[1]{0:T(128)} %bitcast.17.low_ref), custom_call_target="tpu_custom_call" | custom-call | flops 1048576 | bytes 65536 | tf_op jit(solution)/shard_map/pallas_call | solution.py:609
  221.3 1.0 copy-done.4
  222.3 4.2 %shard_map.203 = bf16[8,112,768]{2,1,0:T(8,128)(2,1)} custom-call(bf16[8,96,768]{2,1,0:T(8,128)(2,1)} %copy-done.4, f32[16,768]{1,0:T(8,128)} %pad.19.small_ref, f32[1,768]{1,0:T(1,128)} %get-tuple-element.154.ggain_ref), custom_call_target="tpu_custom_call" | custom-call | flops 1048576 | bytes 65536 | tf_op jit(solution)/shard_map/pallas_call | solution.py:648
  226.5 5.6 %all-to-all-start.5 = ((bf16[8,112,768]{2,1,0:T(8,128)(2,1)}), bf16[8,112,768]{2,1,0:T(8,128)(2,1)S(1)}, u32[]{:S(2)}, u32[]{:S(2)}) async-start(bf16[8,112,768]{2,1,0:T(8,128)(2,1)} %shard_map.203), calls=%async_computation.5 | async-start | bytes 2752512 | tf_op jit(solution)/shard_map/all_to_all | solution.py:752
  232.1 0.8 collective-permute-start.23
  232.9 1.2 collective-permute-start.26
  234.1 14.2 %collective-permute-done.23.refs_2_ = bf16[384,768]{1,0:T(8,128)(2,1)S(1)} collective-permute-done((bf16[384,768]{1,0:T(8,128)(2,1)S(1)}, bf16[384,768]{1,0:T(8,128)(2,1)S(1)}, u32[]{:S(2)}, u32[]{:S(2)}) %collective-permute-start.23) | collective-permute-done | bytes 589856 | tf_op jit(solution)/shard_map/ppermute | solution.py:728
  248.3 11.5 %collective-permute-done.26 = bf16[384,768]{1,0:T(8,128)(2,1)S(1)} collective-permute-done((bf16[384,768]{1,0:T(8,128)(2,1)}, bf16[384,768]{1,0:T(8,128)(2,1)S(1)}, u32[]{:S(2)}, u32[]{:S(2)}) %collective-permute-start.26) | collective-permute-done | bytes 589856 | tf_op jit(solution)/shard_map/ppermute | solution.py:728
  259.8 3.7 %convert_add_fusion = f32[1,768,768]{2,1,0:T(8,128)} fusion(bf16[4,768,768]{2,1,0:T(8,128)(2,1)} %copy-done.3, bf16[1,384,768]{2,1,0:T(8,128)(2,1)S(1)} %bitcast.52, bf16[1,384,768]{2,1,0:T(8,128)(2,1)} %bitcast.25, bf16[4,768,768]{2,1,0:T(8,128)(2,1)} %get-tuple-element.126), kind=kLoop, calls=%fused_computation.3 | loop fusion | flops 4718592 | bytes 5898240 | tf_op jit(solution)/shard_map/add | solution.py:850
  263.5 0.8 copy-done.19
  264.6 7.3 %shard_map.201 = bf16[1024,768]{1,0:T(8,128)(2,1)} custom-call(f32[1024,768]{1,0:T(8,128)} %get-tuple-element.97.hidden_ref, f32[1024,1]{1,0:T(8,128)} %get-tuple-element.98.gate_ref, s32[1024,1]{1,0:T(8,128)} %get-tuple-element.99.flat_ref, s32[1,1536]{1,0:T(1,128)} %broadcast_in_dim.16.ids_ref, bf16[384,768]{1,0:T(8,128)(2,1)} %bitcast.42, ...), custom_call_target="tpu_custom_call" | custom-call | flops 1048576 | bytes 65536 | tf_op jit(solution)/shard_map/pallas_call | solution.py:577
  271.9 1.5 shard_map.204
  274.6 0.7 reshape.224
  (120 shorter events, 11.9 us)
Async XLA Ops:
  0.6 30.7 %collective-permute-start = (bf16[768,768]{1,0:T(8,128)(2,1)}, bf16[768,768]{1,0:T(8,128)(2,1)}, u32[]{:S(2)}, u32[]{:S(2)}) collective-permute-start(bf16[768,768]{1,0:T(8,128)(2,1)} %bitcast.49), channel_id=1, source_target_pairs={{0,2},{1,3},{2,0},{3,1},{4,6},{5,7},{6,4},{7,5},{8,10},{9,11},{10,... | collective-permute-start | bytes 3538952 | tf_op jit(solution)/shard_map/ppermute | solution.py:728
  5.8 8.9 %copy-start.10 = (bf16[192,768]{1,0:T(8,128)(2,1)S(1)}, bf16[192,768]{1,0:T(8,128)(2,1)}, u32[]{:S(2)}) copy-start(bf16[192,768]{1,0:T(8,128)(2,1)} %refs_4_) | copy-start | bytes 884740
  5.8 9.5 %copy-start.29 = (f32[768]{0:T(1024)S(1)}, f32[768]{0:T(1024)}, u32[]{:S(2)}) copy-start(f32[768]{0:T(1024)} %param.13) | copy-start | bytes 9220
  5.8 10.1 %copy-start.28 = (s32[1,1024]{1,0:T(1,128)S(1)}, s32[1,1024]{1,0:T(1,128)}, u32[]{:S(2)}) copy-start(s32[1,1024]{1,0:T(1,128)} %param.22) | copy-start | bytes 12292
  8.9 22.4 %all-to-all-start = ((bf16[8,48,768]{2,1,0:T(8,128)(2,1)}), bf16[8,48,768]{2,1,0:T(8,128)(2,1)S(1)}, u32[]{:S(2)}, u32[]{:S(2)}) async-start(bf16[8,48,768]{2,1,0:T(8,128)(2,1)} %bitcast.4), calls=%async_computation | async-start | bytes 1179648 | tf_op jit(solution)/shard_map/all_to_all | solution.py:752
  14.7 25.0 %collective-permute-start.2 = (bf16[192,768]{1,0:T(8,128)(2,1)S(1)}, bf16[192,768]{1,0:T(8,128)(2,1)}, u32[]{:S(2)}, u32[]{:S(2)}) collective-permute-start(bf16[192,768]{1,0:T(8,128)(2,1)S(1)} %copy-done.10), channel_id=1, source_target_pairs={{0,2},{1,3},{2,0},{3,1},{4,6},{5,7},{6,4},{7,5},{8,10},{9,11},{10,... | collective-permute-start | bytes 884744 | tf_op jit(solution)/shard_map/ppermute | solution.py:728
  16.9 16.3 %copy-start.26 = (s32[1024,1]{0,1:T(1,128)S(1)}, s32[1024,1]{0,1:T(1,128)}, u32[]{:S(2)}) copy-start(s32[1024,1]{0,1:T(1,128)} %param.21) | copy-start | bytes 12292
  16.9 17.5 %copy-start.27 = (bf16[768,8]{0,1:T(8,128)(2,1)S(1)}, bf16[768,8]{0,1:T(8,128)(2,1)}, u32[]{:S(2)}) copy-start(bf16[768,8]{0,1:T(8,128)(2,1)} %param.18) | copy-start | bytes 36868
  31.3 6.4 %copy-start.30 = (f32[768]{0:T(1024)S(1)}, f32[768]{0:T(1024)}, u32[]{:S(2)}) copy-start(f32[768]{0:T(1024)} %param.17) | copy-start | bytes 9220
  31.3 7.8 %copy-start.8 = (bf16[8,48,768]{2,1,0:T(8,128)(2,1)}, bf16[8,48,768]{2,1,0:T(8,128)(2,1)S(1)}, u32[]{:S(2)}) copy-start(bf16[8,48,768]{2,1,0:T(8,128)(2,1)S(1)} %all-to-all-done) | copy-start | bytes 1769476
  31.3 13.4 %collective-permute-start.1 = (bf16[192,1024]{1,0:T(8,128)(2,1)}, bf16[192,1024]{1,0:T(8,128)(2,1)}, u32[]{:S(2)}, u32[]{:S(2)}) collective-permute-start(bf16[192,1024]{1,0:T(8,128)(2,1)} %get-tuple-element.93.refs_0_.att_ref), channel_id=1, source_target_pairs={{0,2},{1,3},{2,0},{3,1},{4,6},{5,7},{6,4},{7,5},{8,10},{9,11},{10,... | collective-permute-start | bytes 1179656 | tf_op jit(solution)/shard_map/ppermute | solution.py:728
  33.5 5.6 %copy-start.2 = (s32[1024,1]{1,0:T(8,128)}, s32[1024,1]{1,0:T(8,128)S(1)}, u32[]{:S(2)}) copy-start(s32[1024,1]{1,0:T(8,128)S(1)} %copy.27.route_ref) | copy-start | bytes 12292
  34.4 10.8 %copy-start.9 = (bf16[192,1024]{1,0:T(8,128)(2,1)S(1)}, bf16[192,1024]{1,0:T(8,128)(2,1)}, u32[]{:S(2)}) copy-start(bf16[192,1024]{1,0:T(8,128)(2,1)} %get-tuple-element.93.refs_0_.att_ref) | copy-start | bytes 1179652
  34.4 11.3 %copy-start.11 = (bf16[1,768,768]{2,1,0:T(8,128)(2,1)S(1)}, bf16[1,768,768]{2,1,0:T(8,128)(2,1)}, u32[]{:S(2)}) copy-start(bf16[1,768,768]{2,1,0:T(8,128)(2,1)} %param.19) | copy-start | bytes 3538948
  44.7 2.0 collective-permute-start.5
  44.7 2.3 collective-permute-start.6
  45.2 4.4 %collective-permute-start.3 = (bf16[192,1024]{1,0:T(8,128)(2,1)S(1)}, bf16[192,1024]{1,0:T(8,128)(2,1)S(1)}, u32[]{:S(2)}, u32[]{:S(2)}) collective-permute-start(bf16[192,1024]{1,0:T(8,128)(2,1)S(1)} %copy-done.9), channel_id=1, source_target_pairs={{0,1},{1,0},{2,3},{3,2},{4,5},{5,4},{6,7},{7,6},{8,9},{9,8},{10,11... | collective-permute-start | bytes 1179656 | tf_op jit(solution)/shard_map/ppermute | solution.py:728
  45.2 4.4 %collective-permute-start.4 = (bf16[192,1024]{1,0:T(8,128)(2,1)}, bf16[192,1024]{1,0:T(8,128)(2,1)S(1)}, u32[]{:S(2)}, u32[]{:S(2)}) collective-permute-start(bf16[192,1024]{1,0:T(8,128)(2,1)} %collective-permute-done.1.refs_2_), channel_id=1, source_target_pairs={{0,1},{1,0},{2,3},{3,2},{4,5},{5,4},{6,7},{7,6},{8,9},{9,8},{10,11... | collective-permute-start | bytes 1179656 | tf_op jit(solution)/shard_map/ppermute | solution.py:728
  45.7 21.0 %collective-permute-start.8 = (bf16[768,768]{1,0:T(8,128)(2,1)S(1)}, bf16[768,768]{1,0:T(8,128)(2,1)}, u32[]{:S(2)}, u32[]{:S(2)}) collective-permute-start(bf16[768,768]{1,0:T(8,128)(2,1)S(1)} %bitcast.51), channel_id=1, source_target_pairs={{0,1},{1,0},{2,3},{3,2},{4,5},{5,4},{6,7},{7,6},{8,9},{9,8},{10,11... | collective-permute-start | bytes 3538952 | tf_op jit(solution)/shard_map/ppermute | solution.py:728
  46.7 2.9 %copy-start.22 = (bf16[192,768]{1,0:T(8,128)(2,1)}, bf16[192,768]{1,0:T(8,128)(2,1)S(1)}, u32[]{:S(2)}) copy-start(bf16[192,768]{1,0:T(8,128)(2,1)S(1)} %collective-permute-done.5.refs_5_) | copy-start | bytes 884740
  46.7 20.1 %collective-permute-start.9 = (bf16[768,768]{1,0:T(8,128)(2,1)}, bf16[768,768]{1,0:T(8,128)(2,1)}, u32[]{:S(2)}, u32[]{:S(2)}) collective-permute-start(bf16[768,768]{1,0:T(8,128)(2,1)} %collective-permute-done.refs_2_), channel_id=1, source_target_pairs={{0,1},{1,0},{2,3},{3,2},{4,5},{5,4},{6,7},{7,6},{8,9},{9,8},{10,11... | collective-permute-start | bytes 3538952 | tf_op jit(solution)/shard_map/ppermute | solution.py:728
  47.0 2.6 copy-start.23
  47.0 28.6 %collective-permute-start.7 = (bf16[768,768]{1,0:T(8,128)(2,1)}, bf16[768,768]{1,0:T(8,128)(2,1)}, u32[]{:S(2)}, u32[]{:S(2)}) collective-permute-start(bf16[768,768]{1,0:T(8,128)(2,1)} %bitcast.6.refs_4_), channel_id=1, source_target_pairs={{0,2},{1,3},{2,0},{3,1},{4,6},{5,7},{6,4},{7,5},{8,10},{9,11},{10,... | collective-permute-start | bytes 3538952 | tf_op jit(solution)/shard_map/ppermute | solution.py:728
  49.6 0.7 copy-start.20
  60.9 22.0 %all-to-all-start.1 = ((bf16[8,48,768]{2,1,0:T(8,128)(2,1)}), bf16[8,48,768]{2,1,0:T(8,128)(2,1)S(1)}, u32[]{:S(2)}, u32[]{:S(2)}) async-start(bf16[8,48,768]{2,1,0:T(8,128)(2,1)} %bitcast.55), calls=%async_computation.1 | async-start | bytes 1179648 | tf_op jit(solution)/shard_map/all_to_all | solution.py:752
  82.9 4.8 %copy-start.1 = (bf16[8,48,768]{2,1,0:T(8,128)(2,1)}, bf16[8,48,768]{2,1,0:T(8,128)(2,1)S(1)}, u32[]{:S(2)}) copy-start(bf16[8,48,768]{2,1,0:T(8,128)(2,1)S(1)} %all-to-all-done.1) | copy-start | bytes 1769476
  82.9 3.1 %collective-permute-start.10 = (bf16[768,768]{1,0:T(8,128)(2,1)}, bf16[768,768]{1,0:T(8,128)(2,1)S(1)}, u32[]{:S(2)}, u32[]{:S(2)}) collective-permute-start(bf16[768,768]{1,0:T(8,128)(2,1)} %bitcast.6.refs_4_), channel_id=1, source_target_pairs={{0,1},{1,0},{2,3},{3,2},{4,5},{5,4},{6,7},{7,6},{8,9},{9,8},{10,11... | collective-permute-start | bytes 3538952 | tf_op jit(solution)/shard_map/ppermute | solution.py:728
  82.9 4.7 %collective-permute-start.11 = (bf16[768,768]{1,0:T(8,128)(2,1)}, bf16[768,768]{1,0:T(8,128)(2,1)S(1)}, u32[]{:S(2)}, u32[]{:S(2)}) collective-permute-start(bf16[768,768]{1,0:T(8,128)(2,1)} %collective-permute-done.7.refs_6_), channel_id=1, source_target_pairs={{0,1},{1,0},{2,3},{3,2},{4,5},{5,4},{6,7},{7,6},{8,9},{9,8},{10,11... | collective-permute-start | bytes 3538952 | tf_op jit(solution)/shard_map/ppermute | solution.py:728
  85.9 1.7 copy-start.13
  87.6 1.0 copy-start.14
  103.6 19.9 %all-to-all-start.2 = ((bf16[8,48,768]{2,1,0:T(8,128)(2,1)}), bf16[8,48,768]{2,1,0:T(8,128)(2,1)S(1)}, u32[]{:S(2)}, u32[]{:S(2)}) async-start(bf16[8,48,768]{2,1,0:T(8,128)(2,1)} %bitcast.54), calls=%async_computation.2 | async-start | bytes 1179648 | tf_op jit(solution)/shard_map/all_to_all | solution.py:752
  108.0 1.2 collective-permute-start.12
  109.9 10.4 %collective-permute-start.13 = (f32[8,768]{1,0:T(8,128)S(1)}, f32[8,768]{1,0:T(8,128)S(1)}, u32[]{:S(2)}, u32[]{:S(2)}) collective-permute-start(f32[8,768]{1,0:T(8,128)S(1)} %slice_add_fusion), channel_id=1, source_target_pairs={{0,2},{1,3},{2,0},{3,1},{4,6},{5,7},{6,4},{7,5},{8,10},{9,11},{10,... | collective-permute-start | bytes 73736 | tf_op jit(solution)/shard_map/ppermute | solution.py:728
  123.5 20.7 %copy-start.7 = (bf16[8,48,768]{2,1,0:T(8,128)(2,1)}, bf16[8,48,768]{2,1,0:T(8,128)(2,1)S(1)}, u32[]{:S(2)}) copy-start(bf16[8,48,768]{2,1,0:T(8,128)(2,1)S(1)} %all-to-all-done.2) | copy-start | bytes 1769476
  123.5 8.1 %collective-permute-start.15 = (bf16[4,768,768]{2,1,0:T(8,128)(2,1)}, bf16[4,768,768]{2,1,0:T(8,128)(2,1)S(1)}, u32[]{:S(2)}, u32[]{:S(2)}) collective-permute-start(bf16[4,768,768]{2,1,0:T(8,128)(2,1)} %get-tuple-element.127), channel_id=1, source_target_pairs={{0,1},{1,0},{2,3},{3,2},{4,5},{5,4},{6,7},{7,6},{8,9},{9,8},{10,11... | collective-permute-start | bytes 14155784 | tf_op jit(solution)/shard_map/ppermute | solution.py:728
  123.5 15.7 %collective-permute-start.14 = (bf16[384,768]{1,0:T(8,128)(2,1)S(1)}, bf16[384,768]{1,0:T(8,128)(2,1)S(1)}, u32[]{:S(2)}, u32[]{:S(2)}) collective-permute-start(bf16[384,768]{1,0:T(8,128)(2,1)S(1)} %bitcast.43), channel_id=1, source_target_pairs={{0,2},{1,3},{2,0},{3,1},{4,6},{5,7},{6,4},{7,5},{8,10},{9,11},{10,... | collective-permute-start | bytes 1769480 | tf_op jit(solution)/shard_map/ppermute | solution.py:728
  131.6 3.4 %copy-start.3 = (bf16[4,768,768]{2,1,0:T(8,128)(2,1)}, bf16[4,768,768]{2,1,0:T(8,128)(2,1)S(1)}, u32[]{:S(2)}) copy-start(bf16[4,768,768]{2,1,0:T(8,128)(2,1)S(1)} %collective-permute-done.15) | copy-start | bytes 14155780
  139.3 0.8 copy-start.16
  139.3 42.0 %collective-permute-start.18 = (bf16[768,768]{1,0:T(8,128)(2,1)S(1)}, bf16[768,768]{1,0:T(8,128)(2,1)S(1)}, u32[]{:S(2)}, u32[]{:S(2)}) collective-permute-start(bf16[768,768]{1,0:T(8,128)(2,1)S(1)} %fusion.6), channel_id=1, source_target_pairs={{0,2},{1,3},{2,0},{3,1},{4,6},{5,7},{6,4},{7,5},{8,10},{9,11},{10,... | collective-permute-start | bytes 3538952 | tf_op jit(solution)/shard_map/ppermute | solution.py:728
  140.1 41.2 %all-to-all-start.3 = ((bf16[8,48,768]{2,1,0:T(8,128)(2,1)}), bf16[8,48,768]{2,1,0:T(8,128)(2,1)S(1)}, u32[]{:S(2)}, u32[]{:S(2)}) async-start(bf16[8,48,768]{2,1,0:T(8,128)(2,1)} %bitcast.53), calls=%async_computation.3 | async-start | bytes 1179648 | tf_op jit(solution)/shard_map/all_to_all | solution.py:752
  144.2 2.2 collective-permute-start.16
  144.3 3.2 %collective-permute-start.17 = (bf16[384,768]{1,0:T(8,128)(2,1)}, bf16[384,768]{1,0:T(8,128)(2,1)}, u32[]{:S(2)}, u32[]{:S(2)}) collective-permute-start(bf16[384,768]{1,0:T(8,128)(2,1)} %copy-done.16), channel_id=1, source_target_pairs={{0,1},{1,0},{2,3},{3,2},{4,5},{5,4},{6,7},{7,6},{8,9},{9,8},{10,11... | collective-permute-start | bytes 1769480 | tf_op jit(solution)/shard_map/ppermute | solution.py:728
  144.8 36.5 %collective-permute-start.19 = (bf16[384,768]{1,0:T(8,128)(2,1)}, bf16[384,768]{1,0:T(8,128)(2,1)}, u32[]{:S(2)}, u32[]{:S(2)}) collective-permute-start(bf16[384,768]{1,0:T(8,128)(2,1)} %get-tuple-element.138), channel_id=1, source_target_pairs={{0,2},{1,3},{2,0},{3,1},{4,6},{5,7},{6,4},{7,5},{8,10},{9,11},{10,... | collective-permute-start | bytes 1769480 | tf_op jit(solution)/shard_map/ppermute | solution.py:728
  181.3 52.9 %copy-start.6 = (bf16[8,48,768]{2,1,0:T(8,128)(2,1)}, bf16[8,48,768]{2,1,0:T(8,128)(2,1)S(1)}, u32[]{:S(2)}) copy-start(bf16[8,48,768]{2,1,0:T(8,128)(2,1)S(1)} %all-to-all-done.3) | copy-start | bytes 1769476
  181.3 1.1 copy-start.12
  182.4 2.5 collective-permute-start.20
  186.4 34.8 %all-to-all-start.4 = ((bf16[8,96,768]{2,1,0:T(8,128)(2,1)}), bf16[8,96,768]{2,1,0:T(8,128)(2,1)S(1)}, u32[]{:S(2)}, u32[]{:S(2)}) async-start(bf16[8,96,768]{2,1,0:T(8,128)(2,1)} %bitcast.48), calls=%async_computation.4 | async-start | bytes 2359296 | tf_op jit(solution)/shard_map/all_to_all | solution.py:752
  192.4 19.4 %copy-start = (f32[512,768]{1,0:T(8,128)S(1)}, f32[512,768]{1,0:T(8,128)}, u32[]{:S(2)}) copy-start(f32[512,768]{1,0:T(8,128)} %get-tuple-element.140) | copy-start | bytes 4718596
  192.4 19.4 %collective-permute-start.21 = (bf16[512,768]{1,0:T(8,128)(2,1)S(1)}, bf16[512,768]{1,0:T(8,128)(2,1)S(1)}, u32[]{:S(2)}, u32[]{:S(2)}) collective-permute-start(bf16[512,768]{1,0:T(8,128)(2,1)S(1)} %fusion.9), channel_id=1, source_target_pairs={{0,2},{1,3},{2,0},{3,1},{4,6},{5,7},{6,4},{7,5},{8,10},{9,11},{10,... | collective-permute-start | bytes 2359304 | tf_op jit(solution)/shard_map/ppermute | solution.py:728
  197.0 15.2 %copy-start.25 = (f32[3,32,128]{2,1,0:T(8,128)S(1)}, f32[3,32,128]{2,1,0:T(8,128)}, u32[]{:S(2)}) copy-start(f32[3,32,128]{2,1,0:T(8,128)} %get-tuple-element.152) | copy-start | bytes 147460
  197.0 15.4 %copy-start.24 = (f32[8,768]{1,0:T(8,128)S(1)}, f32[8,768]{1,0:T(8,128)}, u32[]{:S(2)}) copy-start(f32[8,768]{1,0:T(8,128)} %add.246) | copy-start | bytes 73732
  197.0 15.4 %copy-start.31 = (f32[1,768]{1,0:T(1,128)S(1)}, f32[1,768]{1,0:T(1,128)}, u32[]{:S(2)}) copy-start(f32[1,768]{1,0:T(1,128)} %get-tuple-element.151) | copy-start | bytes 9220
  212.1 2.4 copy-start.5
  212.1 2.4 collective-permute-start.25
  214.4 0.9 copy-start.15
  221.3 1.0 copy-start.4
  226.5 45.4 %all-to-all-start.5 = ((bf16[8,112,768]{2,1,0:T(8,128)(2,1)}), bf16[8,112,768]{2,1,0:T(8,128)(2,1)S(1)}, u32[]{:S(2)}, u32[]{:S(2)}) async-start(bf16[8,112,768]{2,1,0:T(8,128)(2,1)} %shard_map.203), calls=%async_computation.5 | async-start | bytes 2752512 | tf_op jit(solution)/shard_map/all_to_all | solution.py:752
  232.1 16.2 %collective-permute-start.23 = (bf16[384,768]{1,0:T(8,128)(2,1)S(1)}, bf16[384,768]{1,0:T(8,128)(2,1)S(1)}, u32[]{:S(2)}, u32[]{:S(2)}) collective-permute-start(bf16[384,768]{1,0:T(8,128)(2,1)S(1)} %bitcast.40), channel_id=1, source_target_pairs={{0,2},{1,3},{2,0},{3,1},{4,6},{5,7},{6,4},{7,5},{8,10},{9,11},{10,... | collective-permute-start | bytes 1769480 | tf_op jit(solution)/shard_map/ppermute | solution.py:728
  232.9 26.9 %collective-permute-start.26 = (bf16[384,768]{1,0:T(8,128)(2,1)}, bf16[384,768]{1,0:T(8,128)(2,1)S(1)}, u32[]{:S(2)}, u32[]{:S(2)}) collective-permute-start(bf16[384,768]{1,0:T(8,128)(2,1)} %get-tuple-element.162), channel_id=1, source_target_pairs={{0,2},{1,3},{2,0},{3,1},{4,6},{5,7},{6,4},{7,5},{8,10},{9,11},{10,... | collective-permute-start | bytes 1769480 | tf_op jit(solution)/shard_map/ppermute | solution.py:728
  234.1 29.4 %collective-permute-start.22 = (bf16[384,768]{1,0:T(8,128)(2,1)S(1)}, bf16[384,768]{1,0:T(8,128)(2,1)S(1)}, u32[]{:S(2)}, u32[]{:S(2)}) collective-permute-start(bf16[384,768]{1,0:T(8,128)(2,1)S(1)} %bitcast.41), channel_id=1, source_target_pairs={{0,1},{1,0},{2,3},{3,2},{4,5},{5,4},{6,7},{7,6},{8,9},{9,8},{10,11... | collective-permute-start | bytes 1769480 | tf_op jit(solution)/shard_map/ppermute | solution.py:728
  248.3 15.2 %copy-start.17 = (bf16[384,768]{1,0:T(8,128)(2,1)}, bf16[384,768]{1,0:T(8,128)(2,1)S(1)}, u32[]{:S(2)}) copy-start(bf16[384,768]{1,0:T(8,128)(2,1)S(1)} %collective-permute-done.23.refs_2_) | copy-start | bytes 1769476
  248.3 15.2 %collective-permute-start.24 = (bf16[384,768]{1,0:T(8,128)(2,1)S(1)}, bf16[384,768]{1,0:T(8,128)(2,1)S(1)}, u32[]{:S(2)}, u32[]{:S(2)}) collective-permute-start(bf16[384,768]{1,0:T(8,128)(2,1)S(1)} %collective-permute-done.23.refs_2_), channel_id=1, source_target_pairs={{0,1},{1,0},{2,3},{3,2},{4,5},{5,4},{6,7},{7,6},{8,9},{9,8},{10,11... | collective-permute-start | bytes 1769480 | tf_op jit(solution)/shard_map/ppermute | solution.py:728
  263.5 1.1 copy-start.18
  263.5 0.8 copy-start.19
  (1 other events, 0.7 us)

commit v3 on v2

--- a/solution.py
+++ b/solution.py
@@ -13,6 +13,7 @@
 BF16 = jnp.bfloat16
 MASKED = -1e30
 QB = 256
+RB = 512
 PAD = 256
 FAR = FAR_LIMITS[-1]
 SMALL = pl.CostEstimate(flops=1 << 20, bytes_accessed=1 << 16, transcendentals=0)
@@ -84,11 +85,17 @@
     return inside
 
 
+def shares(seg_ref, b, j):
+    return (seg_ref[0, j * QB] <= seg_ref[0, b * QB + QB - 1]) & (
+        seg_ref[0, b * QB] <= seg_ref[0, j * QB + QB - 1]
+    )
+
+
 def attend_kernel(
     length, heads, dim,
-    x_ref, gain_ref, w_ref, doc_ref, bias_ref,
+    x_ref, gain_ref, w_ref, doc_ref, bias_ref, seg_ref,
     att_ref, lse_ref, proj_ref, kt_ref, normed_ref,
-    kh_ref, strip_ref, vt_ref, pad_ref,
+    kh_ref, strip_ref, vt_ref, pad_ref, score_ref, top_ref, sum_ref, out_ref,
 ):
     inner = heads * dim
     build_strip(strip_ref, bias_ref, length, heads)
@@ -122,16 +129,43 @@
 
     def block(b, carry):
         at = pl.multiple_of(b * QB, QB)
-        from_row = pl.multiple_of(length - QB - b * QB, QB)
         queries = proj_ref[pl.ds(at, QB), 0:PAD]
+        top_ref[...] = jnp.full_like(top_ref, -3e38)
+        sum_ref[...] = jnp.zeros_like(sum_ref)
+        out_ref[...] = jnp.zeros_like(out_ref)
+
+        def score(j, carry):
+            @pl.when(shares(seg_ref, b, j))
+            def _():
+                rows = pl.ds(pl.multiple_of(j * QB, QB), QB)
+                bias = pl.ds(pl.multiple_of(length - QB + (j - b) * QB, QB), QB)
+                for h in range(heads):
+                    scores = nt_dot(kh_ref[h, rows, :], queries) + strip_ref[h, bias, :]
+                    score_ref[h, rows, :] = scores
+                    top = jnp.max(scores, 0, keepdims=True)
+                    top_ref[h : h + 1, :] = jnp.maximum(top_ref[h : h + 1, :], top)
+
+            return carry
+
+        def spread(j, carry):
+            @pl.when(shares(seg_ref, b, j))
+            def _():
+                rows = pl.ds(pl.multiple_of(j * QB, QB), QB)
+                for h in range(heads):
+                    probs = jnp.exp(score_ref[h, rows, :] - top_ref[h : h + 1, :])
+                    sum_ref[h : h + 1, :] += jnp.sum(probs, 0, keepdims=True)
+                    mine = slice(h * dim, (h + 1) * dim)
+                    out_ref[mine, :] += nn_dot(vt_ref[mine, rows], probs.astype(BF16))
+
+            return carry
+
+        lax.fori_loop(0, length // QB, score, 0)
+        lax.fori_loop(0, length // QB, spread, 0)
         for h in range(heads):
-            scores = nt_dot(kh_ref[h], queries) + strip_ref[h, pl.ds(from_row, length), :]
-            top = jnp.max(scores, 0, keepdims=True)
-            probs = jnp.exp(scores - top)
-            total = jnp.sum(probs, 0, keepdims=True)
-            out = nn_dot(vt_ref[h * dim : (h + 1) * dim, :], probs.astype(BF16))
-            att_ref[h * dim : (h + 1) * dim, pl.ds(at, QB)] = (out / total).astype(BF16)
-            lse_ref[h : h + 1, pl.ds(at, QB)] = top + jnp.log(total)
+            mine = slice(h * dim, (h + 1) * dim)
+            total = sum_ref[h : h + 1, :]
+            att_ref[mine, pl.ds(at, QB)] = (out_ref[mine, :] / total).astype(BF16)
+            lse_ref[h : h + 1, pl.ds(at, QB)] = top_ref[h : h + 1, :] + jnp.log(total)
         return carry
 
     lax.fori_loop(0, length // QB, block, 0)
@@ -139,10 +173,10 @@
 
 def attend_back_kernel(
     length, heads, dim,
-    proj_ref, kt_ref, lse_ref, da_ref, normed_ref, w_ref, gproj_ref, bias_ref, low_ref,
+    proj_ref, kt_ref, lse_ref, da_ref, normed_ref, w_ref, gproj_ref, bias_ref, low_ref, seg_ref,
     grad_ref, kept_ref, sent_ref, drel_ref,
     kh_ref, vh_ref, strip_ref, dstrip_ref, pcat_ref, dcat_ref, dacat_ref, qcat_ref, dk_ref, dv_ref, dqt_ref,
-    dq_ref, pad_ref,
+    dq_ref, pad_ref, probs_ref, weighted_ref, delta_ref,
 ):
     inner = heads * dim
     scale = dim ** (-0.5)
@@ -161,27 +195,54 @@
 
     def block(b, carry):
         at = pl.multiple_of(b * QB, QB)
-        from_row = pl.multiple_of(length - QB - b * QB, QB)
         queries = proj_ref[pl.ds(at, QB), 0:PAD]
         grads = da_ref[pl.ds(at, QB), :]
+        delta_ref[...] = jnp.zeros_like(delta_ref)
+        dqt_ref[...] = jnp.zeros_like(dqt_ref)
         for h in range(heads):
             mine = head_lanes(QB, h, dim, False, heads)
             cols = slice(h * QB, (h + 1) * QB)
             qcat_ref[cols, :] = jnp.where(mine, queries, jnp.zeros_like(queries))
             dacat_ref[cols, :] = jnp.where(mine, grads, jnp.zeros_like(grads))
-            scores = nt_dot(kh_ref[h], queries) + strip_ref[h, pl.ds(from_row, length), :]
-            probs = jnp.exp(scores - lse_ref[h : h + 1, pl.ds(at, QB)])
-            weighted = probs * nt_dot(vh_ref[h], grads)
-            delta = jnp.sum(weighted, 0, keepdims=True)
-            dscore = weighted - probs * delta
-            dstrip_ref[h, pl.ds(from_row, length), :] += dscore
-            dlow = dscore.astype(BF16)
-            pcat_ref[:, cols] = probs.astype(BF16)
-            dcat_ref[:, cols] = dlow
-            dqt_ref[h * dim : (h + 1) * dim, :] = nn_dot(kt_ref[h * dim : (h + 1) * dim, :], dlow) * scale
-        dk_ref[...] += nn_dot(dcat_ref[...], qcat_ref[...])
-        dv_ref[...] += nn_dot(pcat_ref[...], dacat_ref[...])
-        dq_ref[pl.ds(at, QB), :] = dqt_ref[...].T
+
+        def weigh(j, carry):
+            @pl.when(shares(seg_ref, b, j))
+            def _():
+                rows = pl.ds(pl.multiple_of(j * QB, QB), QB)
+                bias = pl.ds(pl.multiple_of(length - QB + (j - b) * QB, QB), QB)
+                for h in range(heads):
+                    scores = nt_dot(kh_ref[h, rows, :], queries) + strip_ref[h, bias, :]
+                    probs = jnp.exp(scores - lse_ref[h : h + 1, pl.ds(at, QB)])
+                    weighted = probs * nt_dot(vh_ref[h, rows, :], grads)
+                    delta_ref[h : h + 1, :] += jnp.sum(weighted, 0, keepdims=True)
+                    probs_ref[h, rows, :] = probs
+                    weighted_ref[h, rows, :] = weighted
+
+            return carry
+
+        def gather(j, carry):
+            @pl.when(shares(seg_ref, b, j))
+            def _():
+                rows = pl.ds(pl.multiple_of(j * QB, QB), QB)
+                bias = pl.ds(pl.multiple_of(length - QB + (j - b) * QB, QB), QB)
+                for h in range(heads):
+                    cols = slice(h * QB, (h + 1) * QB)
+                    mine = slice(h * dim, (h + 1) * dim)
+                    probs = probs_ref[h, rows, :]
+                    dscore = weighted_ref[h, rows, :] - probs * delta_ref[h : h + 1, :]
+                    dstrip_ref[h, bias, :] += dscore
+                    dlow = dscore.astype(BF16)
+                    pcat_ref[:, cols] = probs.astype(BF16)
+                    dcat_ref[:, cols] = dlow
+                    dqt_ref[mine, :] += nn_dot(kt_ref[mine, rows], dlow)
+                dk_ref[rows, :] += nn_dot(dcat_ref[...], qcat_ref[...])
+                dv_ref[rows, :] += nn_dot(pcat_ref[...], dacat_ref[...])
+
+            return carry
+
+        lax.fori_loop(0, length // QB, weigh, 0)
+        lax.fori_loop(0, length // QB, gather, 0)
+        dq_ref[pl.ds(at, QB), :] = dqt_ref[...].T * scale
         return carry
 
     lax.fori_loop(0, length // QB, block, 0)
@@ -252,7 +313,7 @@
     length, width = tokens.shape
     heads = rel_bias.shape[0]
     inner = w_qkv.shape[1]
-    operands = (tokens, gain[None, :], w_qkv, segments[:, None])
+    operands = (tokens, gain[None, :], w_qkv, segments.reshape(-1, 1))
     results = (
         jax.ShapeDtypeStruct((inner, length), BF16),
         jax.ShapeDtypeStruct((8, length), F32),
@@ -264,20 +325,24 @@
         functools.partial(attend_kernel, length, heads, inner // heads),
         grid=(1,),
         out_shape=results,
-        in_specs=whole_like(*operands) + [pl.BlockSpec(memory_space=pltpu.SMEM)],
+        in_specs=whole_like(*operands) + [pl.BlockSpec(memory_space=pltpu.SMEM)] * 2,
         out_specs=tuple(whole_like(*results)),
         scratch_shapes=[
             pltpu.VMEM((heads, length, PAD), BF16),
             pltpu.VMEM((heads, strip_shape(length), QB), F32),
             pltpu.VMEM((inner, length), BF16),
             pltpu.VMEM((3 * PAD, width), BF16),
+            pltpu.VMEM((heads, length, QB), F32),
+            pltpu.VMEM((8, QB), F32),
+            pltpu.VMEM((8, QB), F32),
+            pltpu.VMEM((inner, QB), F32),
         ],
         compiler_params=pltpu.CompilerParams(vmem_limit_bytes=60 << 20),
         cost_estimate=SMALL,
-    )(*operands, rel_bias)
-
-
-def attend_back(proj, kt, lse, da, normed, w_qkv, grad_proj, rel_bias, low_bit):
+    )(*operands, rel_bias, segments)
+
+
+def attend_back(proj, kt, lse, da, normed, w_qkv, grad_proj, rel_bias, low_bit, segments):
     length, width = normed.shape
     heads, buckets = rel_bias.shape
     inner = w_qkv.shape[1]
@@ -292,15 +357,15 @@
         functools.partial(attend_back_kernel, length, heads, inner // heads),
         grid=(1,),
         out_shape=results,
-        in_specs=whole_like(*operands) + [pl.BlockSpec(memory_space=pltpu.SMEM)] * 2,
+        in_specs=whole_like(*operands) + [pl.BlockSpec(memory_space=pltpu.SMEM)] * 3,
         out_specs=tuple(whole_like(*results)),
         scratch_shapes=[
             pltpu.VMEM((heads, length, PAD), BF16),
             pltpu.VMEM((heads, length, PAD), BF16),
             pltpu.VMEM((heads, strip_shape(length), QB), F32),
             pltpu.VMEM((heads, strip_shape(length), QB), F32),
-            pltpu.VMEM((length, heads * QB), BF16),
-            pltpu.VMEM((length, heads * QB), BF16),
+            pltpu.VMEM((QB, heads * QB), BF16),
+            pltpu.VMEM((QB, heads * QB), BF16),
             pltpu.VMEM((heads * QB, PAD), BF16),
             pltpu.VMEM((heads * QB, PAD), BF16),
             pltpu.VMEM((length, PAD), F32),
@@ -308,10 +373,13 @@
             pltpu.VMEM((PAD, QB), F32),
             pltpu.VMEM((length, PAD), F32),
             pltpu.VMEM((3, PAD, width), BF16),
+            pltpu.VMEM((heads, length, QB), F32),
+            pltpu.VMEM((heads, length, QB), F32),
+            pltpu.VMEM((8, QB), F32),
         ],
         compiler_params=pltpu.CompilerParams(vmem_limit_bytes=60 << 20),
         cost_estimate=SMALL,
-    )(*operands, rel_bias, low_bit)
+    )(*operands, rel_bias, low_bit, segments)
 
 
 def gelu_pair(v):
@@ -397,7 +465,7 @@
         )
     hidden_ref[...] = hidden
     normed = norm_rows(hidden, gain_ref[...]).astype(BF16)
-    lane = lax.broadcasted_iota(jnp.int32, (QB, 128), 1)
+    lane = lax.broadcasted_iota(jnp.int32, (RB, 128), 1)
     logits = jnp.where(lane < experts, nn_dot(normed, router_ref[...]), MASKED)
     raised = jnp.exp(logits - jnp.max(logits, -1, keepdims=True))
     chosen = jnp.sum(jnp.where(lane == route_ref[...], raised, 0.0), -1, keepdims=True)
@@ -422,23 +490,23 @@
     count = ids.shape[0]
     return pl.pallas_call(
         functools.partial(enter_kernel, members, experts),
-        grid=(length // QB,),
+        grid=(length // RB,),
         out_shape=(
             jax.ShapeDtypeStruct((length, width), F32),
             jax.ShapeDtypeStruct((length, 1), F32),
             jax.ShapeDtypeStruct((count, width), BF16),
         ),
         in_specs=[
-            rows_of(QB, width),
+            rows_of(RB, width),
             whole_of(1, width),
             whole_of(width, 128),
-            rows_of(QB, 1),
-            pl.BlockSpec((1, QB), lambda i: (0, i)),
+            rows_of(RB, 1),
+            pl.BlockSpec((1, RB), lambda i: (0, i)),
             whole_of(count, 1),
         ]
-        + [pl.BlockSpec((inner, QB), lambda i: (0, i))] * members
+        + [pl.BlockSpec((inner, RB), lambda i: (0, i))] * members
         + [whole_of(inner, width)] * members,
-        out_specs=(rows_of(QB, width), rows_of(QB, 1), whole_of(count, width)),
+        out_specs=(rows_of(RB, width), rows_of(RB, 1), whole_of(count, width)),
         scratch_shapes=[pltpu.VMEM((count, width), F32)],
         compiler_params=pltpu.CompilerParams(vmem_limit_bytes=60 << 20),
         cost_estimate=SMALL,
@@ -529,7 +597,7 @@
     share = blocks[0].shape[0]
     return pl.pallas_call(
         functools.partial(leave_kernel, members),
-        grid=(length // QB,),
+        grid=(length // RB,),
         out_shape=(
             jax.ShapeDtypeStruct((length, width), F32),
             jax.ShapeDtypeStruct((length, PAD), BF16),
@@ -537,18 +605,18 @@
             jax.ShapeDtypeStruct((inner, width), BF16),
         ),
         in_specs=[
-            rows_of(QB, width),
-            rows_of(QB, width),
+            rows_of(RB, width),
+            rows_of(RB, width),
             whole_of(1, width),
-            rows_of(QB, 1),
+            rows_of(RB, 1),
             whole_of(1, members * share),
             whole_of(PAD, width),
-            pl.BlockSpec((inner, QB), lambda i: (0, i)),
+            pl.BlockSpec((inner, RB), lambda i: (0, i)),
         ]
         + [whole_of(share, width)] * members,
         out_specs=(
-            rows_of(QB, width),
-            rows_of(QB, PAD),
+            rows_of(RB, width),
+            rows_of(RB, PAD),
             whole_of(1, width),
             whole_of(inner, width),
         ),
@@ -576,11 +644,11 @@
     share = blocks[0].shape[0]
     return pl.pallas_call(
         functools.partial(output_kernel, members),
-        grid=(length // QB,),
+        grid=(length // RB,),
         out_shape=jax.ShapeDtypeStruct((length, width), BF16),
-        in_specs=[rows_of(QB, width), rows_of(QB, 1), rows_of(QB, 1), whole_of(1, members * share)]
+        in_specs=[rows_of(RB, width), rows_of(RB, 1), rows_of(RB, 1), whole_of(1, members * share)]
         + [whole_of(share, width)] * members,
-        out_specs=rows_of(QB, width),
+        out_specs=rows_of(RB, width),
         compiler_params=pltpu.CompilerParams(vmem_limit_bytes=60 << 20),
         cost_estimate=SMALL,
     )(hidden1, gate, flat_id, ids, *blocks)
@@ -721,7 +789,6 @@
     member = lax.axis_index("tensor")
     group = lax.axis_index("expert")
     share = capacity // members
-    segments = segment_ids[0]
     route = routes[:, 0]
 
     def swap(value, bit):
@@ -777,7 +844,7 @@
     w_proj_far = gather_far(w_proj)
     w_in_far = gather_far(w_in[0])
     w_qkv_t = jnp.swapaxes(w_qkv, 1, 2)
-    attended_t, lse, proj, keys_t, normed1 = attend(tokens, gain_attn, w_qkv_t, segments, rel_bias)
+    attended_t, lse, proj, keys_t, normed1 = attend(tokens, gain_attn, w_qkv_t, segment_ids, rel_bias)
     attended_t, w_in_far, cot_share = tie((attended_t, w_in_far, cot_share))
 
     attended_far = gather_far(attended_t)
@@ -834,7 +901,7 @@
 
     low_bit = (member & 1)[None]
     grads, kept, sent, rel_parts = attend_back(
-        proj, keys_t, lse, attended_grad, normed1, w_qkv_t, grad_proj, rel_bias, low_bit
+        proj, keys_t, lse, attended_grad, normed1, w_qkv_t, grad_proj, rel_bias, low_bit, segment_ids
     )
     grads, kept, sent, reply_back, out_came, fore_came, rest_sent = tie(
         (grads, kept, sent, reply_back, out_came, fore_came, rest_sent)
@@ -843,14 +910,15 @@
     kept_low, grads = tie((kept.astype(BF16), grads))
     far = swap(kept_low, 2)
     came = exchange(grads.reshape(groups, -1, width))
+    grad_w_out = pair(0, slice(0, width)) + out_came.astype(F32)
+    far, grad_w_out, reply_back, rest_sent = tie((far, grad_w_out, reply_back, rest_sent))
     rest_came = swap(rest_sent, 2)
-    grad_w_out = pair(0, slice(0, width)) + out_came.astype(F32)
-    far, grad_w_out, reply_back = tie((far, grad_w_out, reply_back))
-    reply_far = gather_far(reply_back)
-    grad_w_in = pair(2, slice(0, width)) + jnp.concatenate([fore_came, rest_came], 0).astype(F32)
     kept = (kept + far.astype(F32)).astype(BF16)
     other = swap(kept, 1)
     grad_input, gain_part = input_grads(kept, other, tokens, gain_attn, grad_hidden1, low_bit)
+    gain_part, rest_came, reply_back = tie((gain_part, rest_came, reply_back))
+    reply_far = gather_far(reply_back)
+    grad_w_in = pair(2, slice(0, width)) + jnp.concatenate([fore_came, rest_came], 0).astype(F32)
 
     rel_row = jnp.sum(rel_parts, -1).reshape(1, -1)
     rel_row = jnp.pad(rel_row, ((0, 0), (0, width - rel_row.shape[1])))

time: 276 us -> 273 us (0.989)
  Pallas kernels: 102 us -> 92.8 us
  waiting for transfers between devices: 86.4 us -> 93.9 us
    all_to_all x6, waiting for transfers between devices: 9.94 us -> 16.2 us  [exchange(): lax.all_to_all(value, 'expert', split_axis=0, concat_axis=0, tiled=True)]
    pallas_call x1, Pallas kernels: 22.2 us -> 16.9 us  [attend_back(): pl.pallas_call(functools.partial(attend_back_kernel, length, heads, inner...]
  transfers between devices with their start and end apart: 33 -> 33, of which waited for: 18 -> 22; matrix products, arithmetic and copies ran while one was open for 11% -> 11% of each run, Pallas kernels for 29% -> 27%
where the time goes in v3:
time: 273 us; the launch traced here: 271 us
  waiting for transfers between devices  93.9 us (34%)
  Pallas kernels  92.8 us (34%)
  starting transfers between devices  44.5 us (16%)
  other arithmetic  19.6 us (7%)
  local copies, waits for them, and re-layouts  15.3 us (6%)
  matrix products  4.33 us (2%)
    ppermute x27, waiting for transfers between devices, swap(): return lax.ppermute(value, 'tensor', [(i, i ^ bit) for i in range(members)])  77.7 us
    all_to_all x6, starting transfers between devices, exchange(): lax.all_to_all(value, 'expert', split_axis=0, concat_axis=0, tiled=True)  29.8 us
    pallas_call x1, Pallas kernels, attend_back(): pl.pallas_call(functools.partial(attend_back_kernel, length, heads, inner...  16.9 us
    all_to_all x6, waiting for transfers between devices, exchange(): lax.all_to_all(value, 'expert', split_axis=0, concat_axis=0, tiled=True)  16.2 us
    pallas_call x1, Pallas kernels, expert_step(): pl.pallas_call(functools.partial(expert_kernel, members, experts), grid=(...  14.9 us
    ppermute x27, starting transfers between devices, swap(): return lax.ppermute(value, 'tensor', [(i, i ^ bit) for i in range(members)])  14.7 us
    pallas_call x1, Pallas kernels, attend(): pl.pallas_call(functools.partial(attend_kernel, length, heads, inner // h...  12.2 us
    pallas_call x1, Pallas kernels, leave_experts(): pl.pallas_call(functools.partial(leave_kernel, members), grid=(length //...  11.2 us
  transfers between devices with their start and end apart: 33, of which 22 were waited for; matrix products, arithmetic and copies ran while one was open for 11% of the time, Pallas kernels for 27%

profile of v3, /device:TPU:0, one launch (start us, length us, event | category | flops | bytes accessed | tf_op | source)
XLA Modules:
  0.0 271.3 jit_solution(10541303624647541429)
XLA Ops:
  0.6 3.0 %collective-permute-start = (bf16[768,768]{1,0:T(8,128)(2,1)}, bf16[768,768]{1,0:T(8,128)(2,1)}, u32[]{:S(2)}, u32[]{:S(2)}) collective-permute-start(bf16[768,768]{1,0:T(8,128)(2,1)} %bitcast.49), channel_id=1, source_target_pairs={{0,2},{1,3},{2,0},{3,1},{4,6},{5,7},{6,4},{7,5},{8,10},{9,11},{10,... | collective-permute-start | bytes 3538952 | tf_op jit(solution)/shard_map/ppermute | solution.py:795
  3.7 1.2 fusion.8
  4.9 0.7 multiply_add_fusion.1
  5.8 3.1 %fusion.3 = bf16[384,768]{1,0:T(8,128)(2,1)} fusion(bf16[1024,768]{1,0:T(8,128)(2,1)} %cot_ref.1, s32[1024]{0:T(1024)S(1)} %multiply_add_fusion.1, s32[384]{0:T(512)S(1)} %add.225), kind=kOutput, calls=%fused_computation.9 | convolution fusion | flops 604667904 | bytes 2168320 | tf_op jit(solution)/shard_map/dot_general | solution.py:39
  8.9 5.8 %all-to-all-start = ((bf16[8,48,768]{2,1,0:T(8,128)(2,1)}), bf16[8,48,768]{2,1,0:T(8,128)(2,1)S(1)}, u32[]{:S(2)}, u32[]{:S(2)}) async-start(bf16[8,48,768]{2,1,0:T(8,128)(2,1)} %bitcast.4), calls=%async_computation | async-start | bytes 1179648 | tf_op jit(solution)/shard_map/all_to_all | solution.py:819
  15.9 1.0 copy.25.doc_ref
  16.9 12.2 %shard_map.195 = (bf16[192,1024]{1,0:T(8,128)(2,1)}, f32[8,1024]{1,0:T(8,128)}, bf16[1024,768]{1,0:T(8,128)(2,1)}, bf16[192,1024]{1,0:T(8,128)(2,1)}, bf16[1024,768]{1,0:T(8,128)(2,1)}) custom-call(bf16[1024,768]{1,0:T(8,128)(2,1)} %x_ref.5, f32[1,768]{1,0:T(1,128)} %broadcast_in_dim.14.gain_ref, bf16[3,192,768]{2,1,0:T(8,128)(2,1)} %bitcast.38, ...), custom_call_target="tpu_custom_call" | custom-call | flops 1048576 | bytes 65536 | tf_op jit(solution)/shard_map/pallas_call | solution.py:324
  29.2 1.2 all-to-all-done
  30.8 2.1 collective-permute-start.1
  34.3 0.8 pad.17.wproj_ref
  35.1 0.7 pad.16.router_ref
  36.6 0.9 multiply_add_fusion
  38.1 6.6 %collective-permute-done.1.refs_2_ = bf16[192,1024]{1,0:T(8,128)(2,1)} collective-permute-done((bf16[192,1024]{1,0:T(8,128)(2,1)}, bf16[192,1024]{1,0:T(8,128)(2,1)}, u32[]{:S(2)}, u32[]{:S(2)}) %collective-permute-start.1) | collective-permute-done | bytes 393248 | tf_op jit(solution)/shard_map/ppermute | solution.py:795
  45.7 0.9 collective-permute-done.5.refs_5_
  47.0 1.8 collective-permute-start.7
  48.7 0.8 copy.30.ids_ref
  49.6 0.7 copy-done.20
  50.3 0.7 copy-done.21
  51.1 8.9 %shard_map.196 = (f32[1024,768]{1,0:T(8,128)}, f32[1024,1]{1,0:T(8,128)}, bf16[384,768]{1,0:T(8,128)(2,1)}) custom-call(bf16[1024,768]{1,0:T(8,128)(2,1)} %x_ref.5, f32[1,768]{1,0:T(1,128)} %broadcast_in_dim.15.gain_ref, bf16[768,128]{1,0:T(8,128)(2,1)} %pad.16.router_ref, s32[1024,1]{1,0:T(8,128)} %copy-done.2, s32[1,1024]{1,0:T(1,128)} %add.227.flat_ref, ...), custom_call_target="tpu_custom_call" | custom-call | flops 1048576 | bytes 65536 | tf_op jit(solution)/shard_map/pallas_call | solution.py:491
  60.0 5.8 %all-to-all-start.1 = ((bf16[8,48,768]{2,1,0:T(8,128)(2,1)}), bf16[8,48,768]{2,1,0:T(8,128)(2,1)S(1)}, u32[]{:S(2)}, u32[]{:S(2)}) async-start(bf16[8,48,768]{2,1,0:T(8,128)(2,1)} %bitcast.54), calls=%async_computation.1 | async-start | bytes 1179648 | tf_op jit(solution)/shard_map/all_to_all | solution.py:819
  65.9 9.7 %collective-permute-done.7.refs_6_ = bf16[768,768]{1,0:T(8,128)(2,1)} collective-permute-done((bf16[768,768]{1,0:T(8,128)(2,1)}, bf16[768,768]{1,0:T(8,128)(2,1)}, u32[]{:S(2)}, u32[]{:S(2)}) %collective-permute-start.7) | collective-permute-done | bytes 1179680 | tf_op jit(solution)/shard_map/ppermute | solution.py:795
  75.6 6.4 %all-to-all-done.1 = bf16[8,48,768]{2,1,0:T(8,128)(2,1)S(1)} async-done(((bf16[8,48,768]{2,1,0:T(8,128)(2,1)}), bf16[8,48,768]{2,1,0:T(8,128)(2,1)S(1)}, u32[]{:S(2)}, u32[]{:S(2)}) %all-to-all-start.1) | async-done | bytes 589856 | tf_op jit(solution)/shard_map/all_to_all | solution.py:819
  82.5 2.5 collective-permute-done.10.refs_5_
  85.0 1.7 collective-permute-done.11.refs_7_
  86.7 1.0 copy-done.14
  87.8 14.9 %shard_map.197 = (bf16[384,768]{1,0:T(8,128)(2,1)}, bf16[384,768]{1,0:T(8,128)(2,1)}, bf16[4,384,768]{2,1,0:T(8,128)(2,1)}, bf16[4,384,768]{2,1,0:T(8,128)(2,1)}...) custom-call(bf16[384,768]{1,0:T(8,128)(2,1)} %bitcast.36, bf16[384,768]{1,0:T(8,128)(2,1)} %bitcast.47, ...), custom_call_target="tpu_custom_call" | custom-call | flops 1048576 | bytes 65536 | tf_op jit(solution)/shard_map/pallas_call | solution.py:441
  102.7 3.6 %all-to-all-start.2 = ((bf16[8,48,768]{2,1,0:T(8,128)(2,1)}), bf16[8,48,768]{2,1,0:T(8,128)(2,1)S(1)}, u32[]{:S(2)}, u32[]{:S(2)}) async-start(bf16[8,48,768]{2,1,0:T(8,128)(2,1)} %bitcast.53), calls=%async_computation.2 | async-start | bytes 1179648 | tf_op jit(solution)/shard_map/all_to_all | solution.py:819
  106.3 0.7 slice.37
  107.1 1.1 collective-permute-done.12
  108.2 0.7 slice_add_fusion
  109.5 9.9 %shard_map.198 = (bf16[4,768,768]{2,1,0:T(8,128)(2,1)}, bf16[4,768,768]{2,1,0:T(8,128)(2,1)}) custom-call(bf16[384,768]{1,0:T(8,128)(2,1)} %bitcast.37, bf16[384,768]{1,0:T(8,128)(2,1)} %get-tuple-element.123.grads_ref, bf16[4,384,768]{2,1,0:T(8,128)(2,1)} %get-tuple-element.124.act_ref, bf16[4,384,768]{2,1,0:T(8,128)(2,1)} %get-tuple-element.125.gpre_ref), custom_call_target="tpu_custom_call" | custom-call | flops 1048576 | bytes 65536 | tf_op jit(solution)/shard_map/pallas_call | solution.py:544
  120.0 2.6 all-to-all-done.2
  123.1 7.6 %collective-permute-done.15 = bf16[4,768,768]{2,1,0:T(8,128)(2,1)S(1)} collective-permute-done((bf16[4,768,768]{2,1,0:T(8,128)(2,1)}, bf16[4,768,768]{2,1,0:T(8,128)(2,1)S(1)}, u32[]{:S(2)}, u32[]{:S(2)}) %collective-permute-start.15) | collective-permute-done | bytes 4718624 | tf_op jit(solution)/shard_map/ppermute | solution.py:795
  130.7 3.4 %fusion.13 = (bf16[384,768]{1,0:T(8,128)(2,1)}, bf16[384,768]{1,0:T(8,128)(2,1)}) fusion(bf16[4,768,768]{2,1,0:T(8,128)(2,1)S(1)} %collective-permute-done.15, bf16[4,768,768]{2,1,0:T(8,128)(2,1)} %get-tuple-element.130), kind=kLoop, calls=%fused_computation.19 | loop fusion | flops 2359296 | bytes 3538944 | tf_op jit(solution)/shard_map/convert_element_type | solution.py:893
  134.1 1.6 fusion.6
  135.8 2.6 collective-permute-done.14.refs_2_
  139.2 4.1 %all-to-all-start.3 = ((bf16[8,48,768]{2,1,0:T(8,128)(2,1)}), bf16[8,48,768]{2,1,0:T(8,128)(2,1)S(1)}, u32[]{:S(2)}, u32[]{:S(2)}) async-start(bf16[8,48,768]{2,1,0:T(8,128)(2,1)} %bitcast.52), calls=%async_computation.3 | async-start | bytes 1179648 | tf_op jit(solution)/shard_map/all_to_all | solution.py:819
  143.9 0.9 collective-permute-start.19
  144.7 0.8 collective-permute-done.16.refs_1_
  145.5 1.0 collective-permute-done.17.refs_3_
  146.5 11.2 %shard_map.199 = (f32[1024,768]{1,0:T(8,128)}, bf16[1024,256]{1,0:T(8,128)(2,1)}, f32[1,768]{1,0:T(1,128)}, bf16[192,768]{1,0:T(8,128)(2,1)}) custom-call(f32[1024,768]{1,0:T(8,128)} %get-tuple-element.101.hidden_ref, bf16[1024,768]{1,0:T(8,128)(2,1)} %cot_ref.1, f32[1,768]{1,0:T(1,128)} %broadcast_in_dim.15.gain_ref, ...), custom_call_target="tpu_custom_call" | custom-call | flops 1048576 | bytes 65536 | tf_op jit(solution)/shard_map/pallas_call | solution.py:598
  157.8 16.9 %shard_map.200 = (bf16[768,768]{1,0:T(8,128)(2,1)}, f32[512,768]{1,0:T(8,128)}, bf16[512,768]{1,0:T(8,128)(2,1)}, f32[3,32,128]{2,1,0:T(8,128)}) custom-call(bf16[1024,768]{1,0:T(8,128)(2,1)} %get-tuple-element.105.proj_ref, bf16[192,1024]{1,0:T(8,128)(2,1)} %get-tuple-element.106.kt_ref, f32[8,1024]{1,0:T(8,128)} %get-tuple-element.107.lse_ref, ...), custom_call_target="tpu_custom_call" | custom-call | flops 1048576 | bytes 65536 | tf_op jit(solution)/shard_map/pallas_call | solution.py:356
  174.7 4.0 %collective-permute-done.19 = bf16[384,768]{1,0:T(8,128)(2,1)} collective-permute-done((bf16[384,768]{1,0:T(8,128)(2,1)}, bf16[384,768]{1,0:T(8,128)(2,1)}, u32[]{:S(2)}, u32[]{:S(2)}) %collective-permute-start.19) | collective-permute-done | bytes 589856 | tf_op jit(solution)/shard_map/ppermute | solution.py:795
  178.7 1.0 copy-done.12
  179.7 2.5 collective-permute-done.20
  182.2 1.6 fusion.9
  183.8 4.8 %all-to-all-start.4 = ((bf16[8,96,768]{2,1,0:T(8,128)(2,1)}), bf16[8,96,768]{2,1,0:T(8,128)(2,1)S(1)}, u32[]{:S(2)}, u32[]{:S(2)}) async-start(bf16[8,96,768]{2,1,0:T(8,128)(2,1)} %bitcast.48), calls=%async_computation.4 | async-start | bytes 2359296 | tf_op jit(solution)/shard_map/all_to_all | solution.py:819
  188.6 0.9 collective-permute-start.21
  189.4 3.8 %bitcast_add_fusion = f32[768,768]{1,0:T(8,128)} fusion(bf16[768,768]{1,0:T(8,128)(2,1)} %copy-done.12, bf16[4,768,768]{2,1,0:T(8,128)(2,1)} %copy-done.3, bf16[4,768,768]{2,1,0:T(8,128)(2,1)} %get-tuple-element.130), kind=kLoop, calls=%fused_computation.2 | loop fusion | flops 2949120 | bytes 5898240 | tf_op jit(solution)/shard_map/add | solution.py:913
  193.2 14.7 %collective-permute-done.21 = bf16[512,768]{1,0:T(8,128)(2,1)S(1)} collective-permute-done((bf16[512,768]{1,0:T(8,128)(2,1)S(1)}, bf16[512,768]{1,0:T(8,128)(2,1)S(1)}, u32[]{:S(2)}, u32[]{:S(2)}) %collective-permute-start.21) | collective-permute-done | bytes 786464 | tf_op jit(solution)/shard_map/ppermute | solution.py:795
  208.3 0.9 collective-permute-start.23
  210.6 0.9 copy-done.15
  211.5 5.9 %shard_map.201 = (f32[1024,768]{1,0:T(8,128)}, f32[1,768]{1,0:T(1,128)}) custom-call(bf16[512,768]{1,0:T(8,128)(2,1)} %copy-done.5, bf16[512,768]{1,0:T(8,128)(2,1)} %copy-done.15, bf16[1024,768]{1,0:T(8,128)(2,1)} %x_ref.5, f32[1,768]{1,0:T(1,128)} %broadcast_in_dim.14.gain_ref, f32[1024,768]{1,0:T(8,128)} %get-tuple-element.152.gh_ref, s32[1]{0:T(128)} %bitcast.17.low_ref), custom_call_target="tpu_custom_call" | custom-call | flops 1048576 | bytes 65536 | tf_op jit(solution)/shard_map/pallas_call | solution.py:677
  217.4 7.0 %collective-permute-done.23 = bf16[384,768]{1,0:T(8,128)(2,1)} collective-permute-done((bf16[384,768]{1,0:T(8,128)(2,1)}, bf16[384,768]{1,0:T(8,128)(2,1)}, u32[]{:S(2)}, u32[]{:S(2)}) %collective-permute-start.23) | collective-permute-done | bytes 589856 | tf_op jit(solution)/shard_map/ppermute | solution.py:795
  224.4 1.0 copy-done.4
  225.4 4.2 %shard_map.203 = bf16[8,112,768]{2,1,0:T(8,128)(2,1)} custom-call(bf16[8,96,768]{2,1,0:T(8,128)(2,1)} %copy-done.4, f32[16,768]{1,0:T(8,128)} %pad.19.small_ref, f32[1,768]{1,0:T(1,128)} %get-tuple-element.162.ggain_ref), custom_call_target="tpu_custom_call" | custom-call | flops 1048576 | bytes 65536 | tf_op jit(solution)/shard_map/pallas_call | solution.py:716
  229.6 5.7 %all-to-all-start.5 = ((bf16[8,112,768]{2,1,0:T(8,128)(2,1)}), bf16[8,112,768]{2,1,0:T(8,128)(2,1)S(1)}, u32[]{:S(2)}, u32[]{:S(2)}) async-start(bf16[8,112,768]{2,1,0:T(8,128)(2,1)} %shard_map.203), calls=%async_computation.5 | async-start | bytes 2752512 | tf_op jit(solution)/shard_map/all_to_all | solution.py:819
  235.3 0.8 collective-permute-start.25
  236.1 13.8 %collective-permute-done.25.refs_2_ = bf16[384,768]{1,0:T(8,128)(2,1)S(1)} collective-permute-done((bf16[384,768]{1,0:T(8,128)(2,1)S(1)}, bf16[384,768]{1,0:T(8,128)(2,1)S(1)}, u32[]{:S(2)}, u32[]{:S(2)}) %collective-permute-start.25) | collective-permute-done | bytes 589856 | tf_op jit(solution)/shard_map/ppermute | solution.py:795
  249.9 4.0 %convert_add_fusion = f32[1,768,768]{2,1,0:T(8,128)} fusion(bf16[4,768,768]{2,1,0:T(8,128)(2,1)} %copy-done.3, bf16[1,384,768]{2,1,0:T(8,128)(2,1)} %bitcast.26, bf16[1,384,768]{2,1,0:T(8,128)(2,1)} %bitcast.25, bf16[4,768,768]{2,1,0:T(8,128)(2,1)} %get-tuple-element.130), kind=kLoop, calls=%fused_computation.3 | loop fusion | flops 4718592 | bytes 5898240 | tf_op jit(solution)/shard_map/add | solution.py:921
  253.9 0.8 copy-done.19
  255.0 7.0 %shard_map.202 = bf16[1024,768]{1,0:T(8,128)(2,1)} custom-call(f32[1024,768]{1,0:T(8,128)} %get-tuple-element.101.hidden_ref, f32[1024,1]{1,0:T(8,128)} %get-tuple-element.102.gate_ref, s32[1024,1]{1,0:T(8,128)} %get-tuple-element.103.flat_ref, s32[1,1536]{1,0:T(1,128)} %broadcast_in_dim.16.ids_ref, bf16[384,768]{1,0:T(8,128)(2,1)} %bitcast.42, ...), custom_call_target="tpu_custom_call" | custom-call | flops 1048576 | bytes 65536 | tf_op jit(solution)/shard_map/pallas_call | solution.py:645
  261.9 6.0 %all-to-all-done.5.totals_ref = bf16[8,112,768]{2,1,0:T(8,128)(2,1)S(1)} async-done(((bf16[8,112,768]{2,1,0:T(8,128)(2,1)}), bf16[8,112,768]{2,1,0:T(8,128)(2,1)S(1)}, u32[]{:S(2)}, u32[]{:S(2)}) %all-to-all-start.5) | async-done | bytes 1376288 | tf_op jit(solution)/shard_map/all_to_all | solution.py:819
  267.9 1.5 shard_map.204
  (120 shorter events, 13.5 us)
Async XLA Ops:
  0.6 30.1 %collective-permute-start = (bf16[768,768]{1,0:T(8,128)(2,1)}, bf16[768,768]{1,0:T(8,128)(2,1)}, u32[]{:S(2)}, u32[]{:S(2)}) collective-permute-start(bf16[768,768]{1,0:T(8,128)(2,1)} %bitcast.49), channel_id=1, source_target_pairs={{0,2},{1,3},{2,0},{3,1},{4,6},{5,7},{6,4},{7,5},{8,10},{9,11},{10,... | collective-permute-start | bytes 3538952 | tf_op jit(solution)/shard_map/ppermute | solution.py:795
  5.8 8.9 %copy-start.10 = (bf16[192,768]{1,0:T(8,128)(2,1)S(1)}, bf16[192,768]{1,0:T(8,128)(2,1)}, u32[]{:S(2)}) copy-start(bf16[192,768]{1,0:T(8,128)(2,1)} %refs_4_) | copy-start | bytes 884740
  5.8 9.5 %copy-start.29 = (f32[768]{0:T(1024)S(1)}, f32[768]{0:T(1024)}, u32[]{:S(2)}) copy-start(f32[768]{0:T(1024)} %param.13) | copy-start | bytes 9220
  5.8 10.1 %copy-start.26 = (s32[1,1024]{1,0:T(1,128)S(1)}, s32[1,1024]{1,0:T(1,128)}, u32[]{:S(2)}) copy-start(s32[1,1024]{1,0:T(1,128)} %seg_ref.3) | copy-start | bytes 12292
  8.9 21.4 %all-to-all-start = ((bf16[8,48,768]{2,1,0:T(8,128)(2,1)}), bf16[8,48,768]{2,1,0:T(8,128)(2,1)S(1)}, u32[]{:S(2)}, u32[]{:S(2)}) async-start(bf16[8,48,768]{2,1,0:T(8,128)(2,1)} %bitcast.4), calls=%async_computation | async-start | bytes 1179648 | tf_op jit(solution)/shard_map/all_to_all | solution.py:819
  14.7 23.4 %collective-permute-start.2 = (bf16[192,768]{1,0:T(8,128)(2,1)S(1)}, bf16[192,768]{1,0:T(8,128)(2,1)}, u32[]{:S(2)}, u32[]{:S(2)}) collective-permute-start(bf16[192,768]{1,0:T(8,128)(2,1)S(1)} %copy-done.10), channel_id=1, source_target_pairs={{0,2},{1,3},{2,0},{3,1},{4,6},{5,7},{6,4},{7,5},{8,10},{9,11},{10,... | collective-permute-start | bytes 884744 | tf_op jit(solution)/shard_map/ppermute | solution.py:795
  16.9 16.2 %copy-start.27 = (s32[1024,1]{0,1:T(1,128)S(1)}, s32[1024,1]{0,1:T(1,128)}, u32[]{:S(2)}) copy-start(s32[1024,1]{0,1:T(1,128)} %param.21) | copy-start | bytes 12292
  16.9 16.5 %copy-start.30 = (f32[768]{0:T(1024)S(1)}, f32[768]{0:T(1024)}, u32[]{:S(2)}) copy-start(f32[768]{0:T(1024)} %param.17) | copy-start | bytes 9220
  16.9 17.2 %copy-start.28 = (bf16[768,8]{0,1:T(8,128)(2,1)S(1)}, bf16[768,8]{0,1:T(8,128)(2,1)}, u32[]{:S(2)}) copy-start(bf16[768,8]{0,1:T(8,128)(2,1)} %param.18) | copy-start | bytes 36868
  30.3 7.2 %copy-start.8 = (bf16[8,48,768]{2,1,0:T(8,128)(2,1)}, bf16[8,48,768]{2,1,0:T(8,128)(2,1)S(1)}, u32[]{:S(2)}) copy-start(bf16[8,48,768]{2,1,0:T(8,128)(2,1)S(1)} %all-to-all-done) | copy-start | bytes 1769476
  30.8 13.9 %collective-permute-start.1 = (bf16[192,1024]{1,0:T(8,128)(2,1)}, bf16[192,1024]{1,0:T(8,128)(2,1)}, u32[]{:S(2)}, u32[]{:S(2)}) collective-permute-start(bf16[192,1024]{1,0:T(8,128)(2,1)} %get-tuple-element.97.refs_0_.att_ref), channel_id=1, source_target_pairs={{0,2},{1,3},{2,0},{3,1},{4,6},{5,7},{6,4},{7,5},{8,10},{9,11},{10,... | collective-permute-start | bytes 1179656 | tf_op jit(solution)/shard_map/ppermute | solution.py:795
  33.3 4.2 %copy-start.2 = (s32[1024,1]{1,0:T(8,128)}, s32[1024,1]{1,0:T(8,128)S(1)}, u32[]{:S(2)}) copy-start(s32[1024,1]{1,0:T(8,128)S(1)} %copy.27.route_ref) | copy-start | bytes 12292
  34.3 11.0 %copy-start.9 = (bf16[192,1024]{1,0:T(8,128)(2,1)S(1)}, bf16[192,1024]{1,0:T(8,128)(2,1)}, u32[]{:S(2)}) copy-start(bf16[192,1024]{1,0:T(8,128)(2,1)} %get-tuple-element.97.refs_0_.att_ref) | copy-start | bytes 1179652
  34.3 11.5 %copy-start.11 = (bf16[1,768,768]{2,1,0:T(8,128)(2,1)S(1)}, bf16[1,768,768]{2,1,0:T(8,128)(2,1)}, u32[]{:S(2)}) copy-start(bf16[1,768,768]{2,1,0:T(8,128)(2,1)} %param.19) | copy-start | bytes 3538948
  44.7 2.0 collective-permute-start.5
  44.7 2.3 collective-permute-start.6
  45.2 4.4 %collective-permute-start.3 = (bf16[192,1024]{1,0:T(8,128)(2,1)S(1)}, bf16[192,1024]{1,0:T(8,128)(2,1)S(1)}, u32[]{:S(2)}, u32[]{:S(2)}) collective-permute-start(bf16[192,1024]{1,0:T(8,128)(2,1)S(1)} %copy-done.9), channel_id=1, source_target_pairs={{0,1},{1,0},{2,3},{3,2},{4,5},{5,4},{6,7},{7,6},{8,9},{9,8},{10,11... | collective-permute-start | bytes 1179656 | tf_op jit(solution)/shard_map/ppermute | solution.py:795
  45.2 4.4 %collective-permute-start.4 = (bf16[192,1024]{1,0:T(8,128)(2,1)}, bf16[192,1024]{1,0:T(8,128)(2,1)S(1)}, u32[]{:S(2)}, u32[]{:S(2)}) collective-permute-start(bf16[192,1024]{1,0:T(8,128)(2,1)} %collective-permute-done.1.refs_2_), channel_id=1, source_target_pairs={{0,1},{1,0},{2,3},{3,2},{4,5},{5,4},{6,7},{7,6},{8,9},{9,8},{10,11... | collective-permute-start | bytes 1179656 | tf_op jit(solution)/shard_map/ppermute | solution.py:795
  45.7 20.1 %collective-permute-start.8 = (bf16[768,768]{1,0:T(8,128)(2,1)S(1)}, bf16[768,768]{1,0:T(8,128)(2,1)}, u32[]{:S(2)}, u32[]{:S(2)}) collective-permute-start(bf16[768,768]{1,0:T(8,128)(2,1)S(1)} %bitcast.51), channel_id=1, source_target_pairs={{0,1},{1,0},{2,3},{3,2},{4,5},{5,4},{6,7},{7,6},{8,9},{9,8},{10,11... | collective-permute-start | bytes 3538952 | tf_op jit(solution)/shard_map/ppermute | solution.py:795
  46.7 2.9 %copy-start.22 = (bf16[192,768]{1,0:T(8,128)(2,1)}, bf16[192,768]{1,0:T(8,128)(2,1)S(1)}, u32[]{:S(2)}) copy-start(bf16[192,768]{1,0:T(8,128)(2,1)S(1)} %collective-permute-done.5.refs_5_) | copy-start | bytes 884740
  46.7 19.2 %collective-permute-start.9 = (bf16[768,768]{1,0:T(8,128)(2,1)}, bf16[768,768]{1,0:T(8,128)(2,1)}, u32[]{:S(2)}, u32[]{:S(2)}) collective-permute-start(bf16[768,768]{1,0:T(8,128)(2,1)} %collective-permute-done.refs_2_), channel_id=1, source_target_pairs={{0,1},{1,0},{2,3},{3,2},{4,5},{5,4},{6,7},{7,6},{8,9},{9,8},{10,11... | collective-permute-start | bytes 3538952 | tf_op jit(solution)/shard_map/ppermute | solution.py:795
  47.0 2.6 copy-start.23
  47.0 28.6 %collective-permute-start.7 = (bf16[768,768]{1,0:T(8,128)(2,1)}, bf16[768,768]{1,0:T(8,128)(2,1)}, u32[]{:S(2)}, u32[]{:S(2)}) collective-permute-start(bf16[768,768]{1,0:T(8,128)(2,1)} %bitcast.6.refs_4_), channel_id=1, source_target_pairs={{0,2},{1,3},{2,0},{3,1},{4,6},{5,7},{6,4},{7,5},{8,10},{9,11},{10,... | collective-permute-start | bytes 3538952 | tf_op jit(solution)/shard_map/ppermute | solution.py:795
  49.6 0.7 copy-start.20
  60.0 21.9 %all-to-all-start.1 = ((bf16[8,48,768]{2,1,0:T(8,128)(2,1)}), bf16[8,48,768]{2,1,0:T(8,128)(2,1)S(1)}, u32[]{:S(2)}, u32[]{:S(2)}) async-start(bf16[8,48,768]{2,1,0:T(8,128)(2,1)} %bitcast.54), calls=%async_computation.1 | async-start | bytes 1179648 | tf_op jit(solution)/shard_map/all_to_all | solution.py:819
  82.0 4.8 %copy-start.1 = (bf16[8,48,768]{2,1,0:T(8,128)(2,1)}, bf16[8,48,768]{2,1,0:T(8,128)(2,1)S(1)}, u32[]{:S(2)}) copy-start(bf16[8,48,768]{2,1,0:T(8,128)(2,1)S(1)} %all-to-all-done.1) | copy-start | bytes 1769476
  82.0 3.1 %collective-permute-start.10 = (bf16[768,768]{1,0:T(8,128)(2,1)}, bf16[768,768]{1,0:T(8,128)(2,1)S(1)}, u32[]{:S(2)}, u32[]{:S(2)}) collective-permute-start(bf16[768,768]{1,0:T(8,128)(2,1)} %bitcast.6.refs_4_), channel_id=1, source_target_pairs={{0,1},{1,0},{2,3},{3,2},{4,5},{5,4},{6,7},{7,6},{8,9},{9,8},{10,11... | collective-permute-start | bytes 3538952 | tf_op jit(solution)/shard_map/ppermute | solution.py:795
  82.0 4.7 %collective-permute-start.11 = (bf16[768,768]{1,0:T(8,128)(2,1)}, bf16[768,768]{1,0:T(8,128)(2,1)S(1)}, u32[]{:S(2)}, u32[]{:S(2)}) collective-permute-start(bf16[768,768]{1,0:T(8,128)(2,1)} %collective-permute-done.7.refs_6_), channel_id=1, source_target_pairs={{0,1},{1,0},{2,3},{3,2},{4,5},{5,4},{6,7},{7,6},{8,9},{9,8},{10,11... | collective-permute-start | bytes 3538952 | tf_op jit(solution)/shard_map/ppermute | solution.py:795
  85.0 1.7 copy-start.13
  86.7 1.0 copy-start.14
  102.7 19.9 %all-to-all-start.2 = ((bf16[8,48,768]{2,1,0:T(8,128)(2,1)}), bf16[8,48,768]{2,1,0:T(8,128)(2,1)S(1)}, u32[]{:S(2)}, u32[]{:S(2)}) async-start(bf16[8,48,768]{2,1,0:T(8,128)(2,1)} %bitcast.53), calls=%async_computation.2 | async-start | bytes 1179648 | tf_op jit(solution)/shard_map/all_to_all | solution.py:819
  107.0 1.2 collective-permute-start.12
  109.0 10.4 %collective-permute-start.13 = (f32[8,768]{1,0:T(8,128)S(1)}, f32[8,768]{1,0:T(8,128)S(1)}, u32[]{:S(2)}, u32[]{:S(2)}) collective-permute-start(f32[8,768]{1,0:T(8,128)S(1)} %slice_add_fusion), channel_id=1, source_target_pairs={{0,2},{1,3},{2,0},{3,1},{4,6},{5,7},{6,4},{7,5},{8,10},{9,11},{10,... | collective-permute-start | bytes 73736 | tf_op jit(solution)/shard_map/ppermute | solution.py:795
  122.6 20.7 %copy-start.7 = (bf16[8,48,768]{2,1,0:T(8,128)(2,1)}, bf16[8,48,768]{2,1,0:T(8,128)(2,1)S(1)}, u32[]{:S(2)}) copy-start(bf16[8,48,768]{2,1,0:T(8,128)(2,1)S(1)} %all-to-all-done.2) | copy-start | bytes 1769476
  122.6 8.1 %collective-permute-start.15 = (bf16[4,768,768]{2,1,0:T(8,128)(2,1)}, bf16[4,768,768]{2,1,0:T(8,128)(2,1)S(1)}, u32[]{:S(2)}, u32[]{:S(2)}) collective-permute-start(bf16[4,768,768]{2,1,0:T(8,128)(2,1)} %get-tuple-element.131), channel_id=1, source_target_pairs={{0,1},{1,0},{2,3},{3,2},{4,5},{5,4},{6,7},{7,6},{8,9},{9,8},{10,11... | collective-permute-start | bytes 14155784 | tf_op jit(solution)/shard_map/ppermute | solution.py:795
  122.6 15.7 %collective-permute-start.14 = (bf16[384,768]{1,0:T(8,128)(2,1)S(1)}, bf16[384,768]{1,0:T(8,128)(2,1)S(1)}, u32[]{:S(2)}, u32[]{:S(2)}) collective-permute-start(bf16[384,768]{1,0:T(8,128)(2,1)S(1)} %bitcast.43), channel_id=1, source_target_pairs={{0,2},{1,3},{2,0},{3,1},{4,6},{5,7},{6,4},{7,5},{8,10},{9,11},{10,... | collective-permute-start | bytes 1769480 | tf_op jit(solution)/shard_map/ppermute | solution.py:795
  130.7 3.4 %copy-start.3 = (bf16[4,768,768]{2,1,0:T(8,128)(2,1)}, bf16[4,768,768]{2,1,0:T(8,128)(2,1)S(1)}, u32[]{:S(2)}) copy-start(bf16[4,768,768]{2,1,0:T(8,128)(2,1)S(1)} %collective-permute-done.15) | copy-start | bytes 14155780
  138.4 0.8 copy-start.16
  138.4 40.3 %collective-permute-start.18 = (bf16[768,768]{1,0:T(8,128)(2,1)S(1)}, bf16[768,768]{1,0:T(8,128)(2,1)S(1)}, u32[]{:S(2)}, u32[]{:S(2)}) collective-permute-start(bf16[768,768]{1,0:T(8,128)(2,1)S(1)} %fusion.6), channel_id=1, source_target_pairs={{0,2},{1,3},{2,0},{3,1},{4,6},{5,7},{6,4},{7,5},{8,10},{9,11},{10,... | collective-permute-start | bytes 3538952 | tf_op jit(solution)/shard_map/ppermute | solution.py:795
  139.2 35.5 %all-to-all-start.3 = ((bf16[8,48,768]{2,1,0:T(8,128)(2,1)}), bf16[8,48,768]{2,1,0:T(8,128)(2,1)S(1)}, u32[]{:S(2)}, u32[]{:S(2)}) async-start(bf16[8,48,768]{2,1,0:T(8,128)(2,1)} %bitcast.52), calls=%async_computation.3 | async-start | bytes 1179648 | tf_op jit(solution)/shard_map/all_to_all | solution.py:819
  143.3 2.2 collective-permute-start.16
  143.4 3.2 %collective-permute-start.17 = (bf16[384,768]{1,0:T(8,128)(2,1)}, bf16[384,768]{1,0:T(8,128)(2,1)}, u32[]{:S(2)}, u32[]{:S(2)}) collective-permute-start(bf16[384,768]{1,0:T(8,128)(2,1)} %copy-done.16), channel_id=1, source_target_pairs={{0,1},{1,0},{2,3},{3,2},{4,5},{5,4},{6,7},{7,6},{8,9},{9,8},{10,11... | collective-permute-start | bytes 1769480 | tf_op jit(solution)/shard_map/ppermute | solution.py:795
  143.9 34.8 %collective-permute-start.19 = (bf16[384,768]{1,0:T(8,128)(2,1)}, bf16[384,768]{1,0:T(8,128)(2,1)}, u32[]{:S(2)}, u32[]{:S(2)}) collective-permute-start(bf16[384,768]{1,0:T(8,128)(2,1)} %get-tuple-element.142), channel_id=1, source_target_pairs={{0,2},{1,3},{2,0},{3,1},{4,6},{5,7},{6,4},{7,5},{8,10},{9,11},{10,... | collective-permute-start | bytes 1769480 | tf_op jit(solution)/shard_map/ppermute | solution.py:795
  174.7 61.4 %copy-start.6 = (bf16[8,48,768]{2,1,0:T(8,128)(2,1)}, bf16[8,48,768]{2,1,0:T(8,128)(2,1)S(1)}, u32[]{:S(2)}) copy-start(bf16[8,48,768]{2,1,0:T(8,128)(2,1)S(1)} %all-to-all-done.3) | copy-start | bytes 1769476
  178.7 1.0 copy-start.12
  179.7 2.5 collective-permute-start.20
  183.8 40.6 %all-to-all-start.4 = ((bf16[8,96,768]{2,1,0:T(8,128)(2,1)}), bf16[8,96,768]{2,1,0:T(8,128)(2,1)S(1)}, u32[]{:S(2)}, u32[]{:S(2)}) async-start(bf16[8,96,768]{2,1,0:T(8,128)(2,1)} %bitcast.48), calls=%async_computation.4 | async-start | bytes 2359296 | tf_op jit(solution)/shard_map/all_to_all | solution.py:819
  188.6 19.4 %copy-start = (f32[512,768]{1,0:T(8,128)S(1)}, f32[512,768]{1,0:T(8,128)}, u32[]{:S(2)}) copy-start(f32[512,768]{1,0:T(8,128)} %get-tuple-element.144) | copy-start | bytes 4718596
  188.6 19.4 %collective-permute-start.21 = (bf16[512,768]{1,0:T(8,128)(2,1)S(1)}, bf16[512,768]{1,0:T(8,128)(2,1)S(1)}, u32[]{:S(2)}, u32[]{:S(2)}) collective-permute-start(bf16[512,768]{1,0:T(8,128)(2,1)S(1)} %fusion.9), channel_id=1, source_target_pairs={{0,2},{1,3},{2,0},{3,1},{4,6},{5,7},{6,4},{7,5},{8,10},{9,11},{10,... | collective-permute-start | bytes 2359304 | tf_op jit(solution)/shard_map/ppermute | solution.py:795
  193.2 16.1 %copy-start.25 = (f32[3,32,128]{2,1,0:T(8,128)S(1)}, f32[3,32,128]{2,1,0:T(8,128)}, u32[]{:S(2)}) copy-start(f32[3,32,128]{2,1,0:T(8,128)} %get-tuple-element.160) | copy-start | bytes 147460
  193.2 16.2 %copy-start.24 = (f32[8,768]{1,0:T(8,128)S(1)}, f32[8,768]{1,0:T(8,128)}, u32[]{:S(2)}) copy-start(f32[8,768]{1,0:T(8,128)} %add.246) | copy-start | bytes 73732
  193.2 16.2 %copy-start.31 = (f32[1,768]{1,0:T(1,128)S(1)}, f32[1,768]{1,0:T(1,128)}, u32[]{:S(2)}) copy-start(f32[1,768]{1,0:T(1,128)} %get-tuple-element.159) | copy-start | bytes 9220
  208.2 2.4 copy-start.5
  208.3 2.4 collective-permute-start.22
  208.3 16.1 %collective-permute-start.23 = (bf16[384,768]{1,0:T(8,128)(2,1)}, bf16[384,768]{1,0:T(8,128)(2,1)}, u32[]{:S(2)}, u32[]{:S(2)}) collective-permute-start(bf16[384,768]{1,0:T(8,128)(2,1)} %get-tuple-element.154), channel_id=1, source_target_pairs={{0,2},{1,3},{2,0},{3,1},{4,6},{5,7},{6,4},{7,5},{8,10},{9,11},{10,... | collective-permute-start | bytes 1769480 | tf_op jit(solution)/shard_map/ppermute | solution.py:795
  210.6 0.9 copy-start.15
  224.4 1.0 copy-start.4
  229.6 38.3 %all-to-all-start.5 = ((bf16[8,112,768]{2,1,0:T(8,128)(2,1)}), bf16[8,112,768]{2,1,0:T(8,128)(2,1)S(1)}, u32[]{:S(2)}, u32[]{:S(2)}) async-start(bf16[8,112,768]{2,1,0:T(8,128)(2,1)} %shard_map.203), calls=%async_computation.5 | async-start | bytes 2752512 | tf_op jit(solution)/shard_map/all_to_all | solution.py:819
  235.3 14.6 %collective-permute-start.25 = (bf16[384,768]{1,0:T(8,128)(2,1)S(1)}, bf16[384,768]{1,0:T(8,128)(2,1)S(1)}, u32[]{:S(2)}, u32[]{:S(2)}) collective-permute-start(bf16[384,768]{1,0:T(8,128)(2,1)S(1)} %bitcast.40), channel_id=1, source_target_pairs={{0,2},{1,3},{2,0},{3,1},{4,6},{5,7},{6,4},{7,5},{8,10},{9,11},{10,... | collective-permute-start | bytes 1769480 | tf_op jit(solution)/shard_map/ppermute | solution.py:795
  236.1 17.8 %collective-permute-start.24 = (bf16[384,768]{1,0:T(8,128)(2,1)S(1)}, bf16[384,768]{1,0:T(8,128)(2,1)S(1)}, u32[]{:S(2)}, u32[]{:S(2)}) collective-permute-start(bf16[384,768]{1,0:T(8,128)(2,1)S(1)} %bitcast.41), channel_id=1, source_target_pairs={{0,1},{1,0},{2,3},{3,2},{4,5},{5,4},{6,7},{7,6},{8,9},{9,8},{10,11... | collective-permute-start | bytes 1769480 | tf_op jit(solution)/shard_map/ppermute | solution.py:795
  249.9 4.0 %copy-start.17 = (bf16[384,768]{1,0:T(8,128)(2,1)}, bf16[384,768]{1,0:T(8,128)(2,1)S(1)}, u32[]{:S(2)}) copy-start(bf16[384,768]{1,0:T(8,128)(2,1)S(1)} %collective-permute-done.25.refs_2_) | copy-start | bytes 1769476
  249.9 4.0 %collective-permute-start.26 = (bf16[384,768]{1,0:T(8,128)(2,1)S(1)}, bf16[384,768]{1,0:T(8,128)(2,1)S(1)}, u32[]{:S(2)}, u32[]{:S(2)}) collective-permute-start(bf16[384,768]{1,0:T(8,128)(2,1)S(1)} %collective-permute-done.25.refs_2_), channel_id=1, source_target_pairs={{0,1},{1,0},{2,3},{3,2},{4,5},{5,4},{6,7},{7,6},{8,9},{9,8},{10,11... | collective-permute-start | bytes 1769480 | tf_op jit(solution)/shard_map/ppermute | solution.py:795
  253.9 1.1 copy-start.18
  253.9 0.8 copy-start.19
  (1 other events, 0.7 us)

commit v4 on v3

--- a/solution.py
+++ b/solution.py
@@ -884,7 +884,7 @@
     )
     near_weights = swap(sent_weights, 1)
     grad_far = gather_far(grad_back)
-    cut = width // 2
+    cut = width // 3
 
     def pair(k, rows_cut):
         return kept_weights[k, rows_cut].astype(F32) + near_weights[k, rows_cut].astype(F32)
@@ -907,17 +907,16 @@
         (grads, kept, sent, reply_back, out_came, fore_came, rest_sent)
     )
     kept = kept + swap(sent, 1).astype(F32)
-    kept_low, grads = tie((kept.astype(BF16), grads))
-    far = swap(kept_low, 2)
+    far = swap(kept.astype(BF16), 2)
     came = exchange(grads.reshape(groups, -1, width))
     grad_w_out = pair(0, slice(0, width)) + out_came.astype(F32)
-    far, grad_w_out, reply_back, rest_sent = tie((far, grad_w_out, reply_back, rest_sent))
+    far, grad_w_out, reply_back = tie((far, grad_w_out, reply_back))
+    reply_far = gather_far(reply_back)
+    reply_far, rest_sent = tie((reply_far, rest_sent))
     rest_came = swap(rest_sent, 2)
     kept = (kept + far.astype(F32)).astype(BF16)
     other = swap(kept, 1)
     grad_input, gain_part = input_grads(kept, other, tokens, gain_attn, grad_hidden1, low_bit)
-    gain_part, rest_came, reply_back = tie((gain_part, rest_came, reply_back))
-    reply_far = gather_far(reply_back)
     grad_w_in = pair(2, slice(0, width)) + jnp.concatenate([fore_came, rest_came], 0).astype(F32)
 
     rel_row = jnp.sum(rel_parts, -1).reshape(1, -1)

time: 273 us -> 266 us (0.974)
  waiting for transfers between devices: 93.9 us -> 79.7 us
  Pallas kernels: 92.8 us -> 98.7 us
    all_to_all x6, waiting for transfers between devices: 16.2 us -> 8.58 us  [exchange(): lax.all_to_all(value, 'expert', split_axis=0, concat_axis=0, tiled=True)]
    ppermute x27, waiting for transfers between devices: 77.7 us -> 71.1 us  [swap(): return lax.ppermute(value, 'tensor', [(i, i ^ bit) for i in range(members)])]
    pallas_call x1, Pallas kernels: 16.9 us -> 20.6 us  [attend_back(): pl.pallas_call(functools.partial(attend_back_kernel, length, heads, inner...]
    unnamed x66 -> x68, local copies, waits for them, and re-layouts: 7.21 us -> 6 us
  transfers between devices with their start and end apart: 33 -> 33, of which waited for: 22 -> 18; matrix products, arithmetic and copies ran while one was open for 11% -> 12% of each run, Pallas kernels for 27% -> 29%
where the time goes in v4:
time: 266 us; the launch traced here: 265 us
  Pallas kernels  98.7 us (37%)
  waiting for transfers between devices  79.7 us (30%)
  starting transfers between devices  47 us (18%)
  other arithmetic  20.7 us (8%)
  local copies, waits for them, and re-layouts  14 us (5%)
  matrix products  4.33 us (2%)
    ppermute x27, waiting for transfers between devices, swap(): return lax.ppermute(value, 'tensor', [(i, i ^ bit) for i in range(members)])  71.1 us
    all_to_all x6, starting transfers between devices, exchange(): lax.all_to_all(value, 'expert', split_axis=0, concat_axis=0, tiled=True)  30.1 us
    pallas_call x1, Pallas kernels, attend_back(): pl.pallas_call(functools.partial(attend_back_kernel, length, heads, inner...  20.6 us
    ppermute x27, starting transfers between devices, swap(): return lax.ppermute(value, 'tensor', [(i, i ^ bit) for i in range(members)])  16.9 us
    pallas_call x1, Pallas kernels, expert_step(): pl.pallas_call(functools.partial(expert_kernel, members, experts), grid=(...  14.9 us
    pallas_call x1, Pallas kernels, attend(): pl.pallas_call(functools.partial(attend_kernel, length, heads, inner // h...  14.4 us
    pallas_call x1, Pallas kernels, leave_experts(): pl.pallas_call(functools.partial(leave_kernel, members), grid=(length //...  11.2 us
    pallas_call x1, Pallas kernels, weight_grads(): pl.pallas_call(functools.partial(weight_kernel, members // 2), grid=(memb...  9.91 us
  transfers between devices with their start and end apart: 33, of which 18 were waited for; matrix products, arithmetic and copies ran while one was open for 12% of the time, Pallas kernels for 29%

profile of v4, /device:TPU:0, one launch (start us, length us, event | category | flops | bytes accessed | tf_op | source)
XLA Modules:
  0.0 265.3 jit_solution(6190249911385802671)
XLA Ops:
  0.6 3.0 %collective-permute-start = (bf16[768,768]{1,0:T(8,128)(2,1)}, bf16[768,768]{1,0:T(8,128)(2,1)}, u32[]{:S(2)}, u32[]{:S(2)}) collective-permute-start(bf16[768,768]{1,0:T(8,128)(2,1)} %bitcast.49), channel_id=1, source_target_pairs={{0,2},{1,3},{2,0},{3,1},{4,6},{5,7},{6,4},{7,5},{8,10},{9,11},{10,... | collective-permute-start | bytes 3538952 | tf_op jit(solution)/shard_map/ppermute | solution.py:795
  3.7 1.2 fusion.8
  5.8 3.1 %fusion.3 = bf16[384,768]{1,0:T(8,128)(2,1)} fusion(bf16[1024,768]{1,0:T(8,128)(2,1)} %cot_ref.1, s32[1024]{0:T(1024)S(1)} %multiply_add_fusion.1, s32[384]{0:T(512)S(1)} %add.225), kind=kOutput, calls=%fused_computation.10 | convolution fusion | flops 604667904 | bytes 2168320 | tf_op jit(solution)/shard_map/dot_general | solution.py:39
  8.9 5.8 %all-to-all-start = ((bf16[8,48,768]{2,1,0:T(8,128)(2,1)}), bf16[8,48,768]{2,1,0:T(8,128)(2,1)S(1)}, u32[]{:S(2)}, u32[]{:S(2)}) async-start(bf16[8,48,768]{2,1,0:T(8,128)(2,1)} %bitcast.4), calls=%async_computation | async-start | bytes 1179648 | tf_op jit(solution)/shard_map/all_to_all | solution.py:819
  15.9 1.0 copy.25.doc_ref
  16.9 14.4 %shard_map.195 = (bf16[192,1024]{1,0:T(8,128)(2,1)}, f32[8,1024]{1,0:T(8,128)}, bf16[1024,768]{1,0:T(8,128)(2,1)}, bf16[192,1024]{1,0:T(8,128)(2,1)}, bf16[1024,768]{1,0:T(8,128)(2,1)}) custom-call(bf16[1024,768]{1,0:T(8,128)(2,1)} %x_ref.5, f32[1,768]{1,0:T(1,128)} %broadcast_in_dim.14.gain_ref, bf16[3,192,768]{2,1,0:T(8,128)(2,1)} %bitcast.38, ...), custom_call_target="tpu_custom_call" | custom-call | flops 1048576 | bytes 65536 | tf_op jit(solution)/shard_map/pallas_call | solution.py:324
  31.4 1.6 collective-permute-start.1
  34.9 0.8 pad.17.wproj_ref
  35.7 0.7 pad.16.router_ref
  36.7 0.9 multiply_add_fusion
  38.1 6.5 %collective-permute-done.1.refs_2_ = bf16[192,1024]{1,0:T(8,128)(2,1)S(1)} collective-permute-done((bf16[192,1024]{1,0:T(8,128)(2,1)}, bf16[192,1024]{1,0:T(8,128)(2,1)S(1)}, u32[]{:S(2)}, u32[]{:S(2)}) %collective-permute-start.1) | collective-permute-done | bytes 393248 | tf_op jit(solution)/shard_map/ppermute | solution.py:795
  45.6 0.9 collective-permute-done.5.refs_5_
  46.9 1.8 collective-permute-start.7
  48.6 0.8 copy.30.ids_ref
  49.5 0.7 copy-done.23
  50.2 0.8 copy-done.24
  51.0 8.9 %shard_map.196 = (f32[1024,768]{1,0:T(8,128)}, f32[1024,1]{1,0:T(8,128)}, bf16[384,768]{1,0:T(8,128)(2,1)}) custom-call(bf16[1024,768]{1,0:T(8,128)(2,1)} %x_ref.5, f32[1,768]{1,0:T(1,128)} %broadcast_in_dim.15.gain_ref, bf16[768,128]{1,0:T(8,128)(2,1)} %pad.16.router_ref, s32[1024,1]{1,0:T(8,128)} %copy-done.2, s32[1,1024]{1,0:T(1,128)} %add.227.flat_ref, ...), custom_call_target="tpu_custom_call" | custom-call | flops 1048576 | bytes 65536 | tf_op jit(solution)/shard_map/pallas_call | solution.py:491
  60.0 5.8 %all-to-all-start.1 = ((bf16[8,48,768]{2,1,0:T(8,128)(2,1)}), bf16[8,48,768]{2,1,0:T(8,128)(2,1)S(1)}, u32[]{:S(2)}, u32[]{:S(2)}) async-start(bf16[8,48,768]{2,1,0:T(8,128)(2,1)} %bitcast.58), calls=%async_computation.1 | async-start | bytes 1179648 | tf_op jit(solution)/shard_map/all_to_all | solution.py:819
  65.8 9.7 %collective-permute-done.7.refs_6_ = bf16[768,768]{1,0:T(8,128)(2,1)} collective-permute-done((bf16[768,768]{1,0:T(8,128)(2,1)}, bf16[768,768]{1,0:T(8,128)(2,1)}, u32[]{:S(2)}, u32[]{:S(2)}) %collective-permute-start.7) | collective-permute-done | bytes 1179680 | tf_op jit(solution)/shard_map/ppermute | solution.py:795
  75.4 6.5 %all-to-all-done.1 = bf16[8,48,768]{2,1,0:T(8,128)(2,1)S(1)} async-done(((bf16[8,48,768]{2,1,0:T(8,128)(2,1)}), bf16[8,48,768]{2,1,0:T(8,128)(2,1)S(1)}, u32[]{:S(2)}, u32[]{:S(2)}) %all-to-all-start.1) | async-done | bytes 589856 | tf_op jit(solution)/shard_map/all_to_all | solution.py:819
  82.4 3.3 %collective-permute-done.10.refs_5_ = bf16[768,768]{1,0:T(8,128)(2,1)S(1)} collective-permute-done((bf16[768,768]{1,0:T(8,128)(2,1)S(1)}, bf16[768,768]{1,0:T(8,128)(2,1)S(1)}, u32[]{:S(2)}, u32[]{:S(2)}) %collective-permute-start.10) | collective-permute-done | bytes 1179680 | tf_op jit(solution)/shard_map/ppermute | solution.py:795
  85.7 1.0 collective-permute-done.11.refs_7_
  86.8 14.9 %shard_map.197 = (bf16[384,768]{1,0:T(8,128)(2,1)}, bf16[384,768]{1,0:T(8,128)(2,1)}, bf16[4,384,768]{2,1,0:T(8,128)(2,1)}, bf16[4,384,768]{2,1,0:T(8,128)(2,1)}...) custom-call(bf16[384,768]{1,0:T(8,128)(2,1)} %bitcast.36, bf16[384,768]{1,0:T(8,128)(2,1)} %bitcast.47, ...), custom_call_target="tpu_custom_call" | custom-call | flops 1048576 | bytes 65536 | tf_op jit(solution)/shard_map/pallas_call | solution.py:441
  101.7 3.6 %all-to-all-start.2 = ((bf16[8,48,768]{2,1,0:T(8,128)(2,1)}), bf16[8,48,768]{2,1,0:T(8,128)(2,1)S(1)}, u32[]{:S(2)}, u32[]{:S(2)}) async-start(bf16[8,48,768]{2,1,0:T(8,128)(2,1)} %bitcast.57), calls=%async_computation.2 | async-start | bytes 1179648 | tf_op jit(solution)/shard_map/all_to_all | solution.py:819
  105.4 0.7 slice.37
  106.1 1.2 collective-permute-done.12
  107.3 0.7 slice_add_fusion
  108.0 1.0 collective-permute-start.13
  109.0 9.9 %shard_map.198 = (bf16[4,768,768]{2,1,0:T(8,128)(2,1)}, bf16[4,768,768]{2,1,0:T(8,128)(2,1)}) custom-call(bf16[384,768]{1,0:T(8,128)(2,1)} %bitcast.37, bf16[384,768]{1,0:T(8,128)(2,1)} %get-tuple-element.120.grads_ref, bf16[4,384,768]{2,1,0:T(8,128)(2,1)} %get-tuple-element.121.act_ref, bf16[4,384,768]{2,1,0:T(8,128)(2,1)} %get-tuple-element.122.gpre_ref), custom_call_target="tpu_custom_call" | custom-call | flops 1048576 | bytes 65536 | tf_op jit(solution)/shard_map/pallas_call | solution.py:544
  119.5 2.1 all-to-all-done.2
  121.7 1.0 collective-permute-start.14
  122.6 7.1 %collective-permute-done.15 = bf16[4,768,768]{2,1,0:T(8,128)(2,1)S(1)} collective-permute-done((bf16[4,768,768]{2,1,0:T(8,128)(2,1)}, bf16[4,768,768]{2,1,0:T(8,128)(2,1)S(1)}, u32[]{:S(2)}, u32[]{:S(2)}) %collective-permute-start.15) | collective-permute-done | bytes 4718624 | tf_op jit(solution)/shard_map/ppermute | solution.py:795
  129.8 2.3 fusion.13
  132.1 2.3 fusion.10
  134.4 1.6 fusion.6
  136.0 1.4 collective-permute-done.14.refs_2_
  137.4 1.0 collective-permute-start.18
  138.4 4.0 %all-to-all-start.3 = ((bf16[8,48,768]{2,1,0:T(8,128)(2,1)}), bf16[8,48,768]{2,1,0:T(8,128)(2,1)S(1)}, u32[]{:S(2)}, u32[]{:S(2)}) async-start(bf16[8,48,768]{2,1,0:T(8,128)(2,1)} %bitcast.56), calls=%async_computation.3 | async-start | bytes 1179648 | tf_op jit(solution)/shard_map/all_to_all | solution.py:819
  142.9 1.0 collective-permute-start.19
  144.5 0.8 collective-permute-done.17.refs_3_
  145.4 11.2 %shard_map.199 = (f32[1024,768]{1,0:T(8,128)}, bf16[1024,256]{1,0:T(8,128)(2,1)}, f32[1,768]{1,0:T(1,128)}, bf16[192,768]{1,0:T(8,128)(2,1)}) custom-call(f32[1024,768]{1,0:T(8,128)} %get-tuple-element.98.hidden_ref, bf16[1024,768]{1,0:T(8,128)(2,1)} %cot_ref.1, f32[1,768]{1,0:T(1,128)} %broadcast_in_dim.15.gain_ref, s32[1024,1]{1,0:T(8,128)} %get-tuple-element.100.flat_ref, ...), custom_call_target="tpu_custom_call" | custom-call | flops 1048576 | bytes 65536 | tf_op jit(solution)/shard_map/pallas_call | solution.py:598
  156.6 20.6 %shard_map.200 = (bf16[768,768]{1,0:T(8,128)(2,1)}, f32[512,768]{1,0:T(8,128)}, bf16[512,768]{1,0:T(8,128)(2,1)}, f32[3,32,128]{2,1,0:T(8,128)}) custom-call(bf16[1024,768]{1,0:T(8,128)(2,1)} %get-tuple-element.102.proj_ref, bf16[192,1024]{1,0:T(8,128)(2,1)} %get-tuple-element.103.kt_ref, f32[8,1024]{1,0:T(8,128)} %get-tuple-element.104.lse_ref, ...), custom_call_target="tpu_custom_call" | custom-call | flops 1048576 | bytes 65536 | tf_op jit(solution)/shard_map/pallas_call | solution.py:356
  178.0 5.0 %all-to-all-start.4 = ((bf16[8,96,768]{2,1,0:T(8,128)(2,1)}), bf16[8,96,768]{2,1,0:T(8,128)(2,1)S(1)}, u32[]{:S(2)}, u32[]{:S(2)}) async-start(bf16[8,96,768]{2,1,0:T(8,128)(2,1)} %bitcast.48), calls=%async_computation.4 | async-start | bytes 2359296 | tf_op jit(solution)/shard_map/all_to_all | solution.py:819
  183.2 0.7 copy-done.6
  183.9 1.0 collective-permute-start.21
  184.9 3.8 %bitcast_add_fusion = f32[768,768]{1,0:T(8,128)} fusion(bf16[768,768]{1,0:T(8,128)(2,1)} %collective-permute-done.18, bf16[4,768,768]{2,1,0:T(8,128)(2,1)} %copy-done.3, bf16[4,768,768]{2,1,0:T(8,128)(2,1)} %get-tuple-element.127), kind=kLoop, calls=%fused_computation.2 | loop fusion | flops 2949120 | bytes 5898240 | tf_op jit(solution)/shard_map/add | solution.py:912
  188.8 14.5 %collective-permute-done.21 = bf16[512,768]{1,0:T(8,128)(2,1)S(1)} collective-permute-done((bf16[512,768]{1,0:T(8,128)(2,1)S(1)}, bf16[512,768]{1,0:T(8,128)(2,1)S(1)}, u32[]{:S(2)}, u32[]{:S(2)}) %collective-permute-start.21) | collective-permute-done | bytes 786464 | tf_op jit(solution)/shard_map/ppermute | solution.py:795
  203.7 0.9 reduce_sum.19
  204.8 0.8 fusion.15
  206.2 0.9 copy-done.16
  207.1 5.9 %shard_map.202 = (f32[1024,768]{1,0:T(8,128)}, f32[1,768]{1,0:T(1,128)}) custom-call(bf16[512,768]{1,0:T(8,128)(2,1)} %copy-done.5, bf16[512,768]{1,0:T(8,128)(2,1)} %copy-done.16, bf16[1024,768]{1,0:T(8,128)(2,1)} %x_ref.5, f32[1,768]{1,0:T(1,128)} %broadcast_in_dim.14.gain_ref, f32[1024,768]{1,0:T(8,128)} %get-tuple-element.150.gh_ref, s32[1]{0:T(128)} %bitcast.17.low_ref), custom_call_target="tpu_custom_call" | custom-call | flops 1048576 | bytes 65536 | tf_op jit(solution)/shard_map/pallas_call | solution.py:677
  213.0 1.0 copy-done.4
  214.0 4.2 %shard_map.203 = bf16[8,112,768]{2,1,0:T(8,128)(2,1)} custom-call(bf16[8,96,768]{2,1,0:T(8,128)(2,1)} %copy-done.4, f32[16,768]{1,0:T(8,128)} %pad.19.small_ref, f32[1,768]{1,0:T(1,128)} %get-tuple-element.156.ggain_ref), custom_call_target="tpu_custom_call" | custom-call | flops 1048576 | bytes 65536 | tf_op jit(solution)/shard_map/pallas_call | solution.py:716
  218.3 5.8 %all-to-all-start.5 = ((bf16[8,112,768]{2,1,0:T(8,128)(2,1)}), bf16[8,112,768]{2,1,0:T(8,128)(2,1)S(1)}, u32[]{:S(2)}, u32[]{:S(2)}) async-start(bf16[8,112,768]{2,1,0:T(8,128)(2,1)} %shard_map.203), calls=%async_computation.5 | async-start | bytes 2752512 | tf_op jit(solution)/shard_map/all_to_all | solution.py:819
  224.1 1.1 collective-permute-start.22
  225.2 14.4 %collective-permute-done.22.refs_2_ = bf16[384,768]{1,0:T(8,128)(2,1)S(1)} collective-permute-done((bf16[384,768]{1,0:T(8,128)(2,1)S(1)}, bf16[384,768]{1,0:T(8,128)(2,1)S(1)}, u32[]{:S(2)}, u32[]{:S(2)}) %collective-permute-start.22) | collective-permute-done | bytes 589856 | tf_op jit(solution)/shard_map/ppermute | solution.py:795
  239.6 1.0 collective-permute-start.26
  241.1 1.5 collective-permute-done.23.refs_1_
  242.6 0.8 collective-permute-done.24.refs_3_
  243.4 0.8 copy-done.21
  244.2 7.0 %shard_map.201 = bf16[1024,768]{1,0:T(8,128)(2,1)} custom-call(f32[1024,768]{1,0:T(8,128)} %get-tuple-element.98.hidden_ref, f32[1024,1]{1,0:T(8,128)} %get-tuple-element.99.gate_ref, s32[1024,1]{1,0:T(8,128)} %get-tuple-element.100.flat_ref, s32[1,1536]{1,0:T(1,128)} %broadcast_in_dim.16.ids_ref, bf16[384,768]{1,0:T(8,128)(2,1)} %bitcast.40, ...), custom_call_target="tpu_custom_call" | custom-call | flops 1048576 | bytes 65536 | tf_op jit(solution)/shard_map/pallas_call | solution.py:645
  251.2 7.1 %collective-permute-done.26 = bf16[512,768]{1,0:T(8,128)(2,1)S(1)} collective-permute-done((bf16[512,768]{1,0:T(8,128)(2,1)S(1)}, bf16[512,768]{1,0:T(8,128)(2,1)S(1)}, u32[]{:S(2)}, u32[]{:S(2)}) %collective-permute-start.26) | collective-permute-done | bytes 786464 | tf_op jit(solution)/shard_map/ppermute | solution.py:795
  258.4 3.5 %convert_add_fusion = f32[1,768,768]{2,1,0:T(8,128)} fusion(bf16[4,768,768]{2,1,0:T(8,128)(2,1)} %copy-done.3, bf16[1,512,768]{2,1,0:T(8,128)(2,1)S(1)} %bitcast.55, bf16[1,256,768]{2,1,0:T(8,128)(2,1)} %bitcast.25, bf16[4,768,768]{2,1,0:T(8,128)(2,1)} %get-tuple-element.127), kind=kLoop, calls=%fused_computation.3 | loop fusion | flops 4718592 | bytes 5898240 | tf_op jit(solution)/shard_map/add | solution.py:920
  261.9 1.5 shard_map.204
  (123 shorter events, 13.2 us)
Async XLA Ops:
  0.6 30.7 %collective-permute-start = (bf16[768,768]{1,0:T(8,128)(2,1)}, bf16[768,768]{1,0:T(8,128)(2,1)}, u32[]{:S(2)}, u32[]{:S(2)}) collective-permute-start(bf16[768,768]{1,0:T(8,128)(2,1)} %bitcast.49), channel_id=1, source_target_pairs={{0,2},{1,3},{2,0},{3,1},{4,6},{5,7},{6,4},{7,5},{8,10},{9,11},{10,... | collective-permute-start | bytes 3538952 | tf_op jit(solution)/shard_map/ppermute | solution.py:795
  5.8 8.9 %copy-start.13 = (bf16[192,768]{1,0:T(8,128)(2,1)S(1)}, bf16[192,768]{1,0:T(8,128)(2,1)}, u32[]{:S(2)}) copy-start(bf16[192,768]{1,0:T(8,128)(2,1)} %refs_4_) | copy-start | bytes 884740
  5.8 9.5 %copy-start.30 = (f32[768]{0:T(1024)S(1)}, f32[768]{0:T(1024)}, u32[]{:S(2)}) copy-start(f32[768]{0:T(1024)} %param.13) | copy-start | bytes 9220
  5.8 10.1 %copy-start.27 = (s32[1,1024]{1,0:T(1,128)S(1)}, s32[1,1024]{1,0:T(1,128)}, u32[]{:S(2)}) copy-start(s32[1,1024]{1,0:T(1,128)} %seg_ref.3) | copy-start | bytes 12292
  8.9 22.5 %all-to-all-start = ((bf16[8,48,768]{2,1,0:T(8,128)(2,1)}), bf16[8,48,768]{2,1,0:T(8,128)(2,1)S(1)}, u32[]{:S(2)}, u32[]{:S(2)}) async-start(bf16[8,48,768]{2,1,0:T(8,128)(2,1)} %bitcast.4), calls=%async_computation | async-start | bytes 1179648 | tf_op jit(solution)/shard_map/all_to_all | solution.py:819
  14.7 23.4 %collective-permute-start.2 = (bf16[192,768]{1,0:T(8,128)(2,1)S(1)}, bf16[192,768]{1,0:T(8,128)(2,1)}, u32[]{:S(2)}, u32[]{:S(2)}) collective-permute-start(bf16[192,768]{1,0:T(8,128)(2,1)S(1)} %copy-done.13), channel_id=1, source_target_pairs={{0,2},{1,3},{2,0},{3,1},{4,6},{5,7},{6,4},{7,5},{8,10},{9,11},{10,... | collective-permute-start | bytes 884744 | tf_op jit(solution)/shard_map/ppermute | solution.py:795
  16.9 16.4 %copy-start.28 = (s32[1024,1]{0,1:T(1,128)S(1)}, s32[1024,1]{0,1:T(1,128)}, u32[]{:S(2)}) copy-start(s32[1024,1]{0,1:T(1,128)} %param.21) | copy-start | bytes 12292
  16.9 16.6 %copy-start.31 = (f32[768]{0:T(1024)S(1)}, f32[768]{0:T(1024)}, u32[]{:S(2)}) copy-start(f32[768]{0:T(1024)} %param.17) | copy-start | bytes 9220
  16.9 17.8 %copy-start.29 = (bf16[768,8]{0,1:T(8,128)(2,1)S(1)}, bf16[768,8]{0,1:T(8,128)(2,1)}, u32[]{:S(2)}) copy-start(bf16[768,8]{0,1:T(8,128)(2,1)} %param.18) | copy-start | bytes 36868
  31.4 6.2 %copy-start.11 = (bf16[8,48,768]{2,1,0:T(8,128)(2,1)}, bf16[8,48,768]{2,1,0:T(8,128)(2,1)S(1)}, u32[]{:S(2)}) copy-start(bf16[8,48,768]{2,1,0:T(8,128)(2,1)S(1)} %all-to-all-done) | copy-start | bytes 1769476
  31.4 13.2 %collective-permute-start.1 = (bf16[192,1024]{1,0:T(8,128)(2,1)}, bf16[192,1024]{1,0:T(8,128)(2,1)S(1)}, u32[]{:S(2)}, u32[]{:S(2)}) collective-permute-start(bf16[192,1024]{1,0:T(8,128)(2,1)} %get-tuple-element.94.refs_0_.att_ref), channel_id=1, source_target_pairs={{0,2},{1,3},{2,0},{3,1},{4,6},{5,7},{6,4},{7,5},{8,10},{9,11},{10,... | collective-permute-start | bytes 1179656 | tf_op jit(solution)/shard_map/ppermute | solution.py:795
  33.5 4.0 %copy-start.2 = (s32[1024,1]{1,0:T(8,128)}, s32[1024,1]{1,0:T(8,128)S(1)}, u32[]{:S(2)}) copy-start(s32[1024,1]{1,0:T(8,128)S(1)} %copy.27.route_ref) | copy-start | bytes 12292
  34.9 10.2 %copy-start.12 = (bf16[192,1024]{1,0:T(8,128)(2,1)S(1)}, bf16[192,1024]{1,0:T(8,128)(2,1)}, u32[]{:S(2)}) copy-start(bf16[192,1024]{1,0:T(8,128)(2,1)} %get-tuple-element.94.refs_0_.att_ref) | copy-start | bytes 1179652
  44.6 4.9 %copy-start.22 = (bf16[192,1024]{1,0:T(8,128)(2,1)}, bf16[192,1024]{1,0:T(8,128)(2,1)S(1)}, u32[]{:S(2)}) copy-start(bf16[192,1024]{1,0:T(8,128)(2,1)S(1)} %collective-permute-done.1.refs_2_) | copy-start | bytes 1179652
  44.6 2.0 collective-permute-start.5
  44.6 2.3 collective-permute-start.6
  45.1 4.4 %collective-permute-start.3 = (bf16[192,1024]{1,0:T(8,128)(2,1)S(1)}, bf16[192,1024]{1,0:T(8,128)(2,1)S(1)}, u32[]{:S(2)}, u32[]{:S(2)}) collective-permute-start(bf16[192,1024]{1,0:T(8,128)(2,1)S(1)} %copy-done.12), channel_id=1, source_target_pairs={{0,1},{1,0},{2,3},{3,2},{4,5},{5,4},{6,7},{7,6},{8,9},{9,8},{10,11... | collective-permute-start | bytes 1179656 | tf_op jit(solution)/shard_map/ppermute | solution.py:795
  45.1 4.4 %collective-permute-start.4 = (bf16[192,1024]{1,0:T(8,128)(2,1)S(1)}, bf16[192,1024]{1,0:T(8,128)(2,1)S(1)}, u32[]{:S(2)}, u32[]{:S(2)}) collective-permute-start(bf16[192,1024]{1,0:T(8,128)(2,1)S(1)} %collective-permute-done.1.refs_2_), channel_id=1, source_target_pairs={{0,1},{1,0},{2,3},{3,2},{4,5},{5,4},{6,7},{7,6},{8,9},{9,8},{10,11... | collective-permute-start | bytes 1179656 | tf_op jit(solution)/shard_map/ppermute | solution.py:795
  45.6 20.1 %collective-permute-start.8 = (bf16[768,768]{1,0:T(8,128)(2,1)}, bf16[768,768]{1,0:T(8,128)(2,1)}, u32[]{:S(2)}, u32[]{:S(2)}) collective-permute-start(bf16[768,768]{1,0:T(8,128)(2,1)} %bitcast.50), channel_id=1, source_target_pairs={{0,1},{1,0},{2,3},{3,2},{4,5},{5,4},{6,7},{7,6},{8,9},{9,8},{10,11... | collective-permute-start | bytes 3538952 | tf_op jit(solution)/shard_map/ppermute | solution.py:795
  46.6 2.1 copy-start.25
  46.6 19.2 %collective-permute-start.9 = (bf16[768,768]{1,0:T(8,128)(2,1)}, bf16[768,768]{1,0:T(8,128)(2,1)}, u32[]{:S(2)}, u32[]{:S(2)}) collective-permute-start(bf16[768,768]{1,0:T(8,128)(2,1)} %collective-permute-done.refs_2_), channel_id=1, source_target_pairs={{0,1},{1,0},{2,3},{3,2},{4,5},{5,4},{6,7},{7,6},{8,9},{9,8},{10,11... | collective-permute-start | bytes 3538952 | tf_op jit(solution)/shard_map/ppermute | solution.py:795
  46.9 1.8 copy-start.26
  46.9 28.6 %collective-permute-start.7 = (bf16[768,768]{1,0:T(8,128)(2,1)}, bf16[768,768]{1,0:T(8,128)(2,1)}, u32[]{:S(2)}, u32[]{:S(2)}) collective-permute-start(bf16[768,768]{1,0:T(8,128)(2,1)} %bitcast.52), channel_id=1, source_target_pairs={{0,2},{1,3},{2,0},{3,1},{4,6},{5,7},{6,4},{7,5},{8,10},{9,11},{10,... | collective-permute-start | bytes 3538952 | tf_op jit(solution)/shard_map/ppermute | solution.py:795
  49.5 32.4 %copy-start.14 = (bf16[1,768,768]{2,1,0:T(8,128)(2,1)S(1)}, bf16[1,768,768]{2,1,0:T(8,128)(2,1)}, u32[]{:S(2)}) copy-start(bf16[1,768,768]{2,1,0:T(8,128)(2,1)} %param.20) | copy-start | bytes 3538948
  60.0 22.0 %all-to-all-start.1 = ((bf16[8,48,768]{2,1,0:T(8,128)(2,1)}), bf16[8,48,768]{2,1,0:T(8,128)(2,1)S(1)}, u32[]{:S(2)}, u32[]{:S(2)}) async-start(bf16[8,48,768]{2,1,0:T(8,128)(2,1)} %bitcast.58), calls=%async_computation.1 | async-start | bytes 1179648 | tf_op jit(solution)/shard_map/all_to_all | solution.py:819
  81.9 4.9 %copy-start.1 = (bf16[8,48,768]{2,1,0:T(8,128)(2,1)}, bf16[8,48,768]{2,1,0:T(8,128)(2,1)S(1)}, u32[]{:S(2)}) copy-start(bf16[8,48,768]{2,1,0:T(8,128)(2,1)S(1)} %all-to-all-done.1) | copy-start | bytes 1769476
  81.9 3.8 %collective-permute-start.10 = (bf16[768,768]{1,0:T(8,128)(2,1)S(1)}, bf16[768,768]{1,0:T(8,128)(2,1)S(1)}, u32[]{:S(2)}, u32[]{:S(2)}) collective-permute-start(bf16[768,768]{1,0:T(8,128)(2,1)S(1)} %bitcast.54), channel_id=1, source_target_pairs={{0,1},{1,0},{2,3},{3,2},{4,5},{5,4},{6,7},{7,6},{8,9},{9,8},{10,11... | collective-permute-start | bytes 3538952 | tf_op jit(solution)/shard_map/ppermute | solution.py:795
  81.9 4.9 %collective-permute-start.11 = (bf16[768,768]{1,0:T(8,128)(2,1)}, bf16[768,768]{1,0:T(8,128)(2,1)}, u32[]{:S(2)}, u32[]{:S(2)}) collective-permute-start(bf16[768,768]{1,0:T(8,128)(2,1)} %collective-permute-done.7.refs_6_), channel_id=1, source_target_pairs={{0,1},{1,0},{2,3},{3,2},{4,5},{5,4},{6,7},{7,6},{8,9},{9,8},{10,11... | collective-permute-start | bytes 3538952 | tf_op jit(solution)/shard_map/ppermute | solution.py:795
  85.7 1.1 copy-start.15
  101.7 19.9 %all-to-all-start.2 = ((bf16[8,48,768]{2,1,0:T(8,128)(2,1)}), bf16[8,48,768]{2,1,0:T(8,128)(2,1)S(1)}, u32[]{:S(2)}, u32[]{:S(2)}) async-start(bf16[8,48,768]{2,1,0:T(8,128)(2,1)} %bitcast.57), calls=%async_computation.2 | async-start | bytes 1179648 | tf_op jit(solution)/shard_map/all_to_all | solution.py:819
  106.1 1.2 collective-permute-start.12
  108.0 10.9 %collective-permute-start.13 = (f32[8,768]{1,0:T(8,128)S(1)}, f32[8,768]{1,0:T(8,128)S(1)}, u32[]{:S(2)}, u32[]{:S(2)}) collective-permute-start(f32[8,768]{1,0:T(8,128)S(1)} %slice_add_fusion), channel_id=1, source_target_pairs={{0,2},{1,3},{2,0},{3,1},{4,6},{5,7},{6,4},{7,5},{8,10},{9,11},{10,... | collective-permute-start | bytes 73736 | tf_op jit(solution)/shard_map/ppermute | solution.py:795
  121.7 20.7 %copy-start.10 = (bf16[8,48,768]{2,1,0:T(8,128)(2,1)}, bf16[8,48,768]{2,1,0:T(8,128)(2,1)S(1)}, u32[]{:S(2)}) copy-start(bf16[8,48,768]{2,1,0:T(8,128)(2,1)S(1)} %all-to-all-done.2) | copy-start | bytes 1769476
  121.7 8.1 %collective-permute-start.15 = (bf16[4,768,768]{2,1,0:T(8,128)(2,1)}, bf16[4,768,768]{2,1,0:T(8,128)(2,1)S(1)}, u32[]{:S(2)}, u32[]{:S(2)}) collective-permute-start(bf16[4,768,768]{2,1,0:T(8,128)(2,1)} %get-tuple-element.128), channel_id=1, source_target_pairs={{0,1},{1,0},{2,3},{3,2},{4,5},{5,4},{6,7},{7,6},{8,9},{9,8},{10,11... | collective-permute-start | bytes 14155784 | tf_op jit(solution)/shard_map/ppermute | solution.py:795
  121.7 15.7 %collective-permute-start.14 = (bf16[384,768]{1,0:T(8,128)(2,1)S(1)}, bf16[384,768]{1,0:T(8,128)(2,1)S(1)}, u32[]{:S(2)}, u32[]{:S(2)}) collective-permute-start(bf16[384,768]{1,0:T(8,128)(2,1)S(1)} %bitcast.43), channel_id=1, source_target_pairs={{0,2},{1,3},{2,0},{3,1},{4,6},{5,7},{6,4},{7,5},{8,10},{9,11},{10,... | collective-permute-start | bytes 1769480 | tf_op jit(solution)/shard_map/ppermute | solution.py:795
  129.8 4.6 %copy-start.3 = (bf16[4,768,768]{2,1,0:T(8,128)(2,1)}, bf16[4,768,768]{2,1,0:T(8,128)(2,1)S(1)}, u32[]{:S(2)}) copy-start(bf16[4,768,768]{2,1,0:T(8,128)(2,1)S(1)} %collective-permute-done.15) | copy-start | bytes 14155780
  137.4 8.0 %copy-start.18 = (bf16[384,768]{1,0:T(8,128)(2,1)}, bf16[384,768]{1,0:T(8,128)(2,1)S(1)}, u32[]{:S(2)}) copy-start(bf16[384,768]{1,0:T(8,128)(2,1)S(1)} %collective-permute-done.14.refs_2_) | copy-start | bytes 1769476
  137.4 39.8 %collective-permute-start.18 = (bf16[768,768]{1,0:T(8,128)(2,1)S(1)}, bf16[768,768]{1,0:T(8,128)(2,1)}, u32[]{:S(2)}, u32[]{:S(2)}) collective-permute-start(bf16[768,768]{1,0:T(8,128)(2,1)S(1)} %fusion.6), channel_id=1, source_target_pairs={{0,2},{1,3},{2,0},{3,1},{4,6},{5,7},{6,4},{7,5},{8,10},{9,11},{10,... | collective-permute-start | bytes 3538952 | tf_op jit(solution)/shard_map/ppermute | solution.py:795
  138.4 38.8 %all-to-all-start.3 = ((bf16[8,48,768]{2,1,0:T(8,128)(2,1)}), bf16[8,48,768]{2,1,0:T(8,128)(2,1)S(1)}, u32[]{:S(2)}, u32[]{:S(2)}) async-start(bf16[8,48,768]{2,1,0:T(8,128)(2,1)} %bitcast.56), calls=%async_computation.3 | async-start | bytes 1179648 | tf_op jit(solution)/shard_map/all_to_all | solution.py:819
  142.3 2.2 collective-permute-start.16
  142.4 3.0 %collective-permute-start.17 = (bf16[384,768]{1,0:T(8,128)(2,1)S(1)}, bf16[384,768]{1,0:T(8,128)(2,1)}, u32[]{:S(2)}, u32[]{:S(2)}) collective-permute-start(bf16[384,768]{1,0:T(8,128)(2,1)S(1)} %collective-permute-done.14.refs_2_), channel_id=1, source_target_pairs={{0,1},{1,0},{2,3},{3,2},{4,5},{5,4},{6,7},{7,6},{8,9},{9,8},{10,11... | collective-permute-start | bytes 1769480 | tf_op jit(solution)/shard_map/ppermute | solution.py:795
  142.9 34.3 %collective-permute-start.19 = (bf16[256,768]{1,0:T(8,128)(2,1)}, bf16[256,768]{1,0:T(8,128)(2,1)}, u32[]{:S(2)}, u32[]{:S(2)}) collective-permute-start(bf16[256,768]{1,0:T(8,128)(2,1)} %fusion.13), channel_id=1, source_target_pairs={{0,2},{1,3},{2,0},{3,1},{4,6},{5,7},{6,4},{7,5},{8,10},{9,11},{10,... | collective-permute-start | bytes 1179656 | tf_op jit(solution)/shard_map/ppermute | solution.py:795
  177.2 5.8 %copy-start = (f32[512,768]{1,0:T(8,128)S(1)}, f32[512,768]{1,0:T(8,128)}, u32[]{:S(2)}) copy-start(f32[512,768]{1,0:T(8,128)} %get-tuple-element.141) | copy-start | bytes 4718596
  177.2 0.8 copy-start.8
  177.2 5.8 %collective-permute-start.20 = (bf16[512,768]{1,0:T(8,128)(2,1)}, bf16[512,768]{1,0:T(8,128)(2,1)S(1)}, u32[]{:S(2)}, u32[]{:S(2)}) collective-permute-start(bf16[512,768]{1,0:T(8,128)(2,1)} %get-tuple-element.142), channel_id=1, source_target_pairs={{0,1},{1,0},{2,3},{3,2},{4,5},{5,4},{6,7},{7,6},{8,9},{9,8},{10,11... | collective-permute-start | bytes 2359304 | tf_op jit(solution)/shard_map/ppermute | solution.py:795
  178.0 35.0 %all-to-all-start.4 = ((bf16[8,96,768]{2,1,0:T(8,128)(2,1)}), bf16[8,96,768]{2,1,0:T(8,128)(2,1)S(1)}, u32[]{:S(2)}, u32[]{:S(2)}) async-start(bf16[8,96,768]{2,1,0:T(8,128)(2,1)} %bitcast.48), calls=%async_computation.4 | async-start | bytes 2359296 | tf_op jit(solution)/shard_map/all_to_all | solution.py:819
  183.0 0.9 copy-start.6
  183.9 19.3 %collective-permute-start.21 = (bf16[512,768]{1,0:T(8,128)(2,1)S(1)}, bf16[512,768]{1,0:T(8,128)(2,1)S(1)}, u32[]{:S(2)}, u32[]{:S(2)}) collective-permute-start(bf16[512,768]{1,0:T(8,128)(2,1)S(1)} %fusion.9), channel_id=1, source_target_pairs={{0,2},{1,3},{2,0},{3,1},{4,6},{5,7},{6,4},{7,5},{8,10},{9,11},{10,... | collective-permute-start | bytes 2359304 | tf_op jit(solution)/shard_map/ppermute | solution.py:795
  184.9 18.3 %copy-start.7 = (bf16[512,768]{1,0:T(8,128)(2,1)S(1)}, bf16[512,768]{1,0:T(8,128)(2,1)}, u32[]{:S(2)}) copy-start(bf16[512,768]{1,0:T(8,128)(2,1)} %copy-done.6) | copy-start | bytes 2359300
  188.8 16.0 %copy-start.32 = (f32[1,768]{1,0:T(1,128)S(1)}, f32[1,768]{1,0:T(1,128)}, u32[]{:S(2)}) copy-start(f32[1,768]{1,0:T(1,128)} %get-tuple-element.153) | copy-start | bytes 9220
  203.6 2.6 copy-start.5
  203.6 2.6 collective-permute-start.25
  206.2 0.9 copy-start.16
  213.0 1.0 copy-start.4
  218.3 5.8 %copy-start.9 = (bf16[8,48,768]{2,1,0:T(8,128)(2,1)S(1)}, bf16[8,48,768]{2,1,0:T(8,128)(2,1)}, u32[]{:S(2)}) copy-start(bf16[8,48,768]{2,1,0:T(8,128)(2,1)} %copy-done.8) | copy-start | bytes 1769476
  218.3 21.3 %copy-start.17 = (bf16[512,768]{1,0:T(8,128)(2,1)S(1)}, bf16[512,768]{1,0:T(8,128)(2,1)}, u32[]{:S(2)}) copy-start(bf16[512,768]{1,0:T(8,128)(2,1)} %fusion.10) | copy-start | bytes 2359300
  218.3 43.6 %all-to-all-start.5 = ((bf16[8,112,768]{2,1,0:T(8,128)(2,1)}), bf16[8,112,768]{2,1,0:T(8,128)(2,1)S(1)}, u32[]{:S(2)}, u32[]{:S(2)}) async-start(bf16[8,112,768]{2,1,0:T(8,128)(2,1)} %shard_map.203), calls=%async_computation.5 | async-start | bytes 2752512 | tf_op jit(solution)/shard_map/all_to_all | solution.py:819
  224.1 15.5 %collective-permute-start.22 = (bf16[384,768]{1,0:T(8,128)(2,1)S(1)}, bf16[384,768]{1,0:T(8,128)(2,1)S(1)}, u32[]{:S(2)}, u32[]{:S(2)}) collective-permute-start(bf16[384,768]{1,0:T(8,128)(2,1)S(1)} %bitcast.41), channel_id=1, source_target_pairs={{0,2},{1,3},{2,0},{3,1},{4,6},{5,7},{6,4},{7,5},{8,10},{9,11},{10,... | collective-permute-start | bytes 1769480 | tf_op jit(solution)/shard_map/ppermute | solution.py:795
  239.6 3.0 %copy-start.19 = (bf16[384,768]{1,0:T(8,128)(2,1)}, bf16[384,768]{1,0:T(8,128)(2,1)S(1)}, u32[]{:S(2)}) copy-start(bf16[384,768]{1,0:T(8,128)(2,1)S(1)} %collective-permute-done.22.refs_2_) | copy-start | bytes 1769476
  239.6 18.8 %collective-permute-start.26 = (bf16[512,768]{1,0:T(8,128)(2,1)S(1)}, bf16[512,768]{1,0:T(8,128)(2,1)S(1)}, u32[]{:S(2)}, u32[]{:S(2)}) collective-permute-start(bf16[512,768]{1,0:T(8,128)(2,1)S(1)} %copy-done.17), channel_id=1, source_target_pairs={{0,2},{1,3},{2,0},{3,1},{4,6},{5,7},{6,4},{7,5},{8,10},{9,11},{10,... | collective-permute-start | bytes 2359304 | tf_op jit(solution)/shard_map/ppermute | solution.py:795
  240.6 2.0 collective-permute-start.23
  240.6 2.8 %collective-permute-start.24 = (bf16[384,768]{1,0:T(8,128)(2,1)S(1)}, bf16[384,768]{1,0:T(8,128)(2,1)S(1)}, u32[]{:S(2)}, u32[]{:S(2)}) collective-permute-start(bf16[384,768]{1,0:T(8,128)(2,1)S(1)} %collective-permute-done.22.refs_2_), channel_id=1, source_target_pairs={{0,1},{1,0},{2,3},{3,2},{4,5},{5,4},{6,7},{7,6},{8,9},{9,8},{10,11... | collective-permute-start | bytes 1769480 | tf_op jit(solution)/shard_map/ppermute | solution.py:795
  242.6 0.8 copy-start.20
  243.4 0.8 copy-start.21
  (2 other events, 1.5 us)

commit v5 on v4

--- a/solution.py
+++ b/solution.py
@@ -654,20 +654,45 @@
     )(hidden1, gate, flat_id, ids, *blocks)
 
 
-def input_kernel(halves, kept_ref, other_ref, x_ref, gain_ref, gh_ref, low_ref, out_ref, ggain_ref):
-    step = pl.program_id(0)
-    part = jnp.where(step // halves == low_ref[0], kept_ref[...].astype(F32), other_ref[...].astype(F32))
+def chosen_half(halves, kept_ref, other_ref, low_ref):
+    mine = pl.program_id(0) // halves == low_ref[0]
+    return jnp.where(mine, kept_ref[...].astype(F32), other_ref[...].astype(F32))
+
+
+def gain_kernel(halves, kept_ref, other_ref, x_ref, low_ref, ggain_ref):
+    part = chosen_half(halves, kept_ref, other_ref, low_ref)
+    x = x_ref[...].astype(F32)
+    inverse = lax.rsqrt(jnp.mean(x * x, -1, keepdims=True) + 1e-06)
+
+    @pl.when(pl.program_id(0) == 0)
+    def _():
+        ggain_ref[...] = jnp.zeros_like(ggain_ref)
+
+    ggain_ref[...] += jnp.sum(part * (x * inverse), 0, keepdims=True)
+
+
+def input_kernel(halves, kept_ref, other_ref, x_ref, gain_ref, gh_ref, low_ref, out_ref):
+    part = chosen_half(halves, kept_ref, other_ref, low_ref)
     x = x_ref[...].astype(F32)
     inverse = lax.rsqrt(jnp.mean(x * x, -1, keepdims=True) + 1e-06)
     unit = x * inverse
     scaled = gain_ref[...] * part
     out_ref[...] = gh_ref[...] + inverse * (scaled - unit * jnp.mean(unit * scaled, -1, keepdims=True))
 
-    @pl.when(step == 0)
-    def _():
-        ggain_ref[...] = jnp.zeros_like(ggain_ref)
-
-    ggain_ref[...] += jnp.sum(part * unit, 0, keepdims=True)
+
+def gain_grads(kept, other, tokens, low_bit):
+    length, width = tokens.shape
+    halves = kept.shape[0] // QB
+    half = pl.BlockSpec((QB, width), lambda i: (i % halves, 0))
+    return pl.pallas_call(
+        functools.partial(gain_kernel, halves),
+        grid=(length // QB,),
+        out_shape=jax.ShapeDtypeStruct((1, width), F32),
+        in_specs=[half, half, rows_of(QB, width), pl.BlockSpec(memory_space=pltpu.SMEM)],
+        out_specs=whole_of(1, width),
+        compiler_params=pltpu.CompilerParams(vmem_limit_bytes=60 << 20),
+        cost_estimate=SMALL,
+    )(kept, other, tokens, low_bit)
 
 
 def input_grads(kept, other, tokens, gain, grad_hidden1, low_bit):
@@ -677,10 +702,7 @@
     return pl.pallas_call(
         functools.partial(input_kernel, halves),
         grid=(length // QB,),
-        out_shape=(
-            jax.ShapeDtypeStruct((length, width), F32),
-            jax.ShapeDtypeStruct((1, width), F32),
-        ),
+        out_shape=jax.ShapeDtypeStruct((length, width), F32),
         in_specs=[
             half,
             half,
@@ -689,7 +711,7 @@
             rows_of(QB, width),
             pl.BlockSpec(memory_space=pltpu.SMEM),
         ],
-        out_specs=(rows_of(QB, width), whole_of(1, width)),
+        out_specs=rows_of(QB, width),
         compiler_params=pltpu.CompilerParams(vmem_limit_bytes=60 << 20),
         cost_estimate=SMALL,
     )(kept, other, tokens, gain[None, :], grad_hidden1, low_bit)
@@ -884,15 +906,15 @@
     )
     near_weights = swap(sent_weights, 1)
     grad_far = gather_far(grad_back)
-    cut = width // 3
+    third = width // 3
 
     def pair(k, rows_cut):
         return kept_weights[k, rows_cut].astype(F32) + near_weights[k, rows_cut].astype(F32)
 
     out_sent = pair(1, slice(0, width)).astype(BF16)
-    fore_sent, rest_sent = pair(3, slice(0, cut)).astype(BF16), pair(3, slice(cut, width)).astype(BF16)
-    grad_far, out_sent, fore_sent, rest_sent = tie((grad_far, out_sent, fore_sent, rest_sent))
-    out_came, fore_came = swap(out_sent, 2), swap(fore_sent, 2)
+    in_sent = [pair(3, slice(i * third, (i + 1) * third)).astype(BF16) for i in range(3)]
+    grad_far, out_sent, in_sent = tie((grad_far, out_sent, in_sent))
+    out_came, fore_came = swap(out_sent, 2), swap(in_sent[0], 2)
     grad_blocks = gather_near(grad_far)
     reply_back = exchange(reply.reshape(groups, -1, width)).reshape(-1, width)
     grad_hidden1, attended_grad, grad_gain_ffn, grad_proj = leave_experts(
@@ -903,26 +925,23 @@
     grads, kept, sent, rel_parts = attend_back(
         proj, keys_t, lse, attended_grad, normed1, w_qkv_t, grad_proj, rel_bias, low_bit, segment_ids
     )
-    grads, kept, sent, reply_back, out_came, fore_came, rest_sent = tie(
-        (grads, kept, sent, reply_back, out_came, fore_came, rest_sent)
+    grads, kept, sent, reply_back, out_came, fore_came, in_sent = tie(
+        (grads, kept, sent, reply_back, out_came, fore_came, in_sent)
     )
     kept = kept + swap(sent, 1).astype(F32)
     far = swap(kept.astype(BF16), 2)
     came = exchange(grads.reshape(groups, -1, width))
     grad_w_out = pair(0, slice(0, width)) + out_came.astype(F32)
-    far, grad_w_out, reply_back = tie((far, grad_w_out, reply_back))
-    reply_far = gather_far(reply_back)
-    reply_far, rest_sent = tie((reply_far, rest_sent))
-    rest_came = swap(rest_sent, 2)
-    kept = (kept + far.astype(F32)).astype(BF16)
-    other = swap(kept, 1)
-    grad_input, gain_part = input_grads(kept, other, tokens, gain_attn, grad_hidden1, low_bit)
-    grad_w_in = pair(2, slice(0, width)) + jnp.concatenate([fore_came, rest_came], 0).astype(F32)
-
     rel_row = jnp.sum(rel_parts, -1).reshape(1, -1)
     rel_row = jnp.pad(rel_row, ((0, 0), (0, width - rel_row.shape[1])))
     small = jnp.concatenate([grad_gain_ffn, rel_row, jnp.zeros((1, width), F32), grad_router], 0)
     small = jnp.pad(small, ((0, -small.shape[0] % 16), (0, 0)))
+    far, grad_w_out, reply_back, in_sent, small = tie((far, grad_w_out, reply_back, in_sent, small))
+    middle_came = swap(in_sent[1], 2)
+    kept = (kept + far.astype(F32)).astype(BF16)
+    other = swap(kept, 1)
+    gain_part = gain_grads(kept, other, tokens, low_bit)
+
     large = came.shape[1]
     if large % 16 == 0:
         copies = sum_copies(came, small, gain_part)
@@ -930,7 +949,15 @@
         small = small.at[2].add(gain_part[0])
         copies = jnp.concatenate([jnp.sum(came.astype(F32), 0), small], 0).astype(BF16)
         copies = jnp.broadcast_to(copies[None], (groups,) + copies.shape)
+    copies, middle_came, reply_back, kept, other = tie((copies, middle_came, reply_back, kept, other))
     totals = exchange(copies)
+
+    reply_far = gather_far(reply_back)
+    reply_far, rest_sent = tie((reply_far, in_sent[2]))
+    rest_came = swap(rest_sent, 2)
+    grad_input = input_grads(kept, other, tokens, gain_attn, grad_hidden1, low_bit)
+    in_came = jnp.concatenate([fore_came, middle_came, rest_came], 0)
+    grad_w_in = pair(2, slice(0, width)) + in_came.astype(F32)
     output = output_rows(hidden1, gate, flat_column, back_ids, gather_near(reply_far))
     if large % 16 == 0:
         grad_qkv_t, grad_proj, grad_gain_ffn, rel_row, grad_gain_attn, grad_router = final_weights(

time: 266 us -> 265 us (level)
  waiting for transfers between devices: 79.7 us -> 73.1 us
  Pallas kernels: 98.7 us -> 103 us
    ppermute x27 -> x28, waiting for transfers between devices: 71.1 us -> 64.3 us  [swap(): return lax.ppermute(value, 'tensor', [(i, i ^ bit) for i in range(members)])]
    pallas_call x0 -> x1, Pallas kernels: none -> 4.46 us  [gain_grads(): pl.pallas_call(functools.partial(gain_kernel, halves), grid=(length // QB...]
    ppermute x27 -> x28, starting transfers between devices: 16.9 us -> 18 us  [swap(): return lax.ppermute(value, 'tensor', [(i, i ^ bit) for i in range(members)])]
  transfers between devices with their start and end apart: 33 -> 34, of which waited for: 18 -> 18; matrix products, arithmetic and copies ran while one was open for 12% -> 12% of each run, Pallas kernels for 29% -> 33%
where the time goes in v5:
time: 265 us; the launch traced here: 263 us
  Pallas kernels  103 us (39%)
  waiting for transfers between devices  73.1 us (28%)
  starting transfers between devices  47.7 us (18%)
  other arithmetic  20.4 us (8%)
  local copies, waits for them, and re-layouts  14 us (5%)
  matrix products  4.33 us (2%)
    ppermute x28, waiting for transfers between devices, swap(): return lax.ppermute(value, 'tensor', [(i, i ^ bit) for i in range(members)])  64.3 us
    all_to_all x6, starting transfers between devices, exchange(): lax.all_to_all(value, 'expert', split_axis=0, concat_axis=0, tiled=True)  29.7 us
    pallas_call x1, Pallas kernels, attend_back(): pl.pallas_call(functools.partial(attend_back_kernel, length, heads, inner...  20.6 us
    ppermute x28, starting transfers between devices, swap(): return lax.ppermute(value, 'tensor', [(i, i ^ bit) for i in range(members)])  18 us
    pallas_call x1, Pallas kernels, expert_step(): pl.pallas_call(functools.partial(expert_kernel, members, experts), grid=(...  14.9 us
    pallas_call x1, Pallas kernels, attend(): pl.pallas_call(functools.partial(attend_kernel, length, heads, inner // h...  14.4 us
    pallas_call x1, Pallas kernels, leave_experts(): pl.pallas_call(functools.partial(leave_kernel, members), grid=(length //...  11.2 us
    pallas_call x1, Pallas kernels, weight_grads(): pl.pallas_call(functools.partial(weight_kernel, members // 2), grid=(memb...  9.9 us
  transfers between devices with their start and end apart: 34, of which 18 were waited for; matrix products, arithmetic and copies ran while one was open for 12% of the time, Pallas kernels for 33%

profile of v5, /device:TPU:0, one launch (start us, length us, event | category | flops | bytes accessed | tf_op | source)
XLA Modules:
  0.0 263.5 jit_solution(1246672000883369555)
XLA Ops:
  0.6 3.0 %collective-permute-start = (bf16[768,768]{1,0:T(8,128)(2,1)}, bf16[768,768]{1,0:T(8,128)(2,1)}, u32[]{:S(2)}, u32[]{:S(2)}) collective-permute-start(bf16[768,768]{1,0:T(8,128)(2,1)} %bitcast.52), channel_id=1, source_target_pairs={{0,2},{1,3},{2,0},{3,1},{4,6},{5,7},{6,4},{7,5},{8,10},{9,11},{10,... | collective-permute-start | bytes 3538952 | tf_op jit(solution)/shard_map/ppermute | solution.py:817
  3.7 1.2 fusion.8
  5.8 3.1 %fusion.3 = bf16[384,768]{1,0:T(8,128)(2,1)} fusion(bf16[1024,768]{1,0:T(8,128)(2,1)} %cot_ref.1, s32[1024]{0:T(1024)S(1)} %multiply_add_fusion.1, s32[384]{0:T(512)S(1)} %add.229), kind=kOutput, calls=%fused_computation.9 | convolution fusion | flops 604667904 | bytes 2168320 | tf_op jit(solution)/shard_map/dot_general | solution.py:39
  8.9 5.8 %all-to-all-start = ((bf16[8,48,768]{2,1,0:T(8,128)(2,1)}), bf16[8,48,768]{2,1,0:T(8,128)(2,1)S(1)}, u32[]{:S(2)}, u32[]{:S(2)}) async-start(bf16[8,48,768]{2,1,0:T(8,128)(2,1)} %bitcast.4), calls=%async_computation | async-start | bytes 1179648 | tf_op jit(solution)/shard_map/all_to_all | solution.py:841
  15.9 1.0 copy.25.doc_ref
  16.9 14.4 %shard_map.195 = (bf16[192,1024]{1,0:T(8,128)(2,1)}, f32[8,1024]{1,0:T(8,128)}, bf16[1024,768]{1,0:T(8,128)(2,1)}, bf16[192,1024]{1,0:T(8,128)(2,1)}, bf16[1024,768]{1,0:T(8,128)(2,1)}) custom-call(bf16[1024,768]{1,0:T(8,128)(2,1)} %x_ref.7, f32[1,768]{1,0:T(1,128)} %broadcast_in_dim.14.gain_ref, bf16[3,192,768]{2,1,0:T(8,128)(2,1)} %bitcast.41, ...), custom_call_target="tpu_custom_call" | custom-call | flops 1048576 | bytes 65536 | tf_op jit(solution)/shard_map/pallas_call | solution.py:324
  31.3 1.6 collective-permute-start.1
  34.4 0.8 pad.17.wproj_ref
  36.7 0.9 multiply_add_fusion
  38.2 6.4 %collective-permute-done.1.refs_2_ = bf16[192,1024]{1,0:T(8,128)(2,1)S(1)} collective-permute-done((bf16[192,1024]{1,0:T(8,128)(2,1)}, bf16[192,1024]{1,0:T(8,128)(2,1)S(1)}, u32[]{:S(2)}, u32[]{:S(2)}) %collective-permute-start.1) | collective-permute-done | bytes 393248 | tf_op jit(solution)/shard_map/ppermute | solution.py:817
  45.6 0.9 collective-permute-done.5.refs_5_
  46.9 1.8 collective-permute-start.7
  48.6 0.8 copy.30.ids_ref
  49.5 0.7 copy-done.23
  50.2 0.7 copy-done.24
  51.0 8.9 %shard_map.196 = (f32[1024,768]{1,0:T(8,128)}, f32[1024,1]{1,0:T(8,128)}, bf16[384,768]{1,0:T(8,128)(2,1)}) custom-call(bf16[1024,768]{1,0:T(8,128)(2,1)} %x_ref.7, f32[1,768]{1,0:T(1,128)} %broadcast_in_dim.15.gain_ref, bf16[768,128]{1,0:T(8,128)(2,1)} %pad.16.router_ref, s32[1024,1]{1,0:T(8,128)} %copy-done.4, s32[1,1024]{1,0:T(1,128)} %add.231.flat_ref, ...), custom_call_target="tpu_custom_call" | custom-call | flops 1048576 | bytes 65536 | tf_op jit(solution)/shard_map/pallas_call | solution.py:491
  59.9 5.8 %all-to-all-start.1 = ((bf16[8,48,768]{2,1,0:T(8,128)(2,1)}), bf16[8,48,768]{2,1,0:T(8,128)(2,1)S(1)}, u32[]{:S(2)}, u32[]{:S(2)}) async-start(bf16[8,48,768]{2,1,0:T(8,128)(2,1)} %bitcast.60), calls=%async_computation.1 | async-start | bytes 1179648 | tf_op jit(solution)/shard_map/all_to_all | solution.py:841
  65.7 9.7 %collective-permute-done.7.refs_6_ = bf16[768,768]{1,0:T(8,128)(2,1)} collective-permute-done((bf16[768,768]{1,0:T(8,128)(2,1)}, bf16[768,768]{1,0:T(8,128)(2,1)}, u32[]{:S(2)}, u32[]{:S(2)}) %collective-permute-start.7) | collective-permute-done | bytes 1179680 | tf_op jit(solution)/shard_map/ppermute | solution.py:817
  75.4 6.4 %all-to-all-done.1 = bf16[8,48,768]{2,1,0:T(8,128)(2,1)S(1)} async-done(((bf16[8,48,768]{2,1,0:T(8,128)(2,1)}), bf16[8,48,768]{2,1,0:T(8,128)(2,1)S(1)}, u32[]{:S(2)}, u32[]{:S(2)}) %all-to-all-start.1) | async-done | bytes 589856 | tf_op jit(solution)/shard_map/all_to_all | solution.py:841
  82.4 3.3 %collective-permute-done.10.refs_5_ = bf16[768,768]{1,0:T(8,128)(2,1)S(1)} collective-permute-done((bf16[768,768]{1,0:T(8,128)(2,1)S(1)}, bf16[768,768]{1,0:T(8,128)(2,1)S(1)}, u32[]{:S(2)}, u32[]{:S(2)}) %collective-permute-start.10) | collective-permute-done | bytes 1179680 | tf_op jit(solution)/shard_map/ppermute | solution.py:817
  85.7 1.0 collective-permute-done.11.refs_7_
  86.8 14.9 %shard_map.197 = (bf16[384,768]{1,0:T(8,128)(2,1)}, bf16[384,768]{1,0:T(8,128)(2,1)}, bf16[4,384,768]{2,1,0:T(8,128)(2,1)}, bf16[4,384,768]{2,1,0:T(8,128)(2,1)}...) custom-call(bf16[384,768]{1,0:T(8,128)(2,1)} %bitcast.39, bf16[384,768]{1,0:T(8,128)(2,1)} %bitcast.50, ...), custom_call_target="tpu_custom_call" | custom-call | flops 1048576 | bytes 65536 | tf_op jit(solution)/shard_map/pallas_call | solution.py:441
  101.7 3.6 %all-to-all-start.2 = ((bf16[8,48,768]{2,1,0:T(8,128)(2,1)}), bf16[8,48,768]{2,1,0:T(8,128)(2,1)S(1)}, u32[]{:S(2)}, u32[]{:S(2)}) async-start(bf16[8,48,768]{2,1,0:T(8,128)(2,1)} %bitcast.59), calls=%async_computation.2 | async-start | bytes 1179648 | tf_op jit(solution)/shard_map/all_to_all | solution.py:841
  105.3 0.7 slice.43
  106.1 1.2 collective-permute-done.12
  107.2 0.7 slice_add_fusion
  108.0 1.0 collective-permute-start.13
  109.0 9.9 %shard_map.198 = (bf16[4,768,768]{2,1,0:T(8,128)(2,1)}, bf16[4,768,768]{2,1,0:T(8,128)(2,1)}) custom-call(bf16[384,768]{1,0:T(8,128)(2,1)} %bitcast.40, bf16[384,768]{1,0:T(8,128)(2,1)} %get-tuple-element.128.grads_ref, bf16[4,384,768]{2,1,0:T(8,128)(2,1)} %get-tuple-element.129.act_ref, bf16[4,384,768]{2,1,0:T(8,128)(2,1)} %get-tuple-element.130.gpre_ref), custom_call_target="tpu_custom_call" | custom-call | flops 1048576 | bytes 65536 | tf_op jit(solution)/shard_map/pallas_call | solution.py:544
  119.5 2.1 all-to-all-done.2
  121.6 1.0 collective-permute-start.14
  122.6 7.1 %collective-permute-done.15 = bf16[4,768,768]{2,1,0:T(8,128)(2,1)S(1)} collective-permute-done((bf16[4,768,768]{2,1,0:T(8,128)(2,1)}, bf16[4,768,768]{2,1,0:T(8,128)(2,1)S(1)}, u32[]{:S(2)}, u32[]{:S(2)}) %collective-permute-start.15) | collective-permute-done | bytes 4718624 | tf_op jit(solution)/shard_map/ppermute | solution.py:817
  129.7 3.3 %fusion.14 = (bf16[256,768]{1,0:T(8,128)(2,1)}, bf16[256,768]{1,0:T(8,128)(2,1)}, bf16[256,768]{1,0:T(8,128)(2,1)}) fusion(bf16[4,768,768]{2,1,0:T(8,128)(2,1)S(1)} %collective-permute-done.15, bf16[4,768,768]{2,1,0:T(8,128)(2,1)} %get-tuple-element.135), kind=kLoop, calls=%fused_computation.23 | loop fusion | flops 2359296 | bytes 3538944 | tf_op jit(solution)/shard_map/convert_element_type | solution.py:915
  133.1 1.6 fusion.6
  134.7 2.7 %collective-permute-done.14.refs_2_ = bf16[384,768]{1,0:T(8,128)(2,1)S(1)} collective-permute-done((bf16[384,768]{1,0:T(8,128)(2,1)S(1)}, bf16[384,768]{1,0:T(8,128)(2,1)S(1)}, u32[]{:S(2)}, u32[]{:S(2)}) %collective-permute-start.14) | collective-permute-done | bytes 589856 | tf_op jit(solution)/shard_map/ppermute | solution.py:817
  137.4 1.0 collective-permute-start.18
  138.3 3.9 %all-to-all-start.3 = ((bf16[8,48,768]{2,1,0:T(8,128)(2,1)}), bf16[8,48,768]{2,1,0:T(8,128)(2,1)S(1)}, u32[]{:S(2)}, u32[]{:S(2)}) async-start(bf16[8,48,768]{2,1,0:T(8,128)(2,1)} %bitcast.58), calls=%async_computation.3 | async-start | bytes 1179648 | tf_op jit(solution)/shard_map/all_to_all | solution.py:841
  142.9 1.0 collective-permute-start.19
  144.5 0.8 collective-permute-done.17.refs_3_
  145.3 11.2 %shard_map.199 = (f32[1024,768]{1,0:T(8,128)}, bf16[1024,256]{1,0:T(8,128)(2,1)}, f32[1,768]{1,0:T(1,128)}, bf16[192,768]{1,0:T(8,128)(2,1)}) custom-call(f32[1024,768]{1,0:T(8,128)} %get-tuple-element.106.hidden_ref, bf16[1024,768]{1,0:T(8,128)(2,1)} %cot_ref.1, f32[1,768]{1,0:T(1,128)} %broadcast_in_dim.15.gain_ref, ...), custom_call_target="tpu_custom_call" | custom-call | flops 1048576 | bytes 65536 | tf_op jit(solution)/shard_map/pallas_call | solution.py:598
  156.5 20.6 %shard_map.200 = (bf16[768,768]{1,0:T(8,128)(2,1)}, f32[512,768]{1,0:T(8,128)}, bf16[512,768]{1,0:T(8,128)(2,1)}, f32[3,32,128]{2,1,0:T(8,128)}) custom-call(bf16[1024,768]{1,0:T(8,128)(2,1)} %get-tuple-element.110.proj_ref, bf16[192,1024]{1,0:T(8,128)(2,1)} %get-tuple-element.111.kt_ref, f32[8,1024]{1,0:T(8,128)} %get-tuple-element.112.lse_ref, ...), custom_call_target="tpu_custom_call" | custom-call | flops 1048576 | bytes 65536 | tf_op jit(solution)/shard_map/pallas_call | solution.py:356
  177.9 5.0 %all-to-all-start.4 = ((bf16[8,96,768]{2,1,0:T(8,128)(2,1)}), bf16[8,96,768]{2,1,0:T(8,128)(2,1)S(1)}, u32[]{:S(2)}, u32[]{:S(2)}) async-start(bf16[8,96,768]{2,1,0:T(8,128)(2,1)} %bitcast.51), calls=%async_computation.4 | async-start | bytes 2359296 | tf_op jit(solution)/shard_map/all_to_all | solution.py:841
  183.0 1.0 fusion.9
  184.0 1.0 collective-permute-start.21
  185.1 0.9 reduce_sum.19
  186.0 0.8 fusion.16
  187.5 3.9 %bitcast_add_fusion = f32[768,768]{1,0:T(8,128)} fusion(bf16[768,768]{1,0:T(8,128)(2,1)} %collective-permute-done.18, bf16[4,768,768]{2,1,0:T(8,128)(2,1)} %copy-done.5, bf16[4,768,768]{2,1,0:T(8,128)(2,1)} %get-tuple-element.135), kind=kLoop, calls=%fused_computation.2 | loop fusion | flops 2949120 | bytes 5898240 | tf_op jit(solution)/shard_map/add | solution.py:934
  191.4 12.2 %collective-permute-done.21 = bf16[512,768]{1,0:T(8,128)(2,1)S(1)} collective-permute-done((bf16[512,768]{1,0:T(8,128)(2,1)}, bf16[512,768]{1,0:T(8,128)(2,1)S(1)}, u32[]{:S(2)}, u32[]{:S(2)}) %collective-permute-start.21) | collective-permute-done | bytes 786464 | tf_op jit(solution)/shard_map/ppermute | solution.py:817
  204.0 1.0 collective-permute-start.23
  205.0 1.2 collective-permute-done.22.other_ref
  206.2 0.9 copy-done.7
  207.1 4.5 %shard_map.201.ggain_ref = f32[1,768]{1,0:T(1,128)} custom-call(bf16[512,768]{1,0:T(8,128)(2,1)} %copy-done, bf16[512,768]{1,0:T(8,128)(2,1)} %copy-done.7, bf16[1024,768]{1,0:T(8,128)(2,1)} %x_ref.7, s32[1]{0:T(128)} %bitcast.18.low_ref), custom_call_target="tpu_custom_call" | custom-call | flops 1048576 | bytes 65536 | tf_op jit(solution)/shard_map/pallas_call | solution.py:687
  211.8 1.0 copy-done.6
  212.8 4.2 %shard_map.202 = bf16[8,112,768]{2,1,0:T(8,128)(2,1)} custom-call(bf16[8,96,768]{2,1,0:T(8,128)(2,1)} %copy-done.6, f32[16,768]{1,0:T(8,128)} %pad.19.small_ref, f32[1,768]{1,0:T(1,128)} %shard_map.201.ggain_ref), custom_call_target="tpu_custom_call" | custom-call | flops 1048576 | bytes 65536 | tf_op jit(solution)/shard_map/pallas_call | solution.py:738
  217.1 0.7 copy-done.21
  217.8 5.5 %all-to-all-start.5 = ((bf16[8,112,768]{2,1,0:T(8,128)(2,1)}), bf16[8,112,768]{2,1,0:T(8,128)(2,1)S(1)}, u32[]{:S(2)}, u32[]{:S(2)}) async-start(bf16[8,112,768]{2,1,0:T(8,128)(2,1)} %shard_map.202), calls=%async_computation.5 | async-start | bytes 2752512 | tf_op jit(solution)/shard_map/all_to_all | solution.py:841
  223.3 1.0 collective-permute-start.24
  224.4 14.1 %collective-permute-done.24.refs_2_ = bf16[384,768]{1,0:T(8,128)(2,1)S(1)} collective-permute-done((bf16[384,768]{1,0:T(8,128)(2,1)S(1)}, bf16[384,768]{1,0:T(8,128)(2,1)S(1)}, u32[]{:S(2)}, u32[]{:S(2)}) %collective-permute-start.24) | collective-permute-done | bytes 589856 | tf_op jit(solution)/shard_map/ppermute | solution.py:817
  238.5 1.0 collective-permute-start.27
  240.0 5.9 %shard_map.204 = f32[1024,768]{1,0:T(8,128)} custom-call(bf16[512,768]{1,0:T(8,128)(2,1)} %copy-done, bf16[512,768]{1,0:T(8,128)(2,1)} %copy-done.7, bf16[1024,768]{1,0:T(8,128)(2,1)} %x_ref.7, f32[1,768]{1,0:T(1,128)} %broadcast_in_dim.14.gain_ref, f32[1024,768]{1,0:T(8,128)} %get-tuple-element.170.gh_ref, s32[1]{0:T(128)} %bitcast.18.low_ref), custom_call_target="tpu_custom_call" | custom-call | flops 1048576 | bytes 65536 | tf_op jit(solution)/shard_map/pallas_call | solution.py:702
  245.9 2.7 %collective-permute-done.27 = bf16[256,768]{1,0:T(8,128)(2,1)} collective-permute-done((bf16[256,768]{1,0:T(8,128)(2,1)S(1)}, bf16[256,768]{1,0:T(8,128)(2,1)}, u32[]{:S(2)}, u32[]{:S(2)}) %collective-permute-start.27) | collective-permute-done | bytes 393248 | tf_op jit(solution)/shard_map/ppermute | solution.py:817
  248.6 3.7 %convert_add_fusion = f32[1,768,768]{2,1,0:T(8,128)} fusion(bf16[4,768,768]{2,1,0:T(8,128)(2,1)} %copy-done.5, bf16[1,256,768]{2,1,0:T(8,128)(2,1)} %bitcast.28, bf16[1,256,768]{2,1,0:T(8,128)(2,1)S(1)} %bitcast.61, bf16[1,256,768]{2,1,0:T(8,128)(2,1)} %bitcast.26, bf16[4,768,768]{2,1,0:T(8,128)(2,1)} %get-tuple-element.135), kind=kLoop, calls=%fused_computation.3 | loop fusion | flops 5898240 | bytes 5898240 | tf_op jit(solution)/shard_map/add | solution.py:960
  252.3 0.8 copy-done.18
  253.1 7.0 %shard_map.203 = bf16[1024,768]{1,0:T(8,128)(2,1)} custom-call(f32[1024,768]{1,0:T(8,128)} %get-tuple-element.106.hidden_ref, f32[1024,1]{1,0:T(8,128)} %get-tuple-element.107.gate_ref, s32[1024,1]{1,0:T(8,128)} %get-tuple-element.108.flat_ref, s32[1,1536]{1,0:T(1,128)} %broadcast_in_dim.16.ids_ref, bf16[384,768]{1,0:T(8,128)(2,1)} %bitcast.43, ...), custom_call_target="tpu_custom_call" | custom-call | flops 1048576 | bytes 65536 | tf_op jit(solution)/shard_map/pallas_call | solution.py:645
  260.0 1.5 shard_map.205
  (125 shorter events, 14.0 us)
Async XLA Ops:
  0.6 30.7 %collective-permute-start = (bf16[768,768]{1,0:T(8,128)(2,1)}, bf16[768,768]{1,0:T(8,128)(2,1)}, u32[]{:S(2)}, u32[]{:S(2)}) collective-permute-start(bf16[768,768]{1,0:T(8,128)(2,1)} %bitcast.52), channel_id=1, source_target_pairs={{0,2},{1,3},{2,0},{3,1},{4,6},{5,7},{6,4},{7,5},{8,10},{9,11},{10,... | collective-permute-start | bytes 3538952 | tf_op jit(solution)/shard_map/ppermute | solution.py:817
  5.8 8.9 %copy-start.13 = (bf16[192,768]{1,0:T(8,128)(2,1)S(1)}, bf16[192,768]{1,0:T(8,128)(2,1)}, u32[]{:S(2)}) copy-start(bf16[192,768]{1,0:T(8,128)(2,1)} %refs_4_) | copy-start | bytes 884740
  5.8 9.5 %copy-start.30 = (f32[768]{0:T(1024)S(1)}, f32[768]{0:T(1024)}, u32[]{:S(2)}) copy-start(f32[768]{0:T(1024)} %param.13) | copy-start | bytes 9220
  5.8 10.1 %copy-start.27 = (s32[1,1024]{1,0:T(1,128)S(1)}, s32[1,1024]{1,0:T(1,128)}, u32[]{:S(2)}) copy-start(s32[1,1024]{1,0:T(1,128)} %seg_ref.3) | copy-start | bytes 12292
  8.9 22.4 %all-to-all-start = ((bf16[8,48,768]{2,1,0:T(8,128)(2,1)}), bf16[8,48,768]{2,1,0:T(8,128)(2,1)S(1)}, u32[]{:S(2)}, u32[]{:S(2)}) async-start(bf16[8,48,768]{2,1,0:T(8,128)(2,1)} %bitcast.4), calls=%async_computation | async-start | bytes 1179648 | tf_op jit(solution)/shard_map/all_to_all | solution.py:841
  14.7 23.5 %collective-permute-start.2 = (bf16[192,768]{1,0:T(8,128)(2,1)S(1)}, bf16[192,768]{1,0:T(8,128)(2,1)}, u32[]{:S(2)}, u32[]{:S(2)}) collective-permute-start(bf16[192,768]{1,0:T(8,128)(2,1)S(1)} %copy-done.13), channel_id=1, source_target_pairs={{0,2},{1,3},{2,0},{3,1},{4,6},{5,7},{6,4},{7,5},{8,10},{9,11},{10,... | collective-permute-start | bytes 884744 | tf_op jit(solution)/shard_map/ppermute | solution.py:817
  16.9 16.3 %copy-start.28 = (s32[1024,1]{0,1:T(1,128)S(1)}, s32[1024,1]{0,1:T(1,128)}, u32[]{:S(2)}) copy-start(s32[1024,1]{0,1:T(1,128)} %param.21) | copy-start | bytes 12292
  16.9 16.6 %copy-start.31 = (f32[768]{0:T(1024)S(1)}, f32[768]{0:T(1024)}, u32[]{:S(2)}) copy-start(f32[768]{0:T(1024)} %param.17) | copy-start | bytes 9220
  16.9 17.3 %copy-start.29 = (bf16[768,8]{0,1:T(8,128)(2,1)S(1)}, bf16[768,8]{0,1:T(8,128)(2,1)}, u32[]{:S(2)}) copy-start(bf16[768,8]{0,1:T(8,128)(2,1)} %param.18) | copy-start | bytes 36868
  31.3 6.3 %copy-start.11 = (bf16[8,48,768]{2,1,0:T(8,128)(2,1)}, bf16[8,48,768]{2,1,0:T(8,128)(2,1)S(1)}, u32[]{:S(2)}) copy-start(bf16[8,48,768]{2,1,0:T(8,128)(2,1)S(1)} %all-to-all-done) | copy-start | bytes 1769476
  31.3 13.3 %collective-permute-start.1 = (bf16[192,1024]{1,0:T(8,128)(2,1)}, bf16[192,1024]{1,0:T(8,128)(2,1)S(1)}, u32[]{:S(2)}, u32[]{:S(2)}) collective-permute-start(bf16[192,1024]{1,0:T(8,128)(2,1)} %get-tuple-element.102.refs_0_.att_ref), channel_id=1, source_target_pairs={{0,2},{1,3},{2,0},{3,1},{4,6},{5,7},{6,4},{7,5},{8,10},{9,11},{10,... | collective-permute-start | bytes 1179656 | tf_op jit(solution)/shard_map/ppermute | solution.py:817
  33.4 4.2 %copy-start.4 = (s32[1024,1]{1,0:T(8,128)}, s32[1024,1]{1,0:T(8,128)S(1)}, u32[]{:S(2)}) copy-start(s32[1024,1]{1,0:T(8,128)S(1)} %copy.27.route_ref) | copy-start | bytes 12292
  34.4 10.8 %copy-start.12 = (bf16[192,1024]{1,0:T(8,128)(2,1)S(1)}, bf16[192,1024]{1,0:T(8,128)(2,1)}, u32[]{:S(2)}) copy-start(bf16[192,1024]{1,0:T(8,128)(2,1)} %get-tuple-element.102.refs_0_.att_ref) | copy-start | bytes 1179652
  44.6 4.9 %copy-start.20 = (bf16[192,1024]{1,0:T(8,128)(2,1)}, bf16[192,1024]{1,0:T(8,128)(2,1)S(1)}, u32[]{:S(2)}) copy-start(bf16[192,1024]{1,0:T(8,128)(2,1)S(1)} %collective-permute-done.1.refs_2_) | copy-start | bytes 1179652
  44.6 2.0 collective-permute-start.5
  44.6 2.3 collective-permute-start.6
  45.1 4.4 %collective-permute-start.3 = (bf16[192,1024]{1,0:T(8,128)(2,1)S(1)}, bf16[192,1024]{1,0:T(8,128)(2,1)S(1)}, u32[]{:S(2)}, u32[]{:S(2)}) collective-permute-start(bf16[192,1024]{1,0:T(8,128)(2,1)S(1)} %copy-done.12), channel_id=1, source_target_pairs={{0,1},{1,0},{2,3},{3,2},{4,5},{5,4},{6,7},{7,6},{8,9},{9,8},{10,11... | collective-permute-start | bytes 1179656 | tf_op jit(solution)/shard_map/ppermute | solution.py:817
  45.1 4.4 %collective-permute-start.4 = (bf16[192,1024]{1,0:T(8,128)(2,1)S(1)}, bf16[192,1024]{1,0:T(8,128)(2,1)S(1)}, u32[]{:S(2)}, u32[]{:S(2)}) collective-permute-start(bf16[192,1024]{1,0:T(8,128)(2,1)S(1)} %collective-permute-done.1.refs_2_), channel_id=1, source_target_pairs={{0,1},{1,0},{2,3},{3,2},{4,5},{5,4},{6,7},{7,6},{8,9},{9,8},{10,11... | collective-permute-start | bytes 1179656 | tf_op jit(solution)/shard_map/ppermute | solution.py:817
  45.6 20.1 %collective-permute-start.8 = (bf16[768,768]{1,0:T(8,128)(2,1)}, bf16[768,768]{1,0:T(8,128)(2,1)}, u32[]{:S(2)}, u32[]{:S(2)}) collective-permute-start(bf16[768,768]{1,0:T(8,128)(2,1)} %bitcast.53), channel_id=1, source_target_pairs={{0,1},{1,0},{2,3},{3,2},{4,5},{5,4},{6,7},{7,6},{8,9},{9,8},{10,11... | collective-permute-start | bytes 3538952 | tf_op jit(solution)/shard_map/ppermute | solution.py:817
  46.6 2.1 copy-start.25
  46.6 19.2 %collective-permute-start.9 = (bf16[768,768]{1,0:T(8,128)(2,1)}, bf16[768,768]{1,0:T(8,128)(2,1)}, u32[]{:S(2)}, u32[]{:S(2)}) collective-permute-start(bf16[768,768]{1,0:T(8,128)(2,1)} %collective-permute-done.refs_2_), channel_id=1, source_target_pairs={{0,1},{1,0},{2,3},{3,2},{4,5},{5,4},{6,7},{7,6},{8,9},{9,8},{10,11... | collective-permute-start | bytes 3538952 | tf_op jit(solution)/shard_map/ppermute | solution.py:817
  46.9 1.8 copy-start.26
  46.9 28.6 %collective-permute-start.7 = (bf16[768,768]{1,0:T(8,128)(2,1)}, bf16[768,768]{1,0:T(8,128)(2,1)}, u32[]{:S(2)}, u32[]{:S(2)}) collective-permute-start(bf16[768,768]{1,0:T(8,128)(2,1)} %bitcast.55), channel_id=1, source_target_pairs={{0,2},{1,3},{2,0},{3,1},{4,6},{5,7},{6,4},{7,5},{8,10},{9,11},{10,... | collective-permute-start | bytes 3538952 | tf_op jit(solution)/shard_map/ppermute | solution.py:817
  49.5 32.4 %copy-start.14 = (bf16[1,768,768]{2,1,0:T(8,128)(2,1)S(1)}, bf16[1,768,768]{2,1,0:T(8,128)(2,1)}, u32[]{:S(2)}) copy-start(bf16[1,768,768]{2,1,0:T(8,128)(2,1)} %param.20) | copy-start | bytes 3538948
  59.9 22.0 %all-to-all-start.1 = ((bf16[8,48,768]{2,1,0:T(8,128)(2,1)}), bf16[8,48,768]{2,1,0:T(8,128)(2,1)S(1)}, u32[]{:S(2)}, u32[]{:S(2)}) async-start(bf16[8,48,768]{2,1,0:T(8,128)(2,1)} %bitcast.60), calls=%async_computation.1 | async-start | bytes 1179648 | tf_op jit(solution)/shard_map/all_to_all | solution.py:841
  81.9 4.9 %copy-start.3 = (bf16[8,48,768]{2,1,0:T(8,128)(2,1)}, bf16[8,48,768]{2,1,0:T(8,128)(2,1)S(1)}, u32[]{:S(2)}) copy-start(bf16[8,48,768]{2,1,0:T(8,128)(2,1)S(1)} %all-to-all-done.1) | copy-start | bytes 1769476
  81.9 3.8 %collective-permute-start.10 = (bf16[768,768]{1,0:T(8,128)(2,1)S(1)}, bf16[768,768]{1,0:T(8,128)(2,1)S(1)}, u32[]{:S(2)}, u32[]{:S(2)}) collective-permute-start(bf16[768,768]{1,0:T(8,128)(2,1)S(1)} %bitcast.57), channel_id=1, source_target_pairs={{0,1},{1,0},{2,3},{3,2},{4,5},{5,4},{6,7},{7,6},{8,9},{9,8},{10,11... | collective-permute-start | bytes 3538952 | tf_op jit(solution)/shard_map/ppermute | solution.py:817
  81.9 4.9 %collective-permute-start.11 = (bf16[768,768]{1,0:T(8,128)(2,1)}, bf16[768,768]{1,0:T(8,128)(2,1)}, u32[]{:S(2)}, u32[]{:S(2)}) collective-permute-start(bf16[768,768]{1,0:T(8,128)(2,1)} %collective-permute-done.7.refs_6_), channel_id=1, source_target_pairs={{0,1},{1,0},{2,3},{3,2},{4,5},{5,4},{6,7},{7,6},{8,9},{9,8},{10,11... | collective-permute-start | bytes 3538952 | tf_op jit(solution)/shard_map/ppermute | solution.py:817
  85.7 1.1 copy-start.15
  101.7 19.9 %all-to-all-start.2 = ((bf16[8,48,768]{2,1,0:T(8,128)(2,1)}), bf16[8,48,768]{2,1,0:T(8,128)(2,1)S(1)}, u32[]{:S(2)}, u32[]{:S(2)}) async-start(bf16[8,48,768]{2,1,0:T(8,128)(2,1)} %bitcast.59), calls=%async_computation.2 | async-start | bytes 1179648 | tf_op jit(solution)/shard_map/all_to_all | solution.py:841
  106.0 1.2 collective-permute-start.12
  108.0 10.9 %collective-permute-start.13 = (f32[8,768]{1,0:T(8,128)S(1)}, f32[8,768]{1,0:T(8,128)S(1)}, u32[]{:S(2)}, u32[]{:S(2)}) collective-permute-start(f32[8,768]{1,0:T(8,128)S(1)} %slice_add_fusion), channel_id=1, source_target_pairs={{0,2},{1,3},{2,0},{3,1},{4,6},{5,7},{6,4},{7,5},{8,10},{9,11},{10,... | collective-permute-start | bytes 73736 | tf_op jit(solution)/shard_map/ppermute | solution.py:817
  121.6 20.7 %copy-start.10 = (bf16[8,48,768]{2,1,0:T(8,128)(2,1)}, bf16[8,48,768]{2,1,0:T(8,128)(2,1)S(1)}, u32[]{:S(2)}) copy-start(bf16[8,48,768]{2,1,0:T(8,128)(2,1)S(1)} %all-to-all-done.2) | copy-start | bytes 1769476
  121.6 8.1 %collective-permute-start.15 = (bf16[4,768,768]{2,1,0:T(8,128)(2,1)}, bf16[4,768,768]{2,1,0:T(8,128)(2,1)S(1)}, u32[]{:S(2)}, u32[]{:S(2)}) collective-permute-start(bf16[4,768,768]{2,1,0:T(8,128)(2,1)} %get-tuple-element.136), channel_id=1, source_target_pairs={{0,1},{1,0},{2,3},{3,2},{4,5},{5,4},{6,7},{7,6},{8,9},{9,8},{10,11... | collective-permute-start | bytes 14155784 | tf_op jit(solution)/shard_map/ppermute | solution.py:817
  121.6 15.7 %collective-permute-start.14 = (bf16[384,768]{1,0:T(8,128)(2,1)S(1)}, bf16[384,768]{1,0:T(8,128)(2,1)S(1)}, u32[]{:S(2)}, u32[]{:S(2)}) collective-permute-start(bf16[384,768]{1,0:T(8,128)(2,1)S(1)} %bitcast.46), channel_id=1, source_target_pairs={{0,2},{1,3},{2,0},{3,1},{4,6},{5,7},{6,4},{7,5},{8,10},{9,11},{10,... | collective-permute-start | bytes 1769480 | tf_op jit(solution)/shard_map/ppermute | solution.py:817
  129.7 3.3 %copy-start.5 = (bf16[4,768,768]{2,1,0:T(8,128)(2,1)}, bf16[4,768,768]{2,1,0:T(8,128)(2,1)S(1)}, u32[]{:S(2)}) copy-start(bf16[4,768,768]{2,1,0:T(8,128)(2,1)S(1)} %collective-permute-done.15) | copy-start | bytes 14155780
  137.3 8.0 %copy-start.16 = (bf16[384,768]{1,0:T(8,128)(2,1)}, bf16[384,768]{1,0:T(8,128)(2,1)S(1)}, u32[]{:S(2)}) copy-start(bf16[384,768]{1,0:T(8,128)(2,1)S(1)} %collective-permute-done.14.refs_2_) | copy-start | bytes 1769476
  137.4 39.8 %collective-permute-start.18 = (bf16[768,768]{1,0:T(8,128)(2,1)S(1)}, bf16[768,768]{1,0:T(8,128)(2,1)}, u32[]{:S(2)}, u32[]{:S(2)}) collective-permute-start(bf16[768,768]{1,0:T(8,128)(2,1)S(1)} %fusion.6), channel_id=1, source_target_pairs={{0,2},{1,3},{2,0},{3,1},{4,6},{5,7},{6,4},{7,5},{8,10},{9,11},{10,... | collective-permute-start | bytes 3538952 | tf_op jit(solution)/shard_map/ppermute | solution.py:817
  138.3 38.8 %all-to-all-start.3 = ((bf16[8,48,768]{2,1,0:T(8,128)(2,1)}), bf16[8,48,768]{2,1,0:T(8,128)(2,1)S(1)}, u32[]{:S(2)}, u32[]{:S(2)}) async-start(bf16[8,48,768]{2,1,0:T(8,128)(2,1)} %bitcast.58), calls=%async_computation.3 | async-start | bytes 1179648 | tf_op jit(solution)/shard_map/all_to_all | solution.py:841
  142.3 2.2 collective-permute-start.16
  142.4 3.0 %collective-permute-start.17 = (bf16[384,768]{1,0:T(8,128)(2,1)S(1)}, bf16[384,768]{1,0:T(8,128)(2,1)}, u32[]{:S(2)}, u32[]{:S(2)}) collective-permute-start(bf16[384,768]{1,0:T(8,128)(2,1)S(1)} %collective-permute-done.14.refs_2_), channel_id=1, source_target_pairs={{0,1},{1,0},{2,3},{3,2},{4,5},{5,4},{6,7},{7,6},{8,9},{9,8},{10,11... | collective-permute-start | bytes 1769480 | tf_op jit(solution)/shard_map/ppermute | solution.py:817
  142.9 34.2 %collective-permute-start.19 = (bf16[256,768]{1,0:T(8,128)(2,1)}, bf16[256,768]{1,0:T(8,128)(2,1)}, u32[]{:S(2)}, u32[]{:S(2)}) collective-permute-start(bf16[256,768]{1,0:T(8,128)(2,1)} %get-tuple-element.147), channel_id=1, source_target_pairs={{0,2},{1,3},{2,0},{3,1},{4,6},{5,7},{6,4},{7,5},{8,10},{9,11},{10,... | collective-permute-start | bytes 1179656 | tf_op jit(solution)/shard_map/ppermute | solution.py:817
  177.1 5.9 %copy-start.1 = (f32[512,768]{1,0:T(8,128)S(1)}, f32[512,768]{1,0:T(8,128)}, u32[]{:S(2)}) copy-start(f32[512,768]{1,0:T(8,128)} %get-tuple-element.151) | copy-start | bytes 4718596
  177.1 0.8 copy-start.8
  177.1 5.8 %collective-permute-start.20 = (bf16[512,768]{1,0:T(8,128)(2,1)}, bf16[512,768]{1,0:T(8,128)(2,1)S(1)}, u32[]{:S(2)}, u32[]{:S(2)}) collective-permute-start(bf16[512,768]{1,0:T(8,128)(2,1)} %get-tuple-element.152), channel_id=1, source_target_pairs={{0,1},{1,0},{2,3},{3,2},{4,5},{5,4},{6,7},{7,6},{8,9},{9,8},{10,11... | collective-permute-start | bytes 2359304 | tf_op jit(solution)/shard_map/ppermute | solution.py:817
  177.9 33.9 %all-to-all-start.4 = ((bf16[8,96,768]{2,1,0:T(8,128)(2,1)}), bf16[8,96,768]{2,1,0:T(8,128)(2,1)S(1)}, u32[]{:S(2)}, u32[]{:S(2)}) async-start(bf16[8,96,768]{2,1,0:T(8,128)(2,1)} %bitcast.51), calls=%async_computation.4 | async-start | bytes 2359296 | tf_op jit(solution)/shard_map/all_to_all | solution.py:841
  183.0 3.1 %copy-start.32 = (f32[1,768]{1,0:T(1,128)S(1)}, f32[1,768]{1,0:T(1,128)}, u32[]{:S(2)}) copy-start(f32[1,768]{1,0:T(1,128)} %get-tuple-element.157) | copy-start | bytes 9220
  184.0 19.5 %collective-permute-start.21 = (bf16[512,768]{1,0:T(8,128)(2,1)}, bf16[512,768]{1,0:T(8,128)(2,1)S(1)}, u32[]{:S(2)}, u32[]{:S(2)}) collective-permute-start(bf16[512,768]{1,0:T(8,128)(2,1)} %fusion.9), channel_id=1, source_target_pairs={{0,2},{1,3},{2,0},{3,1},{4,6},{5,7},{6,4},{7,5},{8,10},{9,11},{10,... | collective-permute-start | bytes 2359304 | tf_op jit(solution)/shard_map/ppermute | solution.py:817
  187.5 16.0 %copy-start.2 = (f32[512,768]{1,0:T(8,128)S(1)}, f32[512,768]{1,0:T(8,128)}, u32[]{:S(2)}) copy-start(f32[512,768]{1,0:T(8,128)} %get-tuple-element.151) | copy-start | bytes 4718596
  203.9 2.4 copy-start
  203.9 2.4 collective-permute-start.22
  204.0 13.1 %collective-permute-start.23 = (bf16[256,768]{1,0:T(8,128)(2,1)}, bf16[256,768]{1,0:T(8,128)(2,1)S(1)}, u32[]{:S(2)}, u32[]{:S(2)}) collective-permute-start(bf16[256,768]{1,0:T(8,128)(2,1)} %get-tuple-element.162), channel_id=1, source_target_pairs={{0,2},{1,3},{2,0},{3,1},{4,6},{5,7},{6,4},{7,5},{8,10},{9,11},{10,... | collective-permute-start | bytes 1179656 | tf_op jit(solution)/shard_map/ppermute | solution.py:817
  206.2 0.9 copy-start.7
  211.8 1.0 copy-start.6
  217.1 6.2 %copy-start.9 = (bf16[8,48,768]{2,1,0:T(8,128)(2,1)S(1)}, bf16[8,48,768]{2,1,0:T(8,128)(2,1)}, u32[]{:S(2)}) copy-start(bf16[8,48,768]{2,1,0:T(8,128)(2,1)} %copy-done.8) | copy-start | bytes 1769476
  217.1 21.4 %copy-start.19 = (bf16[256,768]{1,0:T(8,128)(2,1)S(1)}, bf16[256,768]{1,0:T(8,128)(2,1)}, u32[]{:S(2)}) copy-start(bf16[256,768]{1,0:T(8,128)(2,1)} %get-tuple-element.180) | copy-start | bytes 1179652
  217.8 42.2 %all-to-all-start.5 = ((bf16[8,112,768]{2,1,0:T(8,128)(2,1)}), bf16[8,112,768]{2,1,0:T(8,128)(2,1)S(1)}, u32[]{:S(2)}, u32[]{:S(2)}) async-start(bf16[8,112,768]{2,1,0:T(8,128)(2,1)} %shard_map.202), calls=%async_computation.5 | async-start | bytes 2752512 | tf_op jit(solution)/shard_map/all_to_all | solution.py:841
  223.3 15.2 %collective-permute-start.24 = (bf16[384,768]{1,0:T(8,128)(2,1)S(1)}, bf16[384,768]{1,0:T(8,128)(2,1)S(1)}, u32[]{:S(2)}, u32[]{:S(2)}) collective-permute-start(bf16[384,768]{1,0:T(8,128)(2,1)S(1)} %bitcast.44), channel_id=1, source_target_pairs={{0,2},{1,3},{2,0},{3,1},{4,6},{5,7},{6,4},{7,5},{8,10},{9,11},{10,... | collective-permute-start | bytes 1769480 | tf_op jit(solution)/shard_map/ppermute | solution.py:817
  238.5 7.4 %copy-start.17 = (bf16[384,768]{1,0:T(8,128)(2,1)}, bf16[384,768]{1,0:T(8,128)(2,1)S(1)}, u32[]{:S(2)}) copy-start(bf16[384,768]{1,0:T(8,128)(2,1)S(1)} %collective-permute-done.24.refs_2_) | copy-start | bytes 1769476
  238.5 10.1 %collective-permute-start.27 = (bf16[256,768]{1,0:T(8,128)(2,1)S(1)}, bf16[256,768]{1,0:T(8,128)(2,1)}, u32[]{:S(2)}, u32[]{:S(2)}) collective-permute-start(bf16[256,768]{1,0:T(8,128)(2,1)S(1)} %copy-done.19), channel_id=1, source_target_pairs={{0,2},{1,3},{2,0},{3,1},{4,6},{5,7},{6,4},{7,5},{8,10},{9,11},{10,... | collective-permute-start | bytes 1179656 | tf_op jit(solution)/shard_map/ppermute | solution.py:817
  239.5 12.8 %collective-permute-start.25 = (bf16[384,768]{1,0:T(8,128)(2,1)S(1)}, bf16[384,768]{1,0:T(8,128)(2,1)S(1)}, u32[]{:S(2)}, u32[]{:S(2)}) collective-permute-start(bf16[384,768]{1,0:T(8,128)(2,1)S(1)} %bitcast.45), channel_id=1, source_target_pairs={{0,1},{1,0},{2,3},{3,2},{4,5},{5,4},{6,7},{7,6},{8,9},{9,8},{10,11... | collective-permute-start | bytes 1769480 | tf_op jit(solution)/shard_map/ppermute | solution.py:817
  239.5 12.8 %collective-permute-start.26 = (bf16[384,768]{1,0:T(8,128)(2,1)S(1)}, bf16[384,768]{1,0:T(8,128)(2,1)}, u32[]{:S(2)}, u32[]{:S(2)}) collective-permute-start(bf16[384,768]{1,0:T(8,128)(2,1)S(1)} %collective-permute-done.24.refs_2_), channel_id=1, source_target_pairs={{0,1},{1,0},{2,3},{3,2},{4,5},{5,4},{6,7},{7,6},{8,9},{9,8},{10,11... | collective-permute-start | bytes 1769480 | tf_op jit(solution)/shard_map/ppermute | solution.py:817
  240.0 8.6 %copy-start.22 = (bf16[256,768]{1,0:T(8,128)(2,1)S(1)}, bf16[256,768]{1,0:T(8,128)(2,1)}, u32[]{:S(2)}) copy-start(bf16[256,768]{1,0:T(8,128)(2,1)} %copy-done.21) | copy-start | bytes 1179652
  252.3 0.8 copy-start.18
  (3 other events, 2.2 us)

commit v6 on v5

--- a/solution.py
+++ b/solution.py
@@ -953,9 +953,9 @@
     totals = exchange(copies)
 
     reply_far = gather_far(reply_back)
-    reply_far, rest_sent = tie((reply_far, in_sent[2]))
+    grad_input = input_grads(kept, other, tokens, gain_attn, grad_hidden1, low_bit)
+    reply_far, rest_sent, grad_input = tie((reply_far, in_sent[2], grad_input))
     rest_came = swap(rest_sent, 2)
-    grad_input = input_grads(kept, other, tokens, gain_attn, grad_hidden1, low_bit)
     in_came = jnp.concatenate([fore_came, middle_came, rest_came], 0)
     grad_w_in = pair(2, slice(0, width)) + in_came.astype(F32)
     output = output_rows(hidden1, gate, flat_column, back_ids, gather_near(reply_far))

time: 265 us -> 266 us (level)
    unnamed x68 -> x70, local copies, waits for them, and re-layouts: 6 us -> 6.24 us
where the time goes in v6:
time: 266 us; the launch traced here: 264 us
  Pallas kernels  103 us (39%)
  waiting for transfers between devices  72.8 us (27%)
  starting transfers between devices  48.7 us (18%)
  other arithmetic  20.3 us (8%)
  local copies, waits for them, and re-layouts  14.3 us (5%)
  matrix products  4.33 us (2%)
    ppermute x28, waiting for transfers between devices, swap(): return lax.ppermute(value, 'tensor', [(i, i ^ bit) for i in range(members)])  64 us
    all_to_all x6, starting transfers between devices, exchange(): lax.all_to_all(value, 'expert', split_axis=0, concat_axis=0, tiled=True)  30.6 us
    pallas_call x1, Pallas kernels, attend_back(): pl.pallas_call(functools.partial(attend_back_kernel, length, heads, inner...  20.6 us
    ppermute x28, starting transfers between devices, swap(): return lax.ppermute(value, 'tensor', [(i, i ^ bit) for i in range(members)])  18.1 us
    pallas_call x1, Pallas kernels, expert_step(): pl.pallas_call(functools.partial(expert_kernel, members, experts), grid=(...  14.9 us
    pallas_call x1, Pallas kernels, attend(): pl.pallas_call(functools.partial(attend_kernel, length, heads, inner // h...  14.4 us
    pallas_call x1, Pallas kernels, leave_experts(): pl.pallas_call(functools.partial(leave_kernel, members), grid=(length //...  11.2 us
    pallas_call x1, Pallas kernels, weight_grads(): pl.pallas_call(functools.partial(weight_kernel, members // 2), grid=(memb...  9.91 us
  transfers between devices with their start and end apart: 34, of which 18 were waited for; matrix products, arithmetic and copies ran while one was open for 12% of the time, Pallas kernels for 33%

profile of v6, /device:TPU:0, one launch (start us, length us, event | category | flops | bytes accessed | tf_op | source)
XLA Modules:
  0.0 264.4 jit_solution(16720580680990142908)
XLA Ops:
  0.6 3.0 %collective-permute-start = (bf16[768,768]{1,0:T(8,128)(2,1)}, bf16[768,768]{1,0:T(8,128)(2,1)}, u32[]{:S(2)}, u32[]{:S(2)}) collective-permute-start(bf16[768,768]{1,0:T(8,128)(2,1)} %bitcast.52), channel_id=1, source_target_pairs={{0,2},{1,3},{2,0},{3,1},{4,6},{5,7},{6,4},{7,5},{8,10},{9,11},{10,... | collective-permute-start | bytes 3538952 | tf_op jit(solution)/shard_map/ppermute | solution.py:817
  3.7 1.2 fusion.8
  5.8 3.1 %fusion.3 = bf16[384,768]{1,0:T(8,128)(2,1)} fusion(bf16[1024,768]{1,0:T(8,128)(2,1)} %cot_ref.1, s32[1024]{0:T(1024)S(1)} %multiply_add_fusion.1, s32[384]{0:T(512)S(1)} %add.229), kind=kOutput, calls=%fused_computation.9 | convolution fusion | flops 604667904 | bytes 2168320 | tf_op jit(solution)/shard_map/dot_general | solution.py:39
  8.9 5.8 %all-to-all-start = ((bf16[8,48,768]{2,1,0:T(8,128)(2,1)}), bf16[8,48,768]{2,1,0:T(8,128)(2,1)S(1)}, u32[]{:S(2)}, u32[]{:S(2)}) async-start(bf16[8,48,768]{2,1,0:T(8,128)(2,1)} %bitcast.4), calls=%async_computation | async-start | bytes 1179648 | tf_op jit(solution)/shard_map/all_to_all | solution.py:841
  15.9 1.0 copy.25.doc_ref
  16.9 14.4 %shard_map.195 = (bf16[192,1024]{1,0:T(8,128)(2,1)}, f32[8,1024]{1,0:T(8,128)}, bf16[1024,768]{1,0:T(8,128)(2,1)}, bf16[192,1024]{1,0:T(8,128)(2,1)}, bf16[1024,768]{1,0:T(8,128)(2,1)}) custom-call(bf16[1024,768]{1,0:T(8,128)(2,1)} %x_ref.7, f32[1,768]{1,0:T(1,128)} %broadcast_in_dim.14.gain_ref, bf16[3,192,768]{2,1,0:T(8,128)(2,1)} %bitcast.41, ...), custom_call_target="tpu_custom_call" | custom-call | flops 1048576 | bytes 65536 | tf_op jit(solution)/shard_map/pallas_call | solution.py:324
  31.4 1.6 collective-permute-start.1
  34.4 0.8 pad.17.wproj_ref
  35.2 0.7 pad.16.router_ref
  36.7 0.9 multiply_add_fusion
  38.2 6.4 %collective-permute-done.1.refs_2_ = bf16[192,1024]{1,0:T(8,128)(2,1)S(1)} collective-permute-done((bf16[192,1024]{1,0:T(8,128)(2,1)}, bf16[192,1024]{1,0:T(8,128)(2,1)S(1)}, u32[]{:S(2)}, u32[]{:S(2)}) %collective-permute-start.1) | collective-permute-done | bytes 393248 | tf_op jit(solution)/shard_map/ppermute | solution.py:817
  45.6 0.9 collective-permute-done.5.refs_5_
  46.9 1.8 collective-permute-start.7
  48.6 0.8 copy.30.ids_ref
  50.2 0.8 copy-done.25
  51.0 8.9 %shard_map.196 = (f32[1024,768]{1,0:T(8,128)}, f32[1024,1]{1,0:T(8,128)}, bf16[384,768]{1,0:T(8,128)(2,1)}) custom-call(bf16[1024,768]{1,0:T(8,128)(2,1)} %x_ref.7, f32[1,768]{1,0:T(1,128)} %broadcast_in_dim.15.gain_ref, bf16[768,128]{1,0:T(8,128)(2,1)} %pad.16.router_ref, s32[1024,1]{1,0:T(8,128)} %copy-done.4, s32[1,1024]{1,0:T(1,128)} %add.231.flat_ref, ...), custom_call_target="tpu_custom_call" | custom-call | flops 1048576 | bytes 65536 | tf_op jit(solution)/shard_map/pallas_call | solution.py:491
  59.9 5.8 %all-to-all-start.1 = ((bf16[8,48,768]{2,1,0:T(8,128)(2,1)}), bf16[8,48,768]{2,1,0:T(8,128)(2,1)S(1)}, u32[]{:S(2)}, u32[]{:S(2)}) async-start(bf16[8,48,768]{2,1,0:T(8,128)(2,1)} %bitcast.60), calls=%async_computation.1 | async-start | bytes 1179648 | tf_op jit(solution)/shard_map/all_to_all | solution.py:841
  65.8 9.7 %collective-permute-done.7.refs_6_ = bf16[768,768]{1,0:T(8,128)(2,1)} collective-permute-done((bf16[768,768]{1,0:T(8,128)(2,1)}, bf16[768,768]{1,0:T(8,128)(2,1)}, u32[]{:S(2)}, u32[]{:S(2)}) %collective-permute-start.7) | collective-permute-done | bytes 1179680 | tf_op jit(solution)/shard_map/ppermute | solution.py:817
  75.4 6.4 %all-to-all-done.1 = bf16[8,48,768]{2,1,0:T(8,128)(2,1)S(1)} async-done(((bf16[8,48,768]{2,1,0:T(8,128)(2,1)}), bf16[8,48,768]{2,1,0:T(8,128)(2,1)S(1)}, u32[]{:S(2)}, u32[]{:S(2)}) %all-to-all-start.1) | async-done | bytes 589856 | tf_op jit(solution)/shard_map/all_to_all | solution.py:841
  82.4 3.3 %collective-permute-done.10.refs_5_ = bf16[768,768]{1,0:T(8,128)(2,1)S(1)} collective-permute-done((bf16[768,768]{1,0:T(8,128)(2,1)S(1)}, bf16[768,768]{1,0:T(8,128)(2,1)S(1)}, u32[]{:S(2)}, u32[]{:S(2)}) %collective-permute-start.10) | collective-permute-done | bytes 1179680 | tf_op jit(solution)/shard_map/ppermute | solution.py:817
  85.7 1.0 collective-permute-done.11.refs_7_
  86.8 14.9 %shard_map.197 = (bf16[384,768]{1,0:T(8,128)(2,1)}, bf16[384,768]{1,0:T(8,128)(2,1)}, bf16[4,384,768]{2,1,0:T(8,128)(2,1)}, bf16[4,384,768]{2,1,0:T(8,128)(2,1)}...) custom-call(bf16[384,768]{1,0:T(8,128)(2,1)} %bitcast.39, bf16[384,768]{1,0:T(8,128)(2,1)} %bitcast.50, ...), custom_call_target="tpu_custom_call" | custom-call | flops 1048576 | bytes 65536 | tf_op jit(solution)/shard_map/pallas_call | solution.py:441
  101.7 3.6 %all-to-all-start.2 = ((bf16[8,48,768]{2,1,0:T(8,128)(2,1)}), bf16[8,48,768]{2,1,0:T(8,128)(2,1)S(1)}, u32[]{:S(2)}, u32[]{:S(2)}) async-start(bf16[8,48,768]{2,1,0:T(8,128)(2,1)} %bitcast.59), calls=%async_computation.2 | async-start | bytes 1179648 | tf_op jit(solution)/shard_map/all_to_all | solution.py:841
  105.3 0.7 slice.43
  106.1 1.1 collective-permute-done.12
  107.3 0.7 slice_add_fusion
  108.0 1.0 collective-permute-start.13
  109.0 9.9 %shard_map.198 = (bf16[4,768,768]{2,1,0:T(8,128)(2,1)}, bf16[4,768,768]{2,1,0:T(8,128)(2,1)}) custom-call(bf16[384,768]{1,0:T(8,128)(2,1)} %bitcast.40, bf16[384,768]{1,0:T(8,128)(2,1)} %get-tuple-element.129.grads_ref, bf16[4,384,768]{2,1,0:T(8,128)(2,1)} %get-tuple-element.130.act_ref, bf16[4,384,768]{2,1,0:T(8,128)(2,1)} %get-tuple-element.131.gpre_ref), custom_call_target="tpu_custom_call" | custom-call | flops 1048576 | bytes 65536 | tf_op jit(solution)/shard_map/pallas_call | solution.py:544
  119.5 2.1 all-to-all-done.2
  121.6 1.0 collective-permute-start.14
  122.6 7.1 %collective-permute-done.15 = bf16[4,768,768]{2,1,0:T(8,128)(2,1)S(1)} collective-permute-done((bf16[4,768,768]{2,1,0:T(8,128)(2,1)}, bf16[4,768,768]{2,1,0:T(8,128)(2,1)S(1)}, u32[]{:S(2)}, u32[]{:S(2)}) %collective-permute-start.15) | collective-permute-done | bytes 4718624 | tf_op jit(solution)/shard_map/ppermute | solution.py:817
  129.8 3.3 %fusion.14 = (bf16[256,768]{1,0:T(8,128)(2,1)}, bf16[256,768]{1,0:T(8,128)(2,1)}, bf16[256,768]{1,0:T(8,128)(2,1)}) fusion(bf16[4,768,768]{2,1,0:T(8,128)(2,1)S(1)} %collective-permute-done.15, bf16[4,768,768]{2,1,0:T(8,128)(2,1)} %get-tuple-element.136), kind=kLoop, calls=%fused_computation.23 | loop fusion | flops 2359296 | bytes 3538944 | tf_op jit(solution)/shard_map/convert_element_type | solution.py:915
  133.0 1.6 fusion.6
  134.6 2.7 %collective-permute-done.14.refs_2_ = bf16[384,768]{1,0:T(8,128)(2,1)S(1)} collective-permute-done((bf16[384,768]{1,0:T(8,128)(2,1)S(1)}, bf16[384,768]{1,0:T(8,128)(2,1)S(1)}, u32[]{:S(2)}, u32[]{:S(2)}) %collective-permute-start.14) | collective-permute-done | bytes 589856 | tf_op jit(solution)/shard_map/ppermute | solution.py:817
  137.4 1.0 collective-permute-start.18
  138.4 4.0 %all-to-all-start.3 = ((bf16[8,48,768]{2,1,0:T(8,128)(2,1)}), bf16[8,48,768]{2,1,0:T(8,128)(2,1)S(1)}, u32[]{:S(2)}, u32[]{:S(2)}) async-start(bf16[8,48,768]{2,1,0:T(8,128)(2,1)} %bitcast.58), calls=%async_computation.3 | async-start | bytes 1179648 | tf_op jit(solution)/shard_map/all_to_all | solution.py:841
  142.9 1.0 collective-permute-start.19
  144.5 0.8 collective-permute-done.17.refs_3_
  145.4 11.2 %shard_map.199 = (f32[1024,768]{1,0:T(8,128)}, bf16[1024,256]{1,0:T(8,128)(2,1)}, f32[1,768]{1,0:T(1,128)}, bf16[192,768]{1,0:T(8,128)(2,1)}) custom-call(f32[1024,768]{1,0:T(8,128)} %get-tuple-element.107.hidden_ref, bf16[1024,768]{1,0:T(8,128)(2,1)} %cot_ref.1, f32[1,768]{1,0:T(1,128)} %broadcast_in_dim.15.gain_ref, ...), custom_call_target="tpu_custom_call" | custom-call | flops 1048576 | bytes 65536 | tf_op jit(solution)/shard_map/pallas_call | solution.py:598
  156.6 20.6 %shard_map.200 = (bf16[768,768]{1,0:T(8,128)(2,1)}, f32[512,768]{1,0:T(8,128)}, bf16[512,768]{1,0:T(8,128)(2,1)}, f32[3,32,128]{2,1,0:T(8,128)}) custom-call(bf16[1024,768]{1,0:T(8,128)(2,1)} %get-tuple-element.111.proj_ref, bf16[192,1024]{1,0:T(8,128)(2,1)} %get-tuple-element.112.kt_ref, f32[8,1024]{1,0:T(8,128)} %get-tuple-element.113.lse_ref, ...), custom_call_target="tpu_custom_call" | custom-call | flops 1048576 | bytes 65536 | tf_op jit(solution)/shard_map/pallas_call | solution.py:356
  178.0 5.9 %all-to-all-start.4 = ((bf16[8,96,768]{2,1,0:T(8,128)(2,1)}), bf16[8,96,768]{2,1,0:T(8,128)(2,1)S(1)}, u32[]{:S(2)}, u32[]{:S(2)}) async-start(bf16[8,96,768]{2,1,0:T(8,128)(2,1)} %bitcast.51), calls=%async_computation.4 | async-start | bytes 2359296 | tf_op jit(solution)/shard_map/all_to_all | solution.py:841
  183.9 1.0 fusion.9
  184.9 1.0 collective-permute-start.21
  186.0 0.9 reduce_sum.19
  187.0 0.8 fusion.16
  188.4 3.9 %bitcast_add_fusion = f32[768,768]{1,0:T(8,128)} fusion(bf16[768,768]{1,0:T(8,128)(2,1)} %collective-permute-done.18, bf16[4,768,768]{2,1,0:T(8,128)(2,1)} %copy-done.5, bf16[4,768,768]{2,1,0:T(8,128)(2,1)} %get-tuple-element.136), kind=kLoop, calls=%fused_computation.2 | loop fusion | flops 2949120 | bytes 5898240 | tf_op jit(solution)/shard_map/add | solution.py:934
  192.3 12.1 %collective-permute-done.21 = bf16[512,768]{1,0:T(8,128)(2,1)S(1)} collective-permute-done((bf16[512,768]{1,0:T(8,128)(2,1)}, bf16[512,768]{1,0:T(8,128)(2,1)S(1)}, u32[]{:S(2)}, u32[]{:S(2)}) %collective-permute-start.21) | collective-permute-done | bytes 786464 | tf_op jit(solution)/shard_map/ppermute | solution.py:817
  204.9 1.1 collective-permute-start.23
  205.9 1.2 collective-permute-done.22.other_ref
  207.2 0.9 copy-done.7
  208.1 4.5 %shard_map.201.ggain_ref = f32[1,768]{1,0:T(1,128)} custom-call(bf16[512,768]{1,0:T(8,128)(2,1)} %copy-done, bf16[512,768]{1,0:T(8,128)(2,1)} %copy-done.7, bf16[1024,768]{1,0:T(8,128)(2,1)} %x_ref.7, s32[1]{0:T(128)} %bitcast.18.low_ref), custom_call_target="tpu_custom_call" | custom-call | flops 1048576 | bytes 65536 | tf_op jit(solution)/shard_map/pallas_call | solution.py:687
  212.8 1.0 copy-done.6
  213.8 4.2 %shard_map.202 = bf16[8,112,768]{2,1,0:T(8,128)(2,1)} custom-call(bf16[8,96,768]{2,1,0:T(8,128)(2,1)} %copy-done.6, f32[16,768]{1,0:T(8,128)} %pad.19.small_ref, f32[1,768]{1,0:T(1,128)} %shard_map.201.ggain_ref), custom_call_target="tpu_custom_call" | custom-call | flops 1048576 | bytes 65536 | tf_op jit(solution)/shard_map/pallas_call | solution.py:738
  218.0 0.7 copy-done.22
  218.8 5.5 %all-to-all-start.5 = ((bf16[8,112,768]{2,1,0:T(8,128)(2,1)}), bf16[8,112,768]{2,1,0:T(8,128)(2,1)S(1)}, u32[]{:S(2)}, u32[]{:S(2)}) async-start(bf16[8,112,768]{2,1,0:T(8,128)(2,1)} %shard_map.202), calls=%async_computation.5 | async-start | bytes 2752512 | tf_op jit(solution)/shard_map/all_to_all | solution.py:841
  224.2 1.1 collective-permute-start.24
  225.3 6.0 %shard_map.203 = f32[1024,768]{1,0:T(8,128)} custom-call(bf16[512,768]{1,0:T(8,128)(2,1)} %copy-done, bf16[512,768]{1,0:T(8,128)(2,1)} %copy-done.7, bf16[1024,768]{1,0:T(8,128)(2,1)} %x_ref.7, f32[1,768]{1,0:T(1,128)} %broadcast_in_dim.14.gain_ref, f32[1024,768]{1,0:T(8,128)} %get-tuple-element.169.gh_ref, s32[1]{0:T(128)} %bitcast.18.low_ref), custom_call_target="tpu_custom_call" | custom-call | flops 1048576 | bytes 65536 | tf_op jit(solution)/shard_map/pallas_call | solution.py:702
  231.3 8.1 %collective-permute-done.24.refs_2_ = bf16[384,768]{1,0:T(8,128)(2,1)S(1)} collective-permute-done((bf16[384,768]{1,0:T(8,128)(2,1)S(1)}, bf16[384,768]{1,0:T(8,128)(2,1)S(1)}, u32[]{:S(2)}, u32[]{:S(2)}) %collective-permute-start.24) | collective-permute-done | bytes 589856 | tf_op jit(solution)/shard_map/ppermute | solution.py:817
  239.4 1.0 collective-permute-start.27
  240.9 8.5 %collective-permute-done.27 = bf16[256,768]{1,0:T(8,128)(2,1)S(1)} collective-permute-done((bf16[256,768]{1,0:T(8,128)(2,1)S(1)}, bf16[256,768]{1,0:T(8,128)(2,1)S(1)}, u32[]{:S(2)}, u32[]{:S(2)}) %collective-permute-start.27) | collective-permute-done | bytes 393248 | tf_op jit(solution)/shard_map/ppermute | solution.py:817
  249.4 3.6 %convert_add_fusion = f32[1,768,768]{2,1,0:T(8,128)} fusion(bf16[4,768,768]{2,1,0:T(8,128)(2,1)} %copy-done.5, bf16[1,256,768]{2,1,0:T(8,128)(2,1)S(1)} %bitcast.62, bf16[1,256,768]{2,1,0:T(8,128)(2,1)S(1)} %bitcast.61, bf16[1,256,768]{2,1,0:T(8,128)(2,1)} %bitcast.26, bf16[4,768,768]{2,1,0:T(8,128)(2,1)} %get-tuple-element.136), kind=kLoop, calls=%fused_computation.3 | loop fusion | flops 5898240 | bytes 5898240 | tf_op jit(solution)/shard_map/add | solution.py:960
  253.0 0.9 copy-done.19
  254.0 7.0 %shard_map.204 = bf16[1024,768]{1,0:T(8,128)(2,1)} custom-call(f32[1024,768]{1,0:T(8,128)} %get-tuple-element.107.hidden_ref, f32[1024,1]{1,0:T(8,128)} %get-tuple-element.108.gate_ref, s32[1024,1]{1,0:T(8,128)} %get-tuple-element.109.flat_ref, s32[1,1536]{1,0:T(1,128)} %broadcast_in_dim.16.ids_ref, bf16[384,768]{1,0:T(8,128)(2,1)} %bitcast.43, ...), custom_call_target="tpu_custom_call" | custom-call | flops 1048576 | bytes 65536 | tf_op jit(solution)/shard_map/pallas_call | solution.py:645
  261.0 1.5 shard_map.205
  (127 shorter events, 14.2 us)
Async XLA Ops:
  0.6 30.7 %collective-permute-start = (bf16[768,768]{1,0:T(8,128)(2,1)}, bf16[768,768]{1,0:T(8,128)(2,1)}, u32[]{:S(2)}, u32[]{:S(2)}) collective-permute-start(bf16[768,768]{1,0:T(8,128)(2,1)} %bitcast.52), channel_id=1, source_target_pairs={{0,2},{1,3},{2,0},{3,1},{4,6},{5,7},{6,4},{7,5},{8,10},{9,11},{10,... | collective-permute-start | bytes 3538952 | tf_op jit(solution)/shard_map/ppermute | solution.py:817
  5.8 8.9 %copy-start.13 = (bf16[192,768]{1,0:T(8,128)(2,1)S(1)}, bf16[192,768]{1,0:T(8,128)(2,1)}, u32[]{:S(2)}) copy-start(bf16[192,768]{1,0:T(8,128)(2,1)} %refs_4_) | copy-start | bytes 884740
  5.8 9.5 %copy-start.31 = (f32[768]{0:T(1024)S(1)}, f32[768]{0:T(1024)}, u32[]{:S(2)}) copy-start(f32[768]{0:T(1024)} %param.13) | copy-start | bytes 9220
  5.8 10.1 %copy-start.28 = (s32[1,1024]{1,0:T(1,128)S(1)}, s32[1,1024]{1,0:T(1,128)}, u32[]{:S(2)}) copy-start(s32[1,1024]{1,0:T(1,128)} %seg_ref.3) | copy-start | bytes 12292
  8.9 22.5 %all-to-all-start = ((bf16[8,48,768]{2,1,0:T(8,128)(2,1)}), bf16[8,48,768]{2,1,0:T(8,128)(2,1)S(1)}, u32[]{:S(2)}, u32[]{:S(2)}) async-start(bf16[8,48,768]{2,1,0:T(8,128)(2,1)} %bitcast.4), calls=%async_computation | async-start | bytes 1179648 | tf_op jit(solution)/shard_map/all_to_all | solution.py:841
  14.7 23.5 %collective-permute-start.2 = (bf16[192,768]{1,0:T(8,128)(2,1)S(1)}, bf16[192,768]{1,0:T(8,128)(2,1)}, u32[]{:S(2)}, u32[]{:S(2)}) collective-permute-start(bf16[192,768]{1,0:T(8,128)(2,1)S(1)} %copy-done.13), channel_id=1, source_target_pairs={{0,2},{1,3},{2,0},{3,1},{4,6},{5,7},{6,4},{7,5},{8,10},{9,11},{10,... | collective-permute-start | bytes 884744 | tf_op jit(solution)/shard_map/ppermute | solution.py:817
  16.9 16.3 %copy-start.29 = (s32[1024,1]{0,1:T(1,128)S(1)}, s32[1024,1]{0,1:T(1,128)}, u32[]{:S(2)}) copy-start(s32[1024,1]{0,1:T(1,128)} %param.21) | copy-start | bytes 12292
  16.9 16.6 %copy-start.32 = (f32[768]{0:T(1024)S(1)}, f32[768]{0:T(1024)}, u32[]{:S(2)}) copy-start(f32[768]{0:T(1024)} %param.17) | copy-start | bytes 9220
  16.9 17.3 %copy-start.30 = (bf16[768,8]{0,1:T(8,128)(2,1)S(1)}, bf16[768,8]{0,1:T(8,128)(2,1)}, u32[]{:S(2)}) copy-start(bf16[768,8]{0,1:T(8,128)(2,1)} %param.18) | copy-start | bytes 36868
  31.4 6.2 %copy-start.11 = (bf16[8,48,768]{2,1,0:T(8,128)(2,1)}, bf16[8,48,768]{2,1,0:T(8,128)(2,1)S(1)}, u32[]{:S(2)}) copy-start(bf16[8,48,768]{2,1,0:T(8,128)(2,1)S(1)} %all-to-all-done) | copy-start | bytes 1769476
  31.4 13.2 %collective-permute-start.1 = (bf16[192,1024]{1,0:T(8,128)(2,1)}, bf16[192,1024]{1,0:T(8,128)(2,1)S(1)}, u32[]{:S(2)}, u32[]{:S(2)}) collective-permute-start(bf16[192,1024]{1,0:T(8,128)(2,1)} %get-tuple-element.103.refs_0_.att_ref), channel_id=1, source_target_pairs={{0,2},{1,3},{2,0},{3,1},{4,6},{5,7},{6,4},{7,5},{8,10},{9,11},{10,... | collective-permute-start | bytes 1179656 | tf_op jit(solution)/shard_map/ppermute | solution.py:817
  33.4 4.2 %copy-start.4 = (s32[1024,1]{1,0:T(8,128)}, s32[1024,1]{1,0:T(8,128)S(1)}, u32[]{:S(2)}) copy-start(s32[1024,1]{1,0:T(8,128)S(1)} %copy.27.route_ref) | copy-start | bytes 12292
  34.4 10.7 %copy-start.12 = (bf16[192,1024]{1,0:T(8,128)(2,1)S(1)}, bf16[192,1024]{1,0:T(8,128)(2,1)}, u32[]{:S(2)}) copy-start(bf16[192,1024]{1,0:T(8,128)(2,1)} %get-tuple-element.103.refs_0_.att_ref) | copy-start | bytes 1179652
  44.6 4.9 %copy-start.21 = (bf16[192,1024]{1,0:T(8,128)(2,1)}, bf16[192,1024]{1,0:T(8,128)(2,1)S(1)}, u32[]{:S(2)}) copy-start(bf16[192,1024]{1,0:T(8,128)(2,1)S(1)} %collective-permute-done.1.refs_2_) | copy-start | bytes 1179652
  44.6 2.0 collective-permute-start.5
  44.6 2.3 collective-permute-start.6
  45.1 4.4 %collective-permute-start.3 = (bf16[192,1024]{1,0:T(8,128)(2,1)S(1)}, bf16[192,1024]{1,0:T(8,128)(2,1)S(1)}, u32[]{:S(2)}, u32[]{:S(2)}) collective-permute-start(bf16[192,1024]{1,0:T(8,128)(2,1)S(1)} %copy-done.12), channel_id=1, source_target_pairs={{0,1},{1,0},{2,3},{3,2},{4,5},{5,4},{6,7},{7,6},{8,9},{9,8},{10,11... | collective-permute-start | bytes 1179656 | tf_op jit(solution)/shard_map/ppermute | solution.py:817
  45.1 4.4 %collective-permute-start.4 = (bf16[192,1024]{1,0:T(8,128)(2,1)S(1)}, bf16[192,1024]{1,0:T(8,128)(2,1)S(1)}, u32[]{:S(2)}, u32[]{:S(2)}) collective-permute-start(bf16[192,1024]{1,0:T(8,128)(2,1)S(1)} %collective-permute-done.1.refs_2_), channel_id=1, source_target_pairs={{0,1},{1,0},{2,3},{3,2},{4,5},{5,4},{6,7},{7,6},{8,9},{9,8},{10,11... | collective-permute-start | bytes 1179656 | tf_op jit(solution)/shard_map/ppermute | solution.py:817
  45.6 20.1 %collective-permute-start.8 = (bf16[768,768]{1,0:T(8,128)(2,1)}, bf16[768,768]{1,0:T(8,128)(2,1)}, u32[]{:S(2)}, u32[]{:S(2)}) collective-permute-start(bf16[768,768]{1,0:T(8,128)(2,1)} %bitcast.53), channel_id=1, source_target_pairs={{0,1},{1,0},{2,3},{3,2},{4,5},{5,4},{6,7},{7,6},{8,9},{9,8},{10,11... | collective-permute-start | bytes 3538952 | tf_op jit(solution)/shard_map/ppermute | solution.py:817
  46.6 2.1 copy-start.26
  46.6 19.2 %collective-permute-start.9 = (bf16[768,768]{1,0:T(8,128)(2,1)}, bf16[768,768]{1,0:T(8,128)(2,1)}, u32[]{:S(2)}, u32[]{:S(2)}) collective-permute-start(bf16[768,768]{1,0:T(8,128)(2,1)} %collective-permute-done.refs_2_), channel_id=1, source_target_pairs={{0,1},{1,0},{2,3},{3,2},{4,5},{5,4},{6,7},{7,6},{8,9},{9,8},{10,11... | collective-permute-start | bytes 3538952 | tf_op jit(solution)/shard_map/ppermute | solution.py:817
  46.9 1.8 copy-start.27
  46.9 28.6 %collective-permute-start.7 = (bf16[768,768]{1,0:T(8,128)(2,1)}, bf16[768,768]{1,0:T(8,128)(2,1)}, u32[]{:S(2)}, u32[]{:S(2)}) collective-permute-start(bf16[768,768]{1,0:T(8,128)(2,1)} %bitcast.55), channel_id=1, source_target_pairs={{0,2},{1,3},{2,0},{3,1},{4,6},{5,7},{6,4},{7,5},{8,10},{9,11},{10,... | collective-permute-start | bytes 3538952 | tf_op jit(solution)/shard_map/ppermute | solution.py:817
  49.5 32.4 %copy-start.14 = (bf16[1,768,768]{2,1,0:T(8,128)(2,1)S(1)}, bf16[1,768,768]{2,1,0:T(8,128)(2,1)}, u32[]{:S(2)}) copy-start(bf16[1,768,768]{2,1,0:T(8,128)(2,1)} %param.20) | copy-start | bytes 3538948
  59.9 21.9 %all-to-all-start.1 = ((bf16[8,48,768]{2,1,0:T(8,128)(2,1)}), bf16[8,48,768]{2,1,0:T(8,128)(2,1)S(1)}, u32[]{:S(2)}, u32[]{:S(2)}) async-start(bf16[8,48,768]{2,1,0:T(8,128)(2,1)} %bitcast.60), calls=%async_computation.1 | async-start | bytes 1179648 | tf_op jit(solution)/shard_map/all_to_all | solution.py:841
  81.9 4.9 %copy-start.3 = (bf16[8,48,768]{2,1,0:T(8,128)(2,1)}, bf16[8,48,768]{2,1,0:T(8,128)(2,1)S(1)}, u32[]{:S(2)}) copy-start(bf16[8,48,768]{2,1,0:T(8,128)(2,1)S(1)} %all-to-all-done.1) | copy-start | bytes 1769476
  81.9 3.8 %collective-permute-start.10 = (bf16[768,768]{1,0:T(8,128)(2,1)S(1)}, bf16[768,768]{1,0:T(8,128)(2,1)S(1)}, u32[]{:S(2)}, u32[]{:S(2)}) collective-permute-start(bf16[768,768]{1,0:T(8,128)(2,1)S(1)} %bitcast.57), channel_id=1, source_target_pairs={{0,1},{1,0},{2,3},{3,2},{4,5},{5,4},{6,7},{7,6},{8,9},{9,8},{10,11... | collective-permute-start | bytes 3538952 | tf_op jit(solution)/shard_map/ppermute | solution.py:817
  81.9 4.9 %collective-permute-start.11 = (bf16[768,768]{1,0:T(8,128)(2,1)}, bf16[768,768]{1,0:T(8,128)(2,1)}, u32[]{:S(2)}, u32[]{:S(2)}) collective-permute-start(bf16[768,768]{1,0:T(8,128)(2,1)} %collective-permute-done.7.refs_6_), channel_id=1, source_target_pairs={{0,1},{1,0},{2,3},{3,2},{4,5},{5,4},{6,7},{7,6},{8,9},{9,8},{10,11... | collective-permute-start | bytes 3538952 | tf_op jit(solution)/shard_map/ppermute | solution.py:817
  85.7 1.1 copy-start.15
  101.7 19.9 %all-to-all-start.2 = ((bf16[8,48,768]{2,1,0:T(8,128)(2,1)}), bf16[8,48,768]{2,1,0:T(8,128)(2,1)S(1)}, u32[]{:S(2)}, u32[]{:S(2)}) async-start(bf16[8,48,768]{2,1,0:T(8,128)(2,1)} %bitcast.59), calls=%async_computation.2 | async-start | bytes 1179648 | tf_op jit(solution)/shard_map/all_to_all | solution.py:841
  106.1 1.2 collective-permute-start.12
  108.0 10.9 %collective-permute-start.13 = (f32[8,768]{1,0:T(8,128)S(1)}, f32[8,768]{1,0:T(8,128)S(1)}, u32[]{:S(2)}, u32[]{:S(2)}) collective-permute-start(f32[8,768]{1,0:T(8,128)S(1)} %slice_add_fusion), channel_id=1, source_target_pairs={{0,2},{1,3},{2,0},{3,1},{4,6},{5,7},{6,4},{7,5},{8,10},{9,11},{10,... | collective-permute-start | bytes 73736 | tf_op jit(solution)/shard_map/ppermute | solution.py:817
  121.6 20.7 %copy-start.10 = (bf16[8,48,768]{2,1,0:T(8,128)(2,1)}, bf16[8,48,768]{2,1,0:T(8,128)(2,1)S(1)}, u32[]{:S(2)}) copy-start(bf16[8,48,768]{2,1,0:T(8,128)(2,1)S(1)} %all-to-all-done.2) | copy-start | bytes 1769476
  121.6 8.1 %collective-permute-start.15 = (bf16[4,768,768]{2,1,0:T(8,128)(2,1)}, bf16[4,768,768]{2,1,0:T(8,128)(2,1)S(1)}, u32[]{:S(2)}, u32[]{:S(2)}) collective-permute-start(bf16[4,768,768]{2,1,0:T(8,128)(2,1)} %get-tuple-element.137), channel_id=1, source_target_pairs={{0,1},{1,0},{2,3},{3,2},{4,5},{5,4},{6,7},{7,6},{8,9},{9,8},{10,11... | collective-permute-start | bytes 14155784 | tf_op jit(solution)/shard_map/ppermute | solution.py:817
  121.6 15.7 %collective-permute-start.14 = (bf16[384,768]{1,0:T(8,128)(2,1)S(1)}, bf16[384,768]{1,0:T(8,128)(2,1)S(1)}, u32[]{:S(2)}, u32[]{:S(2)}) collective-permute-start(bf16[384,768]{1,0:T(8,128)(2,1)S(1)} %bitcast.46), channel_id=1, source_target_pairs={{0,2},{1,3},{2,0},{3,1},{4,6},{5,7},{6,4},{7,5},{8,10},{9,11},{10,... | collective-permute-start | bytes 1769480 | tf_op jit(solution)/shard_map/ppermute | solution.py:817
  129.8 3.3 %copy-start.5 = (bf16[4,768,768]{2,1,0:T(8,128)(2,1)}, bf16[4,768,768]{2,1,0:T(8,128)(2,1)S(1)}, u32[]{:S(2)}) copy-start(bf16[4,768,768]{2,1,0:T(8,128)(2,1)S(1)} %collective-permute-done.15) | copy-start | bytes 14155780
  137.4 8.0 %copy-start.16 = (bf16[384,768]{1,0:T(8,128)(2,1)}, bf16[384,768]{1,0:T(8,128)(2,1)S(1)}, u32[]{:S(2)}) copy-start(bf16[384,768]{1,0:T(8,128)(2,1)S(1)} %collective-permute-done.14.refs_2_) | copy-start | bytes 1769476
  137.4 39.8 %collective-permute-start.18 = (bf16[768,768]{1,0:T(8,128)(2,1)S(1)}, bf16[768,768]{1,0:T(8,128)(2,1)}, u32[]{:S(2)}, u32[]{:S(2)}) collective-permute-start(bf16[768,768]{1,0:T(8,128)(2,1)S(1)} %fusion.6), channel_id=1, source_target_pairs={{0,2},{1,3},{2,0},{3,1},{4,6},{5,7},{6,4},{7,5},{8,10},{9,11},{10,... | collective-permute-start | bytes 3538952 | tf_op jit(solution)/shard_map/ppermute | solution.py:817
  138.4 38.8 %all-to-all-start.3 = ((bf16[8,48,768]{2,1,0:T(8,128)(2,1)}), bf16[8,48,768]{2,1,0:T(8,128)(2,1)S(1)}, u32[]{:S(2)}, u32[]{:S(2)}) async-start(bf16[8,48,768]{2,1,0:T(8,128)(2,1)} %bitcast.58), calls=%async_computation.3 | async-start | bytes 1179648 | tf_op jit(solution)/shard_map/all_to_all | solution.py:841
  142.3 2.2 collective-permute-start.16
  142.4 3.0 %collective-permute-start.17 = (bf16[384,768]{1,0:T(8,128)(2,1)S(1)}, bf16[384,768]{1,0:T(8,128)(2,1)}, u32[]{:S(2)}, u32[]{:S(2)}) collective-permute-start(bf16[384,768]{1,0:T(8,128)(2,1)S(1)} %collective-permute-done.14.refs_2_), channel_id=1, source_target_pairs={{0,1},{1,0},{2,3},{3,2},{4,5},{5,4},{6,7},{7,6},{8,9},{9,8},{10,11... | collective-permute-start | bytes 1769480 | tf_op jit(solution)/shard_map/ppermute | solution.py:817
  142.9 34.3 %collective-permute-start.19 = (bf16[256,768]{1,0:T(8,128)(2,1)}, bf16[256,768]{1,0:T(8,128)(2,1)}, u32[]{:S(2)}, u32[]{:S(2)}) collective-permute-start(bf16[256,768]{1,0:T(8,128)(2,1)} %get-tuple-element.148), channel_id=1, source_target_pairs={{0,2},{1,3},{2,0},{3,1},{4,6},{5,7},{6,4},{7,5},{8,10},{9,11},{10,... | collective-permute-start | bytes 1179656 | tf_op jit(solution)/shard_map/ppermute | solution.py:817
  177.1 6.8 %copy-start.1 = (f32[512,768]{1,0:T(8,128)S(1)}, f32[512,768]{1,0:T(8,128)}, u32[]{:S(2)}) copy-start(f32[512,768]{1,0:T(8,128)} %get-tuple-element.152) | copy-start | bytes 4718596
  177.2 6.7 %collective-permute-start.20 = (bf16[512,768]{1,0:T(8,128)(2,1)}, bf16[512,768]{1,0:T(8,128)(2,1)S(1)}, u32[]{:S(2)}, u32[]{:S(2)}) collective-permute-start(bf16[512,768]{1,0:T(8,128)(2,1)} %get-tuple-element.153), channel_id=1, source_target_pairs={{0,1},{1,0},{2,3},{3,2},{4,5},{5,4},{6,7},{7,6},{8,9},{9,8},{10,11... | collective-permute-start | bytes 2359304 | tf_op jit(solution)/shard_map/ppermute | solution.py:817
  178.0 34.8 %all-to-all-start.4 = ((bf16[8,96,768]{2,1,0:T(8,128)(2,1)}), bf16[8,96,768]{2,1,0:T(8,128)(2,1)S(1)}, u32[]{:S(2)}, u32[]{:S(2)}) async-start(bf16[8,96,768]{2,1,0:T(8,128)(2,1)} %bitcast.51), calls=%async_computation.4 | async-start | bytes 2359296 | tf_op jit(solution)/shard_map/all_to_all | solution.py:841
  183.9 3.1 %copy-start.33 = (f32[1,768]{1,0:T(1,128)S(1)}, f32[1,768]{1,0:T(1,128)}, u32[]{:S(2)}) copy-start(f32[1,768]{1,0:T(1,128)} %get-tuple-element.158) | copy-start | bytes 9220
  184.9 19.5 %collective-permute-start.21 = (bf16[512,768]{1,0:T(8,128)(2,1)}, bf16[512,768]{1,0:T(8,128)(2,1)S(1)}, u32[]{:S(2)}, u32[]{:S(2)}) collective-permute-start(bf16[512,768]{1,0:T(8,128)(2,1)} %fusion.9), channel_id=1, source_target_pairs={{0,2},{1,3},{2,0},{3,1},{4,6},{5,7},{6,4},{7,5},{8,10},{9,11},{10,... | collective-permute-start | bytes 2359304 | tf_op jit(solution)/shard_map/ppermute | solution.py:817
  188.4 16.0 %copy-start.2 = (f32[512,768]{1,0:T(8,128)S(1)}, f32[512,768]{1,0:T(8,128)}, u32[]{:S(2)}) copy-start(f32[512,768]{1,0:T(8,128)} %get-tuple-element.152) | copy-start | bytes 4718596
  204.8 2.4 copy-start
  204.8 2.4 collective-permute-start.22
  204.9 13.1 %collective-permute-start.23 = (bf16[256,768]{1,0:T(8,128)(2,1)}, bf16[256,768]{1,0:T(8,128)(2,1)S(1)}, u32[]{:S(2)}, u32[]{:S(2)}) collective-permute-start(bf16[256,768]{1,0:T(8,128)(2,1)} %get-tuple-element.163), channel_id=1, source_target_pairs={{0,2},{1,3},{2,0},{3,1},{4,6},{5,7},{6,4},{7,5},{8,10},{9,11},{10,... | collective-permute-start | bytes 1179656 | tf_op jit(solution)/shard_map/ppermute | solution.py:817
  207.2 0.9 copy-start.7
  212.8 1.0 copy-start.6
  218.0 6.2 %copy-start.9 = (bf16[8,48,768]{2,1,0:T(8,128)(2,1)S(1)}, bf16[8,48,768]{2,1,0:T(8,128)(2,1)}, u32[]{:S(2)}) copy-start(bf16[8,48,768]{2,1,0:T(8,128)(2,1)} %copy-done.8) | copy-start | bytes 1769476
  218.8 42.3 %all-to-all-start.5 = ((bf16[8,112,768]{2,1,0:T(8,128)(2,1)}), bf16[8,112,768]{2,1,0:T(8,128)(2,1)S(1)}, u32[]{:S(2)}, u32[]{:S(2)}) async-start(bf16[8,112,768]{2,1,0:T(8,128)(2,1)} %shard_map.202), calls=%async_computation.5 | async-start | bytes 2752512 | tf_op jit(solution)/shard_map/all_to_all | solution.py:841
  224.2 15.2 %collective-permute-start.24 = (bf16[384,768]{1,0:T(8,128)(2,1)S(1)}, bf16[384,768]{1,0:T(8,128)(2,1)S(1)}, u32[]{:S(2)}, u32[]{:S(2)}) collective-permute-start(bf16[384,768]{1,0:T(8,128)(2,1)S(1)} %bitcast.44), channel_id=1, source_target_pairs={{0,2},{1,3},{2,0},{3,1},{4,6},{5,7},{6,4},{7,5},{8,10},{9,11},{10,... | collective-permute-start | bytes 1769480 | tf_op jit(solution)/shard_map/ppermute | solution.py:817
  225.3 14.1 %copy-start.20 = (bf16[256,768]{1,0:T(8,128)(2,1)S(1)}, bf16[256,768]{1,0:T(8,128)(2,1)}, u32[]{:S(2)}) copy-start(bf16[256,768]{1,0:T(8,128)(2,1)} %get-tuple-element.182) | copy-start | bytes 1179652
  225.3 24.1 %copy-start.23 = (bf16[256,768]{1,0:T(8,128)(2,1)S(1)}, bf16[256,768]{1,0:T(8,128)(2,1)}, u32[]{:S(2)}) copy-start(bf16[256,768]{1,0:T(8,128)(2,1)} %copy-done.22) | copy-start | bytes 1179652
  239.4 13.6 %copy-start.17 = (bf16[384,768]{1,0:T(8,128)(2,1)}, bf16[384,768]{1,0:T(8,128)(2,1)S(1)}, u32[]{:S(2)}) copy-start(bf16[384,768]{1,0:T(8,128)(2,1)S(1)} %collective-permute-done.24.refs_2_) | copy-start | bytes 1769476
  239.4 10.0 %collective-permute-start.27 = (bf16[256,768]{1,0:T(8,128)(2,1)S(1)}, bf16[256,768]{1,0:T(8,128)(2,1)S(1)}, u32[]{:S(2)}, u32[]{:S(2)}) collective-permute-start(bf16[256,768]{1,0:T(8,128)(2,1)S(1)} %copy-done.20), channel_id=1, source_target_pairs={{0,2},{1,3},{2,0},{3,1},{4,6},{5,7},{6,4},{7,5},{8,10},{9,11},{10,... | collective-permute-start | bytes 1179656 | tf_op jit(solution)/shard_map/ppermute | solution.py:817
  240.4 12.6 %collective-permute-start.25 = (bf16[384,768]{1,0:T(8,128)(2,1)S(1)}, bf16[384,768]{1,0:T(8,128)(2,1)S(1)}, u32[]{:S(2)}, u32[]{:S(2)}) collective-permute-start(bf16[384,768]{1,0:T(8,128)(2,1)S(1)} %bitcast.45), channel_id=1, source_target_pairs={{0,1},{1,0},{2,3},{3,2},{4,5},{5,4},{6,7},{7,6},{8,9},{9,8},{10,11... | collective-permute-start | bytes 1769480 | tf_op jit(solution)/shard_map/ppermute | solution.py:817
  240.4 12.6 %collective-permute-start.26 = (bf16[384,768]{1,0:T(8,128)(2,1)S(1)}, bf16[384,768]{1,0:T(8,128)(2,1)S(1)}, u32[]{:S(2)}, u32[]{:S(2)}) collective-permute-start(bf16[384,768]{1,0:T(8,128)(2,1)S(1)} %collective-permute-done.24.refs_2_), channel_id=1, source_target_pairs={{0,1},{1,0},{2,3},{3,2},{4,5},{5,4},{6,7},{7,6},{8,9},{9,8},{10,11... | collective-permute-start | bytes 1769480 | tf_op jit(solution)/shard_map/ppermute | solution.py:817
  253.0 1.0 copy-start.18
  253.0 0.9 copy-start.19
  (4 other events, 3.1 us)

commit v7 on v6

--- a/solution.py
+++ b/solution.py
@@ -956,9 +956,10 @@
     grad_input = input_grads(kept, other, tokens, gain_attn, grad_hidden1, low_bit)
     reply_far, rest_sent, grad_input = tie((reply_far, in_sent[2], grad_input))
     rest_came = swap(rest_sent, 2)
+    output = output_rows(hidden1, gate, flat_column, back_ids, gather_near(reply_far))
+    rest_came, output = tie((rest_came, output))
     in_came = jnp.concatenate([fore_came, middle_came, rest_came], 0)
     grad_w_in = pair(2, slice(0, width)) + in_came.astype(F32)
-    output = output_rows(hidden1, gate, flat_column, back_ids, gather_near(reply_far))
     if large % 16 == 0:
         grad_qkv_t, grad_proj, grad_gain_ffn, rel_row, grad_gain_attn, grad_router = final_weights(
             totals, large, inner_here, experts

time: 266 us -> 262 us (0.985)
  Pallas kernels: 103 us -> 97.3 us
    all_to_all x6, waiting for transfers between devices: 8.78 us -> 13.4 us  [exchange(): lax.all_to_all(value, 'expert', split_axis=0, concat_axis=0, tiled=True)]
    ppermute x28, waiting for transfers between devices: 64 us -> 59.5 us  [swap(): return lax.ppermute(value, 'tensor', [(i, i ^ bit) for i in range(members)])]
    pallas_call x1, Pallas kernels: 20.6 us -> 16.9 us  [attend_back(): pl.pallas_call(functools.partial(attend_back_kernel, length, heads, inner...]
    all_to_all x6, starting transfers between devices: 30.6 us -> 33.6 us  [exchange(): lax.all_to_all(value, 'expert', split_axis=0, concat_axis=0, tiled=True)]
    unnamed x70 -> x66, local copies, waits for them, and re-layouts: 6.24 us -> 6.9 us
  transfers between devices with their start and end apart: 34 -> 34, of which waited for: 18 -> 24; matrix products, arithmetic and copies ran while one was open for 12% -> 12% of each run, Pallas kernels for 33% -> 31%
where the time goes in v7:
time: 262 us; the launch traced here: 261 us
  Pallas kernels  97.3 us (37%)
  waiting for transfers between devices  72.9 us (28%)
  starting transfers between devices  50.2 us (19%)
  other arithmetic  20.3 us (8%)
  local copies, waits for them, and re-layouts  14.9 us (6%)
  matrix products  4.33 us (2%)
    ppermute x28, waiting for transfers between devices, swap(): return lax.ppermute(value, 'tensor', [(i, i ^ bit) for i in range(members)])  59.5 us
    all_to_all x6, starting transfers between devices, exchange(): lax.all_to_all(value, 'expert', split_axis=0, concat_axis=0, tiled=True)  33.6 us
    pallas_call x1, Pallas kernels, attend_back(): pl.pallas_call(functools.partial(attend_back_kernel, length, heads, inner...  16.9 us
    ppermute x28, starting transfers between devices, swap(): return lax.ppermute(value, 'tensor', [(i, i ^ bit) for i in range(members)])  16.5 us
    pallas_call x1, Pallas kernels, expert_step(): pl.pallas_call(functools.partial(expert_kernel, members, experts), grid=(...  14.9 us
    all_to_all x6, waiting for transfers between devices, exchange(): lax.all_to_all(value, 'expert', split_axis=0, concat_axis=0, tiled=True)  13.4 us
    pallas_call x1, Pallas kernels, attend(): pl.pallas_call(functools.partial(attend_kernel, length, heads, inner // h...  12.2 us
    pallas_call x1, Pallas kernels, leave_experts(): pl.pallas_call(functools.partial(leave_kernel, members), grid=(length //...  11.2 us
  transfers between devices with their start and end apart: 34, of which 24 were waited for; matrix products, arithmetic and copies ran while one was open for 12% of the time, Pallas kernels for 31%

profile of v7, /device:TPU:0, one launch (start us, length us, event | category | flops | bytes accessed | tf_op | source)
XLA Modules:
  0.0 260.7 jit_solution(986318092026724224)
XLA Ops:
  0.6 3.0 %collective-permute-start = (bf16[768,768]{1,0:T(8,128)(2,1)}, bf16[768,768]{1,0:T(8,128)(2,1)}, u32[]{:S(2)}, u32[]{:S(2)}) collective-permute-start(bf16[768,768]{1,0:T(8,128)(2,1)} %bitcast.2.refs_0_), channel_id=1, source_target_pairs={{0,2},{1,3},{2,0},{3,1},{4,6},{5,7},{6,4},{7,5},{8,10},{9,11},{10,... | collective-permute-start | bytes 3538952 | tf_op jit(solution)/shard_map/ppermute | solution.py:817
  3.8 1.2 fusion.8
  5.8 3.1 %fusion.3 = bf16[384,768]{1,0:T(8,128)(2,1)} fusion(bf16[1024,768]{1,0:T(8,128)(2,1)} %cot_ref.1, s32[1024]{0:T(1024)S(1)} %multiply_add_fusion.1, s32[384]{0:T(512)S(1)} %add.229), kind=kOutput, calls=%fused_computation.9 | convolution fusion | flops 604667904 | bytes 2168320 | tf_op jit(solution)/shard_map/dot_general | solution.py:39
  8.9 5.8 %all-to-all-start = ((bf16[8,48,768]{2,1,0:T(8,128)(2,1)}), bf16[8,48,768]{2,1,0:T(8,128)(2,1)S(1)}, u32[]{:S(2)}, u32[]{:S(2)}) async-start(bf16[8,48,768]{2,1,0:T(8,128)(2,1)} %bitcast.4), calls=%async_computation | async-start | bytes 1179648 | tf_op jit(solution)/shard_map/all_to_all | solution.py:841
  15.9 1.0 copy.25.doc_ref
  16.9 12.2 %shard_map.195 = (bf16[192,1024]{1,0:T(8,128)(2,1)}, f32[8,1024]{1,0:T(8,128)}, bf16[1024,768]{1,0:T(8,128)(2,1)}, bf16[192,1024]{1,0:T(8,128)(2,1)}, bf16[1024,768]{1,0:T(8,128)(2,1)}) custom-call(bf16[1024,768]{1,0:T(8,128)(2,1)} %x_ref.7, f32[1,768]{1,0:T(1,128)} %broadcast_in_dim.14.gain_ref, bf16[3,192,768]{2,1,0:T(8,128)(2,1)} %bitcast.41, ...), custom_call_target="tpu_custom_call" | custom-call | flops 1048576 | bytes 65536 | tf_op jit(solution)/shard_map/pallas_call | solution.py:324
  29.1 1.2 all-to-all-done
  30.8 2.1 collective-permute-start.1
  34.5 0.8 pad.17.wproj_ref
  36.6 0.9 multiply_add_fusion
  38.1 6.5 %collective-permute-done.1.refs_2_ = bf16[192,1024]{1,0:T(8,128)(2,1)S(1)} collective-permute-done((bf16[192,1024]{1,0:T(8,128)(2,1)}, bf16[192,1024]{1,0:T(8,128)(2,1)S(1)}, u32[]{:S(2)}, u32[]{:S(2)}) %collective-permute-start.1) | collective-permute-done | bytes 393248 | tf_op jit(solution)/shard_map/ppermute | solution.py:817
  45.6 1.1 collective-permute-done.5.refs_5_
  47.0 1.8 collective-permute-start.7
  48.8 0.8 copy.30.ids_ref
  49.6 0.7 copy-done.24
  50.3 0.7 copy-done.25
  51.1 8.9 %shard_map.196 = (f32[1024,768]{1,0:T(8,128)}, f32[1024,1]{1,0:T(8,128)}, bf16[384,768]{1,0:T(8,128)(2,1)}) custom-call(bf16[1024,768]{1,0:T(8,128)(2,1)} %x_ref.7, f32[1,768]{1,0:T(1,128)} %broadcast_in_dim.15.gain_ref, bf16[768,128]{1,0:T(8,128)(2,1)} %pad.16.router_ref, s32[1024,1]{1,0:T(8,128)} %copy-done.4, s32[1,1024]{1,0:T(1,128)} %add.231.flat_ref, ...), custom_call_target="tpu_custom_call" | custom-call | flops 1048576 | bytes 65536 | tf_op jit(solution)/shard_map/pallas_call | solution.py:491
  60.0 5.8 %all-to-all-start.1 = ((bf16[8,48,768]{2,1,0:T(8,128)(2,1)}), bf16[8,48,768]{2,1,0:T(8,128)(2,1)S(1)}, u32[]{:S(2)}, u32[]{:S(2)}) async-start(bf16[8,48,768]{2,1,0:T(8,128)(2,1)} %bitcast.54), calls=%async_computation.1 | async-start | bytes 1179648 | tf_op jit(solution)/shard_map/all_to_all | solution.py:841
  65.9 9.7 %collective-permute-done.7.refs_6_ = bf16[768,768]{1,0:T(8,128)(2,1)} collective-permute-done((bf16[768,768]{1,0:T(8,128)(2,1)}, bf16[768,768]{1,0:T(8,128)(2,1)}, u32[]{:S(2)}, u32[]{:S(2)}) %collective-permute-start.7) | collective-permute-done | bytes 1179680 | tf_op jit(solution)/shard_map/ppermute | solution.py:817
  75.6 6.4 %all-to-all-done.1 = bf16[8,48,768]{2,1,0:T(8,128)(2,1)S(1)} async-done(((bf16[8,48,768]{2,1,0:T(8,128)(2,1)}), bf16[8,48,768]{2,1,0:T(8,128)(2,1)S(1)}, u32[]{:S(2)}, u32[]{:S(2)}) %all-to-all-start.1) | async-done | bytes 589856 | tf_op jit(solution)/shard_map/all_to_all | solution.py:841
  82.5 4.2 %collective-permute-done.10.refs_5_ = bf16[768,768]{1,0:T(8,128)(2,1)S(1)} collective-permute-done((bf16[768,768]{1,0:T(8,128)(2,1)}, bf16[768,768]{1,0:T(8,128)(2,1)S(1)}, u32[]{:S(2)}, u32[]{:S(2)}) %collective-permute-start.10) | collective-permute-done | bytes 1179680 | tf_op jit(solution)/shard_map/ppermute | solution.py:817
  86.9 0.9 copy-done.15
  87.8 14.9 %shard_map.197 = (bf16[384,768]{1,0:T(8,128)(2,1)}, bf16[384,768]{1,0:T(8,128)(2,1)}, bf16[4,384,768]{2,1,0:T(8,128)(2,1)}, bf16[4,384,768]{2,1,0:T(8,128)(2,1)}...) custom-call(bf16[384,768]{1,0:T(8,128)(2,1)} %bitcast.39, bf16[384,768]{1,0:T(8,128)(2,1)} %bitcast.50, ...), custom_call_target="tpu_custom_call" | custom-call | flops 1048576 | bytes 65536 | tf_op jit(solution)/shard_map/pallas_call | solution.py:441
  102.7 3.5 %all-to-all-start.2 = ((bf16[8,48,768]{2,1,0:T(8,128)(2,1)}), bf16[8,48,768]{2,1,0:T(8,128)(2,1)S(1)}, u32[]{:S(2)}, u32[]{:S(2)}) async-start(bf16[8,48,768]{2,1,0:T(8,128)(2,1)} %bitcast.53), calls=%async_computation.2 | async-start | bytes 1179648 | tf_op jit(solution)/shard_map/all_to_all | solution.py:841
  106.2 0.7 slice.43
  107.1 1.1 collective-permute-done.12
  108.2 0.7 slice_add_fusion
  109.4 9.9 %shard_map.198 = (bf16[4,768,768]{2,1,0:T(8,128)(2,1)}, bf16[4,768,768]{2,1,0:T(8,128)(2,1)}) custom-call(bf16[384,768]{1,0:T(8,128)(2,1)} %bitcast.40, bf16[384,768]{1,0:T(8,128)(2,1)} %get-tuple-element.130.grads_ref, bf16[4,384,768]{2,1,0:T(8,128)(2,1)} %get-tuple-element.131.act_ref, bf16[4,384,768]{2,1,0:T(8,128)(2,1)} %get-tuple-element.132.gpre_ref), custom_call_target="tpu_custom_call" | custom-call | flops 1048576 | bytes 65536 | tf_op jit(solution)/shard_map/pallas_call | solution.py:544
  119.9 2.7 %all-to-all-done.2 = bf16[8,48,768]{2,1,0:T(8,128)(2,1)S(1)} async-done(((bf16[8,48,768]{2,1,0:T(8,128)(2,1)}), bf16[8,48,768]{2,1,0:T(8,128)(2,1)S(1)}, u32[]{:S(2)}, u32[]{:S(2)}) %all-to-all-start.2) | async-done | bytes 589856 | tf_op jit(solution)/shard_map/all_to_all | solution.py:841
  123.1 7.6 %collective-permute-done.15 = bf16[4,768,768]{2,1,0:T(8,128)(2,1)S(1)} collective-permute-done((bf16[4,768,768]{2,1,0:T(8,128)(2,1)}, bf16[4,768,768]{2,1,0:T(8,128)(2,1)S(1)}, u32[]{:S(2)}, u32[]{:S(2)}) %collective-permute-start.15) | collective-permute-done | bytes 4718624 | tf_op jit(solution)/shard_map/ppermute | solution.py:817
  130.7 3.3 %fusion.14 = (bf16[256,768]{1,0:T(8,128)(2,1)}, bf16[256,768]{1,0:T(8,128)(2,1)}, bf16[256,768]{1,0:T(8,128)(2,1)}) fusion(bf16[4,768,768]{2,1,0:T(8,128)(2,1)S(1)} %collective-permute-done.15, bf16[4,768,768]{2,1,0:T(8,128)(2,1)} %get-tuple-element.137), kind=kLoop, calls=%fused_computation.23 | loop fusion | flops 2359296 | bytes 3538944 | tf_op jit(solution)/shard_map/convert_element_type | solution.py:915
  134.1 1.6 fusion.6
  135.7 2.7 %collective-permute-done.14.refs_2_ = bf16[384,768]{1,0:T(8,128)(2,1)S(1)} collective-permute-done((bf16[384,768]{1,0:T(8,128)(2,1)S(1)}, bf16[384,768]{1,0:T(8,128)(2,1)S(1)}, u32[]{:S(2)}, u32[]{:S(2)}) %collective-permute-start.14) | collective-permute-done | bytes 589856 | tf_op jit(solution)/shard_map/ppermute | solution.py:817
  138.9 4.3 %all-to-all-start.3 = ((bf16[8,48,768]{2,1,0:T(8,128)(2,1)}), bf16[8,48,768]{2,1,0:T(8,128)(2,1)S(1)}, u32[]{:S(2)}, u32[]{:S(2)}) async-start(bf16[8,48,768]{2,1,0:T(8,128)(2,1)} %bitcast.52), calls=%async_computation.3 | async-start | bytes 1179648 | tf_op jit(solution)/shard_map/all_to_all | solution.py:841
  143.7 1.0 collective-permute-start.19
  145.4 0.8 collective-permute-done.17.refs_3_
  146.2 11.2 %shard_map.199 = (f32[1024,768]{1,0:T(8,128)}, bf16[1024,256]{1,0:T(8,128)(2,1)}, f32[1,768]{1,0:T(1,128)}, bf16[192,768]{1,0:T(8,128)(2,1)}) custom-call(f32[1024,768]{1,0:T(8,128)} %get-tuple-element.112.hidden_ref, bf16[1024,768]{1,0:T(8,128)(2,1)} %cot_ref.1, f32[1,768]{1,0:T(1,128)} %broadcast_in_dim.15.gain_ref, ...), custom_call_target="tpu_custom_call" | custom-call | flops 1048576 | bytes 65536 | tf_op jit(solution)/shard_map/pallas_call | solution.py:598
  157.4 16.9 %shard_map.200 = (bf16[768,768]{1,0:T(8,128)(2,1)}, f32[512,768]{1,0:T(8,128)}, bf16[512,768]{1,0:T(8,128)(2,1)}, f32[3,32,128]{2,1,0:T(8,128)}) custom-call(bf16[1024,768]{1,0:T(8,128)(2,1)} %get-tuple-element.99.proj_ref, bf16[192,1024]{1,0:T(8,128)(2,1)} %get-tuple-element.100.kt_ref, f32[8,1024]{1,0:T(8,128)} %get-tuple-element.101.lse_ref, ...), custom_call_target="tpu_custom_call" | custom-call | flops 1048576 | bytes 65536 | tf_op jit(solution)/shard_map/pallas_call | solution.py:356
  175.1 8.7 %all-to-all-start.4 = ((bf16[8,96,768]{2,1,0:T(8,128)(2,1)}), bf16[8,96,768]{2,1,0:T(8,128)(2,1)S(1)}, u32[]{:S(2)}, u32[]{:S(2)}) async-start(bf16[8,96,768]{2,1,0:T(8,128)(2,1)} %bitcast.51), calls=%async_computation.4 | async-start | bytes 2359296 | tf_op jit(solution)/shard_map/all_to_all | solution.py:841
  183.9 1.0 fusion.9
  184.9 0.9 collective-permute-start.21
  185.8 0.9 reduce_sum.19
  186.8 0.8 fusion.16
  188.3 3.9 %bitcast_add_fusion = f32[768,768]{1,0:T(8,128)} fusion(bf16[768,768]{1,0:T(8,128)(2,1)} %collective-permute-done.18, bf16[4,768,768]{2,1,0:T(8,128)(2,1)} %copy-done.5, bf16[4,768,768]{2,1,0:T(8,128)(2,1)} %get-tuple-element.137), kind=kLoop, calls=%fused_computation.2 | loop fusion | flops 2949120 | bytes 5898240 | tf_op jit(solution)/shard_map/add | solution.py:934
  192.1 12.3 %collective-permute-done.21 = bf16[512,768]{1,0:T(8,128)(2,1)S(1)} collective-permute-done((bf16[512,768]{1,0:T(8,128)(2,1)}, bf16[512,768]{1,0:T(8,128)(2,1)S(1)}, u32[]{:S(2)}, u32[]{:S(2)}) %collective-permute-start.21) | collective-permute-done | bytes 786464 | tf_op jit(solution)/shard_map/ppermute | solution.py:817
  204.9 0.9 collective-permute-start.23
  205.8 1.3 collective-permute-done.22.other_ref
  207.1 0.9 copy-done.7
  208.0 4.5 %shard_map.201.ggain_ref = f32[1,768]{1,0:T(1,128)} custom-call(bf16[512,768]{1,0:T(8,128)(2,1)} %copy-done, bf16[512,768]{1,0:T(8,128)(2,1)} %copy-done.7, bf16[1024,768]{1,0:T(8,128)(2,1)} %x_ref.7, s32[1]{0:T(128)} %bitcast.18.low_ref), custom_call_target="tpu_custom_call" | custom-call | flops 1048576 | bytes 65536 | tf_op jit(solution)/shard_map/pallas_call | solution.py:687
  212.7 1.0 copy-done.6
  213.7 4.2 %shard_map.202 = bf16[8,112,768]{2,1,0:T(8,128)(2,1)} custom-call(bf16[8,96,768]{2,1,0:T(8,128)(2,1)} %copy-done.6, f32[16,768]{1,0:T(8,128)} %pad.19.small_ref, f32[1,768]{1,0:T(1,128)} %shard_map.201.ggain_ref), custom_call_target="tpu_custom_call" | custom-call | flops 1048576 | bytes 65536 | tf_op jit(solution)/shard_map/pallas_call | solution.py:738
  218.0 0.7 copy-done.22
  218.7 5.5 %all-to-all-start.5 = ((bf16[8,112,768]{2,1,0:T(8,128)(2,1)}), bf16[8,112,768]{2,1,0:T(8,128)(2,1)S(1)}, u32[]{:S(2)}, u32[]{:S(2)}) async-start(bf16[8,112,768]{2,1,0:T(8,128)(2,1)} %shard_map.202), calls=%async_computation.5 | async-start | bytes 2752512 | tf_op jit(solution)/shard_map/all_to_all | solution.py:841
  224.2 0.9 collective-permute-start.24
  225.1 5.9 %shard_map.203 = f32[1024,768]{1,0:T(8,128)} custom-call(bf16[512,768]{1,0:T(8,128)(2,1)} %copy-done, bf16[512,768]{1,0:T(8,128)(2,1)} %copy-done.7, bf16[1024,768]{1,0:T(8,128)(2,1)} %x_ref.7, f32[1,768]{1,0:T(1,128)} %broadcast_in_dim.14.gain_ref, f32[1024,768]{1,0:T(8,128)} %get-tuple-element.170.gh_ref, s32[1]{0:T(128)} %bitcast.18.low_ref), custom_call_target="tpu_custom_call" | custom-call | flops 1048576 | bytes 65536 | tf_op jit(solution)/shard_map/pallas_call | solution.py:702
  231.1 8.3 %collective-permute-done.24.refs_2_ = bf16[384,768]{1,0:T(8,128)(2,1)S(1)} collective-permute-done((bf16[384,768]{1,0:T(8,128)(2,1)S(1)}, bf16[384,768]{1,0:T(8,128)(2,1)S(1)}, u32[]{:S(2)}, u32[]{:S(2)}) %collective-permute-start.24) | collective-permute-done | bytes 589856 | tf_op jit(solution)/shard_map/ppermute | solution.py:817
  239.9 0.9 collective-permute-start.25
  241.4 0.8 collective-permute-done.27.refs_3_
  242.2 0.8 copy-done.19
  243.0 7.0 %shard_map.204 = bf16[1024,768]{1,0:T(8,128)(2,1)} custom-call(f32[1024,768]{1,0:T(8,128)} %get-tuple-element.112.hidden_ref, f32[1024,1]{1,0:T(8,128)} %get-tuple-element.172.gate_ref, s32[1024,1]{1,0:T(8,128)} %get-tuple-element.113.flat_ref, s32[1,1536]{1,0:T(1,128)} %broadcast_in_dim.16.ids_ref, bf16[384,768]{1,0:T(8,128)(2,1)} %bitcast.43, ...), custom_call_target="tpu_custom_call" | custom-call | flops 1048576 | bytes 65536 | tf_op jit(solution)/shard_map/pallas_call | solution.py:645
  250.1 0.8 collective-permute-done.25
  250.9 3.5 %convert_add_fusion = f32[1,768,768]{2,1,0:T(8,128)} fusion(bf16[4,768,768]{2,1,0:T(8,128)(2,1)} %copy-done.5, bf16[1,256,768]{2,1,0:T(8,128)(2,1)S(1)} %bitcast.56, bf16[1,256,768]{2,1,0:T(8,128)(2,1)S(1)} %bitcast.55, bf16[1,256,768]{2,1,0:T(8,128)(2,1)} %bitcast.26, bf16[4,768,768]{2,1,0:T(8,128)(2,1)} %get-tuple-element.137), kind=kLoop, calls=%fused_computation.3 | loop fusion | flops 5898240 | bytes 5898240 | tf_op jit(solution)/shard_map/add | solution.py:962
  254.4 2.8 %all-to-all-done.5.totals_ref = bf16[8,112,768]{2,1,0:T(8,128)(2,1)S(1)} async-done(((bf16[8,112,768]{2,1,0:T(8,128)(2,1)}), bf16[8,112,768]{2,1,0:T(8,128)(2,1)S(1)}, u32[]{:S(2)}, u32[]{:S(2)}) %all-to-all-start.5) | async-done | bytes 1376288 | tf_op jit(solution)/shard_map/all_to_all | solution.py:841
  257.3 1.5 shard_map.205
  (123 shorter events, 16.8 us)
Async XLA Ops:
  0.6 30.1 %collective-permute-start = (bf16[768,768]{1,0:T(8,128)(2,1)}, bf16[768,768]{1,0:T(8,128)(2,1)}, u32[]{:S(2)}, u32[]{:S(2)}) collective-permute-start(bf16[768,768]{1,0:T(8,128)(2,1)} %bitcast.2.refs_0_), channel_id=1, source_target_pairs={{0,2},{1,3},{2,0},{3,1},{4,6},{5,7},{6,4},{7,5},{8,10},{9,11},{10,... | collective-permute-start | bytes 3538952 | tf_op jit(solution)/shard_map/ppermute | solution.py:817
  5.8 8.9 %copy-start.13 = (bf16[192,768]{1,0:T(8,128)(2,1)S(1)}, bf16[192,768]{1,0:T(8,128)(2,1)}, u32[]{:S(2)}) copy-start(bf16[192,768]{1,0:T(8,128)(2,1)} %refs_4_) | copy-start | bytes 884740
  5.8 9.5 %copy-start.29 = (f32[768]{0:T(1024)S(1)}, f32[768]{0:T(1024)}, u32[]{:S(2)}) copy-start(f32[768]{0:T(1024)} %param.13) | copy-start | bytes 9220
  5.8 10.1 %copy-start.26 = (s32[1,1024]{1,0:T(1,128)S(1)}, s32[1,1024]{1,0:T(1,128)}, u32[]{:S(2)}) copy-start(s32[1,1024]{1,0:T(1,128)} %seg_ref.3) | copy-start | bytes 12292
  8.9 21.4 %all-to-all-start = ((bf16[8,48,768]{2,1,0:T(8,128)(2,1)}), bf16[8,48,768]{2,1,0:T(8,128)(2,1)S(1)}, u32[]{:S(2)}, u32[]{:S(2)}) async-start(bf16[8,48,768]{2,1,0:T(8,128)(2,1)} %bitcast.4), calls=%async_computation | async-start | bytes 1179648 | tf_op jit(solution)/shard_map/all_to_all | solution.py:841
  14.7 23.4 %collective-permute-start.2 = (bf16[192,768]{1,0:T(8,128)(2,1)S(1)}, bf16[192,768]{1,0:T(8,128)(2,1)}, u32[]{:S(2)}, u32[]{:S(2)}) collective-permute-start(bf16[192,768]{1,0:T(8,128)(2,1)S(1)} %copy-done.13), channel_id=1, source_target_pairs={{0,2},{1,3},{2,0},{3,1},{4,6},{5,7},{6,4},{7,5},{8,10},{9,11},{10,... | collective-permute-start | bytes 884744 | tf_op jit(solution)/shard_map/ppermute | solution.py:817
  16.9 16.3 %copy-start.27 = (s32[1024,1]{0,1:T(1,128)S(1)}, s32[1024,1]{0,1:T(1,128)}, u32[]{:S(2)}) copy-start(s32[1024,1]{0,1:T(1,128)} %param.21) | copy-start | bytes 12292
  16.9 17.4 %copy-start.28 = (bf16[768,8]{0,1:T(8,128)(2,1)S(1)}, bf16[768,8]{0,1:T(8,128)(2,1)}, u32[]{:S(2)}) copy-start(bf16[768,8]{0,1:T(8,128)(2,1)} %param.18) | copy-start | bytes 36868
  29.1 6.9 %copy-start.30 = (f32[768]{0:T(1024)S(1)}, f32[768]{0:T(1024)}, u32[]{:S(2)}) copy-start(f32[768]{0:T(1024)} %param.17) | copy-start | bytes 9220
  30.3 7.1 %copy-start.11 = (bf16[8,48,768]{2,1,0:T(8,128)(2,1)}, bf16[8,48,768]{2,1,0:T(8,128)(2,1)S(1)}, u32[]{:S(2)}) copy-start(bf16[8,48,768]{2,1,0:T(8,128)(2,1)S(1)} %all-to-all-done) | copy-start | bytes 1769476
  30.8 13.8 %collective-permute-start.1 = (bf16[192,1024]{1,0:T(8,128)(2,1)}, bf16[192,1024]{1,0:T(8,128)(2,1)S(1)}, u32[]{:S(2)}, u32[]{:S(2)}) collective-permute-start(bf16[192,1024]{1,0:T(8,128)(2,1)} %get-tuple-element.108.refs_0_.att_ref), channel_id=1, source_target_pairs={{0,2},{1,3},{2,0},{3,1},{4,6},{5,7},{6,4},{7,5},{8,10},{9,11},{10,... | collective-permute-start | bytes 1179656 | tf_op jit(solution)/shard_map/ppermute | solution.py:817
  33.4 4.0 %copy-start.4 = (s32[1024,1]{1,0:T(8,128)}, s32[1024,1]{1,0:T(8,128)S(1)}, u32[]{:S(2)}) copy-start(s32[1024,1]{1,0:T(8,128)S(1)} %copy.27.route_ref) | copy-start | bytes 12292
  34.3 10.8 %copy-start.12 = (bf16[192,1024]{1,0:T(8,128)(2,1)S(1)}, bf16[192,1024]{1,0:T(8,128)(2,1)}, u32[]{:S(2)}) copy-start(bf16[192,1024]{1,0:T(8,128)(2,1)} %get-tuple-element.108.refs_0_.att_ref) | copy-start | bytes 1179652
  44.6 5.0 %copy-start.21 = (bf16[192,1024]{1,0:T(8,128)(2,1)}, bf16[192,1024]{1,0:T(8,128)(2,1)S(1)}, u32[]{:S(2)}) copy-start(bf16[192,1024]{1,0:T(8,128)(2,1)S(1)} %collective-permute-done.1.refs_2_) | copy-start | bytes 1179652
  44.6 2.1 collective-permute-start.5
  44.6 2.4 collective-permute-start.6
  45.1 4.5 %collective-permute-start.3 = (bf16[192,1024]{1,0:T(8,128)(2,1)S(1)}, bf16[192,1024]{1,0:T(8,128)(2,1)S(1)}, u32[]{:S(2)}, u32[]{:S(2)}) collective-permute-start(bf16[192,1024]{1,0:T(8,128)(2,1)S(1)} %copy-done.12), channel_id=1, source_target_pairs={{0,1},{1,0},{2,3},{3,2},{4,5},{5,4},{6,7},{7,6},{8,9},{9,8},{10,11... | collective-permute-start | bytes 1179656 | tf_op jit(solution)/shard_map/ppermute | solution.py:817
  45.1 4.5 %collective-permute-start.4 = (bf16[192,1024]{1,0:T(8,128)(2,1)S(1)}, bf16[192,1024]{1,0:T(8,128)(2,1)S(1)}, u32[]{:S(2)}, u32[]{:S(2)}) collective-permute-start(bf16[192,1024]{1,0:T(8,128)(2,1)S(1)} %collective-permute-done.1.refs_2_), channel_id=1, source_target_pairs={{0,1},{1,0},{2,3},{3,2},{4,5},{5,4},{6,7},{7,6},{8,9},{9,8},{10,11... | collective-permute-start | bytes 1179656 | tf_op jit(solution)/shard_map/ppermute | solution.py:817
  45.6 20.2 %collective-permute-start.8 = (bf16[768,768]{1,0:T(8,128)(2,1)}, bf16[768,768]{1,0:T(8,128)(2,1)}, u32[]{:S(2)}, u32[]{:S(2)}) collective-permute-start(bf16[768,768]{1,0:T(8,128)(2,1)} %bitcast.2.refs_0_), channel_id=1, source_target_pairs={{0,1},{1,0},{2,3},{3,2},{4,5},{5,4},{6,7},{7,6},{8,9},{9,8},{10,11... | collective-permute-start | bytes 3538952 | tf_op jit(solution)/shard_map/ppermute | solution.py:817
  46.7 19.1 %collective-permute-start.9 = (bf16[768,768]{1,0:T(8,128)(2,1)}, bf16[768,768]{1,0:T(8,128)(2,1)S(1)}, u32[]{:S(2)}, u32[]{:S(2)}) collective-permute-start(bf16[768,768]{1,0:T(8,128)(2,1)} %collective-permute-done.refs_2_), channel_id=1, source_target_pairs={{0,1},{1,0},{2,3},{3,2},{4,5},{5,4},{6,7},{7,6},{8,9},{9,8},{10,11... | collective-permute-start | bytes 3538952 | tf_op jit(solution)/shard_map/ppermute | solution.py:817
  47.0 28.6 %collective-permute-start.7 = (bf16[768,768]{1,0:T(8,128)(2,1)}, bf16[768,768]{1,0:T(8,128)(2,1)}, u32[]{:S(2)}, u32[]{:S(2)}) collective-permute-start(bf16[768,768]{1,0:T(8,128)(2,1)} %bitcast.6.refs_4_), channel_id=1, source_target_pairs={{0,2},{1,3},{2,0},{3,1},{4,6},{5,7},{6,4},{7,5},{8,10},{9,11},{10,... | collective-permute-start | bytes 3538952 | tf_op jit(solution)/shard_map/ppermute | solution.py:817
  49.6 0.7 copy-start.24
  60.0 22.0 %all-to-all-start.1 = ((bf16[8,48,768]{2,1,0:T(8,128)(2,1)}), bf16[8,48,768]{2,1,0:T(8,128)(2,1)S(1)}, u32[]{:S(2)}, u32[]{:S(2)}) async-start(bf16[8,48,768]{2,1,0:T(8,128)(2,1)} %bitcast.54), calls=%async_computation.1 | async-start | bytes 1179648 | tf_op jit(solution)/shard_map/all_to_all | solution.py:841
  65.8 21.0 %copy-start.14 = (bf16[768,768]{1,0:T(8,128)(2,1)}, bf16[768,768]{1,0:T(8,128)(2,1)S(1)}, u32[]{:S(2)}) copy-start(bf16[768,768]{1,0:T(8,128)(2,1)S(1)} %collective-permute-done.9.refs_3_) | copy-start | bytes 3538948
  82.0 4.9 %copy-start.3 = (bf16[8,48,768]{2,1,0:T(8,128)(2,1)}, bf16[8,48,768]{2,1,0:T(8,128)(2,1)S(1)}, u32[]{:S(2)}) copy-start(bf16[8,48,768]{2,1,0:T(8,128)(2,1)S(1)} %all-to-all-done.1) | copy-start | bytes 1769476
  82.0 4.7 %collective-permute-start.10 = (bf16[768,768]{1,0:T(8,128)(2,1)}, bf16[768,768]{1,0:T(8,128)(2,1)S(1)}, u32[]{:S(2)}, u32[]{:S(2)}) collective-permute-start(bf16[768,768]{1,0:T(8,128)(2,1)} %bitcast.6.refs_4_), channel_id=1, source_target_pairs={{0,1},{1,0},{2,3},{3,2},{4,5},{5,4},{6,7},{7,6},{8,9},{9,8},{10,11... | collective-permute-start | bytes 3538952 | tf_op jit(solution)/shard_map/ppermute | solution.py:817
  82.0 4.9 %collective-permute-start.11 = (bf16[768,768]{1,0:T(8,128)(2,1)}, bf16[768,768]{1,0:T(8,128)(2,1)}, u32[]{:S(2)}, u32[]{:S(2)}) collective-permute-start(bf16[768,768]{1,0:T(8,128)(2,1)} %collective-permute-done.7.refs_6_), channel_id=1, source_target_pairs={{0,1},{1,0},{2,3},{3,2},{4,5},{5,4},{6,7},{7,6},{8,9},{9,8},{10,11... | collective-permute-start | bytes 3538952 | tf_op jit(solution)/shard_map/ppermute | solution.py:817
  86.7 1.1 copy-start.15
  102.7 19.9 %all-to-all-start.2 = ((bf16[8,48,768]{2,1,0:T(8,128)(2,1)}), bf16[8,48,768]{2,1,0:T(8,128)(2,1)S(1)}, u32[]{:S(2)}, u32[]{:S(2)}) async-start(bf16[8,48,768]{2,1,0:T(8,128)(2,1)} %bitcast.53), calls=%async_computation.2 | async-start | bytes 1179648 | tf_op jit(solution)/shard_map/all_to_all | solution.py:841
  107.0 1.2 collective-permute-start.12
  108.9 10.4 %collective-permute-start.13 = (f32[8,768]{1,0:T(8,128)S(1)}, f32[8,768]{1,0:T(8,128)S(1)}, u32[]{:S(2)}, u32[]{:S(2)}) collective-permute-start(f32[8,768]{1,0:T(8,128)S(1)} %slice_add_fusion), channel_id=1, source_target_pairs={{0,2},{1,3},{2,0},{3,1},{4,6},{5,7},{6,4},{7,5},{8,10},{9,11},{10,... | collective-permute-start | bytes 73736 | tf_op jit(solution)/shard_map/ppermute | solution.py:817
  122.6 20.5 %copy-start.10 = (bf16[8,48,768]{2,1,0:T(8,128)(2,1)}, bf16[8,48,768]{2,1,0:T(8,128)(2,1)S(1)}, u32[]{:S(2)}) copy-start(bf16[8,48,768]{2,1,0:T(8,128)(2,1)S(1)} %all-to-all-done.2) | copy-start | bytes 1769476
  122.6 8.1 %collective-permute-start.15 = (bf16[4,768,768]{2,1,0:T(8,128)(2,1)}, bf16[4,768,768]{2,1,0:T(8,128)(2,1)S(1)}, u32[]{:S(2)}, u32[]{:S(2)}) collective-permute-start(bf16[4,768,768]{2,1,0:T(8,128)(2,1)} %get-tuple-element.138), channel_id=1, source_target_pairs={{0,1},{1,0},{2,3},{3,2},{4,5},{5,4},{6,7},{7,6},{8,9},{9,8},{10,11... | collective-permute-start | bytes 14155784 | tf_op jit(solution)/shard_map/ppermute | solution.py:817
  122.6 15.7 %collective-permute-start.14 = (bf16[384,768]{1,0:T(8,128)(2,1)S(1)}, bf16[384,768]{1,0:T(8,128)(2,1)S(1)}, u32[]{:S(2)}, u32[]{:S(2)}) collective-permute-start(bf16[384,768]{1,0:T(8,128)(2,1)S(1)} %bitcast.46), channel_id=1, source_target_pairs={{0,2},{1,3},{2,0},{3,1},{4,6},{5,7},{6,4},{7,5},{8,10},{9,11},{10,... | collective-permute-start | bytes 1769480 | tf_op jit(solution)/shard_map/ppermute | solution.py:817
  130.7 3.3 %copy-start.5 = (bf16[4,768,768]{2,1,0:T(8,128)(2,1)}, bf16[4,768,768]{2,1,0:T(8,128)(2,1)S(1)}, u32[]{:S(2)}) copy-start(bf16[4,768,768]{2,1,0:T(8,128)(2,1)S(1)} %collective-permute-done.15) | copy-start | bytes 14155780
  138.4 7.8 %copy-start.16 = (bf16[384,768]{1,0:T(8,128)(2,1)}, bf16[384,768]{1,0:T(8,128)(2,1)S(1)}, u32[]{:S(2)}) copy-start(bf16[384,768]{1,0:T(8,128)(2,1)S(1)} %collective-permute-done.14.refs_2_) | copy-start | bytes 1769476
  138.4 36.1 %collective-permute-start.18 = (bf16[768,768]{1,0:T(8,128)(2,1)S(1)}, bf16[768,768]{1,0:T(8,128)(2,1)}, u32[]{:S(2)}, u32[]{:S(2)}) collective-permute-start(bf16[768,768]{1,0:T(8,128)(2,1)S(1)} %fusion.6), channel_id=1, source_target_pairs={{0,2},{1,3},{2,0},{3,1},{4,6},{5,7},{6,4},{7,5},{8,10},{9,11},{10,... | collective-permute-start | bytes 3538952 | tf_op jit(solution)/shard_map/ppermute | solution.py:817
  138.9 35.4 %all-to-all-start.3 = ((bf16[8,48,768]{2,1,0:T(8,128)(2,1)}), bf16[8,48,768]{2,1,0:T(8,128)(2,1)S(1)}, u32[]{:S(2)}, u32[]{:S(2)}) async-start(bf16[8,48,768]{2,1,0:T(8,128)(2,1)} %bitcast.52), calls=%async_computation.3 | async-start | bytes 1179648 | tf_op jit(solution)/shard_map/all_to_all | solution.py:841
  143.2 2.2 collective-permute-start.16
  143.2 3.0 %collective-permute-start.17 = (bf16[384,768]{1,0:T(8,128)(2,1)S(1)}, bf16[384,768]{1,0:T(8,128)(2,1)}, u32[]{:S(2)}, u32[]{:S(2)}) collective-permute-start(bf16[384,768]{1,0:T(8,128)(2,1)S(1)} %collective-permute-done.14.refs_2_), channel_id=1, source_target_pairs={{0,1},{1,0},{2,3},{3,2},{4,5},{5,4},{6,7},{7,6},{8,9},{9,8},{10,11... | collective-permute-start | bytes 1769480 | tf_op jit(solution)/shard_map/ppermute | solution.py:817
  143.7 30.8 %collective-permute-start.19 = (bf16[256,768]{1,0:T(8,128)(2,1)}, bf16[256,768]{1,0:T(8,128)(2,1)}, u32[]{:S(2)}, u32[]{:S(2)}) collective-permute-start(bf16[256,768]{1,0:T(8,128)(2,1)} %get-tuple-element.149), channel_id=1, source_target_pairs={{0,2},{1,3},{2,0},{3,1},{4,6},{5,7},{6,4},{7,5},{8,10},{9,11},{10,... | collective-permute-start | bytes 1179656 | tf_op jit(solution)/shard_map/ppermute | solution.py:817
  174.3 9.5 %copy-start.1 = (f32[512,768]{1,0:T(8,128)S(1)}, f32[512,768]{1,0:T(8,128)}, u32[]{:S(2)}) copy-start(f32[512,768]{1,0:T(8,128)} %get-tuple-element.153) | copy-start | bytes 4718596
  174.3 0.8 copy-start.8
  174.5 9.3 %collective-permute-start.20 = (bf16[512,768]{1,0:T(8,128)(2,1)}, bf16[512,768]{1,0:T(8,128)(2,1)S(1)}, u32[]{:S(2)}, u32[]{:S(2)}) collective-permute-start(bf16[512,768]{1,0:T(8,128)(2,1)} %get-tuple-element.154), channel_id=1, source_target_pairs={{0,1},{1,0},{2,3},{3,2},{4,5},{5,4},{6,7},{7,6},{8,9},{9,8},{10,11... | collective-permute-start | bytes 2359304 | tf_op jit(solution)/shard_map/ppermute | solution.py:817
  175.1 37.6 %all-to-all-start.4 = ((bf16[8,96,768]{2,1,0:T(8,128)(2,1)}), bf16[8,96,768]{2,1,0:T(8,128)(2,1)S(1)}, u32[]{:S(2)}, u32[]{:S(2)}) async-start(bf16[8,96,768]{2,1,0:T(8,128)(2,1)} %bitcast.51), calls=%async_computation.4 | async-start | bytes 2359296 | tf_op jit(solution)/shard_map/all_to_all | solution.py:841
  183.8 3.0 %copy-start.31 = (f32[1,768]{1,0:T(1,128)S(1)}, f32[1,768]{1,0:T(1,128)}, u32[]{:S(2)}) copy-start(f32[1,768]{1,0:T(1,128)} %get-tuple-element.159) | copy-start | bytes 9220
  184.9 19.5 %collective-permute-start.21 = (bf16[512,768]{1,0:T(8,128)(2,1)}, bf16[512,768]{1,0:T(8,128)(2,1)S(1)}, u32[]{:S(2)}, u32[]{:S(2)}) collective-permute-start(bf16[512,768]{1,0:T(8,128)(2,1)} %fusion.9), channel_id=1, source_target_pairs={{0,2},{1,3},{2,0},{3,1},{4,6},{5,7},{6,4},{7,5},{8,10},{9,11},{10,... | collective-permute-start | bytes 2359304 | tf_op jit(solution)/shard_map/ppermute | solution.py:817
  188.3 16.2 %copy-start.2 = (f32[512,768]{1,0:T(8,128)S(1)}, f32[512,768]{1,0:T(8,128)}, u32[]{:S(2)}) copy-start(f32[512,768]{1,0:T(8,128)} %get-tuple-element.153) | copy-start | bytes 4718596
  204.8 2.4 copy-start
  204.8 2.4 collective-permute-start.22
  204.9 13.1 %collective-permute-start.23 = (bf16[256,768]{1,0:T(8,128)(2,1)}, bf16[256,768]{1,0:T(8,128)(2,1)S(1)}, u32[]{:S(2)}, u32[]{:S(2)}) collective-permute-start(bf16[256,768]{1,0:T(8,128)(2,1)} %get-tuple-element.164), channel_id=1, source_target_pairs={{0,2},{1,3},{2,0},{3,1},{4,6},{5,7},{6,4},{7,5},{8,10},{9,11},{10,... | collective-permute-start | bytes 1179656 | tf_op jit(solution)/shard_map/ppermute | solution.py:817
  207.1 0.9 copy-start.7
  212.7 1.0 copy-start.6
  218.0 6.2 %copy-start.9 = (bf16[8,48,768]{2,1,0:T(8,128)(2,1)S(1)}, bf16[8,48,768]{2,1,0:T(8,128)(2,1)}, u32[]{:S(2)}) copy-start(bf16[8,48,768]{2,1,0:T(8,128)(2,1)} %copy-done.8) | copy-start | bytes 1769476
  218.7 38.6 %all-to-all-start.5 = ((bf16[8,112,768]{2,1,0:T(8,128)(2,1)}), bf16[8,112,768]{2,1,0:T(8,128)(2,1)S(1)}, u32[]{:S(2)}, u32[]{:S(2)}) async-start(bf16[8,112,768]{2,1,0:T(8,128)(2,1)} %shard_map.202), calls=%async_computation.5 | async-start | bytes 2752512 | tf_op jit(solution)/shard_map/all_to_all | solution.py:841
  224.2 15.2 %collective-permute-start.24 = (bf16[384,768]{1,0:T(8,128)(2,1)S(1)}, bf16[384,768]{1,0:T(8,128)(2,1)S(1)}, u32[]{:S(2)}, u32[]{:S(2)}) collective-permute-start(bf16[384,768]{1,0:T(8,128)(2,1)S(1)} %bitcast.44), channel_id=1, source_target_pairs={{0,2},{1,3},{2,0},{3,1},{4,6},{5,7},{6,4},{7,5},{8,10},{9,11},{10,... | collective-permute-start | bytes 1769480 | tf_op jit(solution)/shard_map/ppermute | solution.py:817
  225.1 14.7 %copy-start.20 = (bf16[256,768]{1,0:T(8,128)(2,1)S(1)}, bf16[256,768]{1,0:T(8,128)(2,1)}, u32[]{:S(2)}) copy-start(bf16[256,768]{1,0:T(8,128)(2,1)} %get-tuple-element.171) | copy-start | bytes 1179652
  239.4 3.7 %copy-start.17 = (bf16[384,768]{1,0:T(8,128)(2,1)}, bf16[384,768]{1,0:T(8,128)(2,1)S(1)}, u32[]{:S(2)}) copy-start(bf16[384,768]{1,0:T(8,128)(2,1)S(1)} %collective-permute-done.24.refs_2_) | copy-start | bytes 1769476
  239.4 2.0 collective-permute-start.26
  239.4 2.8 %collective-permute-start.27 = (bf16[384,768]{1,0:T(8,128)(2,1)S(1)}, bf16[384,768]{1,0:T(8,128)(2,1)S(1)}, u32[]{:S(2)}, u32[]{:S(2)}) collective-permute-start(bf16[384,768]{1,0:T(8,128)(2,1)S(1)} %collective-permute-done.24.refs_2_), channel_id=1, source_target_pairs={{0,1},{1,0},{2,3},{3,2},{4,5},{5,4},{6,7},{7,6},{8,9},{9,8},{10,11... | collective-permute-start | bytes 1769480 | tf_op jit(solution)/shard_map/ppermute | solution.py:817
  239.9 11.0 %collective-permute-start.25 = (bf16[256,768]{1,0:T(8,128)(2,1)S(1)}, bf16[256,768]{1,0:T(8,128)(2,1)S(1)}, u32[]{:S(2)}, u32[]{:S(2)}) collective-permute-start(bf16[256,768]{1,0:T(8,128)(2,1)S(1)} %copy-done.20), channel_id=1, source_target_pairs={{0,2},{1,3},{2,0},{3,1},{4,6},{5,7},{6,4},{7,5},{8,10},{9,11},{10,... | collective-permute-start | bytes 1179656 | tf_op jit(solution)/shard_map/ppermute | solution.py:817
  241.4 1.7 copy-start.18
  242.2 0.8 copy-start.19
  243.0 7.9 %copy-start.23 = (bf16[256,768]{1,0:T(8,128)(2,1)S(1)}, bf16[256,768]{1,0:T(8,128)(2,1)}, u32[]{:S(2)}) copy-start(bf16[256,768]{1,0:T(8,128)(2,1)} %copy-done.22) | copy-start | bytes 1179652
  (2 other events, 1.5 us)
